TPU v7x, 32 devices: a whole 2x2x4 slice. The times are simulated.
32 devices in a mesh: dp: 16 (over z, y, core), tensor: 2 (over x).
Axes of the slice: x: 2, y: 2, z: 4, core: 2. Of those that a mesh axis runs over, the one named last changes fastest.
Arguments:
- tokens: bfloat16 [49152, 1024], P(('dp', 'tensor')), may hold values from -6 to 6
- lengths: int32 [48], replicated, may hold values from 1 to 1024, 36864 in all
- order: int32 [48], replicated, may hold values from 0 to 47, each once
- gain_attn: float32 [1024], replicated, may hold values from 0.25 to 1.75
- w_qkv: bfloat16 [1024, 3, 1024], P(None, None, 'tensor'), may hold values from -0.1875 to 0.1875
- w_out: bfloat16 [1024, 1024], P('tensor'), may hold values from -0.75 to 0.75
- gain_mlp: float32 [1024], replicated, may hold values from 0.25 to 1.75
- w_in: bfloat16 [1024, 2, 2624], P(None, None, 'tensor'), may hold values from -0.1875 to 0.1875
- w_down: bfloat16 [2624, 1024], P('tensor'), may hold values from -0.25 to 0.25
- cotangent: bfloat16 [49152, 1024], P(('dp', 'tensor')), may hold values from -6 to 6
Outputs:
- output: bfloat16 [49152, 1024], P(('dp', 'tensor'))
- input_grad: float32 [49152, 1024], P(('dp', 'tensor'))
- grad_gain_attn: float32 [1024], replicated
- grad_w_qkv: float32 [1024, 3, 1024], P(None, None, 'tensor')
- grad_w_out: float32 [1024, 1024], P('tensor')
- grad_gain_mlp: float32 [1024], replicated
- grad_w_in: float32 [1024, 2, 2624], P(None, None, 'tensor')
- grad_w_down: float32 [2624, 1024], P('tensor')
Inputs may be any that keep to these rules, and one draw needn't show every extreme that they name: The lengths sum to 36864 and the largest equals 1024. `order`: each sequence number appears exactly once.
All inputs are finite; a program needn't handle non-finite values.
Results may differ from a plain program's by a relative error of at most 0.02.
Values may be sent and summed in bfloat16 or wider, within the bound.
A program may use at most 320 MiB of HBM per device.

v0:
```python
import jax
import jax.numpy as jnp
from jax import lax
from jax.sharding import PartitionSpec as P

HEAD_DIM = 64
HALF = 64
MAXLEN = 1024
QBLOCK = 512


def layer_norm(values, gain):
    center = values - jnp.mean(values, -1, keepdims=True)
    spread = jnp.mean(center * center, -1, keepdims=True)
    return center * lax.rsqrt(spread + 1e-05) * gain


def gelu_gate(lifted):
    return jax.nn.gelu(lifted[:, 0], approximate=False) * lifted[:, 1]


def contract_rows(left, right):
    return lax.dot_general(
        left, right, (((0,), (0,)), ((), ())), preferred_element_type=jnp.float32
    )


def contract_cols(left, right):
    return lax.dot_general(
        left, right, (((1,), (1,)), ((), ())), preferred_element_type=jnp.float32
    )


def allowed_pairs(offset, length):
    query_pos = offset + jnp.arange(QBLOCK, dtype=jnp.int32)
    key_pos = offset - HALF + jnp.arange(QBLOCK + 2 * HALF, dtype=jnp.int32)
    nearby = jnp.abs(query_pos[:, None] - key_pos[None, :]) <= HALF
    inside = (key_pos >= 0) & (key_pos < MAXLEN)
    living = (key_pos[None, :] < length) | (query_pos[:, None] == key_pos[None, :])
    return nearby & inside[None, :] & living


def band_forward(queries, keyset, values, length):
    scale_qk = HEAD_DIM ** (-0.5)
    pad_width = ((HALF, HALF), (0, 0), (0, 0))
    keys_pad = jnp.pad(keyset, pad_width)
    values_pad = jnp.pad(values, pad_width)
    window = QBLOCK + 2 * HALF

    def one_block(block_id):
        offset = block_id * QBLOCK
        query_blk = lax.dynamic_slice_in_dim(queries, offset, QBLOCK, 0)
        keys_blk = lax.dynamic_slice_in_dim(keys_pad, offset, window, 0)
        values_blk = lax.dynamic_slice_in_dim(values_pad, offset, window, 0)
        scores = (
            jnp.einsum("qhd,khd->hqk", query_blk, keys_blk, preferred_element_type=jnp.float32)
            * scale_qk
        )
        scores = jnp.where(allowed_pairs(offset, length)[None], scores, -1e30)
        row_max = jnp.max(scores, -1, keepdims=True)
        expons = jnp.exp(scores - row_max)
        summed = jnp.sum(expons, -1, keepdims=True)
        attn_prob = (expons / summed).astype(jnp.bfloat16)
        attended = jnp.einsum(
            "hqk,khd->qhd", attn_prob, values_blk, preferred_element_type=jnp.float32
        )
        return (attended, row_max + jnp.log(summed))

    block_ids = jnp.arange(MAXLEN // QBLOCK, dtype=jnp.int32)
    attended, log_all = lax.map(one_block, block_ids)
    return (attended.reshape(MAXLEN, queries.shape[1], HEAD_DIM), log_all)


def band_backward(queries, keyset, values, length, grad_attended, log_all):
    scale_qk = HEAD_DIM ** (-0.5)
    pad_width = ((HALF, HALF), (0, 0), (0, 0))
    keys_pad = jnp.pad(keyset, pad_width)
    values_pad = jnp.pad(values, pad_width)
    window = QBLOCK + 2 * HALF

    def one_block(carried, block_id):
        keys_grad, values_grad = carried
        offset = block_id * QBLOCK
        query_blk = lax.dynamic_slice_in_dim(queries, offset, QBLOCK, 0)
        keys_blk = lax.dynamic_slice_in_dim(keys_pad, offset, window, 0)
        values_blk = lax.dynamic_slice_in_dim(values_pad, offset, window, 0)
        grad_blk = lax.dynamic_slice_in_dim(grad_attended, offset, QBLOCK, 0)
        scores = (
            jnp.einsum("qhd,khd->hqk", query_blk, keys_blk, preferred_element_type=jnp.float32)
            * scale_qk
        )
        scores = jnp.where(allowed_pairs(offset, length)[None], scores, -1e30)
        attn_prob = jnp.exp(scores - log_all[block_id])
        prob_grad = jnp.einsum(
            "qhd,khd->hqk", grad_blk, values_blk, preferred_element_type=jnp.float32
        )
        inner_sum = jnp.sum(attn_prob * prob_grad, -1, keepdims=True)
        score_grad = (attn_prob * (prob_grad - inner_sum)).astype(jnp.bfloat16)
        query_grad = (
            jnp.einsum("hqk,khd->qhd", score_grad, keys_blk, preferred_element_type=jnp.float32)
            * scale_qk
        )
        key_part = (
            jnp.einsum("hqk,qhd->khd", score_grad, query_blk, preferred_element_type=jnp.float32)
            * scale_qk
        )
        value_part = jnp.einsum(
            "hqk,qhd->khd",
            attn_prob.astype(jnp.bfloat16),
            grad_blk,
            preferred_element_type=jnp.float32,
        )
        keys_grad = lax.dynamic_update_slice_in_dim(
            keys_grad, lax.dynamic_slice_in_dim(keys_grad, offset, window, 0) + key_part, offset, 0
        )
        values_grad = lax.dynamic_update_slice_in_dim(
            values_grad,
            lax.dynamic_slice_in_dim(values_grad, offset, window, 0) + value_part,
            offset,
            0,
        )
        return ((keys_grad, values_grad), query_grad)

    blank_grad = jnp.zeros((MAXLEN + 2 * HALF, queries.shape[1], HEAD_DIM), jnp.float32)
    block_ids = jnp.arange(MAXLEN // QBLOCK, dtype=jnp.int32)
    (keys_grad, values_grad), query_grads = lax.scan(one_block, (blank_grad, blank_grad), block_ids)
    query_grads = query_grads.reshape(MAXLEN, queries.shape[1], HEAD_DIM)
    return (query_grads, keys_grad[HALF : HALF + MAXLEN], values_grad[HALF : HALF + MAXLEN])


def on_device(tokens, lengths, order, gain_attn, w_qkv, w_out, gain_mlp, w_in, w_down, cotangent):
    shard_rows = tokens.shape[0]
    group_rows = shard_rows * lax.axis_size("tensor")
    slot_count = group_rows // MAXLEN
    local_width = w_qkv.shape[2]
    local_heads = local_width // HEAD_DIM
    first_slot = lax.axis_index("dp") * slot_count
    my_order = lax.dynamic_slice_in_dim(order, first_slot, slot_count, 0)
    chosen = my_order[:, None] == jnp.arange(lengths.shape[0], dtype=jnp.int32)[None, :]
    slot_len = jnp.sum(jnp.where(chosen, lengths[None, :], 0), 1)
    row_index = lax.axis_index("tensor") * shard_rows + jnp.arange(shard_rows, dtype=jnp.int32)
    in_slot = (row_index // MAXLEN)[:, None] == jnp.arange(slot_count, dtype=jnp.int32)[None, :]
    row_len = jnp.sum(jnp.where(in_slot, slot_len[None, :], 0), 1)
    keep_row = (row_index % MAXLEN < row_len).astype(jnp.float32)[:, None]
    tokens_f = tokens.astype(jnp.float32)
    qkv_flat = w_qkv.reshape(w_qkv.shape[0], -1)
    in_flat = w_in.reshape(w_in.shape[0], -1)
    normed, attn_norm_pull = jax.vjp(layer_norm, tokens_f, gain_attn)
    normed_all = lax.all_gather(normed.astype(jnp.bfloat16), "tensor", axis=0, tiled=True)
    packed = jnp.dot(normed_all, qkv_flat, preferred_element_type=jnp.float32).astype(jnp.bfloat16)
    packed = packed.reshape(slot_count, MAXLEN, 3, local_heads, HEAD_DIM)
    attended, log_all = jax.vmap(band_forward)(
        packed[:, :, 0], packed[:, :, 1], packed[:, :, 2], slot_len
    )
    attended = attended.reshape(group_rows, local_width).astype(jnp.bfloat16)
    attn_branch = lax.psum_scatter(
        jnp.dot(attended, w_out, preferred_element_type=jnp.float32),
        "tensor",
        scatter_dimension=0,
        tiled=True,
    )
    hidden_in = tokens_f + attn_branch
    normed_mlp, mlp_norm_pull = jax.vjp(layer_norm, hidden_in, gain_mlp)
    mlp_all = lax.all_gather(normed_mlp.astype(jnp.bfloat16), "tensor", axis=0, tiled=True)
    lifted = jnp.dot(mlp_all, in_flat, preferred_element_type=jnp.float32).reshape(
        group_rows, 2, -1
    )
    gate_out, gate_pull = jax.vjp(gelu_gate, lifted)
    gate_out = gate_out.astype(jnp.bfloat16)
    branch = lax.psum_scatter(
        jnp.dot(gate_out, w_down, preferred_element_type=jnp.float32).astype(jnp.bfloat16),
        "tensor",
        scatter_dimension=0,
        tiled=True,
    ).astype(jnp.float32)
    output = (keep_row * (hidden_in + branch)).astype(jnp.bfloat16)
    out_grad = keep_row * cotangent.astype(jnp.float32)
    out_grad_all = lax.all_gather(out_grad.astype(jnp.bfloat16), "tensor", axis=0, tiled=True)
    grad_w_down = contract_rows(gate_out, out_grad_all)
    gate_grad = contract_cols(out_grad_all, w_down)
    lift_grad = gate_pull(gate_grad)[0].astype(jnp.bfloat16).reshape(group_rows, -1)
    grad_w_in = contract_rows(mlp_all, lift_grad).reshape(w_in.shape)
    mlp_norm_grad = lax.psum_scatter(
        contract_cols(lift_grad, in_flat).astype(jnp.bfloat16),
        "tensor",
        scatter_dimension=0,
        tiled=True,
    ).astype(jnp.float32)
    hidden_part, gain_mlp_grad = mlp_norm_pull(mlp_norm_grad)
    hidden_grad = out_grad + hidden_part
    hidden_all = lax.all_gather(hidden_grad.astype(jnp.bfloat16), "tensor", axis=0, tiled=True)
    grad_w_out = contract_rows(attended, hidden_all)
    attended_grad = contract_cols(hidden_all, w_out).astype(jnp.bfloat16)
    attended_grad = attended_grad.reshape(slot_count, MAXLEN, local_heads, HEAD_DIM)
    query_grad, keys_grad, values_grad = jax.vmap(band_backward)(
        packed[:, :, 0], packed[:, :, 1], packed[:, :, 2], slot_len, attended_grad, log_all
    )
    packed_grad = jnp.stack((query_grad, keys_grad, values_grad), 2).astype(jnp.bfloat16)
    packed_grad = packed_grad.reshape(group_rows, 3 * local_width)
    grad_w_qkv = contract_rows(normed_all, packed_grad).reshape(w_qkv.shape)
    attn_norm_grad = lax.psum_scatter(
        contract_cols(packed_grad, qkv_flat).astype(jnp.bfloat16),
        "tensor",
        scatter_dimension=0,
        tiled=True,
    ).astype(jnp.float32)
    input_part, gain_attn_grad = attn_norm_pull(attn_norm_grad)
    input_grad = hidden_grad + input_part
    grad_w_qkv, grad_w_out, grad_w_in, grad_w_down = (
        lax.psum(grad_w_qkv.astype(jnp.bfloat16), "dp").astype(jnp.float32),
        lax.psum(grad_w_out.astype(jnp.bfloat16), "dp").astype(jnp.float32),
        lax.psum(grad_w_in.astype(jnp.bfloat16), "dp").astype(jnp.float32),
        lax.psum(grad_w_down.astype(jnp.bfloat16), "dp").astype(jnp.float32),
    )
    gain_total = lax.psum(jnp.stack((gain_attn_grad, gain_mlp_grad)), ("dp", "tensor"))
    return (
        output,
        input_grad,
        gain_total[0],
        grad_w_qkv,
        grad_w_out,
        gain_total[1],
        grad_w_in,
        grad_w_down,
    )


def solution(mesh):
    return jax.shard_map(
        on_device,
        mesh=mesh,
        in_specs=(
            P(("dp", "tensor"), None),
            P(),
            P(),
            P(),
            P(None, None, "tensor"),
            P("tensor", None),
            P(),
            P(None, None, "tensor"),
            P("tensor", None),
            P(("dp", "tensor"), None),
        ),
        out_specs=(
            P(("dp", "tensor"), None),
            P(("dp", "tensor"), None),
            P(),
            P(None, None, "tensor"),
            P("tensor", None),
            P(),
            P(None, None, "tensor"),
            P("tensor", None),
        ),
        check_vma=False,
    )
```

profile of v0, /device:TPU:0, one launch (start us, length us, event | category | flops | bytes accessed | tf_op | source)
XLA Modules:
  0.0 1787.4 jit_solution(4810545400805343947)
XLA Ops:
  21.4 78.2 %all-gather.5.cloned.1.call-done = bf16[3072,1024]{1,0:T(8,128)(2,1)} async-done(((bf16[1536,1024]{1,0:T(8,128)(2,1)}), bf16[3072,1024]{1,0:T(8,128)(2,1)}) %all-gather.5.cloned.1.call-update) | async-done | bytes 6291472 | tf_op jit(solution)/shard_map/all_gather | solution.py:149
  99.6 15.8 convolution_convert_fusion
  115.4 12.6 copy.38
  128.0 26.2 %reshape.522 = bf16[3,1024,3,8,64]{1,0,4,3,2:T(4,128)(2,1)} reshape(bf16[3072,1536]{0,1:T(8,128)(2,1)} %copy.38) | data formatting | bytes 18874368 | tf_op jit(solution)/shard_map/reshape | solution.py:151
  177.1 103.1 %while.42 = (s32[]{:T(128)}, bf16[2,3,512,8,64]{2,4,3,1,0:T(8,128)(2,1)}, f32[2,3,8,512,1]{3,2,1,4,0:T(8,128)S(1)}, s32[2]{0:T(128)S(1)}, bf16[3,1152,8,64]{1,3,...) while((s32[]{:T(128)}, ...), condition=%wide.region_7.8_spmd, body=%wide.region_4.7_spmd.sunk | while | flops 2111235584 | bytes 147998080 | solution.py:70
  180.1 16.7 fusion.147
  196.8 15.3 fusion.148
  212.2 15.0 bitcast_dynamic-update-slice_fusion.6
  231.5 16.6 fusion.147
  248.1 15.3 fusion.148
  263.5 15.0 bitcast_dynamic-update-slice_fusion.6
  310.5 139.6 %reduce-scatter.5.cloned.1.call-done = f32[1536,1024]{1,0:T(8,128)} async-done(((f32[3072,1024]{1,0:T(8,128)}), f32[1536,1024]{1,0:T(8,128)}) %reduce-scatter.5.cloned.1.call-update) | async-done | bytes 6291472 | tf_op jit(solution)/shard_map/reduce_scatter | solution.py:156
  460.3 72.4 %all-gather.9.cloned.1.call-done = bf16[3072,1024]{1,0:T(8,128)(2,1)} async-done(((bf16[1536,1024]{1,0:T(8,128)(2,1)}), bf16[3072,1024]{1,0:T(8,128)(2,1)}) %all-gather.9.cloned.1.call-update) | async-done | bytes 6291472 | tf_op jit(solution)/shard_map/all_gather | solution.py:178
  532.7 14.4 fusion.108
  547.1 68.0 %all-gather.7.cloned.1.call-done = bf16[3072,1024]{1,0:T(8,128)(2,1)} async-done(((bf16[1536,1024]{1,0:T(8,128)(2,1)}), bf16[3072,1024]{1,0:T(8,128)(2,1)}) %all-gather.7.cloned.1.call-update) | async-done | bytes 6291472 | tf_op jit(solution)/shard_map/all_gather | solution.py:164
  615.1 24.8 %fusion.78 = f32[3072,2,1312]{0,2,1:T(8,128)} fusion(bf16[3072,1024]{1,0:T(8,128)(2,1)} %all-gather.7.cloned.1.call-done, bf16[1024,2,1312]{0,2,1:T(8,128)(2,1)} %param.25), kind=kOutput, calls=%fused_computation.131 | convolution fusion | flops 16508780544 | bytes 43909120 | tf_op jit(solution)/shard_map/dot_general | solution.py:165
  639.9 37.5 %multiply_bitcast_fusion = (f32[3072,1,1312]{0,2,1:T(8,128)}, f32[3072,1312]{0,1:T(8,128)}) fusion(f32[3072,1312]{0,1:T(8,128)S(1)} %copy-done.5, f32[3072,2,1312]{0,2,1:T(8,128)} %fusion.78), kind=kLoop, calls=%fused_computation.87 | loop fusion | flops 261980160 | bytes 64487424 | tf_op jit(solution)/shard_map/transpose(jvp())/broadcast_in_dim | solution.py:19
  677.4 31.7 %fusion.48 = (f32[3072,1,1312]{0,2,1:T(8,128)}, bf16[3072,1312]{0,1:T(8,128)(2,1)}) fusion(f32[3072,1312]{0,1:T(8,128)} %get-tuple-element.486, f32[3072,1312]{0,1:T(8,128)} %fusion.108, f32[3072,2,1312]{0,2,1:T(8,128)} %fusion.78), kind=kLoop, calls=%fused_computation.86 | loop fusion | flops 68517888 | bytes 88670208 | tf_op jit(solution)/shard_map/transpose(jvp())/broadcast_in_dim | solution.py:19
  709.1 24.7 %bitcast_convert_fusion = bf16[3072,1024]{1,0:T(8,128)(2,1)} fusion(bf16[1024,2,1312]{0,2,1:T(8,128)(2,1)S(1)} %bitcast.311, f32[3072,1,1312]{0,2,1:T(8,128)} %get-tuple-element.501, f32[3072,1,1312]{0,2,1:T(8,128)} %get-tuple-element.485), kind=kOutput, calls=%fused_computation.103 | convolution fusion | flops 16528048128 | bytes 43909120 | tf_op jit(solution)/shard_map/dot_general | solution.py:29
  733.9 14.6 convolution_convert_fusion.2
  748.6 62.5 %reduce-scatter.9.cloned.1.call-done = bf16[1536,1024]{1,0:T(8,128)(2,1)} async-done(((bf16[3072,1024]{1,0:T(8,128)(2,1)}), bf16[1536,1024]{1,0:T(8,128)(2,1)}) %reduce-scatter.9.cloned.1.call-update) | async-done | bytes 3145744 | tf_op jit(solution)/shard_map/reduce_scatter | solution.py:183
  816.8 73.7 %reduce-scatter.7.cloned.1.call-done = bf16[1536,1024]{1,0:T(8,128)(2,1)} async-done(((bf16[3072,1024]{1,0:T(8,128)(2,1)}), bf16[1536,1024]{1,0:T(8,128)(2,1)}) %reduce-scatter.7.cloned.1.call-update) | async-done | bytes 3145744 | tf_op jit(solution)/shard_map/reduce_scatter | solution.py:170
  902.9 13.9 convolution_convert_fusion.4
  916.8 25.1 %fusion.82 = bf16[1024,2,1312]{0,2,1:T(8,128)(2,1)} fusion(bf16[3072,1024]{1,0:T(8,128)(2,1)} %all-gather.7.cloned.1.call-done, f32[3072,1,1312]{0,2,1:T(8,128)} %get-tuple-element.501, f32[3072,1,1312]{0,2,1:T(8,128)} %get-tuple-element.485), kind=kOutput, calls=%fused_computation.145 | convolution fusion | flops 16527589376 | bytes 43909120 | tf_op jit(solution)/shard_map/dot_general | solution.py:23
  941.9 41.5 %all-gather.11.cloned.1.call-done = bf16[3072,1024]{1,0:T(8,128)(2,1)} async-done(((bf16[1536,1024]{1,0:T(8,128)(2,1)}), bf16[3072,1024]{1,0:T(8,128)(2,1)}) %all-gather.11.cloned.1.call-update) | async-done | bytes 6291472 | tf_op jit(solution)/shard_map/all_gather | solution.py:191
  1017.0 311.0 %while.43 = (s32[]{:T(128)}, f32[3,1152,8,64]{1,3,2,0:T(8,128)}, f32[3,1152,8,64]{1,3,2,0:T(8,128)}, bf16[2,3,512,8,64]{2,4,3,1,0:T(8,128)(2,1)}, s32[2]{0:T(128...) while((s32[]{:T(128)}, f32[3,1152,8,64]{1,3,2,0:T(8,128)}, ...), condition=%wide.region_18.19_spmd, body=%wide.region_15.18_spmd.sunk | while | flops 5160429056 | bytes 296192000 | solution.py:126
  1022.8 17.1 fusion.157
  1039.9 20.9 %fusion.160 = f32[3,640,8,64]{1,3,2,0:T(8,128)} fusion(f32[3,1152,8,64]{1,3,2,0:T(8,128)} %get-tuple-element.716, s32[]{:T(128)S(1)} %bitcast.290, s32[]{:T(128)S(1)} %bitcast.294, f32[3,8,512,640]{3,2,1,0:T(8,128)} %fusion.157, f32[3,8,512]{2,1,0:T(8,128)S(1)} %dynamic-slice_bitcast_fusion.2, pred[3,512,640]{2,1,0:T(8,128)(4,1)S(1)} %or_and_fusion.5, ...), kind=kOutput, calls=%fused_computation.33.clone.1 | convolution fusion | flops 1040056320 | bytes 45859340 | tf_op jit(solution)/shard_map/vmap()/while/body/eval_jaxpr/hqk,qhd->khd/dot_general | solution.py:107
  1060.7 16.5 scatter.13
  1077.3 27.3 %multiply_reduce_fusion.3 = (f32[3,8,512]{2,1,0:T(8,128)S(1)}, f32[3,8,512,640]{3,2,1,0:T(8,128)}) fusion(f32[3,8,512,640]{3,2,1,0:T(8,128)} %fusion.157, f32[3,8,512]{2,1,0:T(8,128)S(1)} %dynamic-slice_bitcast_fusion.2, pred[3,512,640]{2,1,0:T(8,128)(4,1)S(1)} %or_and_fusion.5, bf16[3,1152,8,64]{1,3,2,0:T(8,128)(2,1)} %get-tuple-element.745, ...), kind=kOutput, calls=%fused_computation.27.clone.1 | convolution fusion | flops 1045942272 | bytes 67534856 | tf_op jit(solution)/shard_map/vmap()/while/body/eval_jaxpr/qhd,khd->hqk/dot_general | solution.py:94
  1104.5 26.0 %multiply_convert_fusion.5 = bf16[3,8,512,640]{3,2,1,0:T(8,128)(2,1)} fusion(f32[3,8,512,640]{3,2,1,0:T(8,128)} %get-tuple-element.649, f32[3,8,512,640]{3,2,1,0:T(8,128)} %fusion.157, f32[3,8,512]{2,1,0:T(8,128)S(1)} %get-tuple-element.650, f32[3,8,512]{2,1,0:T(8,128)S(1)} %dynamic-slice_bitcast_fusion.2, pred[3,512,640]{2,1,0:T(8,128)(4,1)S(1)} %or_and_fusion.5), kind=kLoop, calls=%fused_computation.26.clone.1 | loop fusion | flops 47185920 | bytes 79724544 | tf_op jit(solution)/shard_map/vmap()/while/body/eval_jaxpr/convert_element_type | solution.py:98
  1130.5 12.4 bitcast_dynamic-update-slice_fusion.8
  1142.9 15.0 fusion.159
  1157.9 16.5 scatter.12
  1179.8 16.8 fusion.157
  1196.6 19.9 %fusion.160 = f32[3,640,8,64]{1,3,2,0:T(8,128)} fusion(f32[3,1152,8,64]{1,3,2,0:T(8,128)} %get-tuple-element.716, s32[]{:T(128)S(1)} %bitcast.290, s32[]{:T(128)S(1)} %bitcast.294, f32[3,8,512,640]{3,2,1,0:T(8,128)} %fusion.157, f32[3,8,512]{2,1,0:T(8,128)S(1)} %dynamic-slice_bitcast_fusion.2, pred[3,512,640]{2,1,0:T(8,128)(4,1)S(1)} %or_and_fusion.5, ...), kind=kOutput, calls=%fused_computation.33.clone.1 | convolution fusion | flops 1040056320 | bytes 45859340 | tf_op jit(solution)/shard_map/vmap()/while/body/eval_jaxpr/hqk,qhd->khd/dot_general | solution.py:107
  1216.5 15.8 scatter.13
  1232.3 27.1 %multiply_reduce_fusion.3 = (f32[3,8,512]{2,1,0:T(8,128)S(1)}, f32[3,8,512,640]{3,2,1,0:T(8,128)}) fusion(f32[3,8,512,640]{3,2,1,0:T(8,128)} %fusion.157, f32[3,8,512]{2,1,0:T(8,128)S(1)} %dynamic-slice_bitcast_fusion.2, pred[3,512,640]{2,1,0:T(8,128)(4,1)S(1)} %or_and_fusion.5, bf16[3,1152,8,64]{1,3,2,0:T(8,128)(2,1)} %get-tuple-element.745, ...), kind=kOutput, calls=%fused_computation.27.clone.1 | convolution fusion | flops 1045942272 | bytes 67534856 | tf_op jit(solution)/shard_map/vmap()/while/body/eval_jaxpr/qhd,khd->hqk/dot_general | solution.py:94
  1259.4 26.0 %multiply_convert_fusion.5 = bf16[3,8,512,640]{3,2,1,0:T(8,128)(2,1)} fusion(f32[3,8,512,640]{3,2,1,0:T(8,128)} %get-tuple-element.649, f32[3,8,512,640]{3,2,1,0:T(8,128)} %fusion.157, f32[3,8,512]{2,1,0:T(8,128)S(1)} %get-tuple-element.650, f32[3,8,512]{2,1,0:T(8,128)S(1)} %dynamic-slice_bitcast_fusion.2, pred[3,512,640]{2,1,0:T(8,128)(4,1)S(1)} %or_and_fusion.5), kind=kLoop, calls=%fused_computation.26.clone.1 | loop fusion | flops 47185920 | bytes 79724544 | tf_op jit(solution)/shard_map/vmap()/while/body/eval_jaxpr/convert_element_type | solution.py:98
  1297.6 14.4 fusion.159
  1312.1 15.8 scatter.12
  1359.6 14.0 copy.49
  1373.6 14.5 copy.57
  1396.4 13.5 fusion.89
  1410.0 15.5 convolution_convert_fusion.1
  1425.5 216.0 %all-reduce.11.cloned.1.call-done = (bf16[1024,3,512]{2,0,1:T(8,128)(2,1)}, bf16[512,1024]{1,0:T(8,128)(2,1)}, bf16[1024,2,1312]{0,2,1:T(8,128)(2,1)}, bf16[1312,1024]{1,0:T(8,128)(2,1)}) async-done(((bf16[1024,3,512]{2,0,1:T(8,128)(2,1)}, bf16[512,1024]{1,0:T(8,128)(2,1)}, bf16[1024,2,1312]{0,2,1:T(8,128)(2,1)}, bf16[1312,1024]{1,0:T(8,128)(2,1)}), (bf16[1024,3,512]{2,0,1:T(8,128)(2,1)}, ...) | async-done | bytes 12255248 | tf_op jit(solution)/shard_map/psum | solution.py:210
  1658.7 62.4 %reduce-scatter.11.cloned.1.call-done = bf16[1536,1024]{1,0:T(8,128)(2,1)} async-done(((bf16[3072,1024]{1,0:T(8,128)(2,1)}), bf16[1536,1024]{1,0:T(8,128)(2,1)}) %reduce-scatter.11.cloned.1.call-update) | async-done | bytes 3145744 | tf_op jit(solution)/shard_map/reduce_scatter | solution.py:201
  1729.9 39.4 %psum.35 = f32[2,1024]{1,0:T(2,128)S(1)} all-reduce(f32[2,1024]{1,0:T(2,128)S(1)} %pad_maximum_fusion), channel_id=1, replica_groups=mesh['dp'=16,'tensor'=2] {'dp','tensor'}, use_global_device_ids=true, to_apply=%region_24.25 | all-reduce | flops 2048 | bytes 16384 | tf_op jit(solution)/shard_map/psum | solution.py:215
  (226 shorter events, 230.8 us)
Async XLA Ops:
  7.2 525.5 %copy-start = (bf16[1312,1024]{1,0:T(8,128)(2,1)S(1)}, bf16[1312,1024]{1,0:T(8,128)(2,1)}, u32[]{:S(2)}) copy-start(bf16[1312,1024]{1,0:T(8,128)(2,1)} %param.26) | copy-start | bytes 8060932
  7.2 6.8 copy-start.33
  7.2 92.4 %all-gather.5.cloned.1.call-start = ((), (), s32[]{:S(2)}) async-start(), calls=%async_computation.4 | async-start | bytes 9437184 | tf_op jit(solution)/shard_map/all_gather | solution.py:149
  7.2 6.7 copy-start.3
  16.3 4.8 copy-start.42
  16.3 4.8 copy-start.43
  16.4 433.8 %reduce-scatter.5.cloned.1.call-start = ((), (), s32[]{:S(2)}) async-start(), calls=%async_computation.5 | async-start | bytes 18874368 | tf_op jit(solution)/shard_map/reduce_scatter | solution.py:156
  196.8 15.3 copy-start.7
  196.8 15.4 copy-start.10
  248.1 15.3 copy-start.7
  248.1 15.4 copy-start.10
  280.1 15.2 copy-start.14
  280.2 25.5 %copy-start.35 = (s32[3]{0:T(128)}, s32[3]{0:T(128)S(1)}, u32[]{:S(2)}) copy-start(s32[3]{0:T(128)S(1)} %get-tuple-element.805) | copy-start | bytes 40
  305.6 227.2 %all-gather.9.cloned.1.call-start = ((), (), s32[]{:S(2)}) async-start(), calls=%async_computation.8 | async-start | bytes 9437184 | tf_op jit(solution)/shard_map/all_gather | solution.py:178
  310.5 304.6 %all-gather.7.cloned.1.call-start = ((), (), s32[]{:S(2)}) async-start(), calls=%async_computation.6 | async-start | bytes 9437184 | tf_op jit(solution)/shard_map/all_gather | solution.py:164
  460.3 350.8 %reduce-scatter.9.cloned.1.call-start = ((), (), s32[]{:S(2)}) async-start(), calls=%async_computation.9 | async-start | bytes 9437184 | tf_op jit(solution)/shard_map/reduce_scatter | solution.py:183
  615.1 24.8 %copy-start.5 = (f32[3072,1312]{0,1:T(8,128)S(1)}, f32[3072,1312]{0,1:T(8,128)}, u32[]{:S(2)}) copy-start(f32[3072,1312]{0,1:T(8,128)} %fusion.108) | copy-start | bytes 48365572
  639.9 69.2 %slice-start.2 = ((s8[5373952]{0:T(1024)(128)(4,1)}), s8[1179648]{0:T(1024)(128)(4,1)S(1)}, s32[]{:S(2)}) async-start(s8[5373952]{0:T(1024)(128)(4,1)} %bitcast.310), calls=%async_computation.15 | async-start | bytes 2359296
  677.4 31.7 %slice-start.3 = ((s8[5373952]{0:T(1024)(128)(4,1)}), s8[4194304]{0:T(1024)(128)(4,1)S(1)}, s32[]{:S(2)}) async-start(s8[5373952]{0:T(1024)(128)(4,1)} %bitcast.310), calls=%async_computation.16 | async-start | bytes 8388608
  733.9 156.6 %reduce-scatter.7.cloned.1.call-start = ((), (), s32[]{:S(2)}) async-start(), calls=%async_computation.7 | async-start | bytes 9437184 | tf_op jit(solution)/shard_map/reduce_scatter | solution.py:170
  748.5 62.6 %copy-start.22 = (f32[1536]{0:T(1024)S(1)}, f32[1536]{0:T(1024)}, u32[]{:S(2)}) copy-start(f32[1536]{0:T(1024)} %copy-done.21) | copy-start | bytes 18436
  748.5 62.6 %copy-start.26 = (f32[1536]{0:T(1024)S(1)}, f32[1536]{0:T(1024)}, u32[]{:S(2)}) copy-start(f32[1536]{0:T(1024)} %copy-done.25) | copy-start | bytes 18436
  748.5 62.6 %copy-start.38 = (f32[1024]{0:T(1024)S(1)}, f32[1024]{0:T(1024)}, u32[]{:S(2)}) copy-start(f32[1024]{0:T(1024)} %param.24) | copy-start | bytes 12292
  748.5 68.2 %copy-start.32 = (f32[1536]{0:T(1024)S(1)}, f32[1536]{0:T(1024)}, u32[]{:S(2)}) copy-start(f32[1536]{0:T(1024)} %copy-done.31) | copy-start | bytes 18436
  748.5 141.9 %copy-start.19 = (f32[1536]{0:T(1024)S(1)}, f32[1536]{0:T(1024)}, u32[]{:S(2)}) copy-start(f32[1536]{0:T(1024)} %copy-done.18) | copy-start | bytes 18436
  748.5 234.9 %all-gather.11.cloned.1.call-start = ((), (), s32[]{:S(2)}) async-start(), calls=%async_computation.10 | async-start | bytes 9437184 | tf_op jit(solution)/shard_map/all_gather | solution.py:191
  890.4 10.1 copy-start.8
  897.9 4.9 copy-start.27
  902.9 738.6 %all-reduce.11.cloned.1.call-start = ((), (), s32[]{:S(2)}) async-start(), calls=%async_computation.12 | async-start | bytes 24510464 | tf_op jit(solution)/shard_map/psum | solution.py:210
  916.8 66.6 %copy-start.41 = (bf16[512,1024]{1,0:T(8,128)(2,1)S(1)}, bf16[512,1024]{1,0:T(8,128)(2,1)}, u32[]{:S(2)}) copy-start(bf16[512,1024]{1,0:T(8,128)(2,1)} %param.23) | copy-start | bytes 3145732
  1009.6 7.4 copy-start.15
  1009.6 7.4 copy-start.36
  1009.6 7.4 copy-start.40
  1009.6 7.4 copy-start.44
  1388.2 8.3 copy-start.12
  1410.0 311.1 %reduce-scatter.11.cloned.1.call-start = ((), (), s32[]{:S(2)}) async-start(), calls=%async_computation.11 | async-start | bytes 9437184 | tf_op jit(solution)/shard_map/reduce_scatter | solution.py:201
  1641.5 8.6 copy-start.13
  1641.5 11.7 slice-start
  1644.5 8.7 slice-start.1
  1653.2 67.9 %copy-start.17 = (f32[1536]{0:T(1024)S(1)}, f32[1536]{0:T(1024)}, u32[]{:S(2)}) copy-start(f32[1536]{0:T(1024)} %copy-done.16) | copy-start | bytes 18436
  1653.2 67.9 %copy-start.34 = (f32[1024]{0:T(1024)S(1)}, f32[1024]{0:T(1024)}, u32[]{:S(2)}) copy-start(f32[1024]{0:T(1024)} %param.21) | copy-start | bytes 12292
  1658.7 66.8 %copy-start.30 = (f32[1536]{0:T(1024)S(1)}, f32[1536]{0:T(1024)}, u32[]{:S(2)}) copy-start(f32[1536]{0:T(1024)} %copy-done.29) | copy-start | bytes 18436
  1658.7 66.9 %copy-start.24 = (f32[1536]{0:T(1024)S(1)}, f32[1536]{0:T(1024)}, u32[]{:S(2)}) copy-start(f32[1536]{0:T(1024)} %copy-done.23) | copy-start | bytes 18436
  1658.7 71.2 %copy-start.39 = (f32[1024]{0:T(1024)S(1)}, f32[1024]{0:T(1024)}, u32[]{:S(2)}) copy-start(f32[1024]{0:T(1024)} %get-tuple-element.437) | copy-start | bytes 12292
  1658.7 111.3 %copy-start.20 = (f32[1536]{0:T(1024)S(1)}, f32[1536]{0:T(1024)}, u32[]{:S(2)}) copy-start(f32[1536]{0:T(1024)} %copy-done.18) | copy-start | bytes 18436
  1658.7 111.3 %copy-start.28 = (f32[1536]{0:T(1024)S(1)}, f32[1536]{0:T(1024)}, u32[]{:S(2)}) copy-start(f32[1536]{0:T(1024)} %copy-done.27) | copy-start | bytes 18436
  1721.1 4.7 copy-start.9
  1770.0 10.4 copy-start.1
  (13 other events, 25.6 us)
Sparse Core Ops, SparseCore 0:
  16.5 83.0 all-gather.4
  305.7 144.4 reduce-scatter.4
  452.3 80.3 all-gather.8
  534.7 80.3 all-gather.6
  734.0 77.0 reduce-scatter.8
  813.3 77.0 reduce-scatter.6
  903.0 80.3 all-gather.10
  1410.1 231.3 all-reduce.10
  1644.5 76.5 reduce-scatter.10
where the time goes:
time: 1800 us; the launch traced here: 1790 us
  waiting for transfers between devices  814 us (45%)
  matrix products  435 us (24%)
  other arithmetic  239 us (13%)
  local copies, waits for them, and re-layouts  237 us (13%)
  blocking collectives  39.4 us (2%)
    psum x1, waiting for transfers between devices, on_device(): lax.psum(grad_w_qkv.astype(jnp.bfloat16), 'dp').astype(jnp.float32)  216 us
    reduce_scatter x1, waiting for transfers between devices, on_device(): lax.psum_scatter(jnp.dot(attended, w_out, preferred_element_type=jnp.floa...  140 us
    all_gather x1, waiting for transfers between devices, on_device(): lax.all_gather(normed.astype(jnp.bfloat16), 'tensor', axis=0, tiled=True)  78.2 us
    reduce_scatter x1, waiting for transfers between devices, on_device(): lax.psum_scatter(jnp.dot(gate_out, w_down, preferred_element_type=jnp.flo...  73.7 us
    all_gather x1, waiting for transfers between devices, on_device(): lax.all_gather(out_grad.astype(jnp.bfloat16), 'tensor', axis=0, tiled=True)  72.4 us
    broadcast_in_dim x2, other arithmetic, gelu_gate(): return jax.nn.gelu(lifted[:, 0], approximate=False) * lifted[:, 1]  69.2 us
    all_gather x1, waiting for transfers between devices, on_device(): lax.all_gather(normed_mlp.astype(jnp.bfloat16), 'tensor', axis=0, tiled=T...  68 us
    dot_general x4, matrix products, one_block(): jnp.einsum('qhd,khd->hqk', query_blk, keys_blk, preferred_element_type=jn...  67.3 us
  transfers between devices with their start and end apart: 9, of which 9 were waited for; matrix products, arithmetic and copies ran while one was open for 7% of the time, Pallas kernels for 0%

commit v1 on v0

v1 whole, which is shorter than its diff:
```python
import math
import jax
import jax.numpy as jnp
from jax import lax
from jax.experimental import pallas as pl
from jax.experimental.pallas import tpu as pltpu
from jax.sharding import PartitionSpec as P

HEAD_DIM = 64
HALF = 64
MAXLEN = 1024
BQ = 128
LOW = jnp.bfloat16
NEG = -1e30


def cols_dot(left, right):
    return lax.dot_general(left, right, (((1,), (1,)), ((), ())), preferred_element_type=jnp.float32)


def rows_dot(left, right):
    return lax.dot_general(left, right, (((0,), (0,)), ((), ())), preferred_element_type=jnp.float32)


def plain_dot(left, right):
    return lax.dot_general(left, right, (((1,), (0,)), ((), ())), preferred_element_type=jnp.float32)


def window_masks(pos0, length):
    j = lax.broadcasted_iota(jnp.int32, (BQ, 2 * BQ), 0)
    i = lax.broadcasted_iota(jnp.int32, (BQ, 2 * BQ), 1) % BQ
    near = i <= j
    key_pos = pos0 - HALF + j + jnp.where(near, 0, BQ)
    top = jnp.minimum(length, MAXLEN)
    own = j == (i + HALF) % BQ
    bias = jnp.where(((key_pos >= 0) & (key_pos < top)) | own, 0.0, NEG)
    lane = lax.broadcasted_iota(jnp.int32, (1, 2 * BQ), 1) % BQ
    last_bias = jnp.where(pos0 + HALF + lane < top, 0.0, NEG)
    return near, i == j, bias, last_bias


def split_heads(pair):
    lane = lax.broadcasted_iota(jnp.int32, pair.shape, 1)
    zero = jnp.zeros_like(pair)
    return jnp.concatenate([jnp.where(lane < HEAD_DIM, pair, zero), jnp.where(lane >= HEAD_DIM, pair, zero)], 0)


def join_heads(wide, scale=None):
    first, second = wide[:HEAD_DIM, :BQ], wide[HEAD_DIM:, BQ:]
    if scale is not None:
        first, second = first * scale[:, :BQ], second * scale[:, BQ:]
    return jnp.concatenate([first, second], 0).T


def fold(near, diag, wide):
    low = wide[BQ:]
    return jnp.where(near, wide[:BQ], low), jnp.sum(jnp.where(diag, low, 0.0), 0, keepdims=True)


def unfold(near, diag, tile, last):
    zero = jnp.zeros_like(tile)
    return jnp.concatenate(
        [jnp.where(near, tile, zero), jnp.where(near, jnp.where(diag, last, zero), tile)], 0
    ).astype(LOW)


def window_rows(before, here, after, c):
    return jnp.concatenate([before[:, c], here[:, c], after[:, c]], 0)


def attend_kernel(place, q, kb, kh, ka, vb, vh, va, out_ref, log_ref):
    blk = pl.program_id(0)
    near, diag, bias, last_bias = window_masks(place[0, blk], place[1, blk])
    for pair in range(out_ref.shape[1] // BQ):
        c = slice(pair * BQ, (pair + 1) * BQ)
        queries = split_heads(q[:, c] * 0.125)
        keyset = window_rows(kb, kh, ka, c)
        values = window_rows(vb, vh, va, c)
        scores, last = fold(near, diag, cols_dot(keyset, queries))
        scores, last = scores + bias, last + last_bias
        row_max = jnp.maximum(jnp.max(scores, 0, keepdims=True), last)
        expons, last = jnp.exp(scores - row_max), jnp.exp(last - row_max)
        summed = jnp.sum(expons, 0, keepdims=True) + last
        probs = unfold(near, diag, expons, last)
        out_ref[:, c] = join_heads(rows_dot(values, probs), 1.0 / summed).astype(LOW)
        log_ref[0, pair:pair + 1] = row_max + jnp.log(summed)


def attend_back_kernel(
    place, q, kb, kh, ka, vb, vh, va, g_ref, log_ref, dq_ref, dk_ref, dv_ref, edge_ref, carry, tail, dq_keep
):
    step = pl.program_id(0)
    steps = pl.num_programs(0)
    width = g_ref.shape[1]

    @pl.when(step == 0)
    def _():
        carry[...] = jnp.zeros_like(carry)
        tail[...] = jnp.zeros_like(tail)
        dq_keep[...] = jnp.zeros_like(dq_keep)

    dq_ref[...] = dq_keep[...]
    dk_ref[:HALF] = tail[:, :width]
    dv_ref[:HALF] = tail[:, width:]

    @pl.when(step < steps - 1)
    def _():
        near, diag, bias, last_bias = window_masks(place[0, step], place[1, step])
        for pair in range(width // BQ):
            c = slice(pair * BQ, (pair + 1) * BQ)
            v = slice(width + pair * BQ, width + (pair + 1) * BQ)
            queries = split_heads(q[:, c] * 0.125)
            keyset = window_rows(kb, kh, ka, c)
            values = window_rows(vb, vh, va, c)
            grads = split_heads(g_ref[:, c])
            log_row = log_ref[0, pair:pair + 1]
            scores, last = fold(near, diag, cols_dot(keyset, queries))
            expons, last = jnp.exp(scores + (bias - log_row)), jnp.exp(last + (last_bias - log_row))
            prob_grad, last_grad = fold(near, diag, cols_dot(values, grads))
            inner = jnp.sum(expons * prob_grad, 0, keepdims=True) + last * last_grad
            score_grad = unfold(near, diag, expons * (prob_grad - inner), last * (last_grad - inner))
            probs = unfold(near, diag, expons, last)
            dq_keep[:, c] = join_heads(rows_dot(keyset, score_grad) * 0.125).astype(LOW)
            for lanes, out, grad in ((c, dk_ref, plain_dot(score_grad, queries)), (v, dv_ref, plain_dot(probs, grads))):
                done = (carry[:, lanes] + grad[:BQ]).astype(LOW)
                carry[:, lanes] = grad[BQ:]
                out[HALF:, c] = done[:HALF]
                tail[:, lanes] = done[HALF:]
                edge_ref[0, :, lanes] = jnp.where(step == 0, done[:HALF], edge_ref[0, :, lanes])

    @pl.when(step == steps - 1)
    def _():
        done = carry[...].astype(LOW)
        dk_ref[HALF:] = done[:HALF, :width]
        dv_ref[HALF:] = done[:HALF, width:]
        edge_ref[1] = done[HALF:]


def window_specs(width, blocks):
    last = blocks - 1
    here = lambda b, _: (jnp.minimum(b, last), 0)
    before = lambda b, _: (jnp.where(b == 0, 2 * blocks, 2 * jnp.minimum(b, last) - 1), 0)
    after = lambda b, _: (jnp.where(b >= last, 2 * blocks + 1, 2 * b + 2), 0)
    one = [pl.BlockSpec((HALF, width), before), pl.BlockSpec((BQ, width), here), pl.BlockSpec((HALF, width), after)]
    return [one[1]] + one + one


def attend(place, q, k, v):
    blocks, width = k.shape[0] // BQ - 1, k.shape[1]
    pairs = width // BQ
    return pl.pallas_call(
        attend_kernel,
        grid_spec=pltpu.PrefetchScalarGridSpec(
            num_scalar_prefetch=1,
            grid=(blocks,),
            in_specs=window_specs(width, blocks),
            out_specs=[
                pl.BlockSpec((BQ, width), lambda b, _: (b, 0)),
                pl.BlockSpec((1, pairs, 2 * BQ), lambda b, _: (b, 0, 0)),
            ],
        ),
        out_shape=[
            jax.ShapeDtypeStruct((blocks * BQ, width), LOW),
            jax.ShapeDtypeStruct((blocks, pairs, 2 * BQ), jnp.float32),
        ],
        compiler_params=pltpu.CompilerParams(vmem_limit_bytes=48 << 20),
        cost_estimate=pl.CostEstimate(
            flops=blocks * pairs * BQ * BQ * BQ * 256, bytes_accessed=blocks * BQ * width * 16, transcendentals=0
        ),
        name="attend",
    )(place, q, k, k, k, v, v, v)


def attend_back(place, q, k, v, grads, logs):
    blocks, width = grads.shape[0] // BQ, k.shape[1]
    pairs = width // BQ
    here = lambda b, _: (jnp.minimum(b, blocks - 1), 0)
    done = pl.BlockSpec((BQ, width), lambda b, _: (jnp.maximum(b - 1, 0), 0))
    return pl.pallas_call(
        attend_back_kernel,
        grid_spec=pltpu.PrefetchScalarGridSpec(
            num_scalar_prefetch=1,
            grid=(blocks + 1,),
            in_specs=window_specs(width, blocks)
            + [
                pl.BlockSpec((BQ, width), here),
                pl.BlockSpec((1, pairs, 2 * BQ), lambda b, _: (jnp.minimum(b, blocks - 1), 0, 0)),
            ],
            out_specs=[done, done, done, pl.BlockSpec((2, HALF, 2 * width), lambda b, _: (0, 0, 0))],
            scratch_shapes=[
                pltpu.VMEM((BQ, 2 * width), jnp.float32),
                pltpu.VMEM((HALF, 2 * width), LOW),
                pltpu.VMEM((BQ, width), LOW),
            ],
        ),
        out_shape=[jax.ShapeDtypeStruct((blocks * BQ, width), LOW)] * 3
        + [jax.ShapeDtypeStruct((2, HALF, 2 * width), LOW)],
        compiler_params=pltpu.CompilerParams(vmem_limit_bytes=48 << 20),
        cost_estimate=pl.CostEstimate(
            flops=blocks * pairs * BQ * BQ * BQ * 512, bytes_accessed=blocks * BQ * width * 26, transcendentals=0
        ),
        name="attend_back",
    )(place, q, k, k, k, v, v, v, grads, logs)


AXES = ("dp", "tensor")
EPS = 1e-05


def erf_parts(first, second):
    first, second = first.astype(jnp.float32), second.astype(jnp.float32)
    phi_sum = 0.5 * (1.0 + lax.erf(first * (2.0 ** -0.5)))
    density = jnp.exp(-0.5 * first * first) * ((2.0 * math.pi) ** -0.5)
    gelu = first * phi_sum
    return (gelu * second).astype(LOW), (second * (phi_sum + first * density)).astype(LOW), gelu.astype(LOW)


def norm_parts(values):
    center = values - jnp.mean(values, -1, keepdims=True)
    rate = lax.rsqrt(jnp.mean(center * center, -1, keepdims=True) + EPS)
    return center * rate, rate


def norm_back(values, gain, grad):
    unit, rate = norm_parts(values)
    pulled = grad * gain
    mean_one = jnp.mean(pulled, -1, keepdims=True)
    mean_two = jnp.mean(pulled * unit, -1, keepdims=True)
    return rate * (pulled - mean_one - unit * mean_two), jnp.sum(grad * unit, 0)


class Links:
    def __init__(self, dp, tensor):
        self.dp, self.tensor = dp, tensor

    def move(self, value, bit=0, across=0):
        pairs = [
            (d * self.tensor + t, (d ^ bit) * self.tensor + (t ^ across))
            for d in range(self.dp) for t in range(self.tensor)
        ]
        return lax.ppermute(value, AXES, pairs)

    def shift(self, value, by):
        pairs = [
            (d * self.tensor + t, d * self.tensor + t + by)
            for d in range(self.dp) for t in range(self.tensor) if 0 <= t + by < self.tensor
        ]
        return lax.ppermute(value, AXES, pairs)


def cut(value, index, count, axis):
    size = value.shape[axis] // 4
    return lax.dynamic_slice_in_dim(value, index * size, count * size, axis)


def fetch_other(links, value, axis, me):
    direct = links.move(cut(value, me, 1, axis), across=1)
    relayed = links.move(direct, bit=2)
    return jnp.concatenate([direct, relayed, links.move(direct, bit=1), links.move(relayed, bit=1)], axis)


def partner_order(value, me):
    a, b, c, d = jnp.split(value, 4, -1)
    odd = me % 2 == 1
    a, b, c, d = jnp.where(odd, b, a), jnp.where(odd, a, b), jnp.where(odd, d, c), jnp.where(odd, c, d)
    low, high = jnp.concatenate([a, b], -1), jnp.concatenate([c, d], -1)
    swap = me // 2 == 1
    return jnp.concatenate([jnp.where(swap, high, low), jnp.where(swap, low, high)], -1)


def reduce_grad(links, own, other, axis, me):
    core, row = me // 2, me % 2
    got_other = links.move(cut(other, 2, 2, axis), bit=1)
    got_own = links.move(cut(own, 2 * (1 - core), 2, axis), bit=1)
    far = cut(other, 0, 2, axis) + got_other
    near = cut(own, 2 * core, 2, axis) + got_own
    got = links.move(far, across=1)
    half = near.shape[axis] // 2
    keep = lax.dynamic_slice_in_dim(near, row * half, half, axis) + lax.slice_in_dim(got, 0, half, axis=axis)
    send = lax.dynamic_slice_in_dim(near, (1 - row) * half, half, axis) + lax.slice_in_dim(got, half, 2 * half, axis=axis)
    total = keep + links.move(send, bit=2)
    bit = 4
    while bit < links.dp:
        total = total + links.move(total, bit=bit)
        bit = 2 * bit
    second = links.move(total, bit=2)
    quarters = [total, second, links.move(total, bit=1), links.move(second, bit=1)]
    out = []
    for place in range(4):
        piece = quarters[3]
        for k in range(3):
            piece = jnp.where(me == place ^ k, quarters[k], piece)
        out.append(piece.astype(jnp.float32))
    return jnp.concatenate(out, axis)


def on_device(tokens, lengths, order, gain_attn, w_qkv, w_out, gain_mlp, w_in, w_down, cotangent):
    rows, model = tokens.shape
    dp, tensor = lax.axis_size("dp"), lax.axis_size("tensor")
    dp_id, tensor_id = lax.axis_index("dp"), lax.axis_index("tensor")
    links = Links(dp, tensor)
    paired = tensor == 2 and dp >= 4 and dp & (dp - 1) == 0
    me = 2 * (dp_id % 2) + dp_id // 2 % 2

    slot_count = rows * tensor // MAXLEN
    my_order = lax.dynamic_slice_in_dim(order, dp_id * slot_count, slot_count, 0)
    chosen = my_order[:, None] == jnp.arange(lengths.shape[0], dtype=jnp.int32)[None, :]
    slot_len = jnp.sum(jnp.where(chosen, lengths[None, :], 0), 1)
    slots = jnp.arange(slot_count, dtype=jnp.int32)[None, :]
    row_index = tensor_id * rows + jnp.arange(rows, dtype=jnp.int32)
    row_len = jnp.sum(jnp.where((row_index // MAXLEN)[:, None] == slots, slot_len[None, :], 0), 1)
    keep_row = (row_index % MAXLEN < row_len).astype(jnp.float32)[:, None]
    place = jnp.stack([row_index[::BQ] % MAXLEN, row_len[::BQ]])

    w_qkv = w_qkv.transpose(1, 0, 2)
    w_in = w_in.transpose(1, 2, 0)

    if paired:
        w_all = [
            (w_qkv, w_out, w_in, w_down),
            tuple(fetch_other(links, w, axis, me) for w, axis in ((w_qkv, 2), (w_out, 0), (w_in, 1), (w_down, 0))),
        ]
    else:
        full = [
            lax.all_gather(w, "tensor", axis=axis, tiled=True)
            for w, axis in ((w_qkv, 2), (w_out, 0), (w_in, 1), (w_down, 0))
        ]
        w_all = [tuple(full)]

    around = jnp.concatenate([tokens, links.shift(tokens[rows - HALF:], 1), links.shift(tokens[:HALF], -1)], 0)
    normed = (norm_parts(around.astype(jnp.float32))[0] * gain_attn).astype(LOW)
    normed_own = normed[:rows]
    tokens_f = tokens.astype(jnp.float32)

    saved = []
    branch = None
    for wqkv, wout, _, _ in w_all:
        q, k, v = (plain_dot(normed, wqkv[i]).astype(LOW) for i in range(3))
        attended, logs = attend(place, q, k, v)
        part = plain_dot(attended, wout)
        branch = part if branch is None else branch + part
        saved.append((q, k, v, attended, logs))
    hidden_in = tokens_f + branch
    normed_mlp = (norm_parts(hidden_in)[0] * gain_mlp).astype(LOW)
    out_grad = keep_row * cotangent.astype(jnp.float32)
    out_low = out_grad.astype(LOW)

    gates = []
    branch = None
    for _, _, win, wdown in w_all:
        gate_out, slope, gelu = erf_parts(cols_dot(normed_mlp, win[0]).astype(LOW), cols_dot(normed_mlp, win[1]).astype(LOW))
        part = plain_dot(gate_out, wdown)
        branch = part if branch is None else branch + part
        gates.append((gate_out, slope, gelu))
    output = (keep_row * (hidden_in + branch)).astype(LOW)

    down_grads = [rows_dot(gate_out, out_low).astype(LOW) for gate_out, _, _ in gates]
    in_grads = []
    mlp_grad = None
    for (_, _, win, wdown), (_, slope, gelu) in zip(w_all, gates):
        gate_grad = cols_dot(out_low, wdown)
        lift = ((gate_grad * slope).astype(LOW), (gate_grad * gelu).astype(LOW))
        in_grads.append([rows_dot(g, normed_mlp).astype(LOW) for g in lift])
        for g, w in zip(lift, win):
            part = plain_dot(g, w)
            mlp_grad = part if mlp_grad is None else mlp_grad + part
    hidden_part, gain_mlp_grad = norm_back(hidden_in, gain_mlp, mlp_grad)
    hidden_grad = out_grad + hidden_part
    hidden_low = hidden_grad.astype(LOW)

    out_grads, edges, pulled = [], [], []
    for (wqkv, wout, _, _), (q, k, v, attended, logs) in zip(w_all, saved):
        out_grads.append(rows_dot(attended, hidden_low).astype(LOW))
        attended_grad = cols_dot(hidden_low, wout).astype(LOW)
        dq, dk, dv, edge = attend_back(place, q, k, v, attended_grad, logs)
        width = dk.shape[1]
        edge = [edge[side, :, part * width:(part + 1) * width] for side in range(2) for part in range(2)]
        if paired:
            edge = [partner_order(e, me) for e in edge]
        edges.append([links.shift(e, 1 if side else -1) for e, side in zip(edge, (0, 0, 1, 1))])
        pulled.append((dq, dk, dv))
    if paired:
        edges = edges[::-1]
    qkv_grads = []
    attn_grad = None
    for (wqkv, _, _, _), (dq, dk, dv), (dk_after, dv_after, dk_before, dv_before) in zip(w_all, pulled, edges):
        dk = dk.at[:HALF].add(dk_before).at[rows - HALF:].add(dk_after)
        dv = dv.at[:HALF].add(dv_before).at[rows - HALF:].add(dv_after)
        qkv_grads.append(jnp.stack([rows_dot(normed_own, g).astype(LOW) for g in (dq, dk, dv)]))
        for g, w in zip((dq, dk, dv), wqkv):
            part = cols_dot(g, w)
            attn_grad = part if attn_grad is None else attn_grad + part
    input_part, gain_attn_grad = norm_back(tokens_f, gain_attn, attn_grad)
    input_grad = hidden_grad + input_part

    if paired:
        grad_w_down = reduce_grad(links, down_grads[0], down_grads[1], 0, me)
        grad_w_in = jnp.stack([reduce_grad(links, in_grads[0][i], in_grads[1][i], 0, me) for i in range(2)])
        grad_w_out = reduce_grad(links, out_grads[0], out_grads[1], 0, me)
        grad_w_qkv = reduce_grad(links, qkv_grads[0], qkv_grads[1], 2, me)
    else:
        grad_w_down, grad_w_in, grad_w_out, grad_w_qkv = (
            lax.psum(lax.psum_scatter(g, "tensor", scatter_dimension=axis, tiled=True), "dp").astype(jnp.float32)
            for g, axis in ((down_grads[0], 0), (jnp.stack(in_grads[0]), 1), (out_grads[0], 0), (qkv_grads[0], 2))
        )
    gain_total = lax.psum(jnp.stack((gain_attn_grad, gain_mlp_grad)), AXES)
    return (
        output,
        input_grad,
        gain_total[0],
        grad_w_qkv.transpose(1, 0, 2),
        grad_w_out,
        gain_total[1],
        grad_w_in.transpose(2, 0, 1),
        grad_w_down,
    )


def solution(mesh):
    split = P(AXES, None)
    wide = P(None, None, "tensor")
    tall = P("tensor", None)
    return jax.shard_map(
        on_device,
        mesh=mesh,
        in_specs=(split, P(), P(), P(), wide, tall, P(), wide, tall, split),
        out_specs=(split, split, P(), wide, tall, P(), wide, tall),
        check_vma=False,
    )
```

time: 1800 us -> 816 us (0.45)
  waiting for transfers between devices: 814 us -> 246 us
  matrix products: 435 us -> 224 us
  local copies, waits for them, and re-layouts: 237 us -> 59.9 us
  other arithmetic: 239 us -> 75.6 us
  Pallas kernels: 0 us -> 85.9 us
  starting transfers between devices: 0.37 us -> 69 us
    reduce_scatter x4 -> x0, waiting for transfers between devices: 338 us -> none  [the longest x1 140 us: on_device(): lax.psum_scatter(jnp.dot(attended, w_out, preferred_element_type=jnp.floa...]
    all_gather x4 -> x0, waiting for transfers between devices: 260 us -> none  [the longest x1 78.2 us: on_device(): lax.all_gather(normed.astype(jnp.bfloat16), 'tensor', axis=0, tiled=True)]
    ppermute x0 -> x71, waiting for transfers between devices: none -> 246 us  [the longest x61 231 us: move(): return lax.ppermute(value, AXES, pairs)]
    psum x1 -> x0, waiting for transfers between devices: 216 us -> none  [on_device(): lax.psum(grad_w_qkv.astype(jnp.bfloat16), 'dp').astype(jnp.float32)]
    dot_general x26 -> x42, matrix products: 435 us -> 224 us  [the longest x14 89.3 us: cols_dot(): lax.dot_general(left, right, (((1,), (1,)), ((), ())), preferred_element_...]
    pallas_call x0 -> x4, Pallas kernels: none -> 85.9 us  [the longest x2 47.3 us: attend_back(): pl.pallas_call(attend_back_kernel, grid_spec=pltpu.PrefetchScalarGridSpec...]
    convert_element_type x11 -> x3, other arithmetic: 88.7 us -> 8.41 us  [the longest x1 4.73 us: on_device(): hidden_low = hidden_grad.astype(LOW)]
    broadcast_in_dim x3 -> x0, other arithmetic: 69.2 us -> none  [the longest x2 69.2 us: gelu_gate(): return jax.nn.gelu(lifted[:, 0], approximate=False) * lifted[:, 1]]
  transfers between devices with their start and end apart: 9 -> 71, of which waited for: 9 -> 19; matrix products, arithmetic and copies ran while one was open for 7% -> 32% of each run, Pallas kernels for 0% -> 8%
where the time goes in v1:
time: 816 us; the launch traced here: 807 us
  waiting for transfers between devices  246 us (30%)
  matrix products  224 us (27%)
  Pallas kernels  85.9 us (11%)
  other arithmetic  75.6 us (9%)
  starting transfers between devices  69 us (8%)
  local copies, waits for them, and re-layouts  59.9 us (7%)
  blocking collectives  42.9 us (5%)
    ppermute x61, waiting for transfers between devices, move(): return lax.ppermute(value, AXES, pairs)  231 us
    dot_general x14, matrix products, cols_dot(): lax.dot_general(left, right, (((1,), (1,)), ((), ())), preferred_element_...  89.3 us
    dot_general x14, matrix products, plain_dot(): lax.dot_general(left, right, (((1,), (0,)), ((), ())), preferred_element_...  82.3 us
    dot_general x14, matrix products, rows_dot(): lax.dot_general(left, right, (((0,), (0,)), ((), ())), preferred_element_...  52.6 us
    ppermute x61, starting transfers between devices, move(): return lax.ppermute(value, AXES, pairs)  49.2 us
    pallas_call x2, Pallas kernels, attend_back(): pl.pallas_call(attend_back_kernel, grid_spec=pltpu.PrefetchScalarGridSpec...  47.3 us
    unnamed x195, local copies, waits for them, and re-layouts  44.2 us
    psum x1, blocking collectives, on_device(): gain_total = lax.psum(jnp.stack((gain_attn_grad, gain_mlp_grad)), AXES)  42.9 us
  transfers between devices with their start and end apart: 71, of which 19 were waited for; matrix products, arithmetic and copies ran while one was open for 32% of the time, Pallas kernels for 8%

profile of v1, /device:TPU:0, one launch (start us, length us, event | category | flops | bytes accessed | tf_op | source)
XLA Modules:
  0.0 806.5 jit_solution(12623580812015730518)
XLA Ops:
  2.5 4.8 collective-permute-start
  17.9 4.7 copy.28
  22.7 4.7 copy.31
  48.3 19.4 %attend.2 = (bf16[1536,512]{1,0:T(8,128)(2,1)S(1)}, f32[12,4,256]{2,1,0:T(4,128)S(1)}) custom-call(s32[2,12]{1,0:T(2,128)S(1)} %pad_add_fusion.place, bf16[1664,512]{1,0:T(8,128)(2,1)S(1)} %convolution_convert_fusion.17.q, bf16[1664,512]{1,0:T(8,128)(2,1)S(1)} %convolution_convert_fusion.16.kb.kh.ka, ...), custom_call_target="tpu_custom_call" | custom-call | flops 25769803776 | bytes 12582912 | tf_op jit(solution)/shard_map/attend/pallas_call | solution.py:151
  79.0 12.4 %collective-permute-done.15 = bf16[328,1024]{1,0:T(8,128)(2,1)S(1)} collective-permute-done((bf16[328,1024]{1,0:T(8,128)(2,1)}, bf16[328,1024]{1,0:T(8,128)(2,1)S(1)}, u32[]{:S(2)}, u32[]{:S(2)}) %collective-permute-start.15) | collective-permute-done | bytes 671776 | tf_op jit(solution)/shard_map/ppermute | solution.py:241
  93.2 14.5 %collective-permute-done.3 = bf16[3,1024,128]{2,1,0:T(8,128)(2,1)S(1)} collective-permute-done((bf16[3,1024,128]{2,1,0:T(8,128)(2,1)}, bf16[3,1024,128]{2,1,0:T(8,128)(2,1)S(1)}, u32[]{:S(2)}, u32[]{:S(2)}) %collective-permute-start.3) | collective-permute-done | bytes 786464 | tf_op jit(solution)/shard_map/ppermute | solution.py:241
  119.8 19.2 %attend.3 = (bf16[1536,512]{1,0:T(8,128)(2,1)S(1)}, f32[12,4,256]{2,1,0:T(4,128)S(1)}) custom-call(s32[2,12]{1,0:T(2,128)S(1)} %pad_add_fusion.place, bf16[1664,512]{1,0:T(8,128)(2,1)S(1)} %convolution_convert_fusion.14.q, bf16[1664,512]{1,0:T(8,128)(2,1)S(1)} %convolution_convert_fusion.13.kb.kh.ka, ...), custom_call_target="tpu_custom_call" | custom-call | flops 25769803776 | bytes 12582912 | tf_op jit(solution)/shard_map/attend/pallas_call | solution.py:151
  139.1 6.7 fusion.83
  155.4 5.8 convolution_convert_fusion.2
  161.3 13.3 %multiply_convert_fusion.2 = (bf16[1536,1312]{0,1:T(8,128)(2,1)}, bf16[1536,1312]{0,1:T(8,128)(2,1)}, bf16[1536,1312]{0,1:T(8,128)(2,1)}) fusion(bf16[1536,1312]{0,1:T(8,128)(2,1)S(1)} %convolution_convert_fusion.3, bf16[1536,1312]{0,1:T(8,128)(2,1)} %convolution_convert_fusion.2, bf16[1312,1024]{1,0:T(8,128)(2,1)S(1)} %copy-done, ...), kind=kOutput, calls=%fused_computation.40 | convolution fusion | flops 4176248832 | bytes 25991168 | tf_op jit(solution)/shard_map/dot_general | solution.py:18
  174.6 6.8 convolution_convert_fusion.9
  181.4 9.6 %fusion.35 = f32[1536,1024]{0,1:T(8,128)} fusion(bf16[1536,1312]{0,1:T(8,128)(2,1)} %get-tuple-element.153, bf16[2,1312,1024]{2,1,0:T(8,128)(2,1)S(1)} %bitcast.157), kind=kOutput, calls=%fused_computation.100 | convolution fusion | flops 4127195136 | bytes 13008896 | tf_op jit(solution)/shard_map/dot_general | solution.py:26
  191.0 4.6 convolution_convert_fusion.7
  195.7 7.1 fusion.36
  210.3 9.9 %fusion.85 = f32[1536,1024]{0,1:T(8,128)} fusion(bf16[1536,1312]{0,1:T(8,128)(2,1)} %get-tuple-element.154, bf16[1312,1024]{1,0:T(8,128)(2,1)S(1)} %copy-done), kind=kOutput, calls=%fused_computation.340 | convolution fusion | flops 4127195136 | bytes 13008896 | tf_op jit(solution)/shard_map/dot_general | solution.py:26
  232.7 5.9 convolution_convert_fusion
  238.6 10.9 %multiply_convert_fusion = (bf16[1536,1312]{0,1:T(8,128)(2,1)S(1)}, bf16[1536,1312]{0,1:T(8,128)(2,1)S(1)}, bf16[1536,1312]{0,1:T(8,128)(2,1)}) fusion(bf16[1536,1312]{0,1:T(8,128)(2,1)S(1)} %convolution_convert_fusion.1, bf16[1536,1312]{0,1:T(8,128)(2,1)} %convolution_convert_fusion, bf16[1312,1024]{1,0:T(8,128)(2,1)S(1)} %copy-done.51, ...), kind=kOutput, calls=%fused_computation.38 | convolution fusion | flops 4176248832 | bytes 25991168 | tf_op jit(solution)/shard_map/dot_general | solution.py:18
  249.4 5.8 convolution_convert_fusion.8
  255.2 7.2 fusion.37
  262.4 5.9 convolution_convert_fusion.6
  268.3 16.2 %multiply_reduce_fusion = (f32[1024]{0:T(1024)}, f32[1536]{0:T(1024)S(1)}, f32[1536]{0:T(1024)S(1)}, f32[1536,1024]{0,1:T(8,128)}) fusion(f32[1536,1024]{0,1:T(8,128)S(1)} %bitcast.150, f32[1536]{0:T(1024)S(1)} %copy-done.54, f32[1536]{0:T(1024)S(1)} %copy-done.46, f32[1024]{0:T(1024)S(1)} %copy-done.68, bf16[1536,1312]{0,1:T(8,128)(2,1)} %copy-done.73, ...), kind=kOutput, calls=%fused_computation.61 | convolution fusion | flops 4144492544 | bytes 38207488 | tf_op jit(solution)/shard_map/dot_general | solution.py:26
  284.5 4.7 fusion.80
  301.0 23.9 %attend_back.2 = (bf16[1536,512]{1,0:T(8,128)(2,1)S(1)}, bf16[1536,512]{1,0:T(8,128)(2,1)S(1)}, bf16[1536,512]{1,0:T(8,128)(2,1)S(1)}, bf16[2,64,1024]{2,1,0:T(8,128)(2,1)S(1)}) custom-call(s32[2,12]{1,0:T(2,128)S(1)} %pad_add_fusion.place, bf16[1664,512]{1,0:T(8,128)(2,1)} %copy-done.9, bf16[1664,512]{1,0:T(8,128)(2,1)} %copy-done.8, ...), custom_call_target="tpu_custom_call" | custom-call | flops 51539607552 | bytes 20447232 | tf_op jit(solution)/shard_map/attend_back/pallas_call | solution.py:179
  327.8 5.9 fusion.57
  336.6 7.0 convolution_convert_fusion.4
  346.5 7.0 multiply_convert_fusion.4
  353.5 4.6 copy.35
  360.0 23.4 %attend_back.3 = (bf16[1536,512]{1,0:T(8,128)(2,1)S(1)}, bf16[1536,512]{1,0:T(8,128)(2,1)S(1)}, bf16[1536,512]{1,0:T(8,128)(2,1)S(1)}, bf16[2,64,1024]{2,1,0:T(8,128)(2,1)S(1)}) custom-call(s32[2,12]{1,0:T(2,128)S(1)} %copy-done.5, bf16[1664,512]{1,0:T(8,128)(2,1)} %copy-done.11, bf16[1664,512]{1,0:T(8,128)(2,1)} %copy-done.10, ...), custom_call_target="tpu_custom_call" | custom-call | flops 51539607552 | bytes 20447232 | tf_op jit(solution)/shard_map/attend_back/pallas_call | solution.py:179
  392.5 4.8 collective-permute-done.23
  402.1 4.8 collective-permute-done.25
  411.8 4.8 collective-permute-done.21
  436.5 11.2 %collective-permute-done.37 = bf16[256,1024]{1,0:T(8,128)(2,1)S(1)} collective-permute-done((bf16[256,1024]{1,0:T(8,128)(2,1)S(1)}, bf16[256,1024]{1,0:T(8,128)(2,1)S(1)}, u32[]{:S(2)}, u32[]{:S(2)}) %collective-permute-start.37) | collective-permute-done | bytes 524320 | tf_op jit(solution)/shard_map/ppermute | solution.py:241
  465.3 17.1 %collective-permute-done.55 = bf16[656,1024]{1,0:T(8,128)(2,1)S(1)} collective-permute-done((bf16[656,1024]{1,0:T(8,128)(2,1)S(1)}, bf16[656,1024]{1,0:T(8,128)(2,1)S(1)}, u32[]{:S(2)}, u32[]{:S(2)}) %collective-permute-start.55) | collective-permute-done | bytes 1343520 | tf_op jit(solution)/shard_map/ppermute | solution.py:241
  484.0 27.2 %collective-permute-done.46 = bf16[656,1024]{1,0:T(8,128)(2,1)S(1)} collective-permute-done((bf16[656,1024]{1,0:T(8,128)(2,1)S(1)}, bf16[656,1024]{1,0:T(8,128)(2,1)S(1)}, u32[]{:S(2)}, u32[]{:S(2)}) %collective-permute-start.46) | collective-permute-done | bytes 1343520 | tf_op jit(solution)/shard_map/ppermute | solution.py:241
  512.8 27.2 %collective-permute-done.64 = bf16[656,1024]{1,0:T(8,128)(2,1)S(1)} collective-permute-done((bf16[656,1024]{1,0:T(8,128)(2,1)S(1)}, bf16[656,1024]{1,0:T(8,128)(2,1)S(1)}, u32[]{:S(2)}, u32[]{:S(2)}) %collective-permute-start.64) | collective-permute-done | bytes 1343520 | tf_op jit(solution)/shard_map/ppermute | solution.py:241
  541.6 31.3 %collective-permute-done.28 = bf16[3,1024,256]{1,2,0:T(8,128)(2,1)S(1)} collective-permute-done((bf16[3,1024,256]{1,2,0:T(8,128)(2,1)S(1)}, bf16[3,1024,256]{1,2,0:T(8,128)(2,1)S(1)}, u32[]{:S(2)}, u32[]{:S(2)}) %collective-permute-start.28) | collective-permute-done | bytes 1572896 | tf_op jit(solution)/shard_map/ppermute | solution.py:241
  587.0 5.3 collective-permute-done.29
  601.7 26.0 %collective-permute-done.48 = bf16[328,1024]{1,0:T(8,128)(2,1)S(1)} collective-permute-done((bf16[328,1024]{1,0:T(8,128)(2,1)S(1)}, bf16[328,1024]{1,0:T(8,128)(2,1)S(1)}, u32[]{:S(2)}, u32[]{:S(2)}) %collective-permute-start.48) | collective-permute-done | bytes 671776 | tf_op jit(solution)/shard_map/ppermute | solution.py:241
  630.5 26.0 %collective-permute-done.66 = bf16[328,1024]{1,0:T(8,128)(2,1)S(1)} collective-permute-done((bf16[328,1024]{1,0:T(8,128)(2,1)S(1)}, bf16[328,1024]{1,0:T(8,128)(2,1)S(1)}, u32[]{:S(2)}, u32[]{:S(2)}) %collective-permute-start.66) | collective-permute-done | bytes 671776 | tf_op jit(solution)/shard_map/ppermute | solution.py:241
  658.7 14.4 %fusion.30 = (f32[1024]{0:T(1024)S(1)}, f32[1536]{0:T(1024)S(1)}, f32[1536]{0:T(1024)S(1)}, f32[1536,1024]{0,1:T(8,128)}) fusion(bf16[1536,1024]{0,1:T(8,128)(2,1)S(1)} %copy-done.14, f32[1536]{0:T(1024)S(1)} %copy-done.62, f32[1536]{0:T(1024)S(1)} %copy-done.57, f32[1024]{0:T(1024)S(1)} %copy-done.66, f32[1536,1024]{0,1:T(8,128)} %fusion.61, ...), kind=kOutput, calls=%fused_computation.58 | convolution fusion | flops 1632628736 | bytes 43548672 | tf_op jit(solution)/shard_map/dot_general | solution.py:18
  674.9 5.6 collective-permute-done.42
  690.5 11.9 %collective-permute-done.67 = bf16[328,1024]{1,0:T(8,128)(2,1)} collective-permute-done((bf16[328,1024]{1,0:T(8,128)(2,1)}, bf16[328,1024]{1,0:T(8,128)(2,1)}, u32[]{:S(2)}, u32[]{:S(2)}) %collective-permute-start.67) | collective-permute-done | bytes 671776 | tf_op jit(solution)/shard_map/ppermute | solution.py:241
  702.5 9.5 %fusion.29 = f32[1536,1024]{0,1:T(8,128)} fusion(bf16[1536,1024]{0,1:T(8,128)(2,1)S(1)} %copy-done.14, f32[1536,1024]{0,1:T(8,128)} %get-tuple-element.239, f32[1536]{0:T(1024)S(1)} %broadcast_multiply_fusion, f32[1536]{0:T(1024)S(1)} %broadcast_multiply_fusion.1, f32[1024]{0:T(1024)S(1)} %copy-done.66, f32[1536]{0:T(1024)S(1)} %copy-done.62, ...), kind=kLoop, calls=%fused_computation.57 | loop fusion | flops 29884416 | bytes 31520768 | tf_op jit(solution)/shard_map/add | solution.py:394
  715.0 6.6 copy.36
  721.5 42.9 %psum.7 = f32[2,1024]{1,0:T(2,128)S(1)} all-reduce(f32[2,1024]{1,0:T(2,128)S(1)} %pad_maximum_fusion.27), channel_id=1, replica_groups=mesh['dp'=16,'tensor'=2] {'dp','tensor'}, use_global_device_ids=true, to_apply=%region_14.15 | all-reduce | flops 2048 | bytes 16384 | tf_op jit(solution)/shard_map/psum | solution.py:406
  779.8 10.9 %collective-permute-done.33 = bf16[3,1024,128]{1,2,0:T(8,128)(2,1)S(1)} collective-permute-done((bf16[3,1024,128]{1,2,0:T(8,128)(2,1)S(1)}, bf16[3,1024,128]{1,2,0:T(8,128)(2,1)S(1)}, u32[]{:S(2)}, u32[]{:S(2)}) %collective-permute-start.33) | collective-permute-done | bytes 786464 | tf_op jit(solution)/shard_map/ppermute | solution.py:241
  791.0 4.9 convert_bitcast_fusion
  799.4 6.7 copy.37
  (468 shorter events, 232.6 us)
Async XLA Ops:
  2.5 31.9 %collective-permute-start = (bf16[64,1024]{1,0:T(8,128)(2,1)}, bf16[64,1024]{1,0:T(8,128)(2,1)S(1)}, u32[]{:S(2)}, u32[]{:S(2)}) collective-permute-start(bf16[64,1024]{1,0:T(8,128)(2,1)} %get-tuple-element.160), channel_id=1, source_target_pairs={{0,1},{2,3},{4,5},{6,7},{8,9},{10,11},{12,13},{14,15},{16,17},{18,... | collective-permute-start | bytes 393224 | tf_op jit(solution)/shard_map/ppermute | solution.py:248
  7.4 27.1 %collective-permute-start.1 = (bf16[64,1024]{1,0:T(8,128)(2,1)}, bf16[64,1024]{1,0:T(8,128)(2,1)S(1)}, u32[]{:S(2)}, u32[]{:S(2)}) collective-permute-start(bf16[64,1024]{1,0:T(8,128)(2,1)} %get-tuple-element.161), channel_id=1, source_target_pairs={{1,0},{3,2},{5,4},{7,6},{9,8},{11,10},{13,12},{15,14},{17,16},{19,... | collective-permute-start | bytes 393224 | tf_op jit(solution)/shard_map/ppermute | solution.py:248
  9.7 58.0 %collective-permute-start.6 = (bf16[128,1024]{1,0:T(8,128)(2,1)S(1)}, bf16[128,1024]{1,0:T(8,128)(2,1)S(1)}, u32[]{:S(2)}, u32[]{:S(2)}) collective-permute-start(bf16[128,1024]{1,0:T(8,128)(2,1)S(1)} %constant_dynamic-slice_fusion.6), channel_id=1, source_target_pairs={{0,1},{1,0},{2,3},{3,2},{4,5},{5,4},{6,7},{7,6},{8,9},{9,8},{10,11... | collective-permute-start | bytes 786440 | tf_op jit(solution)/shard_map/ppermute | solution.py:241
  13.3 56.1 %collective-permute-start.14 = (bf16[328,1024]{1,0:T(8,128)(2,1)}, bf16[328,1024]{1,0:T(8,128)(2,1)}, u32[]{:S(2)}, u32[]{:S(2)}) collective-permute-start(bf16[328,1024]{1,0:T(8,128)(2,1)} %constant_dynamic-slice_fusion.5), channel_id=1, source_target_pairs={{0,1},{1,0},{2,3},{3,2},{4,5},{5,4},{6,7},{7,6},{8,9},{9,8},{10,11... | collective-permute-start | bytes 2015240 | tf_op jit(solution)/shard_map/ppermute | solution.py:241
  15.4 54.5 %collective-permute-start.2 = (bf16[3,1024,128]{2,1,0:T(8,128)(2,1)}, bf16[3,1024,128]{2,1,0:T(8,128)(2,1)}, u32[]{:S(2)}, u32[]{:S(2)}) collective-permute-start(bf16[3,1024,128]{2,1,0:T(8,128)(2,1)} %dynamic-slice_bitcast_fusion.1), channel_id=1, source_target_pairs={{0,1},{1,0},{2,3},{3,2},{4,5},{5,4},{6,7},{7,6},{8,9},{9,8},{10,11... | collective-permute-start | bytes 2359304 | tf_op jit(solution)/shard_map/ppermute | solution.py:241
  34.4 58.3 %collective-permute-start.10 = (bf16[2,328,1024]{2,1,0:T(8,128)(2,1)}, bf16[2,328,1024]{2,1,0:T(8,128)(2,1)}, u32[]{:S(2)}, u32[]{:S(2)}) collective-permute-start(bf16[2,328,1024]{2,1,0:T(8,128)(2,1)} %dynamic-slice_bitcast_fusion), channel_id=1, source_target_pairs={{0,1},{1,0},{2,3},{3,2},{4,5},{5,4},{6,7},{7,6},{8,9},{9,8},{10,11... | collective-permute-start | bytes 4030472 | tf_op jit(solution)/shard_map/ppermute | solution.py:241
  69.4 22.0 %collective-permute-start.15 = (bf16[328,1024]{1,0:T(8,128)(2,1)}, bf16[328,1024]{1,0:T(8,128)(2,1)S(1)}, u32[]{:S(2)}, u32[]{:S(2)}) collective-permute-start(bf16[328,1024]{1,0:T(8,128)(2,1)} %collective-permute-done.14), channel_id=1, source_target_pairs={{0,4},{1,5},{2,6},{3,7},{4,0},{5,1},{6,2},{7,3},{8,12},{9,13},{10,... | collective-permute-start | bytes 2015240 | tf_op jit(solution)/shard_map/ppermute | solution.py:241
  69.9 37.9 %collective-permute-start.3 = (bf16[3,1024,128]{2,1,0:T(8,128)(2,1)}, bf16[3,1024,128]{2,1,0:T(8,128)(2,1)S(1)}, u32[]{:S(2)}, u32[]{:S(2)}) collective-permute-start(bf16[3,1024,128]{2,1,0:T(8,128)(2,1)} %collective-permute-done.2), channel_id=1, source_target_pairs={{0,4},{1,5},{2,6},{3,7},{4,0},{5,1},{6,2},{7,3},{8,12},{9,13},{10,... | collective-permute-start | bytes 2359304 | tf_op jit(solution)/shard_map/ppermute | solution.py:241
  77.0 30.8 %collective-permute-start.16 = (bf16[328,1024]{1,0:T(8,128)(2,1)}, bf16[328,1024]{1,0:T(8,128)(2,1)S(1)}, u32[]{:S(2)}, u32[]{:S(2)}) collective-permute-start(bf16[328,1024]{1,0:T(8,128)(2,1)} %collective-permute-done.14), channel_id=1, source_target_pairs={{0,2},{1,3},{2,0},{3,1},{4,6},{5,7},{6,4},{7,5},{8,10},{9,11},{10,... | collective-permute-start | bytes 2015240 | tf_op jit(solution)/shard_map/ppermute | solution.py:241
  78.8 33.4 %collective-permute-start.4 = (bf16[3,1024,128]{2,1,0:T(8,128)(2,1)}, bf16[3,1024,128]{2,1,0:T(8,128)(2,1)S(1)}, u32[]{:S(2)}, u32[]{:S(2)}) collective-permute-start(bf16[3,1024,128]{2,1,0:T(8,128)(2,1)} %collective-permute-done.2), channel_id=1, source_target_pairs={{0,2},{1,3},{2,0},{3,1},{4,6},{5,7},{6,4},{7,5},{8,10},{9,11},{10,... | collective-permute-start | bytes 2359304 | tf_op jit(solution)/shard_map/ppermute | solution.py:241
  91.4 21.0 %collective-permute-start.17 = (bf16[328,1024]{1,0:T(8,128)(2,1)S(1)}, bf16[328,1024]{1,0:T(8,128)(2,1)S(1)}, u32[]{:S(2)}, u32[]{:S(2)}) collective-permute-start(bf16[328,1024]{1,0:T(8,128)(2,1)S(1)} %collective-permute-done.15), channel_id=1, source_target_pairs={{0,2},{1,3},{2,0},{3,1},{4,6},{5,7},{6,4},{7,5},{8,10},{9,11},{10,... | collective-permute-start | bytes 2015240 | tf_op jit(solution)/shard_map/ppermute | solution.py:241
  92.7 129.0 %collective-permute-start.12 = (bf16[2,328,1024]{2,1,0:T(8,128)(2,1)}, bf16[2,328,1024]{2,1,0:T(8,128)(2,1)}, u32[]{:S(2)}, u32[]{:S(2)}) collective-permute-start(bf16[2,328,1024]{2,1,0:T(8,128)(2,1)} %collective-permute-done.10), channel_id=1, source_target_pairs={{0,2},{1,3},{2,0},{3,1},{4,6},{5,7},{6,4},{7,5},{8,10},{9,11},{10,... | collective-permute-start | bytes 4030472 | tf_op jit(solution)/shard_map/ppermute | solution.py:241
  107.8 102.1 %collective-permute-start.11 = (bf16[2,328,1024]{2,1,0:T(8,128)(2,1)}, bf16[2,328,1024]{2,1,0:T(8,128)(2,1)}, u32[]{:S(2)}, u32[]{:S(2)}) collective-permute-start(bf16[2,328,1024]{2,1,0:T(8,128)(2,1)} %collective-permute-done.10), channel_id=1, source_target_pairs={{0,4},{1,5},{2,6},{3,7},{4,0},{5,1},{6,2},{7,3},{8,12},{9,13},{10,... | collective-permute-start | bytes 4030472 | tf_op jit(solution)/shard_map/ppermute | solution.py:241
  202.9 20.2 %collective-permute-start.53 = (bf16[656,1024]{1,0:T(8,128)(2,1)S(1)}, bf16[656,1024]{1,0:T(8,128)(2,1)S(1)}, u32[]{:S(2)}, u32[]{:S(2)}) collective-permute-start(bf16[656,1024]{1,0:T(8,128)(2,1)S(1)} %constant_dynamic-slice_fusion.1), channel_id=1, source_target_pairs={{0,2},{1,3},{2,0},{3,1},{4,6},{5,7},{6,4},{7,5},{8,10},{9,11},{10,... | collective-permute-start | bytes 4030472 | tf_op jit(solution)/shard_map/ppermute | solution.py:241
  203.3 21.4 %collective-permute-start.44 = (bf16[656,1024]{1,0:T(8,128)(2,1)S(1)}, bf16[656,1024]{1,0:T(8,128)(2,1)S(1)}, u32[]{:S(2)}, u32[]{:S(2)}) collective-permute-start(bf16[656,1024]{1,0:T(8,128)(2,1)S(1)} %constant_dynamic-slice_fusion.2), channel_id=1, source_target_pairs={{0,2},{1,3},{2,0},{3,1},{4,6},{5,7},{6,4},{7,5},{8,10},{9,11},{10,... | collective-permute-start | bytes 4030472 | tf_op jit(solution)/shard_map/ppermute | solution.py:241
  210.0 18.0 %collective-permute-start.13 = (bf16[2,328,1024]{2,1,0:T(8,128)(2,1)}, bf16[2,328,1024]{2,1,0:T(8,128)(2,1)S(1)}, u32[]{:S(2)}, u32[]{:S(2)}) collective-permute-start(bf16[2,328,1024]{2,1,0:T(8,128)(2,1)} %collective-permute-done.11), channel_id=1, source_target_pairs={{0,2},{1,3},{2,0},{3,1},{4,6},{5,7},{6,4},{7,5},{8,10},{9,11},{10,... | collective-permute-start | bytes 4030472 | tf_op jit(solution)/shard_map/ppermute | solution.py:241
  334.8 112.9 %collective-permute-start.54 = (bf16[656,1024]{1,0:T(8,128)(2,1)}, bf16[656,1024]{1,0:T(8,128)(2,1)}, u32[]{:S(2)}, u32[]{:S(2)}) collective-permute-start(bf16[656,1024]{1,0:T(8,128)(2,1)} %dynamic_slice.147), channel_id=1, source_target_pairs={{0,2},{1,3},{2,0},{3,1},{4,6},{5,7},{6,4},{7,5},{8,10},{9,11},{10,... | collective-permute-start | bytes 4030472 | tf_op jit(solution)/shard_map/ppermute | solution.py:241
  336.3 113.8 %collective-permute-start.45 = (bf16[656,1024]{1,0:T(8,128)(2,1)}, bf16[656,1024]{1,0:T(8,128)(2,1)}, u32[]{:S(2)}, u32[]{:S(2)}) collective-permute-start(bf16[656,1024]{1,0:T(8,128)(2,1)} %dynamic_slice.145), channel_id=1, source_target_pairs={{0,2},{1,3},{2,0},{3,1},{4,6},{5,7},{6,4},{7,5},{8,10},{9,11},{10,... | collective-permute-start | bytes 4030472 | tf_op jit(solution)/shard_map/ppermute | solution.py:241
  346.3 107.0 %collective-permute-start.63 = (bf16[656,1024]{1,0:T(8,128)(2,1)}, bf16[656,1024]{1,0:T(8,128)(2,1)}, u32[]{:S(2)}, u32[]{:S(2)}) collective-permute-start(bf16[656,1024]{1,0:T(8,128)(2,1)} %dynamic_slice.149), channel_id=1, source_target_pairs={{0,2},{1,3},{2,0},{3,1},{4,6},{5,7},{6,4},{7,5},{8,10},{9,11},{10,... | collective-permute-start | bytes 4030472 | tf_op jit(solution)/shard_map/ppermute | solution.py:241
  383.6 40.9 %collective-permute-start.18 = (bf16[64,512]{1,0:T(8,128)(2,1)S(1)}, bf16[64,512]{1,0:T(8,128)(2,1)S(1)}, u32[]{:S(2)}, u32[]{:S(2)}) collective-permute-start(bf16[64,512]{1,0:T(8,128)(2,1)S(1)} %pad_maximum_fusion.3), channel_id=1, source_target_pairs={{0,1},{2,3},{4,5},{6,7},{8,9},{10,11},{12,13},{14,15},{16,17},{18,... | collective-permute-start | bytes 196616 | tf_op jit(solution)/shard_map/ppermute | solution.py:248
  436.0 19.2 %collective-permute-start.27 = (bf16[3,1024,256]{1,2,0:T(8,128)(2,1)S(1)}, bf16[3,1024,256]{1,2,0:T(8,128)(2,1)S(1)}, u32[]{:S(2)}, u32[]{:S(2)}) collective-permute-start(bf16[3,1024,256]{1,2,0:T(8,128)(2,1)S(1)} %dynamic_slice.141), channel_id=1, source_target_pairs={{0,2},{1,3},{2,0},{3,1},{4,6},{5,7},{6,4},{7,5},{8,10},{9,11},{10,... | collective-permute-start | bytes 4718600 | tf_op jit(solution)/shard_map/ppermute | solution.py:241
  450.0 32.4 %collective-permute-start.55 = (bf16[656,1024]{1,0:T(8,128)(2,1)S(1)}, bf16[656,1024]{1,0:T(8,128)(2,1)S(1)}, u32[]{:S(2)}, u32[]{:S(2)}) collective-permute-start(bf16[656,1024]{1,0:T(8,128)(2,1)S(1)} %slice_add_fusion.2), channel_id=1, source_target_pairs={{0,1},{1,0},{2,3},{3,2},{4,5},{5,4},{6,7},{7,6},{8,9},{9,8},{10,11... | collective-permute-start | bytes 4030472 | tf_op jit(solution)/shard_map/ppermute | solution.py:241
  453.4 57.9 %collective-permute-start.46 = (bf16[656,1024]{1,0:T(8,128)(2,1)S(1)}, bf16[656,1024]{1,0:T(8,128)(2,1)S(1)}, u32[]{:S(2)}, u32[]{:S(2)}) collective-permute-start(bf16[656,1024]{1,0:T(8,128)(2,1)S(1)} %slice_add_fusion.3), channel_id=1, source_target_pairs={{0,1},{1,0},{2,3},{3,2},{4,5},{5,4},{6,7},{7,6},{8,9},{9,8},{10,11... | collective-permute-start | bytes 4030472 | tf_op jit(solution)/shard_map/ppermute | solution.py:241
  455.2 84.8 %collective-permute-start.64 = (bf16[656,1024]{1,0:T(8,128)(2,1)S(1)}, bf16[656,1024]{1,0:T(8,128)(2,1)S(1)}, u32[]{:S(2)}, u32[]{:S(2)}) collective-permute-start(bf16[656,1024]{1,0:T(8,128)(2,1)S(1)} %slice_add_fusion.1), channel_id=1, source_target_pairs={{0,1},{1,0},{2,3},{3,2},{4,5},{5,4},{6,7},{7,6},{8,9},{9,8},{10,11... | collective-permute-start | bytes 4030472 | tf_op jit(solution)/shard_map/ppermute | solution.py:241
  457.2 115.8 %collective-permute-start.28 = (bf16[3,1024,256]{1,2,0:T(8,128)(2,1)S(1)}, bf16[3,1024,256]{1,2,0:T(8,128)(2,1)S(1)}, u32[]{:S(2)}, u32[]{:S(2)}) collective-permute-start(bf16[3,1024,256]{1,2,0:T(8,128)(2,1)S(1)} %slice_add_fusion), channel_id=1, source_target_pairs={{0,1},{1,0},{2,3},{3,2},{4,5},{5,4},{6,7},{7,6},{8,9},{9,8},{10,11... | collective-permute-start | bytes 4718600 | tf_op jit(solution)/shard_map/ppermute | solution.py:241
  462.9 121.3 %collective-permute-start.39 = (bf16[128,1024]{1,0:T(8,128)(2,1)S(1)}, bf16[128,1024]{1,0:T(8,128)(2,1)S(1)}, u32[]{:S(2)}, u32[]{:S(2)}) collective-permute-start(bf16[128,1024]{1,0:T(8,128)(2,1)S(1)} %fusion.66), channel_id=1, source_target_pairs={{0,8},{1,9},{2,10},{3,11},{4,12},{5,13},{6,14},{7,15},{8,0},{9,1},... | collective-permute-start | bytes 786440 | tf_op jit(solution)/shard_map/ppermute | solution.py:241
  482.7 92.2 %collective-permute-start.56 = (bf16[328,1024]{1,0:T(8,128)(2,1)S(1)}, bf16[328,1024]{1,0:T(8,128)(2,1)S(1)}, u32[]{:S(2)}, u32[]{:S(2)}) collective-permute-start(bf16[328,1024]{1,0:T(8,128)(2,1)S(1)} %slice_add_fusion.8), channel_id=1, source_target_pairs={{0,4},{1,5},{2,6},{3,7},{4,0},{5,1},{6,2},{7,3},{8,12},{9,13},{10,... | collective-permute-start | bytes 2015240 | tf_op jit(solution)/shard_map/ppermute | solution.py:241
  511.5 65.4 %collective-permute-start.47 = (bf16[328,1024]{1,0:T(8,128)(2,1)S(1)}, bf16[328,1024]{1,0:T(8,128)(2,1)S(1)}, u32[]{:S(2)}, u32[]{:S(2)}) collective-permute-start(bf16[328,1024]{1,0:T(8,128)(2,1)S(1)} %slice_add_fusion.10), channel_id=1, source_target_pairs={{0,4},{1,5},{2,6},{3,7},{4,0},{5,1},{6,2},{7,3},{8,12},{9,13},{10,... | collective-permute-start | bytes 2015240 | tf_op jit(solution)/shard_map/ppermute | solution.py:241
  540.3 37.5 %collective-permute-start.65 = (bf16[328,1024]{1,0:T(8,128)(2,1)S(1)}, bf16[328,1024]{1,0:T(8,128)(2,1)S(1)}, u32[]{:S(2)}, u32[]{:S(2)}) collective-permute-start(bf16[328,1024]{1,0:T(8,128)(2,1)S(1)} %slice_add_fusion.6), channel_id=1, source_target_pairs={{0,4},{1,5},{2,6},{3,7},{4,0},{5,1},{6,2},{7,3},{8,12},{9,13},{10,... | collective-permute-start | bytes 2015240 | tf_op jit(solution)/shard_map/ppermute | solution.py:241
  573.5 18.9 %collective-permute-start.29 = (bf16[3,1024,128]{1,2,0:T(8,128)(2,1)S(1)}, bf16[3,1024,128]{1,2,0:T(8,128)(2,1)S(1)}, u32[]{:S(2)}, u32[]{:S(2)}) collective-permute-start(bf16[3,1024,128]{1,2,0:T(8,128)(2,1)S(1)} %slice_add_fusion.4), channel_id=1, source_target_pairs={{0,4},{1,5},{2,6},{3,7},{4,0},{5,1},{6,2},{7,3},{8,12},{9,13},{10,... | collective-permute-start | bytes 2359304 | tf_op jit(solution)/shard_map/ppermute | solution.py:241
  575.2 23.7 %collective-permute-start.57 = (bf16[328,1024]{1,0:T(8,128)(2,1)S(1)}, bf16[328,1024]{1,0:T(8,128)(2,1)S(1)}, u32[]{:S(2)}, u32[]{:S(2)}) collective-permute-start(bf16[328,1024]{1,0:T(8,128)(2,1)S(1)} %fusion.64), channel_id=1, source_target_pairs={{0,8},{1,9},{2,10},{3,11},{4,12},{5,13},{6,14},{7,15},{8,0},{9,1},... | collective-permute-start | bytes 2015240 | tf_op jit(solution)/shard_map/ppermute | solution.py:241
  577.2 50.5 %collective-permute-start.48 = (bf16[328,1024]{1,0:T(8,128)(2,1)S(1)}, bf16[328,1024]{1,0:T(8,128)(2,1)S(1)}, u32[]{:S(2)}, u32[]{:S(2)}) collective-permute-start(bf16[328,1024]{1,0:T(8,128)(2,1)S(1)} %fusion.65), channel_id=1, source_target_pairs={{0,8},{1,9},{2,10},{3,11},{4,12},{5,13},{6,14},{7,15},{8,0},{9,1},... | collective-permute-start | bytes 2015240 | tf_op jit(solution)/shard_map/ppermute | solution.py:241
  578.1 78.4 %collective-permute-start.66 = (bf16[328,1024]{1,0:T(8,128)(2,1)S(1)}, bf16[328,1024]{1,0:T(8,128)(2,1)S(1)}, u32[]{:S(2)}, u32[]{:S(2)}) collective-permute-start(bf16[328,1024]{1,0:T(8,128)(2,1)S(1)} %fusion.63), channel_id=1, source_target_pairs={{0,8},{1,9},{2,10},{3,11},{4,12},{5,13},{6,14},{7,15},{8,0},{9,1},... | collective-permute-start | bytes 2015240 | tf_op jit(solution)/shard_map/ppermute | solution.py:241
  584.4 88.7 %collective-permute-start.40 = (bf16[128,1024]{1,0:T(8,128)(2,1)S(1)}, bf16[128,1024]{1,0:T(8,128)(2,1)}, u32[]{:S(2)}, u32[]{:S(2)}) collective-permute-start(bf16[128,1024]{1,0:T(8,128)(2,1)S(1)} %add.410), channel_id=1, source_target_pairs={{0,16},{1,17},{2,18},{3,19},{4,20},{5,21},{6,22},{7,23},{8,24},{9,... | collective-permute-start | bytes 786440 | tf_op jit(solution)/shard_map/ppermute | solution.py:241
  593.6 92.9 %collective-permute-start.30 = (bf16[3,1024,128]{1,2,0:T(8,128)(2,1)}, bf16[3,1024,128]{1,2,0:T(8,128)(2,1)}, u32[]{:S(2)}, u32[]{:S(2)}) collective-permute-start(bf16[3,1024,128]{1,2,0:T(8,128)(2,1)} %fusion.62), channel_id=1, source_target_pairs={{0,8},{1,9},{2,10},{3,11},{4,12},{5,13},{6,14},{7,15},{8,0},{9,1},... | collective-permute-start | bytes 2359304 | tf_op jit(solution)/shard_map/ppermute | solution.py:241
  600.0 80.6 %collective-permute-start.58 = (bf16[328,1024]{1,0:T(8,128)(2,1)}, bf16[328,1024]{1,0:T(8,128)(2,1)}, u32[]{:S(2)}, u32[]{:S(2)}) collective-permute-start(bf16[328,1024]{1,0:T(8,128)(2,1)} %add.428), channel_id=1, source_target_pairs={{0,16},{1,17},{2,18},{3,19},{4,20},{5,21},{6,22},{7,23},{8,24},{9,... | collective-permute-start | bytes 2015240 | tf_op jit(solution)/shard_map/ppermute | solution.py:241
  628.8 54.7 %collective-permute-start.49 = (bf16[328,1024]{1,0:T(8,128)(2,1)}, bf16[328,1024]{1,0:T(8,128)(2,1)}, u32[]{:S(2)}, u32[]{:S(2)}) collective-permute-start(bf16[328,1024]{1,0:T(8,128)(2,1)} %add.421), channel_id=1, source_target_pairs={{0,16},{1,17},{2,18},{3,19},{4,20},{5,21},{6,22},{7,23},{8,24},{9,... | collective-permute-start | bytes 2015240 | tf_op jit(solution)/shard_map/ppermute | solution.py:241
  657.7 44.7 %collective-permute-start.67 = (bf16[328,1024]{1,0:T(8,128)(2,1)}, bf16[328,1024]{1,0:T(8,128)(2,1)}, u32[]{:S(2)}, u32[]{:S(2)}) collective-permute-start(bf16[328,1024]{1,0:T(8,128)(2,1)} %add.435), channel_id=1, source_target_pairs={{0,16},{1,17},{2,18},{3,19},{4,20},{5,21},{6,22},{7,23},{8,24},{9,... | collective-permute-start | bytes 2015240 | tf_op jit(solution)/shard_map/ppermute | solution.py:241
  680.6 32.9 %collective-permute-start.41 = (bf16[128,1024]{1,0:T(8,128)(2,1)S(1)}, bf16[128,1024]{1,0:T(8,128)(2,1)S(1)}, u32[]{:S(2)}, u32[]{:S(2)}) collective-permute-start(bf16[128,1024]{1,0:T(8,128)(2,1)S(1)} %add.411), channel_id=1, source_target_pairs={{0,2},{1,3},{2,0},{3,1},{4,6},{5,7},{6,4},{7,5},{8,10},{9,11},{10,... | collective-permute-start | bytes 786440 | tf_op jit(solution)/shard_map/ppermute | solution.py:241
  680.6 33.0 %collective-permute-start.43 = (bf16[128,1024]{1,0:T(8,128)(2,1)S(1)}, bf16[128,1024]{1,0:T(8,128)(2,1)S(1)}, u32[]{:S(2)}, u32[]{:S(2)}) collective-permute-start(bf16[128,1024]{1,0:T(8,128)(2,1)S(1)} %collective-permute-done.42), channel_id=1, source_target_pairs={{0,2},{1,3},{2,0},{3,1},{4,6},{5,7},{6,4},{7,5},{8,10},{9,11},{10,... | collective-permute-start | bytes 786440 | tf_op jit(solution)/shard_map/ppermute | solution.py:241
  683.5 31.4 %collective-permute-start.60 = (bf16[328,1024]{1,0:T(8,128)(2,1)}, bf16[328,1024]{1,0:T(8,128)(2,1)}, u32[]{:S(2)}, u32[]{:S(2)}) collective-permute-start(bf16[328,1024]{1,0:T(8,128)(2,1)} %add.429), channel_id=1, source_target_pairs={{0,4},{1,5},{2,6},{3,7},{4,0},{5,1},{6,2},{7,3},{8,12},{9,13},{10,... | collective-permute-start | bytes 2015240 | tf_op jit(solution)/shard_map/ppermute | solution.py:241
  686.5 78.5 %collective-permute-start.51 = (bf16[328,1024]{1,0:T(8,128)(2,1)}, bf16[328,1024]{1,0:T(8,128)(2,1)}, u32[]{:S(2)}, u32[]{:S(2)}) collective-permute-start(bf16[328,1024]{1,0:T(8,128)(2,1)} %add.422), channel_id=1, source_target_pairs={{0,4},{1,5},{2,6},{3,7},{4,0},{5,1},{6,2},{7,3},{8,12},{9,13},{10,... | collective-permute-start | bytes 2015240 | tf_op jit(solution)/shard_map/ppermute | solution.py:241
  702.4 62.6 %collective-permute-start.31 = (bf16[3,1024,128]{1,2,0:T(8,128)(2,1)}, bf16[3,1024,128]{1,2,0:T(8,128)(2,1)}, u32[]{:S(2)}, u32[]{:S(2)}) collective-permute-start(bf16[3,1024,128]{1,2,0:T(8,128)(2,1)} %add.403), channel_id=1, source_target_pairs={{0,16},{1,17},{2,18},{3,19},{4,20},{5,21},{6,22},{7,23},{8,24},{9,... | collective-permute-start | bytes 2359304 | tf_op jit(solution)/shard_map/ppermute | solution.py:241
  713.5 56.5 %collective-permute-start.59 = (bf16[328,1024]{1,0:T(8,128)(2,1)}, bf16[328,1024]{1,0:T(8,128)(2,1)S(1)}, u32[]{:S(2)}, u32[]{:S(2)}) collective-permute-start(bf16[328,1024]{1,0:T(8,128)(2,1)} %add.429), channel_id=1, source_target_pairs={{0,2},{1,3},{2,0},{3,1},{4,6},{5,7},{6,4},{7,5},{8,10},{9,11},{10,... | collective-permute-start | bytes 2015240 | tf_op jit(solution)/shard_map/ppermute | solution.py:241
  714.2 56.0 %collective-permute-start.69 = (bf16[328,1024]{1,0:T(8,128)(2,1)S(1)}, bf16[328,1024]{1,0:T(8,128)(2,1)S(1)}, u32[]{:S(2)}, u32[]{:S(2)}) collective-permute-start(bf16[328,1024]{1,0:T(8,128)(2,1)S(1)} %add.436), channel_id=1, source_target_pairs={{0,4},{1,5},{2,6},{3,7},{4,0},{5,1},{6,2},{7,3},{8,12},{9,13},{10,... | collective-permute-start | bytes 2015240 | tf_op jit(solution)/shard_map/ppermute | solution.py:241
  714.9 55.7 %collective-permute-start.61 = (bf16[328,1024]{1,0:T(8,128)(2,1)}, bf16[328,1024]{1,0:T(8,128)(2,1)}, u32[]{:S(2)}, u32[]{:S(2)}) collective-permute-start(bf16[328,1024]{1,0:T(8,128)(2,1)} %collective-permute-done.60), channel_id=1, source_target_pairs={{0,2},{1,3},{2,0},{3,1},{4,6},{5,7},{6,4},{7,5},{8,10},{9,11},{10,... | collective-permute-start | bytes 2015240 | tf_op jit(solution)/shard_map/ppermute | solution.py:241
  770.6 20.1 %collective-permute-start.33 = (bf16[3,1024,128]{1,2,0:T(8,128)(2,1)S(1)}, bf16[3,1024,128]{1,2,0:T(8,128)(2,1)S(1)}, u32[]{:S(2)}, u32[]{:S(2)}) collective-permute-start(bf16[3,1024,128]{1,2,0:T(8,128)(2,1)S(1)} %add.404), channel_id=1, source_target_pairs={{0,4},{1,5},{2,6},{3,7},{4,0},{5,1},{6,2},{7,3},{8,12},{9,13},{10,... | collective-permute-start | bytes 2359304 | tf_op jit(solution)/shard_map/ppermute | solution.py:241
  774.7 21.2 %collective-permute-start.32 = (bf16[3,1024,128]{1,2,0:T(8,128)(2,1)S(1)}, bf16[3,1024,128]{1,2,0:T(8,128)(2,1)S(1)}, u32[]{:S(2)}, u32[]{:S(2)}) collective-permute-start(bf16[3,1024,128]{1,2,0:T(8,128)(2,1)S(1)} %add.404), channel_id=1, source_target_pairs={{0,2},{1,3},{2,0},{3,1},{4,6},{5,7},{6,4},{7,5},{8,10},{9,11},{10,... | collective-permute-start | bytes 2359304 | tf_op jit(solution)/shard_map/ppermute | solution.py:241
  (112 other events, 1816.2 us)

commit v2 on v1

v2 whole, which is shorter than its diff:
```python
import functools
import math

import jax
import jax.numpy as jnp
from jax import lax
from jax.experimental import pallas as pl
from jax.experimental.pallas import tpu as pltpu
from jax.sharding import PartitionSpec as P

AXES = ("dp", "tensor")
EPS = 1e-05
HEAD_DIM = 64
HALF = 64
MAXLEN = 1024
BQ = 128
LOW = jnp.bfloat16
NEG = -1e30


def cols_dot(left, right):
    return lax.dot_general(left, right, (((1,), (1,)), ((), ())), preferred_element_type=jnp.float32)


def rows_dot(left, right):
    return lax.dot_general(left, right, (((0,), (0,)), ((), ())), preferred_element_type=jnp.float32)


def plain_dot(left, right):
    return lax.dot_general(left, right, (((1,), (0,)), ((), ())), preferred_element_type=jnp.float32)


def norm_parts(values):
    center = values - jnp.mean(values, -1, keepdims=True)
    rate = lax.rsqrt(jnp.mean(center * center, -1, keepdims=True) + EPS)
    return center * rate, rate


def shaped(shape, dtype=LOW):
    return jax.ShapeDtypeStruct(shape, dtype)


def run(body, name, grid, ins, outs, after=(), place=None, scratch=(), flops=0, vmem=56, seen=False):
    extra = [a for a in after if a is not None]
    count = len(ins)

    def kernel(*refs):
        lead = refs[:1] if place is not None else ()
        refs = refs[len(lead):]
        body(*lead, *refs[:count], *refs[count + len(extra):])

    def spec(block, index):
        if place is not None and not seen:
            return pl.BlockSpec(block, lambda *a: index(*a[:-1]))
        return pl.BlockSpec(block, index)

    call = pl.pallas_call(
        kernel,
        grid_spec=pltpu.PrefetchScalarGridSpec(
            num_scalar_prefetch=0 if place is None else 1,
            grid=grid,
            in_specs=[spec(b, m) for _, b, m in ins] + [pl.BlockSpec(memory_space=pl.ANY)] * len(extra),
            out_specs=[spec(b, m) for _, b, m in outs],
            scratch_shapes=list(scratch),
        ),
        out_shape=[s for s, _, _ in outs],
        compiler_params=pltpu.CompilerParams(vmem_limit_bytes=vmem << 20),
        cost_estimate=pl.CostEstimate(flops=1000, bytes_accessed=1000, transcendentals=0),
        name=name,
    )
    lead = () if place is None else (place,)
    return call(*lead, *[a for a, _, _ in ins], *extra)


def window_masks(pos0, length):
    j = lax.broadcasted_iota(jnp.int32, (BQ, 2 * BQ), 0)
    i = lax.broadcasted_iota(jnp.int32, (BQ, 2 * BQ), 1) % BQ
    near = i <= j
    key_pos = pos0 - HALF + j + jnp.where(near, 0, BQ)
    top = jnp.minimum(length, MAXLEN)
    own = j == (i + HALF) % BQ
    bias = jnp.where(((key_pos >= 0) & (key_pos < top)) | own, 0.0, NEG)
    lane = lax.broadcasted_iota(jnp.int32, (1, 2 * BQ), 1) % BQ
    last_bias = jnp.where(pos0 + HALF + lane < top, 0.0, NEG)
    return near, i == j, bias, last_bias


def split_heads(pair):
    lane = lax.broadcasted_iota(jnp.int32, pair.shape, 1)
    zero = jnp.zeros_like(pair)
    return jnp.concatenate([jnp.where(lane < HEAD_DIM, pair, zero), jnp.where(lane >= HEAD_DIM, pair, zero)], 0)


def join_heads(wide, scale=None):
    first, second = wide[:HEAD_DIM, :BQ], wide[HEAD_DIM:, BQ:]
    if scale is not None:
        first, second = first * scale[:, :BQ], second * scale[:, BQ:]
    return jnp.concatenate([first, second], 0).T


def fold(near, diag, wide):
    low = wide[BQ:]
    return jnp.where(near, wide[:BQ], low), jnp.sum(jnp.where(diag, low, 0.0), 0, keepdims=True)


def unfold(near, diag, tile, last):
    zero = jnp.zeros_like(tile)
    return jnp.concatenate(
        [jnp.where(near, tile, zero), jnp.where(near, jnp.where(diag, last, zero), tile)], 0
    ).astype(LOW)


def window_rows(before, here, after, c):
    return jnp.concatenate([before[:, c], here[:, c], after[:, c]], 0)


def attend_kernel(place, q, kb, kh, ka, vb, vh, va, out_ref, log_ref):
    blk = pl.program_id(0)
    near, diag, bias, last_bias = window_masks(place[0, blk], place[1, blk])
    for pair in range(out_ref.shape[1] // BQ):
        c = slice(pair * BQ, (pair + 1) * BQ)
        queries = split_heads(q[:, c] * 0.125)
        keyset = window_rows(kb, kh, ka, c)
        values = window_rows(vb, vh, va, c)
        scores, last = fold(near, diag, cols_dot(keyset, queries))
        scores, last = scores + bias, last + last_bias
        row_max = jnp.maximum(jnp.max(scores, 0, keepdims=True), last)
        expons, last = jnp.exp(scores - row_max), jnp.exp(last - row_max)
        summed = jnp.sum(expons, 0, keepdims=True) + last
        probs = unfold(near, diag, expons, last)
        out_ref[:, c] = join_heads(rows_dot(values, probs), 1.0 / summed).astype(LOW)
        log_ref[0, pair:pair + 1] = row_max + jnp.log(summed)


def attend_back_kernel(place, q, kb, kh, ka, vb, vh, va, g_ref, log_ref, d_ref, edge_ref, carry, tail, dq_keep):
    step = pl.program_id(0)
    steps = pl.num_programs(0)
    width = g_ref.shape[1]

    @pl.when(step == 0)
    def _():
        carry[...] = jnp.zeros_like(carry)
        tail[...] = jnp.zeros_like(tail)
        dq_keep[...] = jnp.zeros_like(dq_keep)

    d_ref[:, :width] = dq_keep[...]
    d_ref[:HALF, width:] = tail[...]

    @pl.when(step < steps - 1)
    def _():
        near, diag, bias, last_bias = window_masks(place[0, step], place[1, step])
        for pair in range(width // BQ):
            c = slice(pair * BQ, (pair + 1) * BQ)
            v = slice(width + pair * BQ, width + (pair + 1) * BQ)
            queries = split_heads(q[:, c] * 0.125)
            keyset = window_rows(kb, kh, ka, c)
            values = window_rows(vb, vh, va, c)
            grads = split_heads(g_ref[:, c])
            log_row = log_ref[0, pair:pair + 1]
            scores, last = fold(near, diag, cols_dot(keyset, queries))
            expons, last = jnp.exp(scores + (bias - log_row)), jnp.exp(last + (last_bias - log_row))
            prob_grad, last_grad = fold(near, diag, cols_dot(values, grads))
            inner = jnp.sum(expons * prob_grad, 0, keepdims=True) + last * last_grad
            score_grad = unfold(near, diag, expons * (prob_grad - inner), last * (last_grad - inner))
            probs = unfold(near, diag, expons, last)
            dq_keep[:, c] = join_heads(rows_dot(keyset, score_grad) * 0.125).astype(LOW)
            for lanes, grad in ((c, plain_dot(score_grad, queries)), (v, plain_dot(probs, grads))):
                done = (carry[:, lanes] + grad[:BQ]).astype(LOW)
                carry[:, lanes] = grad[BQ:]
                d_ref[HALF:, lanes.start + width:lanes.stop + width] = done[:HALF]
                tail[:, lanes] = done[HALF:]
                edge_ref[0, :, lanes] = jnp.where(step == 0, done[:HALF], edge_ref[0, :, lanes])

    @pl.when(step == steps - 1)
    def _():
        done = carry[...].astype(LOW)
        d_ref[HALF:, width:] = done[:HALF]
        edge_ref[1] = done[HALF:]


def window_specs(q, k, v, blocks):
    last, width = blocks - 1, k.shape[1]
    here = lambda b: (jnp.minimum(b, last), 0)
    before = lambda b: (jnp.where(b == 0, 2 * blocks, 2 * jnp.minimum(b, last) - 1), 0)
    after = lambda b: (jnp.where(b >= last, 2 * blocks + 1, 2 * b + 2), 0)
    specs = [(q, (BQ, width), here)]
    for value in (k, v):
        specs += [(value, (HALF, width), before), (value, (BQ, width), here), (value, (HALF, width), after)]
    return specs


def attend(place, q, k, v, after=()):
    blocks, width = k.shape[0] // BQ - 1, k.shape[1]
    pairs = width // BQ
    return run(
        attend_kernel, "attend", (blocks,), window_specs(q, k, v, blocks),
        [
            (shaped((blocks * BQ, width)), (BQ, width), lambda b: (b, 0)),
            (shaped((blocks, pairs, 2 * BQ), jnp.float32), (1, pairs, 2 * BQ), lambda b: (b, 0, 0)),
        ],
        after, place, flops=blocks * pairs * BQ * BQ * BQ * 256,
    )


def attend_back(place, q, k, v, grads, logs, after=()):
    blocks, width = grads.shape[0] // BQ, k.shape[1]
    pairs = width // BQ
    last = blocks - 1
    return run(
        attend_back_kernel, "attend_back", (blocks + 1,),
        window_specs(q, k, v, blocks)
        + [
            (grads, (BQ, width), lambda b: (jnp.minimum(b, last), 0)),
            (logs, (1, pairs, 2 * BQ), lambda b: (jnp.minimum(b, last), 0, 0)),
        ],
        [
            (shaped((blocks * BQ, 3 * width)), (BQ, 3 * width), lambda b: (jnp.maximum(b - 1, 0), 0)),
            (shaped((2, HALF, 2 * width)), (2, HALF, 2 * width), lambda b: (0, 0, 0)),
        ],
        after, place,
        scratch=[
            pltpu.VMEM((BQ, 2 * width), jnp.float32),
            pltpu.VMEM((HALF, 2 * width), LOW),
            pltpu.VMEM((BQ, width), LOW),
        ],
        flops=blocks * pairs * BQ * BQ * BQ * 512,
    )


def norm_kernel(tokens, before, after, gain, out):
    step, tile = pl.program_id(0), tokens.shape[0]

    @pl.when(step < pl.num_programs(0) - 1)
    def _():
        out[...] = (norm_parts(tokens[...].astype(jnp.float32))[0] * gain[...]).astype(LOW)

    @pl.when(step == pl.num_programs(0) - 1)
    def _():
        values = jnp.concatenate([before[...], after[...]], 0).astype(jnp.float32)
        out[:BQ] = (norm_parts(values)[0] * gain[...]).astype(LOW)


def norm_rows(tokens, before, after, gain):
    rows, model = tokens.shape
    tile = 3 * BQ
    blocks = rows // tile
    full = lambda i: (0, 0)
    return run(
        norm_kernel, "norm_rows", (blocks + 1,),
        [
            (tokens, (tile, model), lambda i: (jnp.minimum(i, blocks - 1), 0)),
            (before, (HALF, model), full), (after, (HALF, model), full), (gain, (1, model), full),
        ],
        [(shaped((rows + BQ, model)), (tile, model), lambda i: (i, 0))],
    )[0]


def project_kernel(normed, weights, *outs):
    for i, out in enumerate(outs):
        out[...] = plain_dot(normed[...], weights[i]).astype(LOW)


def project(normed, weights, after=()):
    rows, model = normed.shape
    width = weights.shape[2]
    tile = rows // 4 if rows % 64 == 0 else rows
    return run(
        project_kernel, "project", (rows // tile,),
        [(normed, (tile, model), lambda i: (i, 0)), (weights, (3, model, width), lambda i: (0, 0, 0))],
        [(shaped((rows, width)), (tile, width), lambda i: (i, 0))] * 3,
        after, flops=6 * rows * model * width,
    )


def project_parts_kernel(normed, mine, other, *outs):
    size = mine.shape[2]
    for i, out in enumerate(outs):
        out[:, :size] = plain_dot(normed[...], mine[i]).astype(LOW)
        out[:, size:] = plain_dot(normed[...], other[i]).astype(LOW)


def project_parts(normed, parts, after=()):
    rows, model = normed.shape
    size = parts[0].shape[2]
    tile = rows // 4
    return run(
        project_parts_kernel, "project_parts", (rows // tile,),
        [(normed, (tile, model), lambda i: (i, 0))] + [(p, (3, model, size), lambda i: (0, 0, 0)) for p in parts],
        [(shaped((rows, 2 * size)), (tile, 2 * size), lambda i: (i, 0))] * 3,
        after,
    )


def out_rows(part):
    size = part.shape[2]
    return jnp.concatenate([part[3, k * size:(k + 1) * size] for k in range(part.shape[1] // size)], 1)


def row_tile(rows):
    return 256 if rows % 256 == 0 else 128


def keep_rows(place, step, tile):
    row = lax.broadcasted_iota(jnp.int32, (BQ, 1), 0)
    parts = []
    for i in range(tile // BQ):
        b = step * (tile // BQ) + i
        parts.append(jnp.where(row + place[0, b] < place[1, b], 1.0, 0.0))
    return jnp.concatenate(parts, 0)


def mix_kernel(tokens, gain, attended, weights, *refs):
    attended_more, parts, (hidden, normed) = refs[:1], refs[1:-2], refs[-2:]
    total = tokens[...].astype(jnp.float32) + plain_dot(attended[...], weights[...])
    for side, part in enumerate(parts):
        size = part.shape[2]
        total = total + plain_dot(attended_more[0][:, side * size:(side + 1) * size], out_rows(part))
    hidden[...] = total
    normed[...] = (norm_parts(total)[0] * gain[...]).astype(LOW)


def mix(tokens, gain, attended, weights, more=None, parts=(), after=()):
    rows, model = tokens.shape
    tile = row_tile(rows)
    row, full = (lambda i: (i, 0)), (lambda i: (0, 0))
    width = weights.shape[0]
    return run(
        mix_kernel, "mix", (rows // tile,),
        [(tokens, (tile, model), row), (gain, (1, model), full), (attended, (tile, width), row), (weights, weights.shape, full)]
        + [(attended if more is None else more, (tile, width), row)]
        + [(p, p.shape, lambda i: (0, 0, 0)) for p in parts],
        [(shaped((rows, model), jnp.float32), (tile, model), row), (shaped((rows, model)), (tile, model), row)],
        after,
    )


def gelu_parts(value):
    size = jnp.abs(value)
    bell = jnp.exp(-0.5 * value * value)
    t = 1.0 / (1.0 + (0.3275911 * 2.0 ** -0.5) * size)
    series = t * (0.254829592 + t * (-0.284496736 + t * (1.421413741 + t * (-1.453152027 + t * 1.061405429))))
    tail = 0.5 * series * bell
    below = jnp.where(value < 0, tail, 1.0 - tail)
    return value * below, below + value * bell * ((2.0 * math.pi) ** -0.5)


def mlp_body(place, normed, cotangent, win, wdown, gate_ref, lift_ref):
    tile = normed.shape[0]
    kept = keep_rows(place, pl.program_id(0), tile)
    out_grad = kept * cotangent[...].astype(jnp.float32)
    out_low = out_grad.astype(LOW)
    first = cols_dot(normed[...], win[0])
    second = cols_dot(normed[...], win[1])
    gelu, slope = gelu_parts(first)
    gate = (gelu * second).astype(LOW)
    gate_ref[0] = gate
    branch = plain_dot(gate, wdown[...])
    grad = cols_dot(out_low, wdown[...])
    lift1 = (grad * second * slope).astype(LOW)
    lift2 = (grad * gelu).astype(LOW)
    lift_ref[0] = lift1
    lift_ref[1] = lift2
    pulled = plain_dot(lift1, win[0]) + plain_dot(lift2, win[1])
    return kept, out_grad, out_low, branch, pulled


def mlp_first_kernel(place, normed, cotangent, win, wdown, gate_ref, lift_ref, low_ref, branch_ref, pulled_ref):
    _, _, out_low, branch, pulled = mlp_body(place, normed, cotangent, win, wdown, gate_ref, lift_ref)
    low_ref[...] = out_low
    branch_ref[...] = branch
    pulled_ref[...] = pulled


def norm_back_rows(values, gain, grad):
    unit, rate = norm_parts(values)
    pulled = grad * gain
    mean_one = jnp.mean(pulled, -1, keepdims=True)
    mean_two = jnp.mean(pulled * unit, -1, keepdims=True)
    return rate * (pulled - mean_one - unit * mean_two), jnp.sum(grad * unit, 0, keepdims=True)


def add_gain(gain_ref, part):
    @pl.when(pl.program_id(0) == 0)
    def _():
        gain_ref[...] = jnp.zeros_like(gain_ref)

    gain_ref[...] += part


def mlp_last_kernel(fetched, place, normed, cotangent, *refs):
    if fetched:
        pieces, refs = refs[:8], refs[8:]
        win, wdown = refs[-2:]

        @pl.when(pl.program_id(0) == 0)
        def _():
            units, model = pieces[0].shape[1:]
            for part in range(4):
                rows = slice(part // 2 * units, (part // 2 + 1) * units)
                columns = pl.ds(pl.multiple_of((place[2, 1] ^ (part % 2)) * model, model), model)
                for side in range(2):
                    win[side, rows, columns] = pieces[part][side]
                wdown[rows, columns] = pieces[4 + part][0]
    else:
        (win, wdown), refs = refs[:2], refs[2:]
    hidden, gain, branch_in, pulled_in, weights = refs[:5]
    parts, refs = (refs[5:7], refs[7:]) if fetched else ((), refs[5:])
    gate_ref, lift_ref, out_ref, grad_ref, low_ref, gain_ref, attn = refs[:7]
    kept, out_grad, _, branch, pulled = mlp_body(place, normed, cotangent, win, wdown, gate_ref, lift_ref)
    out_ref[...] = (kept * (hidden[...] + (branch_in[...] + branch))).astype(LOW)
    back, gain_part = norm_back_rows(hidden[...], gain[...], pulled_in[...] + pulled)
    total = out_grad + back
    grad_ref[...] = total
    low = total.astype(LOW)
    low_ref[...] = low
    attn[...] = cols_dot(low, weights[...]).astype(LOW)
    for side, part in enumerate(parts):
        size = part.shape[2]
        refs[7][:, side * size:(side + 1) * size] = cols_dot(low, out_rows(part)).astype(LOW)
    add_gain(gain_ref, gain_part)


def mlp_specs(normed, cotangent, units):
    rows, model = normed.shape
    tile = row_tile(rows)
    row = lambda i: (i, 0)
    ins = [(normed, (tile, model), row), (cotangent, (tile, model), row)]
    outs = [
        (shaped((1, rows, units)), (1, tile, units), lambda i: (0, i, 0)),
        (shaped((2, rows, units)), (2, tile, units), lambda i: (0, i, 0)),
    ]
    return rows, model, tile, row, ins, outs


def whole(value):
    return (value, value.shape, lambda i: (0,) * value.ndim)


def mlp_first(place, normed, cotangent, win, wdown, after=()):
    rows, model, tile, row, ins, outs = mlp_specs(normed, cotangent, wdown.shape[0])
    outs = outs + [(shaped((rows, model)), (tile, model), row)]
    outs = outs + [(shaped((rows, model), jnp.float32), (tile, model), row)] * 2
    return run(mlp_first_kernel, "mlp_first", (rows // tile,), ins + [whole(win), whole(wdown)], outs, after, place)


def mlp_last(place, normed, cotangent, weights, hidden, gain, branch, pulled, w_out, parts=(), after=()):
    fetched = len(weights) == 8
    units = 2 * weights[4].shape[1] if fetched else weights[1].shape[0]
    rows, model, tile, row, ins, outs = mlp_specs(normed, cotangent, units)
    block = (tile, model)
    ins = ins + [whole(w) for w in weights]
    ins = ins + [(hidden, block, row), whole(gain), (branch, block, row), (pulled, block, row), whole(w_out)]
    ins = ins + [whole(p) for p in parts]
    outs = outs + [
        (shaped((rows, model)), block, row), (shaped((rows, model), jnp.float32), block, row),
        (shaped((rows, model)), block, row), (shaped((1, model), jnp.float32), (1, model), lambda i: (0, 0)),
    ]
    width = w_out.shape[0]
    outs = outs + [(shaped((rows, width)), (tile, width), row)] * (2 if fetched else 1)
    scratch = [pltpu.VMEM((2, units, model), LOW), pltpu.VMEM((units, model), LOW)] if fetched else []
    return run(
        functools.partial(mlp_last_kernel, fetched), "mlp_last", (rows // tile,), ins, outs, after, place, scratch, vmem=60
    )


def store_halves(value, core, keep, send, index):
    size = value.shape[0] // 2
    low, high = value[:size].astype(LOW), value[size:].astype(LOW)
    if core is None:
        keep[index], send[index] = low, high
    else:
        keep[index] = jnp.where(core == 0, low, high)
        send[index] = jnp.where(core == 0, high, low)


def outer_kernel(own, flags, left, right, keep, send):
    store_halves(rows_dot(left[0], right[...]), flags[0] if own else None, keep, send, 0)


def outer(flags, own, left, right, after=(), side=None):
    sides, rows, units = left.shape
    model = right.shape[1]
    tile = min(512, model)
    first = 0 if side is None else side
    sides = sides if side is None else 1
    out = (shaped((sides, units // 2, model)), (1, units // 2, tile), lambda s, j: (s, 0, j))
    return run(
        functools.partial(outer_kernel, own), "outer", (sides, model // tile),
        [(left, (1, rows, units), lambda s, j: (s + first, 0, 0)), (right, (rows, tile), lambda s, j: (0, j))],
        [out, out], after, flags,
    )


def outer_down_kernel(own, flags, gate, attended, low, hidden, keep, send):
    first, second = rows_dot(gate[0], low[...]), rows_dot(attended[...], hidden[...])
    core = flags[0] if own else None
    size = first.shape[0] // 2
    store_halves(first, core, keep.at[:, :size], send.at[:, :size], 0)
    store_halves(second, core, keep.at[:, size:], send.at[:, size:], 0)


def outer_down(flags, own, gate, attended, low, hidden, after=()):
    _, rows, units = gate.shape
    width, model = attended.shape[1], low.shape[1]
    tile = min(512, model)
    part = lambda j: (0, j)
    out = (shaped((1, (units + width) // 2, model)), (1, (units + width) // 2, tile), lambda j: (0, 0, j))
    return run(
        functools.partial(outer_down_kernel, own), "outer_down", (model // tile,),
        [(gate, (1, rows, units), lambda j: (0, 0, 0)), (attended, (rows, width), lambda j: (0, 0)),
         (low, (rows, tile), part), (hidden, (rows, tile), part)],
        [out, out], after, flags,
    )


def outer_attn_kernel(own, flags, normed, grads, keep, send):
    width = grads.shape[1] // 3
    size = width // 2
    for i in range(3):
        value = rows_dot(normed[...], grads[:, i * width:(i + 1) * width])
        low, high = value[:, :size].astype(LOW), value[:, size:].astype(LOW)
        if own:
            low, high = jnp.where(flags[0] == 0, low, high), jnp.where(flags[0] == 0, high, low)
        keep[i] = low
        send[i] = high


def outer_attn(flags, own, normed, grads, after=()):
    rows, width = grads.shape[0], grads.shape[1] // 3
    model = normed.shape[1]
    tile = min(512, model)
    out = (shaped((3, model, width // 2)), (3, tile, width // 2), lambda i: (0, i, 0))
    return run(
        functools.partial(outer_attn_kernel, own), "outer_attn", (model // tile,),
        [(normed, (rows, tile), lambda i: (0, i)), (grads, (rows, 3 * width), lambda i: (0, 0))],
        [out, out], after, flags,
    )


def pull_kernel(tokens, hidden_grad, gain, grads, weights, *refs):
    more, parts, (out, gain_ref) = refs[:1], refs[1:-2], refs[-2:]
    width = weights.shape[2]
    total = None
    for i in range(3):
        terms = [cols_dot(grads[:, i * width:(i + 1) * width], weights[i])]
        for side, part in enumerate(parts):
            size = part.shape[2]
            first = i * width + side * size
            terms.append(cols_dot(more[0][:, first:first + size], part[i]))
        for term in terms:
            total = term if total is None else total + term
    back, gain_part = norm_back_rows(tokens[...].astype(jnp.float32), gain[...], total)
    out[...] = hidden_grad[...] + back
    add_gain(gain_ref, gain_part)


def pull(tokens, hidden_grad, gain, grads, weights, more=None, parts=(), after=()):
    rows, model = tokens.shape
    tile = row_tile(rows)
    row = lambda i: (i, 0)
    size = grads.shape[1]
    return run(
        pull_kernel, "pull", (rows // tile,),
        [(tokens, (tile, model), row), (hidden_grad, (tile, model), row), whole(gain), (grads, (tile, size), row), whole(weights)]
        + [(grads if more is None else more, (tile, size), row)]
        + [(p, (3,) + p.shape[1:], lambda i: (0, 0, 0)) for p in parts],
        [(shaped((rows, model), jnp.float32), (tile, model), row), (shaped((1, model), jnp.float32), (1, model), lambda i: (0, 0))],
        after,
    )


def assemble_call(body, mine, other, core, outs, after):
    same = lambda i, s: (0,) * mine.ndim
    return pl.pallas_call(
        lambda *refs: body(*refs[:3], *refs[3 + len(after):]),
        grid_spec=pltpu.PrefetchScalarGridSpec(
            num_scalar_prefetch=1, grid=(2,),
            in_specs=[pl.BlockSpec(mine.shape, same)] * 2 + [pl.BlockSpec(memory_space=pl.ANY)] * len(after),
            out_specs=[
                pl.BlockSpec(block, functools.partial(lambda axis, rank, i, s: tuple((i ^ s[0]) * (d == axis) for d in range(rank)), axis, len(block)))
                for _, block, axis in outs
            ],
        ),
        out_shape=[shaped(shape, jnp.float32) for shape, _, _ in outs],
        compiler_params=pltpu.CompilerParams(vmem_limit_bytes=56 << 20),
        name="assemble",
    )(jnp.reshape(core, (1,)).astype(jnp.int32), mine, other, *after)


def assemble_kernel(side, mine, other, out):
    out[...] = jnp.where(pl.program_id(0) == 0, mine[...], other[...]).astype(jnp.float32)


def assemble(mine, other, core, axis, after=()):
    shape = tuple(2 * n if d == axis else n for d, n in enumerate(mine.shape))
    return assemble_call(assemble_kernel, mine, other, core, [(shape, mine.shape, axis)], after)[0]


def assemble_down_kernel(side, mine, other, down, out):
    chosen = jnp.where(pl.program_id(0) == 0, mine[0], other[0]).astype(jnp.float32)
    size = down.shape[0]
    down[...] = chosen[:size]
    out[...] = chosen[size:]


def assemble_down(mine, other, core, units, after=()):
    _, rows, model = mine.shape
    sizes = (units // 2, rows - units // 2)
    return assemble_call(
        assemble_down_kernel, mine, other, core, [((2 * n, model), (n, model), 0) for n in sizes], after
    )


class Links:
    def __init__(self, dp, tensor):
        self.dp, self.tensor = dp, tensor
        self.id = lax.axis_index("dp")
        self.core, self.row = self.id % 2, self.id // 2 % 2

    def send(self, value, target):
        pairs = [
            (d * self.tensor + t, to)
            for d in range(self.dp) for t in range(self.tensor)
            for to in [target(d, t)] if to is not None
        ]
        return lax.ppermute(value, AXES, pairs)

    def cross(self, value):
        return self.send(value, lambda d, t: d * self.tensor + (1 - t))

    def flip(self, value, even, odd=None):
        bits = (even, even if odd is None else odd)
        return self.send(value, lambda d, t: (d ^ bits[d % 2]) * self.tensor + t)

    def shift(self, value, by):
        return self.send(value, lambda d, t: d * self.tensor + t + by if 0 <= t + by < self.tensor else None)

    def bit_of(self, even, odd):
        return jnp.where(self.core == 0, (self.id & even) // even, (self.id & odd) // odd)


def tie(value, *others):
    return lax.optimization_barrier((value,) + others)[0]


def half(value, index, axis):
    size = value.shape[axis] // 2
    if isinstance(index, int):
        return lax.slice_in_dim(value, index * size, (index + 1) * size, axis=axis)
    return lax.dynamic_slice_in_dim(value, index * size, size, axis)


def order(bit, first, second, axis):
    return jnp.where(bit == 0, jnp.concatenate([first, second], axis), jnp.concatenate([second, first], axis))


class Summing:
    ROW_FIRST = ((2, 2, 1), (4, 4, 2), (8, 8, 3))
    SPLIT = ((2, 4, 4), (4, 8, 5), (8, 2, 6))

    def __init__(self, links, flags, axis, steps):
        self.links, self.flags, self.axis, self.steps = links, flags, axis, steps

    def cores_other(self, keep, send):
        self.keep_other, self.got_other = keep, self.links.flip(send, 1)

    def cores_own(self, keep, send):
        self.keep_own, self.got_own = keep, self.links.flip(send, 1)

    def add_other(self, *after):
        self.far = tie(self.keep_other, *after) + self.got_other
        self.crossed = self.links.cross(self.far)

    def add_own(self, *after):
        self.near = tie(self.keep_own, *after) + self.got_own

    def across(self, *after, parts=None):
        self.split(0, self.near, self.crossed if parts is None else jnp.concatenate(parts, 0), after)

    def split(self, step, a, b, after):
        even, odd, which = self.steps[step]
        a, bit = tie(a, *after), self.flags[which]
        part = lambda k: half(a, k, self.axis) + half(b, k, self.axis)
        self.held, self.moved = part(bit), self.links.flip(part(1 - bit), even, odd)

    def scatter(self, *after):
        self.split(1, self.held, self.moved, after)

    def both(self, *after):
        self.held = tie(self.held, *after) + self.moved
        self.moved = self.links.flip(self.held, *self.steps[2][:2])

    def both_add(self, *after):
        self.held = tie(self.held, *after) + self.moved
        self.moved = self.links.flip(self.held, *self.steps[1][:2])

    def gather(self, *after):
        self.held = order(self.flags[self.steps[1][2]], tie(self.held, *after), self.moved, self.axis)
        self.moved = self.links.flip(self.held, *self.steps[0][:2])

    def last(self, *after):
        self.held = order(self.flags[self.steps[0][2]], tie(self.held, *after), self.moved, self.axis)
        self.moved = self.links.flip(self.held, 1)
        return self.held, self.moved, self.links.core


def on_device(tokens, lengths, order_, gain_attn, w_qkv, w_out, gain_mlp, w_in, w_down, cotangent):
    rows, model = tokens.shape
    dp, tensor = lax.axis_size("dp"), lax.axis_size("tensor")
    tensor_id = lax.axis_index("tensor")
    links = Links(dp, tensor)
    paired = tensor == 2 and dp == 16

    slot_count = rows * tensor // MAXLEN
    my_order = lax.dynamic_slice_in_dim(order_, links.id * slot_count, slot_count, 0)
    chosen = my_order[:, None] == jnp.arange(lengths.shape[0], dtype=jnp.int32)[None, :]
    slot_len = jnp.sum(jnp.where(chosen, lengths[None, :], 0), 1)
    slots = jnp.arange(slot_count, dtype=jnp.int32)[None, :]
    block_row = tensor_id * rows + BQ * jnp.arange(rows // BQ, dtype=jnp.int32)
    block_len = jnp.sum(jnp.where((block_row // MAXLEN)[:, None] == slots, slot_len[None, :], 0), 1)
    place = jnp.stack([block_row % MAXLEN, block_len])

    w_qkv = w_qkv.transpose(1, 0, 2)
    w_in = w_in.transpose(1, 2, 0)
    gain_attn, gain_mlp = gain_attn[None], gain_mlp[None]
    if not paired:
        before, after = links.shift(tokens[rows - HALF:], 1), links.shift(tokens[:HALF], -1)
        return general(
            links, place, tokens, before, after, gain_attn, w_qkv, w_out, gain_mlp, w_in, w_down, cotangent
        )

    start = jnp.where(tensor_id == 0, rows - HALF, 0)
    border = links.cross(lax.dynamic_slice_in_dim(tokens, start, HALF, 0))
    core = links.core
    bits = [links.id // bit % 2 for bit in (1, 2, 4, 8)]
    split_bits = [jnp.where(core == 0, bits[i], bits[j]) for i, j in ((1, 2), (2, 3), (3, 1))]
    flags = jnp.stack(bits + split_bits).astype(jnp.int32)
    place = jnp.concatenate([place, jnp.pad(flags, (0, place.shape[1] - flags.shape[0]))[None]], 0)
    width, units = w_out.shape[0], w_down.shape[0]
    size = width // 2
    out_half = half(tie(w_out, border), core, 0)
    stacked = jnp.concatenate([out_half[:, k * size:(k + 1) * size] for k in range(model // size)], 0)
    piece = jnp.concatenate([half(tie(w_qkv, border), core, 2), stacked[None]], 0)
    attn_direct = links.cross(piece)

    normed = norm_rows(tokens, border, border, gain_attn)
    quarter = lambda w, a, b: half(half(w, core, a), bits[1], b)
    in_direct = links.cross(quarter(tie(w_in, normed), 1, 2))
    down_direct = links.cross(quarter(tie(w_down, normed)[None], 1, 2))
    q0, k0, v0 = project(normed, w_qkv)
    attended0, logs0 = attend(place, q0, k0, v0)
    attn_parts = (attn_direct, links.flip(tie(attn_direct, attended0), 1))
    q1, k1, v1 = project_parts(normed, attn_parts, after=[attended0])
    attended1, logs1 = attend(place, q1, k1, v1)
    in_direct = tie(in_direct, attended1)
    in_relayed = links.flip(in_direct, 2)
    in_core = links.flip(in_direct, 1)
    hidden, normed_mlp = mix(tokens, gain_mlp, attended0, w_out, attended1, attn_parts, after=[in_direct])
    gate0, lift0, out_low, branch, pulled = mlp_first(place, normed_mlp, cotangent, w_in, w_down, after=[in_core])
    down_direct = tie(down_direct, hidden)
    down_relayed = links.flip(down_direct, 2)
    down_core = links.flip(down_direct, 1)
    in_relayed = tie(in_relayed, branch)
    down_relayed = tie(down_relayed, in_relayed)
    weights = (
        in_direct, in_relayed, in_core, links.flip(in_relayed, 1),
        down_direct, down_relayed, down_core, links.flip(down_relayed, 1),
    )
    gate1, lift1, output, hidden_grad, hidden_low, gain_mlp_grad, back0, back1 = mlp_last(
        place, normed_mlp, cotangent, weights, hidden, gain_mlp, branch, pulled, w_out, attn_parts
    )
    inner = Summing(links, flags, 2, Summing.ROW_FIRST)
    inner_a, inner_b = (Summing(links, flags, 2, Summing.ROW_FIRST) for _ in range(2))
    down = Summing(links, flags, 2, Summing.SPLIT)
    attn = Summing(links, flags, 1, Summing.SPLIT)

    inner_a.cores_other(*outer(flags, False, lift1, normed_mlp, after=[back1], side=0))
    inner_b.cores_other(*outer(flags, False, lift1, normed_mlp, after=[inner_a.keep_other], side=1))
    inner_a.add_other(inner_b.keep_other)
    inner.cores_own(*outer(flags, True, lift0, normed_mlp, after=[inner_a.far]))
    inner_b.add_other(inner.keep_own)
    d1, edge1 = attend_back(place, q1, k1, v1, back1, logs1, after=[inner_b.far])
    inner.add_own(d1, inner_a.crossed)
    down.cores_other(*outer_down(flags, False, gate1, attended1, out_low, hidden_low, after=[inner.near]))
    d0, edge0 = attend_back(place, q0, k0, v0, back0, logs0, after=[down.keep_other])
    down.add_other(d0)
    inner.across(down.far, parts=[inner_a.crossed, inner_b.crossed])

    swap = lambda e: jnp.where(core == 0, e, jnp.concatenate([e[:, size:], e[:, :size]], 1))
    edge_out = lambda e: jnp.concatenate([swap(e[:, :width]), swap(e[:, width:])], 1)
    edges = jnp.stack([edge_out(jnp.where(tensor_id == 0, e[1], e[0])) for e in (edge1, edge0)])
    edges = links.cross(edges)

    def add_edge(d, edge):
        held = lax.dynamic_slice(d, (start, width), (HALF, 2 * width))
        return lax.dynamic_update_slice(d, held + edge, (start, width))

    d1, d0 = add_edge(d1, edges[1]), add_edge(d0, edges[0])
    attn.cores_other(*outer_attn(flags, False, normed, d1, after=[inner.held]))
    attn.cores_own(*outer_attn(flags, True, normed, d0, after=[attn.keep_other]))
    attn.add_other(attn.keep_own)
    down.cores_own(*outer_down(flags, True, gate0, attended0, out_low, hidden_low, after=[attn.far]))
    inner.scatter(down.keep_own)
    attn.add_own(inner.held)
    down.add_own(attn.near)
    input_grad, gain_attn_grad = pull(
        tokens, hidden_grad, gain_attn, d0, w_qkv, d1, attn_parts, after=[down.near, inner.held]
    )
    inner.both(input_grad)
    down.across(inner.held)
    gain_total = jnp.concatenate((gain_attn_grad, gain_mlp_grad))
    gain_total = gain_total + tie(links.cross(gain_total), down.held)
    attn.across(down.held, gain_total)
    down.scatter(attn.held)
    gain_total = gain_total + tie(links.flip(gain_total, 1), down.held)
    inner.both_add(down.held)
    attn.scatter(inner.held, gain_total)
    gain_total = gain_total + tie(links.flip(gain_total, 2), attn.held)
    down.both(attn.held)
    inner.gather(down.held)
    attn.both(inner.held, gain_total)
    gain_total = gain_total + tie(links.flip(gain_total, 4), attn.held)
    down.both_add(attn.held)
    grads_in = inner.last(down.held)
    attn.both_add(grads_in[0], gain_total)
    gain_total = gain_total + tie(links.flip(gain_total, 8), attn.held)
    down.gather(attn.held)
    grad_w_in = assemble(*grads_in, 1, after=[down.held])
    attn.gather(grad_w_in, gain_total)
    grads_down = down.last(attn.held)
    grads_attn = attn.last(grads_down[0])
    grad_w_down, grad_w_out = assemble_down(*grads_down, units, after=[grads_attn[0]])
    grad_w_qkv = assemble(*grads_attn, 2, after=[grad_w_down])
    return (
        output,
        input_grad,
        gain_total[0],
        grad_w_qkv.transpose(1, 0, 2),
        grad_w_out,
        gain_total[1],
        grad_w_in.transpose(2, 0, 1),
        grad_w_down,
    )


def general(links, place, tokens, before, after, gain_attn, w_qkv, w_out, gain_mlp, w_in, w_down, cotangent):
    rows = tokens.shape[0]
    w_qkv, w_out, w_in, w_down = (
        lax.all_gather(w, "tensor", axis=axis, tiled=True)
        for w, axis in ((w_qkv, 2), (w_out, 0), (w_in, 1), (w_down, 0))
    )
    normed = norm_rows(tokens, before, after, gain_attn)
    q, k, v = project(normed, w_qkv)
    attended, logs = attend(place, q, k, v)
    hidden, normed_mlp = mix(tokens, gain_mlp, attended, w_out)
    blank = jnp.zeros_like(hidden)
    gate, lift, output, hidden_grad, hidden_low, gain_mlp_grad, back = mlp_last(
        place, normed_mlp, cotangent, (w_in, w_down), hidden, gain_mlp, blank, blank, w_out
    )
    position = jnp.repeat(place[0], BQ) + jnp.tile(jnp.arange(BQ, dtype=jnp.int32), place.shape[1])
    out_low = jnp.where((position < jnp.repeat(place[1], BQ))[:, None], cotangent, jnp.zeros_like(cotangent))
    flags = jnp.zeros((1,), jnp.int32)
    units, width = w_down.shape[0], w_out.shape[0]
    low, high = outer_down(flags, False, gate, attended, out_low, hidden_low)
    down = jnp.concatenate([low[0, :units // 2], high[0, :units // 2]], 0)
    out = jnp.concatenate([low[0, units // 2:], high[0, units // 2:]], 0)
    inner = jnp.concatenate(outer(flags, False, lift, normed_mlp), 1)
    d, edge = attend_back(place, q, k, v, back, logs)
    d = d.at[:HALF, width:].add(links.shift(edge[1], 1)).at[rows - HALF:, width:].add(links.shift(edge[0], -1))
    qkv = jnp.concatenate(outer_attn(flags, False, normed, d), 2)
    input_grad, gain_attn_grad = pull(tokens, hidden_grad, gain_attn, d, w_qkv)
    down, inner, out, qkv = (
        lax.psum(lax.psum_scatter(g, "tensor", scatter_dimension=axis, tiled=True), "dp").astype(jnp.float32)
        for g, axis in ((down, 0), (inner, 1), (out, 0), (qkv, 2))
    )
    gain_total = lax.psum(jnp.concatenate((gain_attn_grad, gain_mlp_grad)), AXES)
    return (
        output, input_grad, gain_total[0], qkv.transpose(1, 0, 2), out, gain_total[1],
        inner.transpose(2, 0, 1), down,
    )


def solution(mesh):
    split = P(AXES, None)
    wide = P(None, None, "tensor")
    tall = P("tensor", None)
    return jax.shard_map(
        on_device,
        mesh=mesh,
        in_specs=(split, P(), P(), P(), wide, tall, P(), wide, tall, split),
        out_specs=(split, split, P(), wide, tall, P(), wide, tall),
        check_vma=False,
    )
```

time: 816 us -> 615 us (0.75)
  Pallas kernels: 85.9 us -> 324 us
  matrix products: 224 us -> 0 us
  waiting for transfers between devices: 246 us -> 151 us
  local copies, waits for them, and re-layouts: 59.9 us -> 15.2 us
  blocking collectives: 42.9 us -> 0 us
  other arithmetic: 75.6 us -> 52.8 us
  starting transfers between devices: 69 us -> 60.1 us
    pallas_call x4 -> x21, Pallas kernels: 85.9 us -> 324 us  [the longest x18 307 us: run(): return call(*lead, *[a for a, _, _ in ins], *extra)]
    dot_general x42 -> x0, matrix products: 224 us -> none  [the longest x14 89.3 us: cols_dot(): lax.dot_general(left, right, (((1,), (1,)), ((), ())), preferred_element_...]
    ppermute x71 -> x46, waiting for transfers between devices: 246 us -> 151 us  [send(): return lax.ppermute(value, AXES, pairs)]
    psum x1 -> x0, blocking collectives: 42.9 us -> none  [on_device(): gain_total = lax.psum(jnp.stack((gain_attn_grad, gain_mlp_grad)), AXES)]
    unnamed x195 -> x71, local copies, waits for them, and re-layouts: 44.2 us -> 5.68 us
    ppermute x71 -> x46, starting transfers between devices: 69 us -> 60.1 us  [send(): return lax.ppermute(value, AXES, pairs)]
    convert_element_type x4 -> x0, other arithmetic: 8.42 us -> none  [the longest x1 4.73 us: on_device(): hidden_low = hidden_grad.astype(LOW)]
    add x31 -> x24, other arithmetic: 39 us -> 36.6 us  [the longest x6 14.9 us: split(): part = lambda k: half(a, k, self.axis) + half(b, k, self.axis)]
  transfers between devices with their start and end apart: 71 -> 46, of which waited for: 19 -> 19; matrix products, arithmetic and copies ran while one was open for 32% -> 8% of each run, Pallas kernels for 8% -> 39%
where the time goes in v2:
time: 615 us; the launch traced here: 605 us
  Pallas kernels  324 us (53%)
  waiting for transfers between devices  151 us (25%)
  starting transfers between devices  60.1 us (10%)
  other arithmetic  52.8 us (9%)
  local copies, waits for them, and re-layouts  15.2 us (2%)
    pallas_call x18, Pallas kernels, run(): return call(*lead, *[a for a, _, _ in ins], *extra)  307 us
    ppermute x46, waiting for transfers between devices, send(): return lax.ppermute(value, AXES, pairs)  151 us
    ppermute x46, starting transfers between devices, send(): return lax.ppermute(value, AXES, pairs)  60.1 us
    pallas_call x3, Pallas kernels, assemble_call(): pl.pallas_call(lambda *refs: body(*refs[:3], *refs[3 + len(after):]), gri...  17.2 us
    add x6, other arithmetic, split(): part = lambda k: half(a, k, self.axis) + half(b, k, self.axis)  14.9 us
  transfers between devices with their start and end apart: 46, of which 19 were waited for; matrix products, arithmetic and copies ran while one was open for 8% of the time, Pallas kernels for 39%

profile of v2, /device:TPU:0, one launch (start us, length us, event | category | flops | bytes accessed | tf_op | source)
XLA Modules:
  0.0 605.4 jit_solution(6622949944600468952)
XLA Ops:
  1.7 3.0 collective-permute-start
  4.7 3.5 collective-permute-done.refs_1_.refs_2_
  13.6 5.6 norm_rows.1.refs_0_.refs_1_
  19.9 8.9 %project.1 = (bf16[1664,512]{1,0:T(8,128)(2,1)}, bf16[1664,512]{1,0:T(8,128)(2,1)}, bf16[1664,512]{1,0:T(8,128)(2,1)}) custom-call(bf16[1664,1024]{1,0:T(8,128)(2,1)} %norm_rows.1.refs_0_.refs_1_, bf16[3,1024,512]{2,1,0:T(8,128)(2,1)} %bitcast.43), custom_call_target="tpu_custom_call" | custom-call | flops 1000 | bytes 1000 | tf_op jit(solution)/shard_map/project/pallas_call | solution.py:72
  28.8 20.2 %attend.2 = (bf16[1536,512]{1,0:T(8,128)(2,1)}, f32[12,4,256]{2,1,0:T(4,128)}) custom-call(s32[3,12]{1,0:T(4,128)} %pad_add_fusion.refs_0_, bf16[1664,512]{1,0:T(8,128)(2,1)} %get-tuple-element.94.refs_1_, bf16[1664,512]{1,0:T(8,128)(2,1)} %get-tuple-element.95.refs_2_.refs_3_.refs_4_, bf16[1664,512]{1,0:T(8,128)(2,1)} %get-tuple-element.95.refs_2_.refs_3_.refs_4_, ...), custom_call_target="tpu_custom_call" | custom-call | flops 1000 | bytes 1000 | tf_op jit(solution)/shard_map/attend/pallas_call | solution.py:72
  49.0 9.5 %collective-permute-done.1.refs_1_.refs_5_.refs_16_.refs_6_ = bf16[4,1024,256]{2,1,0:T(8,128)(2,1)S(1)} collective-permute-done((bf16[4,1024,256]{2,1,0:T(8,128)(2,1)}, bf16[4,1024,256]{2,1,0:T(8,128)(2,1)S(1)}, u32[]{:S(2)}, u32[]{:S(2)}) %collective-permute-start.1) | collective-permute-done | bytes 2097184 | tf_op jit(solution)/shard_map/ppermute | solution.py:626
  58.4 3.0 constant_dynamic-slice_fusion.1
  62.9 8.9 %project_parts.1 = (bf16[1664,512]{1,0:T(8,128)(2,1)}, bf16[1664,512]{1,0:T(8,128)(2,1)}, bf16[1664,512]{1,0:T(8,128)(2,1)}) custom-call(bf16[1664,1024]{1,0:T(8,128)(2,1)} %norm_rows.1.refs_0_.refs_1_, bf16[4,1024,256]{2,1,0:T(8,128)(2,1)} %copy-done, bf16[4,1024,256]{2,1,0:T(8,128)(2,1)} %collective-permute-done.2.refs_2_.refs_6_.refs_17_.refs_7_, ...), custom_call_target="tpu_custom_call" | custom-call | flops 1000 | bytes 1000 | tf_op jit(solution)/shard_map/project_parts/pallas_call | solution.py:72
  71.8 20.2 %attend.3 = (bf16[1536,512]{1,0:T(8,128)(2,1)}, f32[12,4,256]{2,1,0:T(4,128)}) custom-call(s32[3,12]{1,0:T(4,128)} %pad_add_fusion.refs_0_, bf16[1664,512]{1,0:T(8,128)(2,1)} %get-tuple-element.101.refs_1_, bf16[1664,512]{1,0:T(8,128)(2,1)} %get-tuple-element.102.refs_2_.refs_3_.refs_4_, bf16[1664,512]{1,0:T(8,128)(2,1)} %get-tuple-element.102.refs_2_.refs_3_.refs_4_, ...), custom_call_target="tpu_custom_call" | custom-call | flops 1000 | bytes 1000 | tf_op jit(solution)/shard_map/attend/pallas_call | solution.py:72
  97.0 10.9 %mix.1 = (f32[1536,1024]{1,0:T(8,128)}, bf16[1536,1024]{1,0:T(8,128)(2,1)}) custom-call(bf16[1536,1024]{1,0:T(8,128)(2,1)} %refs_0_.5, f32[1,1024]{1,0:T(1,128)} %bitcast.49, bf16[1536,512]{1,0:T(8,128)(2,1)} %get-tuple-element.97.refs_3_.refs_2_, bf16[512,1024]{1,0:T(8,128)(2,1)} %refs_15_.1, bf16[1536,512]{1,0:T(8,128)(2,1)} %get-tuple-element.104.refs_4_.refs_2_, ...), custom_call_target="tpu_custom_call" | custom-call | flops 1000 | bytes 1000 | tf_op jit(solution)/shard_map/mix/pallas_call | solution.py:72
  108.0 4.8 collective-permute-done.7.refs_7_
  114.5 39.1 %mlp_first.1 = (bf16[1,1536,1312]{2,1,0:T(8,128)(2,1)}, bf16[2,1536,1312]{2,1,0:T(8,128)(2,1)}, bf16[1536,1024]{1,0:T(8,128)(2,1)}, f32[1536,1024]{1,0:T(8,128)}, f32[1536,1024]{1,0:T(8,128)}) custom-call(s32[3,12]{1,0:T(4,128)} %pad_add_fusion.refs_0_, bf16[1536,1024]{1,0:T(8,128)(2,1)} %get-tuple-element.107.refs_1_.refs_2_, bf16[1536,1024]{1,0:T(8,128)(2,1)} %refs_2_.3, ...), custom_call_target="tpu_custom_call" | custom-call | flops 1000 | bytes 1000 | tf_op jit(solution)/shard_map/mlp_first/pallas_call | solution.py:72
  154.2 3.4 collective-permute-done.9.refs_9_
  160.6 48.9 %mlp_last.1 = (bf16[1,1536,1312]{2,1,0:T(8,128)(2,1)}, bf16[2,1536,1312]{2,1,0:T(8,128)(2,1)}, bf16[1536,1024]{1,0:T(8,128)(2,1)}, f32[1536,1024]{1,0:T(8,128)},...) custom-call(s32[3,12]{1,0:T(4,128)} %pad_add_fusion.refs_0_, ...), custom_call_target="tpu_custom_call" | custom-call | flops 1000 | bytes 1000 | tf_op jit(solution)/shard_map/mlp_last/pallas_call | solution.py:72
  209.5 8.9 %outer.3 = (bf16[1,656,1024]{2,1,0:T(8,128)(2,1)}, bf16[1,656,1024]{2,1,0:T(8,128)(2,1)}) custom-call(s32[7]{0:T(128)} %copy-done.32, bf16[2,1536,1312]{2,1,0:T(8,128)(2,1)} %get-tuple-element.123.refs_1_, bf16[1536,1024]{1,0:T(8,128)(2,1)} %get-tuple-element.107.refs_1_.refs_2_, bf16[1536,512]{1,0:T(8,128)(2,1)} %get-tuple-element.124.refs_3_.refs_8_), custom_call_target="tpu_custom_call" | custom-call | flops 1000 | bytes 1000 | tf_op jit(solution)/shard_map/outer/pallas_call | solution.py:72
  218.5 9.0 %outer.4 = (bf16[1,656,1024]{2,1,0:T(8,128)(2,1)}, bf16[1,656,1024]{2,1,0:T(8,128)(2,1)}) custom-call(s32[7]{0:T(128)} %copy-done.32, bf16[2,1536,1312]{2,1,0:T(8,128)(2,1)} %get-tuple-element.123.refs_1_, bf16[1536,1024]{1,0:T(8,128)(2,1)} %get-tuple-element.107.refs_1_.refs_2_, bf16[1,656,1024]{2,1,0:T(8,128)(2,1)} %get-tuple-element.127.refs_3_), custom_call_target="tpu_custom_call" | custom-call | flops 1000 | bytes 1000 | tf_op jit(solution)/shard_map/outer/pallas_call | solution.py:72
  229.1 14.9 %outer.5 = (bf16[2,656,1024]{2,1,0:T(8,128)(2,1)}, bf16[2,656,1024]{2,1,0:T(8,128)(2,1)}) custom-call(s32[7]{0:T(128)} %copy-done.32, bf16[2,1536,1312]{2,1,0:T(8,128)(2,1)} %get-tuple-element.122.refs_1_, bf16[1536,1024]{1,0:T(8,128)(2,1)} %get-tuple-element.107.refs_1_.refs_2_, bf16[1,656,1024]{2,1,0:T(8,128)(2,1)} %add.231.refs_3_), custom_call_target="tpu_custom_call" | custom-call | flops 1000 | bytes 1000 | tf_op jit(solution)/shard_map/outer/pallas_call | solution.py:72
  246.0 5.3 collective-permute-done.12
  255.1 24.4 %attend_back.2 = (bf16[1536,1536]{1,0:T(8,128)(2,1)}, bf16[2,64,1024]{2,1,0:T(8,128)(2,1)}) custom-call(s32[3,12]{1,0:T(4,128)} %pad_add_fusion.refs_0_, bf16[1664,512]{1,0:T(8,128)(2,1)} %get-tuple-element.101.refs_1_, bf16[1664,512]{1,0:T(8,128)(2,1)} %get-tuple-element.102.refs_2_.refs_3_.refs_4_, ...), custom_call_target="tpu_custom_call" | custom-call | flops 1000 | bytes 1000 | tf_op jit(solution)/shard_map/attend_back/pallas_call | solution.py:72
  279.6 4.6 add.233.refs_5_
  284.1 12.0 %outer_down.2 = (bf16[1,912,1024]{2,1,0:T(8,128)(2,1)}, bf16[1,912,1024]{2,1,0:T(8,128)(2,1)}) custom-call(s32[7]{0:T(128)} %copy-done.32, bf16[1,1536,1312]{2,1,0:T(8,128)(2,1)} %get-tuple-element.119.refs_1_, bf16[1536,512]{1,0:T(8,128)(2,1)} %get-tuple-element.104.refs_4_.refs_2_, bf16[1536,1024]{1,0:T(8,128)(2,1)} %get-tuple-element.120.refs_3_, ...), custom_call_target="tpu_custom_call" | custom-call | flops 1000 | bytes 1000 | tf_op jit(solution)/shard_map/outer_down/pallas_call | solution.py:72
  296.2 24.5 %attend_back.3 = (bf16[1536,1536]{1,0:T(8,128)(2,1)}, bf16[2,64,1024]{2,1,0:T(8,128)(2,1)}) custom-call(s32[3,12]{1,0:T(4,128)} %pad_add_fusion.refs_0_, bf16[1664,512]{1,0:T(8,128)(2,1)} %get-tuple-element.94.refs_1_, bf16[1664,512]{1,0:T(8,128)(2,1)} %get-tuple-element.95.refs_2_.refs_3_.refs_4_, ...), custom_call_target="tpu_custom_call" | custom-call | flops 1000 | bytes 1000 | tf_op jit(solution)/shard_map/attend_back/pallas_call | solution.py:72
  324.9 5.7 collective-permute-done.15
  334.5 2.9 dynamic-slice_add_fusion
  337.4 9.9 %outer_attn.2 = (bf16[3,1024,256]{2,1,0:T(8,128)(2,1)}, bf16[3,1024,256]{2,1,0:T(8,128)(2,1)}) custom-call(s32[7]{0:T(128)} %copy-done.32, bf16[1664,1024]{1,0:T(8,128)(2,1)} %norm_rows.1.refs_0_.refs_1_, bf16[1536,1536]{1,0:T(8,128)(2,1)} %get-tuple-element.196.refs_2_.refs_5_, bf16[2,656,512]{2,1,0:T(8,128)(2,1)} %get-tuple-element.149.refs_3_), custom_call_target="tpu_custom_call" | custom-call | flops 1000 | bytes 1000 | tf_op jit(solution)/shard_map/outer_attn/pallas_call | solution.py:72
  348.8 10.1 %outer_attn.3 = (bf16[3,1024,256]{2,1,0:T(8,128)(2,1)}, bf16[3,1024,256]{2,1,0:T(8,128)(2,1)}) custom-call(s32[7]{0:T(128)} %copy-done.32, bf16[1664,1024]{1,0:T(8,128)(2,1)} %norm_rows.1.refs_0_.refs_1_, bf16[1536,1536]{1,0:T(8,128)(2,1)} %get-tuple-element.197.refs_2_.refs_3_, bf16[3,1024,256]{2,1,0:T(8,128)(2,1)} %get-tuple-element.146.refs_3_), custom_call_target="tpu_custom_call" | custom-call | flops 1000 | bytes 1000 | tf_op jit(solution)/shard_map/outer_attn/pallas_call | solution.py:72
  360.4 12.0 %outer_down.3 = (bf16[1,912,1024]{2,1,0:T(8,128)(2,1)}, bf16[1,912,1024]{2,1,0:T(8,128)(2,1)}) custom-call(s32[7]{0:T(128)} %copy-done.32, bf16[1,1536,1312]{2,1,0:T(8,128)(2,1)} %get-tuple-element.140.refs_1_, bf16[1536,512]{1,0:T(8,128)(2,1)} %get-tuple-element.97.refs_3_.refs_2_, bf16[1536,1024]{1,0:T(8,128)(2,1)} %get-tuple-element.120.refs_3_, ...), custom_call_target="tpu_custom_call" | custom-call | flops 1000 | bytes 1000 | tf_op jit(solution)/shard_map/outer_down/pallas_call | solution.py:72
  374.7 4.8 collective-permute-done.19
  386.3 3.6 add.244.refs_8_
  389.9 18.7 %pull.1 = (f32[1536,1024]{1,0:T(8,128)}, f32[1,1024]{1,0:T(1,128)}) custom-call(bf16[1536,1024]{1,0:T(8,128)(2,1)} %refs_0_.5, f32[1536,1024]{1,0:T(8,128)} %get-tuple-element.116.refs_1_, f32[1,1024]{1,0:T(1,128)} %bitcast.52, bf16[1536,1536]{1,0:T(8,128)(2,1)} %get-tuple-element.197.refs_2_.refs_3_, bf16[3,1024,512]{2,1,0:T(8,128)(2,1)} %bitcast.44, ...), custom_call_target="tpu_custom_call" | custom-call | flops 1000 | bytes 1000 | tf_op jit(solution)/shard_map/pull/pallas_call | solution.py:72
  408.8 7.7 %collective-permute-done.24 = bf16[1,912,1024]{2,1,0:T(8,128)(2,1)} collective-permute-done((bf16[1,912,1024]{2,1,0:T(8,128)(2,1)}, bf16[1,912,1024]{2,1,0:T(8,128)(2,1)}, u32[]{:S(2)}, u32[]{:S(2)}) %collective-permute-start.24) | collective-permute-done | bytes 1867808 | tf_op jit(solution)/shard_map/ppermute | solution.py:626
  416.5 3.1 dynamic-slice_add_fusion.2
  423.9 25.8 %collective-permute-done.22 = f32[2,1024]{1,0:T(2,128)S(1)} collective-permute-done((f32[2,1024]{1,0:T(2,128)S(1)}, f32[2,1024]{1,0:T(2,128)S(1)}, u32[]{:S(2)}, u32[]{:S(2)}) %collective-permute-start.22) | collective-permute-done | bytes 8224 | tf_op jit(solution)/shard_map/ppermute | solution.py:626
  460.0 4.6 collective-permute-done.30
  466.0 21.6 %collective-permute-done.32 = bf16[1,912,256]{2,1,0:T(8,128)(2,1)S(1)} collective-permute-done((bf16[1,912,256]{2,1,0:T(8,128)(2,1)}, bf16[1,912,256]{2,1,0:T(8,128)(2,1)S(1)}, u32[]{:S(2)}, u32[]{:S(2)}) %collective-permute-start.32) | collective-permute-done | bytes 466976 | tf_op jit(solution)/shard_map/ppermute | solution.py:626
  495.6 26.4 %collective-permute-done.28 = f32[2,1024]{1,0:T(2,128)S(1)} collective-permute-done((f32[2,1024]{1,0:T(2,128)S(1)}, f32[2,1024]{1,0:T(2,128)S(1)}, u32[]{:S(2)}, u32[]{:S(2)}) %collective-permute-start.28) | collective-permute-done | bytes 8224 | tf_op jit(solution)/shard_map/ppermute | solution.py:626
  522.3 3.5 maximum_select_fusion.refs_1_
  525.8 3.2 collective-permute-start.39
  534.0 12.8 %collective-permute-done.31 = f32[2,1024]{1,0:T(2,128)} collective-permute-done((f32[2,1024]{1,0:T(2,128)S(1)}, f32[2,1024]{1,0:T(2,128)}, u32[]{:S(2)}, u32[]{:S(2)}) %collective-permute-start.31) | collective-permute-done | bytes 8224 | tf_op jit(solution)/shard_map/ppermute | solution.py:626
  547.5 7.9 %collective-permute-done.38 = bf16[3,256,256]{2,1,0:T(8,128)(2,1)} collective-permute-done((bf16[3,256,256]{2,1,0:T(8,128)(2,1)S(1)}, bf16[3,256,256]{2,1,0:T(8,128)(2,1)}, u32[]{:S(2)}, u32[]{:S(2)}) %collective-permute-start.38) | collective-permute-done | bytes 393248 | tf_op jit(solution)/shard_map/ppermute | solution.py:626
  560.3 3.5 collective-permute-start.35
  563.8 3.3 collective-permute-done.35
  567.1 7.1 %assemble.3 = f32[2,1312,1024]{2,1,0:T(8,128)} custom-call(s32[1]{0:T(128)} %bitcast.1.refs_0_, bf16[2,656,1024]{2,1,0:T(8,128)(2,1)} %copy-done.5, bf16[2,656,1024]{2,1,0:T(8,128)(2,1)} %collective-permute-done.39.refs_2_, bf16[1,912,512]{2,1,0:T(8,128)(2,1)} %maximum_select_fusion.4.refs_3_), custom_call_target="tpu_custom_call" | custom-call | tf_op jit(solution)/shard_map/assemble/pallas_call | solution.py:574
  575.2 2.8 maximum_select_fusion.1.refs_1_
  578.0 6.9 %collective-permute-start.45 = (bf16[1,912,1024]{2,1,0:T(8,128)(2,1)S(1)}, bf16[1,912,1024]{2,1,0:T(8,128)(2,1)S(1)}, u32[]{:S(2)}, u32[]{:S(2)}) collective-permute-start(bf16[1,912,1024]{2,1,0:T(8,128)(2,1)S(1)} %maximum_select_fusion.1.refs_1_), channel_id=1, source_target_pairs={{0,2},{1,3},{2,0},{3,1},{4,6},{5,7},{6,4},{7,5},{8,10},{9,11},{10,... | collective-permute-start | bytes 5603336 | tf_op jit(solution)/shard_map/ppermute | solution.py:626
  586.9 4.9 collective-permute-start.44
  593.6 5.3 assemble.4
  600.1 4.8 assemble.5
  (193 shorter events, 87.2 us)
Async XLA Ops:
  1.7 6.5 %collective-permute-start = (bf16[64,1024]{1,0:T(8,128)(2,1)S(1)}, bf16[64,1024]{1,0:T(8,128)(2,1)S(1)}, u32[]{:S(2)}, u32[]{:S(2)}) collective-permute-start(bf16[64,1024]{1,0:T(8,128)(2,1)S(1)} %constant_dynamic-slice_fusion.3), channel_id=1, source_target_pairs={{0,1},{1,0},{2,3},{3,2},{4,5},{5,4},{6,7},{7,6},{8,9},{9,8},{10,11... | collective-permute-start | bytes 393224 | tf_op jit(solution)/shard_map/ppermute | solution.py:626
  11.4 47.0 %collective-permute-start.1 = (bf16[4,1024,256]{2,1,0:T(8,128)(2,1)}, bf16[4,1024,256]{2,1,0:T(8,128)(2,1)S(1)}, u32[]{:S(2)}, u32[]{:S(2)}) collective-permute-start(bf16[4,1024,256]{2,1,0:T(8,128)(2,1)} %pad_maximum_fusion), channel_id=1, source_target_pairs={{0,1},{1,0},{2,3},{3,2},{4,5},{5,4},{6,7},{7,6},{8,9},{9,8},{10,11... | collective-permute-start | bytes 6291464 | tf_op jit(solution)/shard_map/ppermute | solution.py:626
  58.4 4.5 collective-permute-start.2
  61.4 31.2 %collective-permute-start.3 = (bf16[2,656,512]{2,1,0:T(8,128)(2,1)S(1)}, bf16[2,656,512]{2,1,0:T(8,128)(2,1)S(1)}, u32[]{:S(2)}, u32[]{:S(2)}) collective-permute-start(bf16[2,656,512]{2,1,0:T(8,128)(2,1)S(1)} %constant_dynamic-slice_fusion.1), channel_id=1, source_target_pairs={{0,1},{1,0},{2,3},{3,2},{4,5},{5,4},{6,7},{7,6},{8,9},{9,8},{10,11... | collective-permute-start | bytes 4030472 | tf_op jit(solution)/shard_map/ppermute | solution.py:626
  92.6 20.8 %collective-permute-start.5 = (bf16[2,656,512]{2,1,0:T(8,128)(2,1)S(1)}, bf16[2,656,512]{2,1,0:T(8,128)(2,1)S(1)}, u32[]{:S(2)}, u32[]{:S(2)}) collective-permute-start(bf16[2,656,512]{2,1,0:T(8,128)(2,1)S(1)} %collective-permute-done.3.refs_7_.refs_3_), channel_id=1, source_target_pairs={{0,2},{1,3},{2,0},{3,1},{4,6},{5,7},{6,4},{7,5},{8,10},{9,11},{10,... | collective-permute-start | bytes 4030472 | tf_op jit(solution)/shard_map/ppermute | solution.py:626
  92.6 60.9 %collective-permute-start.4 = (bf16[2,656,512]{2,1,0:T(8,128)(2,1)S(1)}, bf16[2,656,512]{2,1,0:T(8,128)(2,1)S(1)}, u32[]{:S(2)}, u32[]{:S(2)}) collective-permute-start(bf16[2,656,512]{2,1,0:T(8,128)(2,1)S(1)} %collective-permute-done.3.refs_7_.refs_3_), channel_id=1, source_target_pairs={{0,4},{1,5},{2,6},{3,7},{4,0},{5,1},{6,2},{7,3},{8,12},{9,13},{10,... | collective-permute-start | bytes 4030472 | tf_op jit(solution)/shard_map/ppermute | solution.py:626
  95.5 17.3 %collective-permute-start.7 = (bf16[1,656,512]{2,1,0:T(8,128)(2,1)S(1)}, bf16[1,656,512]{2,1,0:T(8,128)(2,1)S(1)}, u32[]{:S(2)}, u32[]{:S(2)}) collective-permute-start(bf16[1,656,512]{2,1,0:T(8,128)(2,1)S(1)} %dynamic-slice_bitcast_fusion), channel_id=1, source_target_pairs={{0,1},{1,0},{2,3},{3,2},{4,5},{5,4},{6,7},{7,6},{8,9},{9,8},{10,11... | collective-permute-start | bytes 2015240 | tf_op jit(solution)/shard_map/ppermute | solution.py:626
  112.8 40.9 %copy-start.24 = (bf16[1,656,512]{2,1,0:T(8,128)(2,1)}, bf16[1,656,512]{2,1,0:T(8,128)(2,1)S(1)}, u32[]{:S(2)}) copy-start(bf16[1,656,512]{2,1,0:T(8,128)(2,1)S(1)} %collective-permute-done.7.refs_7_) | copy-start | bytes 2015236
  112.8 41.4 %collective-permute-start.8 = (bf16[1,656,512]{2,1,0:T(8,128)(2,1)S(1)}, bf16[1,656,512]{2,1,0:T(8,128)(2,1)S(1)}, u32[]{:S(2)}, u32[]{:S(2)}) collective-permute-start(bf16[1,656,512]{2,1,0:T(8,128)(2,1)S(1)} %collective-permute-done.7.refs_7_), channel_id=1, source_target_pairs={{0,4},{1,5},{2,6},{3,7},{4,0},{5,1},{6,2},{7,3},{8,12},{9,13},{10,... | collective-permute-start | bytes 2015240 | tf_op jit(solution)/shard_map/ppermute | solution.py:626
  153.5 5.1 collective-permute-start.6
  153.6 4.0 collective-permute-start.9
  154.1 4.5 collective-permute-start.10
  218.3 9.2 %collective-permute-start.11 = (bf16[1,656,1024]{2,1,0:T(8,128)(2,1)}, bf16[1,656,1024]{2,1,0:T(8,128)(2,1)S(1)}, u32[]{:S(2)}, u32[]{:S(2)}) collective-permute-start(bf16[1,656,1024]{2,1,0:T(8,128)(2,1)} %get-tuple-element.128), channel_id=1, source_target_pairs={{0,2},{1,3},{2,0},{3,1},{4,6},{5,7},{6,4},{7,5},{8,10},{9,11},{10,... | collective-permute-start | bytes 4030472 | tf_op jit(solution)/shard_map/ppermute | solution.py:626
  244.0 35.5 %collective-permute-start.14 = (bf16[2,656,1024]{2,1,0:T(8,128)(2,1)}, bf16[2,656,1024]{2,1,0:T(8,128)(2,1)}, u32[]{:S(2)}, u32[]{:S(2)}) collective-permute-start(bf16[2,656,1024]{2,1,0:T(8,128)(2,1)} %get-tuple-element.135), channel_id=1, source_target_pairs={{0,2},{1,3},{2,0},{3,1},{4,6},{5,7},{6,4},{7,5},{8,10},{9,11},{10,... | collective-permute-start | bytes 8060936 | tf_op jit(solution)/shard_map/ppermute | solution.py:626
  244.4 6.9 %collective-permute-start.12 = (bf16[1,656,1024]{2,1,0:T(8,128)(2,1)}, bf16[1,656,1024]{2,1,0:T(8,128)(2,1)}, u32[]{:S(2)}, u32[]{:S(2)}) collective-permute-start(bf16[1,656,1024]{2,1,0:T(8,128)(2,1)} %get-tuple-element.132), channel_id=1, source_target_pairs={{0,2},{1,3},{2,0},{3,1},{4,6},{5,7},{6,4},{7,5},{8,10},{9,11},{10,... | collective-permute-start | bytes 4030472 | tf_op jit(solution)/shard_map/ppermute | solution.py:626
  244.5 35.0 %collective-permute-start.13 = (bf16[1,656,1024]{2,1,0:T(8,128)(2,1)S(1)}, bf16[1,656,1024]{2,1,0:T(8,128)(2,1)S(1)}, u32[]{:S(2)}, u32[]{:S(2)}) collective-permute-start(bf16[1,656,1024]{2,1,0:T(8,128)(2,1)S(1)} %copy-done.15), channel_id=1, source_target_pairs={{0,1},{1,0},{2,3},{3,2},{4,5},{5,4},{6,7},{7,6},{8,9},{9,8},{10,11... | collective-permute-start | bytes 4030472 | tf_op jit(solution)/shard_map/ppermute | solution.py:626
  253.6 69.8 %collective-permute-start.17 = (bf16[1,656,1024]{2,1,0:T(8,128)(2,1)S(1)}, bf16[1,656,1024]{2,1,0:T(8,128)(2,1)}, u32[]{:S(2)}, u32[]{:S(2)}) collective-permute-start(bf16[1,656,1024]{2,1,0:T(8,128)(2,1)S(1)} %add.232.refs_10_), channel_id=1, source_target_pairs={{0,1},{1,0},{2,3},{3,2},{4,5},{5,4},{6,7},{7,6},{8,9},{9,8},{10,11... | collective-permute-start | bytes 4030472 | tf_op jit(solution)/shard_map/ppermute | solution.py:626
  296.1 36.3 %collective-permute-start.16 = (bf16[1,912,1024]{2,1,0:T(8,128)(2,1)}, bf16[1,912,1024]{2,1,0:T(8,128)(2,1)S(1)}, u32[]{:S(2)}, u32[]{:S(2)}) collective-permute-start(bf16[1,912,1024]{2,1,0:T(8,128)(2,1)} %get-tuple-element.142), channel_id=1, source_target_pairs={{0,2},{1,3},{2,0},{3,1},{4,6},{5,7},{6,4},{7,5},{8,10},{9,11},{10,... | collective-permute-start | bytes 5603336 | tf_op jit(solution)/shard_map/ppermute | solution.py:626
  321.9 8.7 %collective-permute-start.15 = (bf16[2,64,1024]{2,1,0:T(8,128)(2,1)S(1)}, bf16[2,64,1024]{2,1,0:T(8,128)(2,1)S(1)}, u32[]{:S(2)}, u32[]{:S(2)}) collective-permute-start(bf16[2,64,1024]{2,1,0:T(8,128)(2,1)S(1)} %pad_maximum_fusion.1), channel_id=1, source_target_pairs={{0,1},{1,0},{2,3},{3,2},{4,5},{5,4},{6,7},{7,6},{8,9},{9,8},{10,11... | collective-permute-start | bytes 786440 | tf_op jit(solution)/shard_map/ppermute | solution.py:626
  347.3 11.6 %collective-permute-start.18 = (bf16[3,1024,256]{2,1,0:T(8,128)(2,1)}, bf16[3,1024,256]{2,1,0:T(8,128)(2,1)S(1)}, u32[]{:S(2)}, u32[]{:S(2)}) collective-permute-start(bf16[3,1024,256]{2,1,0:T(8,128)(2,1)} %get-tuple-element.147), channel_id=1, source_target_pairs={{0,2},{1,3},{2,0},{3,1},{4,6},{5,7},{6,4},{7,5},{8,10},{9,11},{10,... | collective-permute-start | bytes 4718600 | tf_op jit(solution)/shard_map/ppermute | solution.py:626
  347.3 32.2 %collective-permute-start.19 = (bf16[2,656,512]{2,1,0:T(8,128)(2,1)}, bf16[2,656,512]{2,1,0:T(8,128)(2,1)}, u32[]{:S(2)}, u32[]{:S(2)}) collective-permute-start(bf16[2,656,512]{2,1,0:T(8,128)(2,1)} %get-tuple-element.180), channel_id=1, source_target_pairs={{0,4},{1,5},{2,6},{3,7},{4,0},{5,1},{6,2},{7,3},{8,12},{9,13},{10,... | collective-permute-start | bytes 4030472 | tf_op jit(solution)/shard_map/ppermute | solution.py:626
  372.4 13.8 %collective-permute-start.21 = (bf16[1,912,1024]{2,1,0:T(8,128)(2,1)}, bf16[1,912,1024]{2,1,0:T(8,128)(2,1)}, u32[]{:S(2)}, u32[]{:S(2)}) collective-permute-start(bf16[1,912,1024]{2,1,0:T(8,128)(2,1)} %get-tuple-element.153), channel_id=1, source_target_pairs={{0,2},{1,3},{2,0},{3,1},{4,6},{5,7},{6,4},{7,5},{8,10},{9,11},{10,... | collective-permute-start | bytes 5603336 | tf_op jit(solution)/shard_map/ppermute | solution.py:626
  372.7 43.9 %collective-permute-start.24 = (bf16[1,912,1024]{2,1,0:T(8,128)(2,1)}, bf16[1,912,1024]{2,1,0:T(8,128)(2,1)}, u32[]{:S(2)}, u32[]{:S(2)}) collective-permute-start(bf16[1,912,1024]{2,1,0:T(8,128)(2,1)} %add.236), channel_id=1, source_target_pairs={{0,1},{1,0},{2,3},{3,2},{4,5},{5,4},{6,7},{7,6},{8,9},{9,8},{10,11... | collective-permute-start | bytes 5603336 | tf_op jit(solution)/shard_map/ppermute | solution.py:626
  373.6 10.2 %collective-permute-start.20 = (bf16[3,1024,256]{2,1,0:T(8,128)(2,1)}, bf16[3,1024,256]{2,1,0:T(8,128)(2,1)}, u32[]{:S(2)}, u32[]{:S(2)}) collective-permute-start(bf16[3,1024,256]{2,1,0:T(8,128)(2,1)} %get-tuple-element.151), channel_id=1, source_target_pairs={{0,2},{1,3},{2,0},{3,1},{4,6},{5,7},{6,4},{7,5},{8,10},{9,11},{10,... | collective-permute-start | bytes 4718600 | tf_op jit(solution)/shard_map/ppermute | solution.py:626
  373.6 76.1 %collective-permute-start.26 = (bf16[3,1024,256]{2,1,0:T(8,128)(2,1)S(1)}, bf16[3,1024,256]{2,1,0:T(8,128)(2,1)}, u32[]{:S(2)}, u32[]{:S(2)}) collective-permute-start(bf16[3,1024,256]{2,1,0:T(8,128)(2,1)S(1)} %copy-done.10), channel_id=1, source_target_pairs={{0,1},{1,0},{2,3},{3,2},{4,5},{5,4},{6,7},{7,6},{8,9},{9,8},{10,11... | collective-permute-start | bytes 4718600 | tf_op jit(solution)/shard_map/ppermute | solution.py:626
  382.3 26.3 %collective-permute-start.23 = (bf16[2,656,256]{2,1,0:T(8,128)(2,1)}, bf16[2,656,256]{2,1,0:T(8,128)(2,1)S(1)}, u32[]{:S(2)}, u32[]{:S(2)}) collective-permute-start(bf16[2,656,256]{2,1,0:T(8,128)(2,1)} %get-tuple-element.186), channel_id=1, source_target_pairs={{0,8},{1,9},{2,10},{3,11},{4,12},{5,13},{6,14},{7,15},{8,0},{9,1},... | collective-permute-start | bytes 2015240 | tf_op jit(solution)/shard_map/ppermute | solution.py:626
  419.7 33.2 %collective-permute-start.27 = (bf16[1,912,512]{2,1,0:T(8,128)(2,1)}, bf16[1,912,512]{2,1,0:T(8,128)(2,1)}, u32[]{:S(2)}, u32[]{:S(2)}) collective-permute-start(bf16[1,912,512]{2,1,0:T(8,128)(2,1)} %get-tuple-element.182), channel_id=1, source_target_pairs={{0,4},{1,5},{2,10},{3,11},{4,0},{5,1},{6,14},{7,15},{8,12},{9,13},... | collective-permute-start | bytes 2801672 | tf_op jit(solution)/shard_map/ppermute | solution.py:626
  420.2 34.8 %collective-permute-start.29 = (bf16[2,656,256]{2,1,0:T(8,128)(2,1)S(1)}, bf16[2,656,256]{2,1,0:T(8,128)(2,1)}, u32[]{:S(2)}, u32[]{:S(2)}) collective-permute-start(bf16[2,656,256]{2,1,0:T(8,128)(2,1)S(1)} %add.247), channel_id=1, source_target_pairs={{0,16},{1,17},{2,18},{3,19},{4,20},{5,21},{6,22},{7,23},{8,24},{9,... | collective-permute-start | bytes 2015240 | tf_op jit(solution)/shard_map/ppermute | solution.py:626
  422.9 26.8 %collective-permute-start.22 = (f32[2,1024]{1,0:T(2,128)S(1)}, f32[2,1024]{1,0:T(2,128)S(1)}, u32[]{:S(2)}, u32[]{:S(2)}) collective-permute-start(f32[2,1024]{1,0:T(2,128)S(1)} %pad_maximum_fusion.2), channel_id=1, source_target_pairs={{0,1},{1,0},{2,3},{3,2},{4,5},{5,4},{6,7},{7,6},{8,9},{9,8},{10,11... | collective-permute-start | bytes 24584 | tf_op jit(solution)/shard_map/ppermute | solution.py:626
  452.3 12.3 %collective-permute-start.30 = (bf16[3,512,256]{2,1,0:T(8,128)(2,1)}, bf16[3,512,256]{2,1,0:T(8,128)(2,1)}, u32[]{:S(2)}, u32[]{:S(2)}) collective-permute-start(bf16[3,512,256]{2,1,0:T(8,128)(2,1)} %get-tuple-element.184), channel_id=1, source_target_pairs={{0,4},{1,5},{2,10},{3,11},{4,0},{5,1},{6,14},{7,15},{8,12},{9,13},... | collective-permute-start | bytes 2359304 | tf_op jit(solution)/shard_map/ppermute | solution.py:626
  456.3 31.3 %collective-permute-start.33 = (bf16[2,656,256]{2,1,0:T(8,128)(2,1)S(1)}, bf16[2,656,256]{2,1,0:T(8,128)(2,1)}, u32[]{:S(2)}, u32[]{:S(2)}) collective-permute-start(bf16[2,656,256]{2,1,0:T(8,128)(2,1)S(1)} %add.257), channel_id=1, source_target_pairs={{0,8},{1,9},{2,10},{3,11},{4,12},{5,13},{6,14},{7,15},{8,0},{9,1},... | collective-permute-start | bytes 2015240 | tf_op jit(solution)/shard_map/ppermute | solution.py:626
  458.0 29.5 %collective-permute-start.32 = (bf16[1,912,256]{2,1,0:T(8,128)(2,1)}, bf16[1,912,256]{2,1,0:T(8,128)(2,1)S(1)}, u32[]{:S(2)}, u32[]{:S(2)}) collective-permute-start(bf16[1,912,256]{2,1,0:T(8,128)(2,1)} %get-tuple-element.188), channel_id=1, source_target_pairs={{0,8},{1,9},{2,18},{3,19},{4,12},{5,13},{6,22},{7,23},{8,0},{9,1},... | collective-permute-start | bytes 1400840 | tf_op jit(solution)/shard_map/ppermute | solution.py:626
  458.4 1.6 collective-permute-start.25
  489.3 33.0 %collective-permute-start.37 = (bf16[2,656,512]{2,1,0:T(8,128)(2,1)S(1)}, bf16[2,656,512]{2,1,0:T(8,128)(2,1)}, u32[]{:S(2)}, u32[]{:S(2)}) collective-permute-start(bf16[2,656,512]{2,1,0:T(8,128)(2,1)S(1)} %maximum_select_fusion.3), channel_id=1, source_target_pairs={{0,4},{1,5},{2,6},{3,7},{4,0},{5,1},{6,2},{7,3},{8,12},{9,13},{10,... | collective-permute-start | bytes 4030472 | tf_op jit(solution)/shard_map/ppermute | solution.py:626
  489.9 32.1 %collective-permute-start.36 = (bf16[1,912,256]{2,1,0:T(8,128)(2,1)S(1)}, bf16[1,912,256]{2,1,0:T(8,128)(2,1)S(1)}, u32[]{:S(2)}, u32[]{:S(2)}) collective-permute-start(bf16[1,912,256]{2,1,0:T(8,128)(2,1)S(1)} %add.263), channel_id=1, source_target_pairs={{0,16},{1,17},{2,6},{3,7},{4,20},{5,21},{6,2},{7,3},{8,24},{9,25},... | collective-permute-start | bytes 1400840 | tf_op jit(solution)/shard_map/ppermute | solution.py:626
  491.7 30.2 %collective-permute-start.34 = (bf16[3,256,256]{2,1,0:T(8,128)(2,1)S(1)}, bf16[3,256,256]{2,1,0:T(8,128)(2,1)S(1)}, u32[]{:S(2)}, u32[]{:S(2)}) collective-permute-start(bf16[3,256,256]{2,1,0:T(8,128)(2,1)S(1)} %get-tuple-element.190), channel_id=1, source_target_pairs={{0,8},{1,9},{2,18},{3,19},{4,12},{5,13},{6,22},{7,23},{8,0},{9,1},... | collective-permute-start | bytes 1179656 | tf_op jit(solution)/shard_map/ppermute | solution.py:626
  494.1 27.9 %collective-permute-start.28 = (f32[2,1024]{1,0:T(2,128)S(1)}, f32[2,1024]{1,0:T(2,128)S(1)}, u32[]{:S(2)}, u32[]{:S(2)}) collective-permute-start(f32[2,1024]{1,0:T(2,128)S(1)} %fusion.9), channel_id=1, source_target_pairs={{0,4},{1,5},{2,6},{3,7},{4,0},{5,1},{6,2},{7,3},{8,12},{9,13},{10,... | collective-permute-start | bytes 24584 | tf_op jit(solution)/shard_map/ppermute | solution.py:626
  525.8 41.3 %copy-start.5 = (bf16[2,656,1024]{2,1,0:T(8,128)(2,1)}, bf16[2,656,1024]{2,1,0:T(8,128)(2,1)S(1)}, u32[]{:S(2)}) copy-start(bf16[2,656,1024]{2,1,0:T(8,128)(2,1)S(1)} %maximum_select_fusion.refs_1_) | copy-start | bytes 8060932
  525.8 41.3 %collective-permute-start.39 = (bf16[2,656,1024]{2,1,0:T(8,128)(2,1)S(1)}, bf16[2,656,1024]{2,1,0:T(8,128)(2,1)}, u32[]{:S(2)}, u32[]{:S(2)}) collective-permute-start(bf16[2,656,1024]{2,1,0:T(8,128)(2,1)S(1)} %maximum_select_fusion.refs_1_), channel_id=1, source_target_pairs={{0,2},{1,3},{2,0},{3,1},{4,6},{5,7},{6,4},{7,5},{8,10},{9,11},{10,... | collective-permute-start | bytes 8060936 | tf_op jit(solution)/shard_map/ppermute | solution.py:626
  529.0 28.4 %collective-permute-start.40 = (bf16[1,912,256]{2,1,0:T(8,128)(2,1)S(1)}, bf16[1,912,256]{2,1,0:T(8,128)(2,1)}, u32[]{:S(2)}, u32[]{:S(2)}) collective-permute-start(bf16[1,912,256]{2,1,0:T(8,128)(2,1)S(1)} %add.267), channel_id=1, source_target_pairs={{0,8},{1,9},{2,18},{3,19},{4,12},{5,13},{6,22},{7,23},{8,0},{9,1},... | collective-permute-start | bytes 1400840 | tf_op jit(solution)/shard_map/ppermute | solution.py:626
  530.3 25.1 %collective-permute-start.38 = (bf16[3,256,256]{2,1,0:T(8,128)(2,1)S(1)}, bf16[3,256,256]{2,1,0:T(8,128)(2,1)}, u32[]{:S(2)}, u32[]{:S(2)}) collective-permute-start(bf16[3,256,256]{2,1,0:T(8,128)(2,1)S(1)} %add.265), channel_id=1, source_target_pairs={{0,16},{1,17},{2,6},{3,7},{4,20},{5,21},{6,2},{7,3},{8,24},{9,25},... | collective-permute-start | bytes 1179656 | tf_op jit(solution)/shard_map/ppermute | solution.py:626
  532.0 14.8 %collective-permute-start.31 = (f32[2,1024]{1,0:T(2,128)S(1)}, f32[2,1024]{1,0:T(2,128)}, u32[]{:S(2)}, u32[]{:S(2)}) collective-permute-start(f32[2,1024]{1,0:T(2,128)S(1)} %add.260), channel_id=1, source_target_pairs={{0,8},{1,9},{2,10},{3,11},{4,12},{5,13},{6,14},{7,15},{8,0},{9,1},... | collective-permute-start | bytes 24584 | tf_op jit(solution)/shard_map/ppermute | solution.py:626
  556.5 17.7 %collective-permute-start.41 = (bf16[3,256,256]{2,1,0:T(8,128)(2,1)S(1)}, bf16[3,256,256]{2,1,0:T(8,128)(2,1)S(1)}, u32[]{:S(2)}, u32[]{:S(2)}) collective-permute-start(bf16[3,256,256]{2,1,0:T(8,128)(2,1)S(1)} %add.268), channel_id=1, source_target_pairs={{0,8},{1,9},{2,18},{3,19},{4,12},{5,13},{6,22},{7,23},{8,0},{9,1},... | collective-permute-start | bytes 1179656 | tf_op jit(solution)/shard_map/ppermute | solution.py:626
  559.7 15.5 %collective-permute-start.42 = (bf16[1,912,512]{2,1,0:T(8,128)(2,1)}, bf16[1,912,512]{2,1,0:T(8,128)(2,1)}, u32[]{:S(2)}, u32[]{:S(2)}) collective-permute-start(bf16[1,912,512]{2,1,0:T(8,128)(2,1)} %maximum_select_fusion.4.refs_3_), channel_id=1, source_target_pairs={{0,4},{1,5},{2,10},{3,11},{4,0},{5,1},{6,14},{7,15},{8,12},{9,13},... | collective-permute-start | bytes 2801672 | tf_op jit(solution)/shard_map/ppermute | solution.py:626
  560.3 6.8 %collective-permute-start.35 = (f32[2,1024]{1,0:T(2,128)S(1)}, f32[2,1024]{1,0:T(2,128)S(1)}, u32[]{:S(2)}, u32[]{:S(2)}) collective-permute-start(f32[2,1024]{1,0:T(2,128)S(1)} %add.266), channel_id=1, source_target_pairs={{0,16},{1,17},{2,18},{3,19},{4,20},{5,21},{6,22},{7,23},{8,24},{9,... | collective-permute-start | bytes 24584 | tf_op jit(solution)/shard_map/ppermute | solution.py:626
  574.5 12.1 %collective-permute-start.43 = (bf16[3,512,256]{2,1,0:T(8,128)(2,1)S(1)}, bf16[3,512,256]{2,1,0:T(8,128)(2,1)S(1)}, u32[]{:S(2)}, u32[]{:S(2)}) collective-permute-start(bf16[3,512,256]{2,1,0:T(8,128)(2,1)S(1)} %maximum_select_fusion.5), channel_id=1, source_target_pairs={{0,4},{1,5},{2,10},{3,11},{4,0},{5,1},{6,14},{7,15},{8,12},{9,13},... | collective-permute-start | bytes 2359304 | tf_op jit(solution)/shard_map/ppermute | solution.py:626
  578.0 14.4 %collective-permute-start.45 = (bf16[1,912,1024]{2,1,0:T(8,128)(2,1)S(1)}, bf16[1,912,1024]{2,1,0:T(8,128)(2,1)S(1)}, u32[]{:S(2)}, u32[]{:S(2)}) collective-permute-start(bf16[1,912,1024]{2,1,0:T(8,128)(2,1)S(1)} %maximum_select_fusion.1.refs_1_), channel_id=1, source_target_pairs={{0,2},{1,3},{2,0},{3,1},{4,6},{5,7},{6,4},{7,5},{8,10},{9,11},{10,... | collective-permute-start | bytes 5603336 | tf_op jit(solution)/shard_map/ppermute | solution.py:626
  586.9 12.0 %collective-permute-start.44 = (bf16[3,1024,256]{2,1,0:T(8,128)(2,1)S(1)}, bf16[3,1024,256]{2,1,0:T(8,128)(2,1)S(1)}, u32[]{:S(2)}, u32[]{:S(2)}) collective-permute-start(bf16[3,1024,256]{2,1,0:T(8,128)(2,1)S(1)} %maximum_select_fusion.2.refs_3_.refs_1_), channel_id=1, source_target_pairs={{0,2},{1,3},{2,0},{3,1},{4,6},{5,7},{6,4},{7,5},{8,10},{9,11},{10,... | collective-permute-start | bytes 4718600 | tf_op jit(solution)/shard_map/ppermute | solution.py:626
  (33 other events, 276.0 us)

commit v3 on v2

--- a/solution.py
+++ b/solution.py
@@ -36,11 +36,18 @@
     return center * rate, rate
 
 
+COST = {
+    "norm_rows": 6, "project": 9, "project_parts": 9, "attend": 20, "mix": 11, "mlp_first": 39, "mlp_last": 49, "outer": 9,
+    "attend_back": 25, "trade_outer": 9, "trade_down": 12, "trade_attn": 10, "outer_down": 12, "outer_attn": 10, "pull": 18,
+}
+SCALE = 100
+
+
 def shaped(shape, dtype=LOW):
     return jax.ShapeDtypeStruct(shape, dtype)
 
 
-def run(body, name, grid, ins, outs, after=(), place=None, scratch=(), flops=0, vmem=56, seen=False):
+def run(body, name, grid, ins, outs, after=(), place=None, scratch=(), flops=0, vmem=56, seen=False, collective=None):
     extra = [a for a in after if a is not None]
     count = len(ins)
 
@@ -64,8 +71,10 @@
             scratch_shapes=list(scratch),
         ),
         out_shape=[s for s, _, _ in outs],
-        compiler_params=pltpu.CompilerParams(vmem_limit_bytes=vmem << 20),
-        cost_estimate=pl.CostEstimate(flops=1000, bytes_accessed=1000, transcendentals=0),
+        compiler_params=pltpu.CompilerParams(
+            vmem_limit_bytes=vmem << 20, collective_id=collective, has_side_effects=collective is not None
+        ),
+        cost_estimate=pl.CostEstimate(flops=int(COST[name] * SCALE), bytes_accessed=1000, transcendentals=0),
         name=name,
     )
     lead = () if place is None else (place,)
@@ -537,6 +546,116 @@
     )
 
 
+def trade_kernel(tiles, compute, store, *refs):
+    ins, out = refs[:-6], refs[-6]
+    keep, send, got, send_sems, got_sems = refs[-5:]
+    step = pl.program_id(0)
+    me = lax.axis_index("dp")
+    other = {"dp": me + 1 - 2 * (me % 2)}
+
+    @pl.when(step == 0)
+    def _():
+        barrier = pltpu.get_barrier_semaphore()
+        pl.semaphore_signal(barrier, inc=1, device_id=other, device_id_type=pl.DeviceIdType.MESH)
+        pl.semaphore_wait(barrier, 1)
+
+    def move(tile):
+        return pltpu.make_async_remote_copy(
+            src_ref=send.at[tile], dst_ref=got.at[tile], send_sem=send_sems.at[tile], recv_sem=got_sems.at[tile],
+            device_id=other, device_id_type=pl.DeviceIdType.MESH,
+        )
+
+    compute(me % 2, ins, keep.at[step], send.at[step])
+    move(step).start()
+
+    @pl.when(step == tiles - 1)
+    def _():
+        for tile in range(tiles):
+            move(tile).wait()
+            store(out, tile, keep[tile] + got[tile])
+
+
+def trade(name, collective, tiles, tile_shape, compute, store, ins, shape, after=()):
+    buffer = pltpu.VMEM((tiles,) + tile_shape, LOW)
+    return run(
+        functools.partial(trade_kernel, tiles, compute, store), name, (tiles,), ins,
+        [(shaped(shape), shape, lambda t: (0,) * len(shape))], after,
+        scratch=[buffer, buffer, buffer, pltpu.SemaphoreType.DMA((tiles,)), pltpu.SemaphoreType.DMA((tiles,))],
+        collective=collective,
+    )[0]
+
+
+def keep_and_send(own, core, value, axis, keep, send, index):
+    size = value.shape[axis] // 2
+    low = lax.slice_in_dim(value, 0, size, axis=axis).astype(LOW)
+    high = lax.slice_in_dim(value, size, 2 * size, axis=axis).astype(LOW)
+    if own:
+        low, high = jnp.where(core == 0, low, high), jnp.where(core == 0, high, low)
+    keep[index] = low
+    send[index] = high
+
+
+def store_columns(count, out, tile, value):
+    size = value.shape[-1]
+    out[tile // count, :, tile % count * size:(tile % count + 1) * size] = value
+
+
+def trade_outer(collective, own, left, right, sides, after=()):
+    _, rows, units = left.shape
+    model = right.shape[1]
+    tile, count = min(512, model), model // min(512, model)
+    first = sides[0]
+
+    def compute(core, ins, keep, send):
+        keep_and_send(own, core, rows_dot(ins[0][0], ins[1][...]), 0, keep, send, slice(None))
+
+    return trade(
+        "trade_outer", collective, len(sides) * count, (units // 2, tile), compute, functools.partial(store_columns, count),
+        [(left, (1, rows, units), lambda t: (first + t // count, 0, 0)), (right, (rows, tile), lambda t: (0, t % count))],
+        (len(sides), units // 2, model), after,
+    )
+
+
+def trade_down(collective, own, gate, attended, low, hidden, after=()):
+    _, rows, units = gate.shape
+    width, model = attended.shape[1], low.shape[1]
+    tile, count = min(512, model), model // min(512, model)
+    part = lambda t: (0, t)
+    size = units // 2
+
+    def compute(core, ins, keep, send):
+        gate, attended, low, hidden = ins
+        keep_and_send(own, core, rows_dot(gate[0], low[...]), 0, keep, send, slice(0, size))
+        keep_and_send(own, core, rows_dot(attended[...], hidden[...]), 0, keep, send, slice(size, size + width // 2))
+
+    return trade(
+        "trade_down", collective, count, (size + width // 2, tile), compute, functools.partial(store_columns, count),
+        [(gate, (1, rows, units), lambda t: (0, 0, 0)), (attended, (rows, width), lambda t: (0, 0)),
+         (low, (rows, tile), part), (hidden, (rows, tile), part)],
+        (1, size + width // 2, model), after,
+    )
+
+
+def trade_attn(collective, own, normed, grads, after=()):
+    rows, width = grads.shape[0], grads.shape[1] // 3
+    model = normed.shape[1]
+    tile, count = min(512, model), model // min(512, model)
+
+    def compute(core, ins, keep, send):
+        for i in range(3):
+            value = rows_dot(ins[0][...], ins[1][:, i * width:(i + 1) * width])
+            keep_and_send(own, core, value, 1, keep, send, i)
+
+    def store(out, t, value):
+        out[:, t * tile:(t + 1) * tile] = value
+
+    return trade(
+        "trade_attn", collective, count, (3, tile, width // 2), compute, store,
+        [(normed, (rows, tile), lambda t: (0, t)), (grads, (rows, 3 * width), lambda t: (0, 0))],
+        (3, model, width // 2), after,
+    )
+
+
 def pull_kernel(tokens, hidden_grad, gain, grads, weights, *refs):
     more, parts, (out, gain_ref) = refs[:1], refs[1:-2], refs[-2:]
     width = weights.shape[2]
@@ -661,18 +780,8 @@
     def __init__(self, links, flags, axis, steps):
         self.links, self.flags, self.axis, self.steps = links, flags, axis, steps
 
-    def cores_other(self, keep, send):
-        self.keep_other, self.got_other = keep, self.links.flip(send, 1)
-
-    def cores_own(self, keep, send):
-        self.keep_own, self.got_own = keep, self.links.flip(send, 1)
-
-    def add_other(self, *after):
-        self.far = tie(self.keep_other, *after) + self.got_other
-        self.crossed = self.links.cross(self.far)
-
-    def add_own(self, *after):
-        self.near = tie(self.keep_own, *after) + self.got_own
+    def send_far(self, far):
+        self.far, self.crossed = far, self.links.cross(far)
 
     def across(self, *after, parts=None):
         self.split(0, self.near, self.crossed if parts is None else jnp.concatenate(parts, 0), after)
@@ -774,62 +883,54 @@
     down = Summing(links, flags, 2, Summing.SPLIT)
     attn = Summing(links, flags, 1, Summing.SPLIT)
 
-    inner_a.cores_other(*outer(flags, False, lift1, normed_mlp, after=[back1], side=0))
-    inner_b.cores_other(*outer(flags, False, lift1, normed_mlp, after=[inner_a.keep_other], side=1))
-    inner_a.add_other(inner_b.keep_other)
-    inner.cores_own(*outer(flags, True, lift0, normed_mlp, after=[inner_a.far]))
-    inner_b.add_other(inner.keep_own)
-    d1, edge1 = attend_back(place, q1, k1, v1, back1, logs1, after=[inner_b.far])
-    inner.add_own(d1, inner_a.crossed)
-    down.cores_other(*outer_down(flags, False, gate1, attended1, out_low, hidden_low, after=[inner.near]))
-    d0, edge0 = attend_back(place, q0, k0, v0, back0, logs0, after=[down.keep_other])
-    down.add_other(d0)
-    inner.across(down.far, parts=[inner_a.crossed, inner_b.crossed])
+    inner_a.send_far(trade_outer(0, False, lift1, normed_mlp, [0], after=[back1]))
+    inner_b.send_far(trade_outer(1, False, lift1, normed_mlp, [1], after=[inner_a.far]))
+    inner.near = trade_outer(2, True, lift0, normed_mlp, [0, 1], after=[inner_b.far])
+    d1, edge1 = attend_back(place, q1, k1, v1, back1, logs1, after=[inner.near])
+    down.send_far(trade_down(3, False, gate1, attended1, out_low, hidden_low, after=[d1, inner_a.crossed]))
+    d0, edge0 = attend_back(place, q0, k0, v0, back0, logs0, after=[down.far])
+    inner.across(d0, parts=[inner_a.crossed, inner_b.crossed])
 
     swap = lambda e: jnp.where(core == 0, e, jnp.concatenate([e[:, size:], e[:, :size]], 1))
     edge_out = lambda e: jnp.concatenate([swap(e[:, :width]), swap(e[:, width:])], 1)
     edges = jnp.stack([edge_out(jnp.where(tensor_id == 0, e[1], e[0])) for e in (edge1, edge0)])
     edges = links.cross(edges)
+    down.near = trade_down(4, True, gate0, attended0, out_low, hidden_low, after=[inner.held])
+    edges = tie(edges, down.near)
 
     def add_edge(d, edge):
         held = lax.dynamic_slice(d, (start, width), (HALF, 2 * width))
         return lax.dynamic_update_slice(d, held + edge, (start, width))
 
     d1, d0 = add_edge(d1, edges[1]), add_edge(d0, edges[0])
-    attn.cores_other(*outer_attn(flags, False, normed, d1, after=[inner.held]))
-    attn.cores_own(*outer_attn(flags, True, normed, d0, after=[attn.keep_other]))
-    attn.add_other(attn.keep_own)
-    down.cores_own(*outer_down(flags, True, gate0, attended0, out_low, hidden_low, after=[attn.far]))
-    inner.scatter(down.keep_own)
-    attn.add_own(inner.held)
-    down.add_own(attn.near)
-    input_grad, gain_attn_grad = pull(
-        tokens, hidden_grad, gain_attn, d0, w_qkv, d1, attn_parts, after=[down.near, inner.held]
-    )
+    attn.send_far(trade_attn(5, False, normed, d1))
+    attn.near = trade_attn(6, True, normed, d0, after=[attn.far])
+    inner.scatter(attn.near)
+    down.across(inner.held)
+    input_grad, gain_attn_grad = pull(tokens, hidden_grad, gain_attn, d0, w_qkv, d1, attn_parts, after=[down.held])
     inner.both(input_grad)
-    down.across(inner.held)
     gain_total = jnp.concatenate((gain_attn_grad, gain_mlp_grad))
-    gain_total = gain_total + tie(links.cross(gain_total), down.held)
-    attn.across(down.held, gain_total)
+    attn.across(inner.held)
     down.scatter(attn.held)
-    gain_total = gain_total + tie(links.flip(gain_total, 1), down.held)
     inner.both_add(down.held)
-    attn.scatter(inner.held, gain_total)
+    gain_total = gain_total + tie(links.cross(gain_total), attn.held)
+    attn.scatter(inner.held)
+    gain_total = gain_total + tie(links.flip(gain_total, 1), attn.held)
+    down.both(attn.held, gain_total)
+    inner.gather(down.held)
+    attn.both(inner.held)
+    down.both_add(attn.held)
+    attn.both_add(down.held)
     gain_total = gain_total + tie(links.flip(gain_total, 2), attn.held)
-    down.both(attn.held)
-    inner.gather(down.held)
-    attn.both(inner.held, gain_total)
-    gain_total = gain_total + tie(links.flip(gain_total, 4), attn.held)
-    down.both_add(attn.held)
-    grads_in = inner.last(down.held)
-    attn.both_add(grads_in[0], gain_total)
-    gain_total = gain_total + tie(links.flip(gain_total, 8), attn.held)
-    down.gather(attn.held)
-    grad_w_in = assemble(*grads_in, 1, after=[down.held])
-    attn.gather(grad_w_in, gain_total)
-    grads_down = down.last(attn.held)
-    grads_attn = attn.last(grads_down[0])
+    grads_in = inner.last(attn.held)
+    down.gather(grads_in[0])
+    attn.gather(down.held, gain_total)
+    grad_w_in = assemble(*grads_in, 1, after=[attn.held])
+    gain_total = gain_total + tie(links.flip(gain_total, 4), grad_w_in)
+    grads_down = down.last(grad_w_in)
+    grads_attn = attn.last(grads_down[0], gain_total)
     grad_w_down, grad_w_out = assemble_down(*grads_down, units, after=[grads_attn[0]])
+    gain_total = gain_total + tie(links.flip(gain_total, 8), grad_w_down)
     grad_w_qkv = assemble(*grads_attn, 2, after=[grad_w_down])
     return (
         output,

time: 615 us -> 578 us (0.940)
  waiting for transfers between devices: 151 us -> 117 us
  other arithmetic: 52.8 us -> 36.4 us
  Pallas kernels: 324 us -> 336 us
    ppermute x46 -> x39, waiting for transfers between devices: 151 us -> 117 us  [send(): return lax.ppermute(value, AXES, pairs)]
    add x11 -> x4, other arithmetic: 18.8 us -> 0.04 us  [the longest x1 0.02 us: on_device(): gain_total = gain_total + tie(links.flip(gain_total, 1), attn.held)]
    pallas_call x18, Pallas kernels: 307 us -> 319 us  [run(): return call(*lead, *[a for a, _, _ in ins], *extra)]
    ppermute x46 -> x39, starting transfers between devices: 60.1 us -> 60.1 us  [send(): return lax.ppermute(value, AXES, pairs)]
  transfers between devices with their start and end apart: 46 -> 39, of which waited for: 19 -> 18; matrix products, arithmetic and copies ran while one was open for 8% -> 6% of each run, Pallas kernels for 39% -> 48%
where the time goes in v3:
time: 578 us; the launch traced here: 569 us
  Pallas kernels  336 us (58%)
  waiting for transfers between devices  117 us (20%)
  starting transfers between devices  60.1 us (10%)
  other arithmetic  36.4 us (6%)
  local copies, waits for them, and re-layouts  16.8 us (3%)
    pallas_call x18, Pallas kernels, run(): return call(*lead, *[a for a, _, _ in ins], *extra)  319 us
    ppermute x39, waiting for transfers between devices, send(): return lax.ppermute(value, AXES, pairs)  117 us
    ppermute x39, starting transfers between devices, send(): return lax.ppermute(value, AXES, pairs)  60.1 us
    pallas_call x3, Pallas kernels, assemble_call(): pl.pallas_call(lambda *refs: body(*refs[:3], *refs[3 + len(after):]), gri...  17.2 us
    add x6, other arithmetic, split(): part = lambda k: half(a, k, self.axis) + half(b, k, self.axis)  14.1 us
    select_n x6, other arithmetic, order(): jnp.where(bit == 0, jnp.concatenate([first, second], axis), jnp.concatena...  12.1 us
  transfers between devices with their start and end apart: 39, of which 18 were waited for; matrix products, arithmetic and copies ran while one was open for 6% of the time, Pallas kernels for 48%

profile of v3, /device:TPU:0, one launch (start us, length us, event | category | flops | bytes accessed | tf_op | source)
XLA Modules:
  0.0 568.7 jit_solution(12013020558528956569)
XLA Ops:
  1.7 3.0 collective-permute-start
  4.7 3.5 collective-permute-done.refs_1_.refs_2_
  13.6 5.6 norm_rows.1.refs_0_
  19.8 8.9 %project.1 = (bf16[1664,512]{1,0:T(8,128)(2,1)}, bf16[1664,512]{1,0:T(8,128)(2,1)}, bf16[1664,512]{1,0:T(8,128)(2,1)}) custom-call(bf16[1664,1024]{1,0:T(8,128)(2,1)} %norm_rows.1.refs_0_, bf16[3,1024,512]{2,1,0:T(8,128)(2,1)} %bitcast.39), custom_call_target="tpu_custom_call" | custom-call | flops 900 | bytes 1000 | tf_op jit(solution)/shard_map/project/pallas_call | solution.py:81
  28.8 20.2 %attend.2 = (bf16[1536,512]{1,0:T(8,128)(2,1)}, f32[12,4,256]{2,1,0:T(4,128)}) custom-call(s32[3,12]{1,0:T(4,128)} %pad_add_fusion.refs_0_, bf16[1664,512]{1,0:T(8,128)(2,1)} %get-tuple-element.74.refs_1_, bf16[1664,512]{1,0:T(8,128)(2,1)} %get-tuple-element.75.refs_2_.refs_3_.refs_4_, bf16[1664,512]{1,0:T(8,128)(2,1)} %get-tuple-element.75.refs_2_.refs_3_.refs_4_, ...), custom_call_target="tpu_custom_call" | custom-call | flops 2000 | bytes 1000 | tf_op jit(solution)/shard_map/attend/pallas_call | solution.py:81
  48.9 9.5 %collective-permute-done.1.refs_1_.refs_5_.refs_16_.refs_6_ = bf16[4,1024,256]{2,1,0:T(8,128)(2,1)S(1)} collective-permute-done((bf16[4,1024,256]{2,1,0:T(8,128)(2,1)}, bf16[4,1024,256]{2,1,0:T(8,128)(2,1)S(1)}, u32[]{:S(2)}, u32[]{:S(2)}) %collective-permute-start.1) | collective-permute-done | bytes 2097184 | tf_op jit(solution)/shard_map/ppermute | solution.py:745
  58.4 3.0 constant_dynamic-slice_fusion.1
  62.9 9.0 %project_parts.1 = (bf16[1664,512]{1,0:T(8,128)(2,1)}, bf16[1664,512]{1,0:T(8,128)(2,1)}, bf16[1664,512]{1,0:T(8,128)(2,1)}) custom-call(bf16[1664,1024]{1,0:T(8,128)(2,1)} %norm_rows.1.refs_0_, bf16[4,1024,256]{2,1,0:T(8,128)(2,1)} %copy-done, bf16[4,1024,256]{2,1,0:T(8,128)(2,1)} %collective-permute-done.2.refs_2_.refs_6_.refs_17_.refs_7_, ...), custom_call_target="tpu_custom_call" | custom-call | flops 900 | bytes 1000 | tf_op jit(solution)/shard_map/project_parts/pallas_call | solution.py:81
  71.9 20.2 %attend.3 = (bf16[1536,512]{1,0:T(8,128)(2,1)}, f32[12,4,256]{2,1,0:T(4,128)}) custom-call(s32[3,12]{1,0:T(4,128)} %pad_add_fusion.refs_0_, bf16[1664,512]{1,0:T(8,128)(2,1)} %get-tuple-element.81.refs_1_, bf16[1664,512]{1,0:T(8,128)(2,1)} %get-tuple-element.82.refs_2_.refs_3_.refs_4_, bf16[1664,512]{1,0:T(8,128)(2,1)} %get-tuple-element.82.refs_2_.refs_3_.refs_4_, ...), custom_call_target="tpu_custom_call" | custom-call | flops 2000 | bytes 1000 | tf_op jit(solution)/shard_map/attend/pallas_call | solution.py:81
  97.0 10.9 %mix.1 = (f32[1536,1024]{1,0:T(8,128)}, bf16[1536,1024]{1,0:T(8,128)(2,1)}) custom-call(bf16[1536,1024]{1,0:T(8,128)(2,1)} %refs_0_.5, f32[1,1024]{1,0:T(1,128)} %bitcast.45, bf16[1536,512]{1,0:T(8,128)(2,1)} %get-tuple-element.77.refs_3_.refs_2_.refs_1_, bf16[512,1024]{1,0:T(8,128)(2,1)} %refs_15_.1, bf16[1536,512]{1,0:T(8,128)(2,1)} %get-tuple-element.84.refs_4_.refs_1_, ...), custom_call_target="tpu_custom_call" | custom-call | flops 1100 | bytes 1000 | tf_op jit(solution)/shard_map/mix/pallas_call | solution.py:81
  108.0 4.8 collective-permute-done.7.refs_7_
  114.5 39.1 %mlp_first.1 = (bf16[1,1536,1312]{2,1,0:T(8,128)(2,1)}, bf16[2,1536,1312]{2,1,0:T(8,128)(2,1)}, bf16[1536,1024]{1,0:T(8,128)(2,1)}, f32[1536,1024]{1,0:T(8,128)}, f32[1536,1024]{1,0:T(8,128)}) custom-call(s32[3,12]{1,0:T(4,128)} %pad_add_fusion.refs_0_, bf16[1536,1024]{1,0:T(8,128)(2,1)} %get-tuple-element.87.refs_1_, bf16[1536,1024]{1,0:T(8,128)(2,1)} %refs_2_.3, ...), custom_call_target="tpu_custom_call" | custom-call | flops 3900 | bytes 1000 | tf_op jit(solution)/shard_map/mlp_first/pallas_call | solution.py:81
  154.2 3.4 collective-permute-done.9.refs_9_
  160.6 48.9 %mlp_last.1 = (bf16[1,1536,1312]{2,1,0:T(8,128)(2,1)}, bf16[2,1536,1312]{2,1,0:T(8,128)(2,1)}, bf16[1536,1024]{1,0:T(8,128)(2,1)}, f32[1536,1024]{1,0:T(8,128)},...) custom-call(s32[3,12]{1,0:T(4,128)} %pad_add_fusion.refs_0_, ...), custom_call_target="tpu_custom_call" | custom-call | flops 4900 | bytes 1000 | tf_op jit(solution)/shard_map/mlp_last/pallas_call | solution.py:81
  209.5 10.7 %trade_outer.3.refs_2_ = bf16[1,656,1024]{2,1,0:T(8,128)(2,1)} custom-call(bf16[2,1536,1312]{2,1,0:T(8,128)(2,1)} %get-tuple-element.105.refs_0_, bf16[1536,1024]{1,0:T(8,128)(2,1)} %get-tuple-element.87.refs_1_, bf16[1536,512]{1,0:T(8,128)(2,1)} %get-tuple-element.102.refs_2_.refs_8_), custom_call_target="tpu_custom_call" | custom-call | flops 900 | bytes 1000 | tf_op jit(solution)/shard_map/trade_outer/pallas_call | solution.py:81
  221.7 10.6 %trade_outer.4.refs_2_ = bf16[1,656,1024]{2,1,0:T(8,128)(2,1)} custom-call(bf16[2,1536,1312]{2,1,0:T(8,128)(2,1)} %get-tuple-element.105.refs_0_, bf16[1536,1024]{1,0:T(8,128)(2,1)} %get-tuple-element.87.refs_1_, bf16[1,656,1024]{2,1,0:T(8,128)(2,1)} %trade_outer.3.refs_2_), custom_call_target="tpu_custom_call" | custom-call | flops 900 | bytes 1000 | tf_op jit(solution)/shard_map/trade_outer/pallas_call | solution.py:81
  233.0 16.3 %trade_outer.5.refs_10_ = bf16[2,656,1024]{2,1,0:T(8,128)(2,1)} custom-call(bf16[2,1536,1312]{2,1,0:T(8,128)(2,1)} %get-tuple-element.104.refs_0_, bf16[1536,1024]{1,0:T(8,128)(2,1)} %get-tuple-element.87.refs_1_, bf16[1,656,1024]{2,1,0:T(8,128)(2,1)} %trade_outer.4.refs_2_), custom_call_target="tpu_custom_call" | custom-call | flops 900 | bytes 1000 | tf_op jit(solution)/shard_map/trade_outer/pallas_call | solution.py:81
  249.3 24.3 %attend_back.2 = (bf16[1536,1536]{1,0:T(8,128)(2,1)}, bf16[2,64,1024]{2,1,0:T(8,128)(2,1)}) custom-call(s32[3,12]{1,0:T(4,128)} %pad_add_fusion.refs_0_, bf16[1664,512]{1,0:T(8,128)(2,1)} %get-tuple-element.81.refs_1_, bf16[1664,512]{1,0:T(8,128)(2,1)} %get-tuple-element.82.refs_2_.refs_3_.refs_4_, ...), custom_call_target="tpu_custom_call" | custom-call | flops 2500 | bytes 1000 | tf_op jit(solution)/shard_map/attend_back/pallas_call | solution.py:81
  275.7 13.7 %trade_down.2.refs_10_ = bf16[1,912,1024]{2,1,0:T(8,128)(2,1)} custom-call(bf16[1,1536,1312]{2,1,0:T(8,128)(2,1)} %get-tuple-element.99.refs_0_, bf16[1536,512]{1,0:T(8,128)(2,1)} %get-tuple-element.84.refs_4_.refs_1_, bf16[1536,1024]{1,0:T(8,128)(2,1)} %get-tuple-element.100.refs_2_, bf16[1536,1024]{1,0:T(8,128)(2,1)} %get-tuple-element.101.refs_3_, ...), custom_call_target="tpu_custom_call" | custom-call | flops 1200 | bytes 1000 | tf_op jit(solution)/shard_map/trade_down/pallas_call | solution.py:81
  290.9 24.4 %attend_back.3 = (bf16[1536,1536]{1,0:T(8,128)(2,1)}, bf16[2,64,1024]{2,1,0:T(8,128)(2,1)}) custom-call(s32[3,12]{1,0:T(4,128)} %pad_add_fusion.refs_0_, bf16[1664,512]{1,0:T(8,128)(2,1)} %get-tuple-element.74.refs_1_, bf16[1664,512]{1,0:T(8,128)(2,1)} %get-tuple-element.75.refs_2_.refs_3_.refs_4_, ...), custom_call_target="tpu_custom_call" | custom-call | flops 2500 | bytes 1000 | tf_op jit(solution)/shard_map/attend_back/pallas_call | solution.py:81
  317.2 2.5 dynamic-slice_add_fusion
  321.9 14.1 %trade_down.3 = bf16[1,912,1024]{2,1,0:T(8,128)(2,1)} custom-call(bf16[1,1536,1312]{2,1,0:T(8,128)(2,1)} %get-tuple-element.110.refs_0_, bf16[1536,512]{1,0:T(8,128)(2,1)} %get-tuple-element.77.refs_3_.refs_2_.refs_1_, bf16[1536,1024]{1,0:T(8,128)(2,1)} %get-tuple-element.100.refs_2_, bf16[1536,1024]{1,0:T(8,128)(2,1)} %get-tuple-element.101.refs_3_, ...), custom_call_target="tpu_custom_call" | custom-call | flops 1200 | bytes 1000 | tf_op jit(solution)/shard_map/trade_down/pallas_call | solution.py:81
  339.8 11.7 %trade_attn.2.refs_2_ = bf16[3,1024,256]{2,1,0:T(8,128)(2,1)} custom-call(bf16[1664,1024]{1,0:T(8,128)(2,1)} %norm_rows.1.refs_0_, bf16[1536,1536]{1,0:T(8,128)(2,1)} %get-tuple-element.156.refs_1_.refs_5_), custom_call_target="tpu_custom_call" | custom-call | flops 1000 | bytes 1000 | tf_op jit(solution)/shard_map/trade_attn/pallas_call | solution.py:81
  353.0 11.8 %trade_attn.3 = bf16[3,1024,256]{2,1,0:T(8,128)(2,1)} custom-call(bf16[1664,1024]{1,0:T(8,128)(2,1)} %norm_rows.1.refs_0_, bf16[1536,1536]{1,0:T(8,128)(2,1)} %get-tuple-element.157.refs_1_.refs_3_, bf16[3,1024,256]{2,1,0:T(8,128)(2,1)} %trade_attn.2.refs_2_), custom_call_target="tpu_custom_call" | custom-call | flops 1000 | bytes 1000 | tf_op jit(solution)/shard_map/trade_attn/pallas_call | solution.py:81
  368.3 3.5 dynamic-slice_add_fusion.2
  373.2 18.6 %pull.1 = (f32[1536,1024]{1,0:T(8,128)}, f32[1,1024]{1,0:T(1,128)}) custom-call(bf16[1536,1024]{1,0:T(8,128)(2,1)} %refs_0_.5, f32[1536,1024]{1,0:T(8,128)} %get-tuple-element.96.refs_1_, f32[1,1024]{1,0:T(1,128)} %bitcast.48, bf16[1536,1536]{1,0:T(8,128)(2,1)} %get-tuple-element.157.refs_1_.refs_3_, bf16[3,1024,512]{2,1,0:T(8,128)(2,1)} %bitcast.40, ...), custom_call_target="tpu_custom_call" | custom-call | flops 1800 | bytes 1000 | tf_op jit(solution)/shard_map/pull/pallas_call | solution.py:81
  393.2 2.7 collective-permute-start.21
  395.9 2.7 dynamic-slice_add_fusion.4
  401.5 22.7 %collective-permute-done.21 = bf16[2,656,256]{2,1,0:T(8,128)(2,1)} collective-permute-done((bf16[2,656,256]{2,1,0:T(8,128)(2,1)S(1)}, bf16[2,656,256]{2,1,0:T(8,128)(2,1)}, u32[]{:S(2)}, u32[]{:S(2)}) %collective-permute-start.21) | collective-permute-done | bytes 671776 | tf_op jit(solution)/shard_map/ppermute | solution.py:745
  426.8 3.1 collective-permute-done.16
  433.4 18.1 %collective-permute-done.24 = bf16[1,912,256]{2,1,0:T(8,128)(2,1)S(1)} collective-permute-done((bf16[1,912,256]{2,1,0:T(8,128)(2,1)S(1)}, bf16[1,912,256]{2,1,0:T(8,128)(2,1)S(1)}, u32[]{:S(2)}, u32[]{:S(2)}) %collective-permute-start.24) | collective-permute-done | bytes 466976 | tf_op jit(solution)/shard_map/ppermute | solution.py:745
  455.2 3.5 collective-permute-start.27
  458.7 7.5 %collective-permute-done.26 = bf16[3,256,256]{2,1,0:T(8,128)(2,1)S(1)} collective-permute-done((bf16[3,256,256]{2,1,0:T(8,128)(2,1)S(1)}, bf16[3,256,256]{2,1,0:T(8,128)(2,1)S(1)}, u32[]{:S(2)}, u32[]{:S(2)}) %collective-permute-start.26) | collective-permute-done | bytes 393248 | tf_op jit(solution)/shard_map/ppermute | solution.py:745
  468.1 10.2 %collective-permute-done.27 = bf16[1,912,256]{2,1,0:T(8,128)(2,1)S(1)} collective-permute-done((bf16[1,912,256]{2,1,0:T(8,128)(2,1)S(1)}, bf16[1,912,256]{2,1,0:T(8,128)(2,1)S(1)}, u32[]{:S(2)}, u32[]{:S(2)}) %collective-permute-start.27) | collective-permute-done | bytes 466976 | tf_op jit(solution)/shard_map/ppermute | solution.py:745
  478.4 4.2 collective-permute-done.28
  484.5 3.5 maximum_select_fusion.refs_1_
  488.0 8.3 %collective-permute-start.31 = (bf16[2,656,1024]{2,1,0:T(8,128)(2,1)S(1)}, bf16[2,656,1024]{2,1,0:T(8,128)(2,1)}, u32[]{:S(2)}, u32[]{:S(2)}) collective-permute-start(bf16[2,656,1024]{2,1,0:T(8,128)(2,1)S(1)} %maximum_select_fusion.refs_1_), channel_id=1, source_target_pairs={{0,2},{1,3},{2,0},{3,1},{4,6},{5,7},{6,4},{7,5},{8,10},{9,11},{10,... | collective-permute-start | bytes 8060936 | tf_op jit(solution)/shard_map/ppermute | solution.py:745
  496.3 4.2 collective-permute-start.32
  500.5 9.9 %collective-permute-done.32 = bf16[1,912,256]{2,1,0:T(8,128)(2,1)} collective-permute-done((bf16[1,912,256]{2,1,0:T(8,128)(2,1)S(1)}, bf16[1,912,256]{2,1,0:T(8,128)(2,1)}, u32[]{:S(2)}, u32[]{:S(2)}) %collective-permute-start.32) | collective-permute-done | bytes 466976 | tf_op jit(solution)/shard_map/ppermute | solution.py:745
  510.4 2.3 maximum_select_fusion.4
  516.6 10.2 %collective-permute-done.23 = f32[2,1024]{1,0:T(2,128)S(1)} collective-permute-done((f32[2,1024]{1,0:T(2,128)S(1)}, f32[2,1024]{1,0:T(2,128)S(1)}, u32[]{:S(2)}, u32[]{:S(2)}) %collective-permute-start.23) | collective-permute-done | bytes 8224 | tf_op jit(solution)/shard_map/ppermute | solution.py:745
  526.8 4.1 collective-permute-done.33
  533.2 7.1 %assemble.3 = f32[2,1312,1024]{2,1,0:T(8,128)} custom-call(s32[1]{0:T(128)} %bitcast.1.refs_0_, bf16[2,656,1024]{2,1,0:T(8,128)(2,1)} %copy-done.4, bf16[2,656,1024]{2,1,0:T(8,128)(2,1)} %collective-permute-done.31.refs_2_, bf16[3,512,256]{2,1,0:T(8,128)(2,1)} %copy-done.8), custom_call_target="tpu_custom_call" | custom-call | tf_op jit(solution)/shard_map/assemble/pallas_call | solution.py:693
  540.3 2.8 maximum_select_fusion.1.refs_1_
  543.1 4.2 collective-permute-start.36
  548.4 2.6 collective-permute-done.29
  556.4 5.3 assemble.4
  563.5 4.8 assemble.5
  (168 shorter events, 70.8 us)
Async XLA Ops:
  1.7 6.5 %collective-permute-start = (bf16[64,1024]{1,0:T(8,128)(2,1)S(1)}, bf16[64,1024]{1,0:T(8,128)(2,1)S(1)}, u32[]{:S(2)}, u32[]{:S(2)}) collective-permute-start(bf16[64,1024]{1,0:T(8,128)(2,1)S(1)} %constant_dynamic-slice_fusion.3), channel_id=1, source_target_pairs={{0,1},{1,0},{2,3},{3,2},{4,5},{5,4},{6,7},{7,6},{8,9},{9,8},{10,11... | collective-permute-start | bytes 393224 | tf_op jit(solution)/shard_map/ppermute | solution.py:745
  11.4 47.0 %collective-permute-start.1 = (bf16[4,1024,256]{2,1,0:T(8,128)(2,1)}, bf16[4,1024,256]{2,1,0:T(8,128)(2,1)S(1)}, u32[]{:S(2)}, u32[]{:S(2)}) collective-permute-start(bf16[4,1024,256]{2,1,0:T(8,128)(2,1)} %pad_maximum_fusion), channel_id=1, source_target_pairs={{0,1},{1,0},{2,3},{3,2},{4,5},{5,4},{6,7},{7,6},{8,9},{9,8},{10,11... | collective-permute-start | bytes 6291464 | tf_op jit(solution)/shard_map/ppermute | solution.py:745
  58.4 4.5 collective-permute-start.2
  61.4 31.2 %collective-permute-start.3 = (bf16[2,656,512]{2,1,0:T(8,128)(2,1)S(1)}, bf16[2,656,512]{2,1,0:T(8,128)(2,1)S(1)}, u32[]{:S(2)}, u32[]{:S(2)}) collective-permute-start(bf16[2,656,512]{2,1,0:T(8,128)(2,1)S(1)} %constant_dynamic-slice_fusion.1), channel_id=1, source_target_pairs={{0,1},{1,0},{2,3},{3,2},{4,5},{5,4},{6,7},{7,6},{8,9},{9,8},{10,11... | collective-permute-start | bytes 4030472 | tf_op jit(solution)/shard_map/ppermute | solution.py:745
  92.6 20.8 %collective-permute-start.5 = (bf16[2,656,512]{2,1,0:T(8,128)(2,1)S(1)}, bf16[2,656,512]{2,1,0:T(8,128)(2,1)S(1)}, u32[]{:S(2)}, u32[]{:S(2)}) collective-permute-start(bf16[2,656,512]{2,1,0:T(8,128)(2,1)S(1)} %collective-permute-done.3.refs_7_.refs_3_), channel_id=1, source_target_pairs={{0,2},{1,3},{2,0},{3,1},{4,6},{5,7},{6,4},{7,5},{8,10},{9,11},{10,... | collective-permute-start | bytes 4030472 | tf_op jit(solution)/shard_map/ppermute | solution.py:745
  92.6 60.9 %collective-permute-start.4 = (bf16[2,656,512]{2,1,0:T(8,128)(2,1)S(1)}, bf16[2,656,512]{2,1,0:T(8,128)(2,1)S(1)}, u32[]{:S(2)}, u32[]{:S(2)}) collective-permute-start(bf16[2,656,512]{2,1,0:T(8,128)(2,1)S(1)} %collective-permute-done.3.refs_7_.refs_3_), channel_id=1, source_target_pairs={{0,4},{1,5},{2,6},{3,7},{4,0},{5,1},{6,2},{7,3},{8,12},{9,13},{10,... | collective-permute-start | bytes 4030472 | tf_op jit(solution)/shard_map/ppermute | solution.py:745
  95.5 17.3 %collective-permute-start.7 = (bf16[1,656,512]{2,1,0:T(8,128)(2,1)S(1)}, bf16[1,656,512]{2,1,0:T(8,128)(2,1)S(1)}, u32[]{:S(2)}, u32[]{:S(2)}) collective-permute-start(bf16[1,656,512]{2,1,0:T(8,128)(2,1)S(1)} %dynamic-slice_bitcast_fusion), channel_id=1, source_target_pairs={{0,1},{1,0},{2,3},{3,2},{4,5},{5,4},{6,7},{7,6},{8,9},{9,8},{10,11... | collective-permute-start | bytes 2015240 | tf_op jit(solution)/shard_map/ppermute | solution.py:745
  112.8 40.9 %copy-start.22 = (bf16[1,656,512]{2,1,0:T(8,128)(2,1)}, bf16[1,656,512]{2,1,0:T(8,128)(2,1)S(1)}, u32[]{:S(2)}) copy-start(bf16[1,656,512]{2,1,0:T(8,128)(2,1)S(1)} %collective-permute-done.7.refs_7_) | copy-start | bytes 2015236
  112.8 41.4 %collective-permute-start.8 = (bf16[1,656,512]{2,1,0:T(8,128)(2,1)S(1)}, bf16[1,656,512]{2,1,0:T(8,128)(2,1)S(1)}, u32[]{:S(2)}, u32[]{:S(2)}) collective-permute-start(bf16[1,656,512]{2,1,0:T(8,128)(2,1)S(1)} %collective-permute-done.7.refs_7_), channel_id=1, source_target_pairs={{0,4},{1,5},{2,6},{3,7},{4,0},{5,1},{6,2},{7,3},{8,12},{9,13},{10,... | collective-permute-start | bytes 2015240 | tf_op jit(solution)/shard_map/ppermute | solution.py:745
  153.6 5.1 collective-permute-start.6
  153.7 4.0 collective-permute-start.9
  154.2 4.5 collective-permute-start.10
  220.2 54.4 %collective-permute-start.11 = (bf16[1,656,1024]{2,1,0:T(8,128)(2,1)}, bf16[1,656,1024]{2,1,0:T(8,128)(2,1)S(1)}, u32[]{:S(2)}, u32[]{:S(2)}) collective-permute-start(bf16[1,656,1024]{2,1,0:T(8,128)(2,1)} %trade_outer.3.refs_2_), channel_id=1, source_target_pairs={{0,1},{1,0},{2,3},{3,2},{4,5},{5,4},{6,7},{7,6},{8,9},{9,8},{10,11... | collective-permute-start | bytes 4030472 | tf_op jit(solution)/shard_map/ppermute | solution.py:745
  232.3 84.0 %collective-permute-start.13 = (bf16[1,656,1024]{2,1,0:T(8,128)(2,1)}, bf16[1,656,1024]{2,1,0:T(8,128)(2,1)S(1)}, u32[]{:S(2)}, u32[]{:S(2)}) collective-permute-start(bf16[1,656,1024]{2,1,0:T(8,128)(2,1)} %trade_outer.4.refs_2_), channel_id=1, source_target_pairs={{0,1},{1,0},{2,3},{3,2},{4,5},{5,4},{6,7},{7,6},{8,9},{9,8},{10,11... | collective-permute-start | bytes 4030472 | tf_op jit(solution)/shard_map/ppermute | solution.py:745
  289.4 78.9 %collective-permute-start.15 = (bf16[1,912,1024]{2,1,0:T(8,128)(2,1)}, bf16[1,912,1024]{2,1,0:T(8,128)(2,1)}, u32[]{:S(2)}, u32[]{:S(2)}) collective-permute-start(bf16[1,912,1024]{2,1,0:T(8,128)(2,1)} %trade_down.2.refs_10_), channel_id=1, source_target_pairs={{0,1},{1,0},{2,3},{3,2},{4,5},{5,4},{6,7},{7,6},{8,9},{9,8},{10,11... | collective-permute-start | bytes 5603336 | tf_op jit(solution)/shard_map/ppermute | solution.py:745
  290.9 24.5 %copy-start.15 = (bf16[1,656,1024]{2,1,0:T(8,128)(2,1)S(1)}, bf16[1,656,1024]{2,1,0:T(8,128)(2,1)}, u32[]{:S(2)}) copy-start(bf16[1,656,1024]{2,1,0:T(8,128)(2,1)} %copy-done.14) | copy-start | bytes 4030468
  319.7 45.1 %collective-permute-start.14 = (bf16[2,656,512]{2,1,0:T(8,128)(2,1)S(1)}, bf16[2,656,512]{2,1,0:T(8,128)(2,1)}, u32[]{:S(2)}, u32[]{:S(2)}) collective-permute-start(bf16[2,656,512]{2,1,0:T(8,128)(2,1)S(1)} %get-tuple-element.140), channel_id=1, source_target_pairs={{0,4},{1,5},{2,6},{3,7},{4,0},{5,1},{6,2},{7,3},{8,12},{9,13},{10,... | collective-permute-start | bytes 4030472 | tf_op jit(solution)/shard_map/ppermute | solution.py:745
  321.3 16.7 %collective-permute-start.12 = (bf16[2,64,1024]{2,1,0:T(8,128)(2,1)S(1)}, bf16[2,64,1024]{2,1,0:T(8,128)(2,1)S(1)}, u32[]{:S(2)}, u32[]{:S(2)}) collective-permute-start(bf16[2,64,1024]{2,1,0:T(8,128)(2,1)S(1)} %pad_maximum_fusion.1), channel_id=1, source_target_pairs={{0,1},{1,0},{2,3},{3,2},{4,5},{5,4},{6,7},{7,6},{8,9},{9,8},{10,11... | collective-permute-start | bytes 786440 | tf_op jit(solution)/shard_map/ppermute | solution.py:745
  351.5 44.4 %collective-permute-start.18 = (bf16[3,1024,256]{2,1,0:T(8,128)(2,1)}, bf16[3,1024,256]{2,1,0:T(8,128)(2,1)}, u32[]{:S(2)}, u32[]{:S(2)}) collective-permute-start(bf16[3,1024,256]{2,1,0:T(8,128)(2,1)} %trade_attn.2.refs_2_), channel_id=1, source_target_pairs={{0,1},{1,0},{2,3},{3,2},{4,5},{5,4},{6,7},{7,6},{8,9},{9,8},{10,11... | collective-permute-start | bytes 4718600 | tf_op jit(solution)/shard_map/ppermute | solution.py:745
  366.6 25.2 %collective-permute-start.17 = (bf16[2,656,256]{2,1,0:T(8,128)(2,1)S(1)}, bf16[2,656,256]{2,1,0:T(8,128)(2,1)}, u32[]{:S(2)}, u32[]{:S(2)}) collective-permute-start(bf16[2,656,256]{2,1,0:T(8,128)(2,1)S(1)} %get-tuple-element.146), channel_id=1, source_target_pairs={{0,8},{1,9},{2,10},{3,11},{4,12},{5,13},{6,14},{7,15},{8,0},{9,1},... | collective-permute-start | bytes 2015240 | tf_op jit(solution)/shard_map/ppermute | solution.py:745
  371.7 27.5 %collective-permute-start.20 = (bf16[1,912,512]{2,1,0:T(8,128)(2,1)}, bf16[1,912,512]{2,1,0:T(8,128)(2,1)}, u32[]{:S(2)}, u32[]{:S(2)}) collective-permute-start(bf16[1,912,512]{2,1,0:T(8,128)(2,1)} %get-tuple-element.142), channel_id=1, source_target_pairs={{0,4},{1,5},{2,10},{3,11},{4,0},{5,1},{6,14},{7,15},{8,12},{9,13},... | collective-permute-start | bytes 2801672 | tf_op jit(solution)/shard_map/ppermute | solution.py:745
  393.2 31.0 %collective-permute-start.21 = (bf16[2,656,256]{2,1,0:T(8,128)(2,1)S(1)}, bf16[2,656,256]{2,1,0:T(8,128)(2,1)}, u32[]{:S(2)}, u32[]{:S(2)}) collective-permute-start(bf16[2,656,256]{2,1,0:T(8,128)(2,1)S(1)} %add.221), channel_id=1, source_target_pairs={{0,16},{1,17},{2,18},{3,19},{4,20},{5,21},{6,22},{7,23},{8,24},{9,... | collective-permute-start | bytes 2015240 | tf_op jit(solution)/shard_map/ppermute | solution.py:745
  398.6 33.5 %collective-permute-start.22 = (bf16[3,512,256]{2,1,0:T(8,128)(2,1)}, bf16[3,512,256]{2,1,0:T(8,128)(2,1)}, u32[]{:S(2)}, u32[]{:S(2)}) collective-permute-start(bf16[3,512,256]{2,1,0:T(8,128)(2,1)} %get-tuple-element.144), channel_id=1, source_target_pairs={{0,4},{1,5},{2,10},{3,11},{4,0},{5,1},{6,14},{7,15},{8,12},{9,13},... | collective-permute-start | bytes 2359304 | tf_op jit(solution)/shard_map/ppermute | solution.py:745
  399.2 27.0 %copy-start.29 = (f32[1,1024]{1,0:T(1,128)S(1)}, f32[1,1024]{1,0:T(1,128)}, u32[]{:S(2)}) copy-start(f32[1,1024]{1,0:T(1,128)} %get-tuple-element.117) | copy-start | bytes 12292
  399.2 27.0 %copy-start.30 = (f32[1,1024]{1,0:T(1,128)S(1)}, f32[1,1024]{1,0:T(1,128)}, u32[]{:S(2)}) copy-start(f32[1,1024]{1,0:T(1,128)} %get-tuple-element.116) | copy-start | bytes 12292
  401.5 28.4 %copy-start.27 = (bf16[1,912,256]{2,1,0:T(8,128)(2,1)S(1)}, bf16[1,912,256]{2,1,0:T(8,128)(2,1)}, u32[]{:S(2)}) copy-start(bf16[1,912,256]{2,1,0:T(8,128)(2,1)} %get-tuple-element.148) | copy-start | bytes 1400836
  401.5 50.0 %copy-start.18 = (bf16[1,912,256]{2,1,0:T(8,128)(2,1)S(1)}, bf16[1,912,256]{2,1,0:T(8,128)(2,1)}, u32[]{:S(2)}) copy-start(bf16[1,912,256]{2,1,0:T(8,128)(2,1)} %get-tuple-element.125) | copy-start | bytes 1400836
  425.5 26.1 %collective-permute-start.25 = (bf16[2,656,256]{2,1,0:T(8,128)(2,1)S(1)}, bf16[2,656,256]{2,1,0:T(8,128)(2,1)S(1)}, u32[]{:S(2)}, u32[]{:S(2)}) collective-permute-start(bf16[2,656,256]{2,1,0:T(8,128)(2,1)S(1)} %add.228), channel_id=1, source_target_pairs={{0,8},{1,9},{2,10},{3,11},{4,12},{5,13},{6,14},{7,15},{8,0},{9,1},... | collective-permute-start | bytes 2015240 | tf_op jit(solution)/shard_map/ppermute | solution.py:745
  426.2 3.7 collective-permute-start.16
  429.9 21.6 %collective-permute-start.24 = (bf16[1,912,256]{2,1,0:T(8,128)(2,1)S(1)}, bf16[1,912,256]{2,1,0:T(8,128)(2,1)S(1)}, u32[]{:S(2)}, u32[]{:S(2)}) collective-permute-start(bf16[1,912,256]{2,1,0:T(8,128)(2,1)S(1)} %copy-done.27), channel_id=1, source_target_pairs={{0,8},{1,9},{2,18},{3,19},{4,12},{5,13},{6,22},{7,23},{8,0},{9,1},... | collective-permute-start | bytes 1400840 | tf_op jit(solution)/shard_map/ppermute | solution.py:745
  431.4 2.0 collective-permute-start.19
  451.9 32.5 %copy-start.16 = (bf16[2,656,512]{2,1,0:T(8,128)(2,1)}, bf16[2,656,512]{2,1,0:T(8,128)(2,1)S(1)}, u32[]{:S(2)}) copy-start(bf16[2,656,512]{2,1,0:T(8,128)(2,1)S(1)} %maximum_select_fusion.3) | copy-start | bytes 4030468
  451.9 32.6 %collective-permute-start.30 = (bf16[2,656,512]{2,1,0:T(8,128)(2,1)S(1)}, bf16[2,656,512]{2,1,0:T(8,128)(2,1)}, u32[]{:S(2)}, u32[]{:S(2)}) collective-permute-start(bf16[2,656,512]{2,1,0:T(8,128)(2,1)S(1)} %maximum_select_fusion.3), channel_id=1, source_target_pairs={{0,4},{1,5},{2,6},{3,7},{4,0},{5,1},{6,2},{7,3},{8,12},{9,13},{10,... | collective-permute-start | bytes 4030472 | tf_op jit(solution)/shard_map/ppermute | solution.py:745
  453.5 12.8 %collective-permute-start.26 = (bf16[3,256,256]{2,1,0:T(8,128)(2,1)S(1)}, bf16[3,256,256]{2,1,0:T(8,128)(2,1)S(1)}, u32[]{:S(2)}, u32[]{:S(2)}) collective-permute-start(bf16[3,256,256]{2,1,0:T(8,128)(2,1)S(1)} %get-tuple-element.150), channel_id=1, source_target_pairs={{0,8},{1,9},{2,18},{3,19},{4,12},{5,13},{6,22},{7,23},{8,0},{9,1},... | collective-permute-start | bytes 1179656 | tf_op jit(solution)/shard_map/ppermute | solution.py:745
  455.2 23.1 %collective-permute-start.27 = (bf16[1,912,256]{2,1,0:T(8,128)(2,1)S(1)}, bf16[1,912,256]{2,1,0:T(8,128)(2,1)S(1)}, u32[]{:S(2)}, u32[]{:S(2)}) collective-permute-start(bf16[1,912,256]{2,1,0:T(8,128)(2,1)S(1)} %add.234), channel_id=1, source_target_pairs={{0,16},{1,17},{2,6},{3,7},{4,20},{5,21},{6,2},{7,3},{8,24},{9,25},... | collective-permute-start | bytes 1400840 | tf_op jit(solution)/shard_map/ppermute | solution.py:745
  466.3 16.3 %collective-permute-start.28 = (bf16[3,256,256]{2,1,0:T(8,128)(2,1)S(1)}, bf16[3,256,256]{2,1,0:T(8,128)(2,1)}, u32[]{:S(2)}, u32[]{:S(2)}) collective-permute-start(bf16[3,256,256]{2,1,0:T(8,128)(2,1)S(1)} %add.236), channel_id=1, source_target_pairs={{0,16},{1,17},{2,6},{3,7},{4,20},{5,21},{6,2},{7,3},{8,24},{9,25},... | collective-permute-start | bytes 1179656 | tf_op jit(solution)/shard_map/ppermute | solution.py:745
  488.0 44.7 %copy-start.4 = (bf16[2,656,1024]{2,1,0:T(8,128)(2,1)}, bf16[2,656,1024]{2,1,0:T(8,128)(2,1)S(1)}, u32[]{:S(2)}) copy-start(bf16[2,656,1024]{2,1,0:T(8,128)(2,1)S(1)} %maximum_select_fusion.refs_1_) | copy-start | bytes 8060932
  488.0 44.7 %collective-permute-start.31 = (bf16[2,656,1024]{2,1,0:T(8,128)(2,1)S(1)}, bf16[2,656,1024]{2,1,0:T(8,128)(2,1)}, u32[]{:S(2)}, u32[]{:S(2)}) collective-permute-start(bf16[2,656,1024]{2,1,0:T(8,128)(2,1)S(1)} %maximum_select_fusion.refs_1_), channel_id=1, source_target_pairs={{0,2},{1,3},{2,0},{3,1},{4,6},{5,7},{6,4},{7,5},{8,10},{9,11},{10,... | collective-permute-start | bytes 8060936 | tf_op jit(solution)/shard_map/ppermute | solution.py:745
  496.3 14.1 %collective-permute-start.32 = (bf16[1,912,256]{2,1,0:T(8,128)(2,1)S(1)}, bf16[1,912,256]{2,1,0:T(8,128)(2,1)}, u32[]{:S(2)}, u32[]{:S(2)}) collective-permute-start(bf16[1,912,256]{2,1,0:T(8,128)(2,1)S(1)} %add.237), channel_id=1, source_target_pairs={{0,8},{1,9},{2,18},{3,19},{4,12},{5,13},{6,22},{7,23},{8,0},{9,1},... | collective-permute-start | bytes 1400840 | tf_op jit(solution)/shard_map/ppermute | solution.py:745
  512.8 27.5 %collective-permute-start.35 = (bf16[1,912,512]{2,1,0:T(8,128)(2,1)}, bf16[1,912,512]{2,1,0:T(8,128)(2,1)}, u32[]{:S(2)}, u32[]{:S(2)}) collective-permute-start(bf16[1,912,512]{2,1,0:T(8,128)(2,1)} %maximum_select_fusion.4), channel_id=1, source_target_pairs={{0,4},{1,5},{2,10},{3,11},{4,0},{5,1},{6,14},{7,15},{8,12},{9,13},... | collective-permute-start | bytes 2801672 | tf_op jit(solution)/shard_map/ppermute | solution.py:745
  514.3 16.5 %collective-permute-start.33 = (bf16[3,256,256]{2,1,0:T(8,128)(2,1)}, bf16[3,256,256]{2,1,0:T(8,128)(2,1)S(1)}, u32[]{:S(2)}, u32[]{:S(2)}) collective-permute-start(bf16[3,256,256]{2,1,0:T(8,128)(2,1)} %add.238), channel_id=1, source_target_pairs={{0,8},{1,9},{2,18},{3,19},{4,12},{5,13},{6,22},{7,23},{8,0},{9,1},... | collective-permute-start | bytes 1179656 | tf_op jit(solution)/shard_map/ppermute | solution.py:745
  516.1 10.6 %collective-permute-start.23 = (f32[2,1024]{1,0:T(2,128)S(1)}, f32[2,1024]{1,0:T(2,128)S(1)}, u32[]{:S(2)}, u32[]{:S(2)}) collective-permute-start(f32[2,1024]{1,0:T(2,128)S(1)} %fusion.7), channel_id=1, source_target_pairs={{0,4},{1,5},{2,6},{3,7},{4,0},{5,1},{6,2},{7,3},{8,12},{9,13},{10,... | collective-permute-start | bytes 24584 | tf_op jit(solution)/shard_map/ppermute | solution.py:745
  532.3 18.7 %collective-permute-start.37 = (bf16[3,512,256]{2,1,0:T(8,128)(2,1)S(1)}, bf16[3,512,256]{2,1,0:T(8,128)(2,1)}, u32[]{:S(2)}, u32[]{:S(2)}) collective-permute-start(bf16[3,512,256]{2,1,0:T(8,128)(2,1)S(1)} %maximum_select_fusion.5.refs_3_), channel_id=1, source_target_pairs={{0,4},{1,5},{2,10},{3,11},{4,0},{5,1},{6,14},{7,15},{8,12},{9,13},... | collective-permute-start | bytes 2359304 | tf_op jit(solution)/shard_map/ppermute | solution.py:745
  543.1 12.0 %copy-start.6 = (bf16[1,912,1024]{2,1,0:T(8,128)(2,1)}, bf16[1,912,1024]{2,1,0:T(8,128)(2,1)S(1)}, u32[]{:S(2)}) copy-start(bf16[1,912,1024]{2,1,0:T(8,128)(2,1)S(1)} %maximum_select_fusion.1.refs_1_) | copy-start | bytes 5603332
  543.1 12.0 %collective-permute-start.36 = (bf16[1,912,1024]{2,1,0:T(8,128)(2,1)S(1)}, bf16[1,912,1024]{2,1,0:T(8,128)(2,1)S(1)}, u32[]{:S(2)}, u32[]{:S(2)}) collective-permute-start(bf16[1,912,1024]{2,1,0:T(8,128)(2,1)S(1)} %maximum_select_fusion.1.refs_1_), channel_id=1, source_target_pairs={{0,2},{1,3},{2,0},{3,1},{4,6},{5,7},{6,4},{7,5},{8,10},{9,11},{10,... | collective-permute-start | bytes 5603336 | tf_op jit(solution)/shard_map/ppermute | solution.py:745
  547.3 3.7 collective-permute-start.29
  552.7 9.6 %collective-permute-start.38 = (bf16[3,1024,256]{2,1,0:T(8,128)(2,1)S(1)}, bf16[3,1024,256]{2,1,0:T(8,128)(2,1)S(1)}, u32[]{:S(2)}, u32[]{:S(2)}) collective-permute-start(bf16[3,1024,256]{2,1,0:T(8,128)(2,1)S(1)} %maximum_select_fusion.2.refs_3_.refs_1_), channel_id=1, source_target_pairs={{0,2},{1,3},{2,0},{3,1},{4,6},{5,7},{6,4},{7,5},{8,10},{9,11},{10,... | collective-permute-start | bytes 4718600 | tf_op jit(solution)/shard_map/ppermute | solution.py:745
  552.8 8.9 %collective-permute-start.34 = (f32[2,1024]{1,0:T(2,128)S(1)}, f32[2,1024]{1,0:T(2,128)S(1)}, u32[]{:S(2)}, u32[]{:S(2)}) collective-permute-start(f32[2,1024]{1,0:T(2,128)S(1)} %add.240), channel_id=1, source_target_pairs={{0,16},{1,17},{2,18},{3,19},{4,20},{5,21},{6,22},{7,23},{8,24},{9,... | collective-permute-start | bytes 24584 | tf_op jit(solution)/shard_map/ppermute | solution.py:745
  (24 other events, 87.2 us)

commit v4 on v3

--- a/solution.py
+++ b/solution.py
@@ -81,17 +81,23 @@
     return call(*lead, *[a for a, _, _ in ins], *extra)
 
 
-def window_masks(pos0, length):
+def window_masks(shared, ones, pos0, length):
     j = lax.broadcasted_iota(jnp.int32, (BQ, 2 * BQ), 0)
     i = lax.broadcasted_iota(jnp.int32, (BQ, 2 * BQ), 1) % BQ
-    near = i <= j
-    key_pos = pos0 - HALF + j + jnp.where(near, 0, BQ)
+
+    @pl.when(pl.program_id(0) == 0)
+    def _():
+        shared[0] = j + jnp.where(i <= j, 0, BQ)
+        shared[1] = jnp.where(j == (i + HALF) % BQ, 1, 0)
+        ones[0] = jnp.where(i <= j, 1.0, 0.0).astype(LOW)
+        ones[1] = jnp.where(i == j, 1.0, 0.0).astype(LOW)
+
+    key = shared[0]
     top = jnp.minimum(length, MAXLEN)
-    own = j == (i + HALF) % BQ
-    bias = jnp.where(((key_pos >= 0) & (key_pos < top)) | own, 0.0, NEG)
+    bias = jnp.where(((key >= HALF - pos0) & (key < top - pos0 + HALF)) | (shared[1] > 0), 0.0, NEG)
     lane = lax.broadcasted_iota(jnp.int32, (1, 2 * BQ), 1) % BQ
     last_bias = jnp.where(pos0 + HALF + lane < top, 0.0, NEG)
-    return near, i == j, bias, last_bias
+    return key < BQ, i == j, bias, last_bias
 
 
 def split_heads(pair):
@@ -112,36 +118,41 @@
     return jnp.where(near, wide[:BQ], low), jnp.sum(jnp.where(diag, low, 0.0), 0, keepdims=True)
 
 
-def unfold(near, diag, tile, last):
-    zero = jnp.zeros_like(tile)
-    return jnp.concatenate(
-        [jnp.where(near, tile, zero), jnp.where(near, jnp.where(diag, last, zero), tile)], 0
-    ).astype(LOW)
+def unfold(ones, tile, last):
+    tile = tile.astype(LOW)
+    upper = tile * ones[0]
+    return jnp.concatenate([upper, (tile - upper) + ones[1] * last.astype(LOW)], 0)
 
 
 def window_rows(before, here, after, c):
     return jnp.concatenate([before[:, c], here[:, c], after[:, c]], 0)
 
 
-def attend_kernel(place, q, kb, kh, ka, vb, vh, va, out_ref, log_ref):
+def attend_kernel(place, q, kb, kh, ka, vb, vh, va, out_ref, log_ref, shared, ones):
     blk = pl.program_id(0)
-    near, diag, bias, last_bias = window_masks(place[0, blk], place[1, blk])
-    for pair in range(out_ref.shape[1] // BQ):
-        c = slice(pair * BQ, (pair + 1) * BQ)
-        queries = split_heads(q[:, c] * 0.125)
-        keyset = window_rows(kb, kh, ka, c)
-        values = window_rows(vb, vh, va, c)
-        scores, last = fold(near, diag, cols_dot(keyset, queries))
+    near, diag, bias, last_bias = window_masks(shared, ones, place[0, blk], place[1, blk])
+    columns = [slice(p * BQ, (p + 1) * BQ) for p in range(out_ref.shape[1] // BQ)]
+
+    def score(c):
+        return cols_dot(window_rows(kb, kh, ka, c), split_heads(q[:, c] * 0.125))
+
+    def soft(wide):
+        scores, last = fold(near, diag, wide)
         scores, last = scores + bias, last + last_bias
         row_max = jnp.maximum(jnp.max(scores, 0, keepdims=True), last)
         expons, last = jnp.exp(scores - row_max), jnp.exp(last - row_max)
         summed = jnp.sum(expons, 0, keepdims=True) + last
-        probs = unfold(near, diag, expons, last)
-        out_ref[:, c] = join_heads(rows_dot(values, probs), 1.0 / summed).astype(LOW)
+        return unfold(ones, expons, last), row_max, summed
+
+    wides = [score(c) for c in columns]
+    softs = [soft(w) for w in wides]
+    for pair, c in enumerate(columns):
+        probs, row_max, summed = softs[pair]
+        out_ref[:, c] = join_heads(rows_dot(window_rows(vb, vh, va, c), probs), 1.0 / summed).astype(LOW)
         log_ref[0, pair:pair + 1] = row_max + jnp.log(summed)
 
 
-def attend_back_kernel(place, q, kb, kh, ka, vb, vh, va, g_ref, log_ref, d_ref, edge_ref, carry, tail, dq_keep):
+def attend_back_kernel(place, q, kb, kh, ka, vb, vh, va, g_ref, log_ref, d_ref, edge_ref, carry, tail, dq_keep, shared, ones):
     step = pl.program_id(0)
     steps = pl.num_programs(0)
     width = g_ref.shape[1]
@@ -157,28 +168,37 @@
 
     @pl.when(step < steps - 1)
     def _():
-        near, diag, bias, last_bias = window_masks(place[0, step], place[1, step])
-        for pair in range(width // BQ):
-            c = slice(pair * BQ, (pair + 1) * BQ)
-            v = slice(width + pair * BQ, width + (pair + 1) * BQ)
+        near, diag, bias, last_bias = window_masks(shared, ones, place[0, step], place[1, step])
+        columns = [slice(p * BQ, (p + 1) * BQ) for p in range(width // BQ)]
+
+        def start(c):
             queries = split_heads(q[:, c] * 0.125)
+            grads = split_heads(g_ref[:, c])
             keyset = window_rows(kb, kh, ka, c)
-            values = window_rows(vb, vh, va, c)
-            grads = split_heads(g_ref[:, c])
+            return queries, grads, keyset, cols_dot(keyset, queries), cols_dot(window_rows(vb, vh, va, c), grads)
+
+        starts = [start(c) for c in columns]
+        for pair, c in enumerate(columns):
+            ready = starts[pair]
+            v = slice(width + c.start, width + c.stop)
+            queries, grads, keyset, wide, wide_grad = ready
             log_row = log_ref[0, pair:pair + 1]
-            scores, last = fold(near, diag, cols_dot(keyset, queries))
+            scores, last = fold(near, diag, wide)
             expons, last = jnp.exp(scores + (bias - log_row)), jnp.exp(last + (last_bias - log_row))
-            prob_grad, last_grad = fold(near, diag, cols_dot(values, grads))
+            prob_grad, last_grad = fold(near, diag, wide_grad)
             inner = jnp.sum(expons * prob_grad, 0, keepdims=True) + last * last_grad
-            score_grad = unfold(near, diag, expons * (prob_grad - inner), last * (last_grad - inner))
-            probs = unfold(near, diag, expons, last)
+            score_grad = unfold(ones, expons * (prob_grad - inner), last * (last_grad - inner))
+            probs = unfold(ones, expons, last)
             dq_keep[:, c] = join_heads(rows_dot(keyset, score_grad) * 0.125).astype(LOW)
             for lanes, grad in ((c, plain_dot(score_grad, queries)), (v, plain_dot(probs, grads))):
                 done = (carry[:, lanes] + grad[:BQ]).astype(LOW)
                 carry[:, lanes] = grad[BQ:]
                 d_ref[HALF:, lanes.start + width:lanes.stop + width] = done[:HALF]
                 tail[:, lanes] = done[HALF:]
-                edge_ref[0, :, lanes] = jnp.where(step == 0, done[:HALF], edge_ref[0, :, lanes])
+
+        @pl.when(step == 0)
+        def _():
+            edge_ref[0] = d_ref[HALF:, width:]
 
     @pl.when(step == steps - 1)
     def _():
@@ -207,7 +227,7 @@
             (shaped((blocks * BQ, width)), (BQ, width), lambda b: (b, 0)),
             (shaped((blocks, pairs, 2 * BQ), jnp.float32), (1, pairs, 2 * BQ), lambda b: (b, 0, 0)),
         ],
-        after, place, flops=blocks * pairs * BQ * BQ * BQ * 256,
+        after, place, scratch=[pltpu.VMEM((2, BQ, 2 * BQ), jnp.int32), pltpu.VMEM((2, BQ, 2 * BQ), LOW)],
     )
 
 
@@ -231,6 +251,8 @@
             pltpu.VMEM((BQ, 2 * width), jnp.float32),
             pltpu.VMEM((HALF, 2 * width), LOW),
             pltpu.VMEM((BQ, width), LOW),
+            pltpu.VMEM((2, BQ, 2 * BQ), jnp.int32),
+            pltpu.VMEM((2, BQ, 2 * BQ), LOW),
         ],
         flops=blocks * pairs * BQ * BQ * BQ * 512,
     )
@@ -398,7 +420,7 @@
 
 def mlp_last_kernel(fetched, place, normed, cotangent, *refs):
     if fetched:
-        pieces, refs = refs[:8], refs[8:]
+        pieces, refs = refs[:6], refs[6:]
         win, wdown = refs[-2:]
 
         @pl.when(pl.program_id(0) == 0)
@@ -409,7 +431,8 @@
                 columns = pl.ds(pl.multiple_of((place[2, 1] ^ (part % 2)) * model, model), model)
                 for side in range(2):
                     win[side, rows, columns] = pieces[part][side]
-                wdown[rows, columns] = pieces[4 + part][0]
+            for side in range(2):
+                wdown[side * units:(side + 1) * units] = pieces[4 + side][...]
     else:
         (win, wdown), refs = refs[:2], refs[2:]
     hidden, gain, branch_in, pulled_in, weights = refs[:5]
@@ -453,8 +476,8 @@
 
 
 def mlp_last(place, normed, cotangent, weights, hidden, gain, branch, pulled, w_out, parts=(), after=()):
-    fetched = len(weights) == 8
-    units = 2 * weights[4].shape[1] if fetched else weights[1].shape[0]
+    fetched = len(weights) == 6
+    units = 2 * weights[4].shape[0] if fetched else weights[1].shape[0]
     rows, model, tile, row, ins, outs = mlp_specs(normed, cotangent, units)
     block = (tile, model)
     ins = ins + [whole(w) for w in weights]
@@ -854,26 +877,23 @@
 
     normed = norm_rows(tokens, border, border, gain_attn)
     quarter = lambda w, a, b: half(half(w, core, a), bits[1], b)
-    in_direct = links.cross(quarter(tie(w_in, normed), 1, 2))
-    down_direct = links.cross(quarter(tie(w_down, normed)[None], 1, 2))
+    in_piece = quarter(tie(w_in, normed), 1, 2)
+    in_direct = links.cross(in_piece)
+    down_direct = links.cross(half(tie(w_down, in_piece), core, 0))
     q0, k0, v0 = project(normed, w_qkv)
     attended0, logs0 = attend(place, q0, k0, v0)
     attn_parts = (attn_direct, links.flip(tie(attn_direct, attended0), 1))
     q1, k1, v1 = project_parts(normed, attn_parts, after=[attended0])
     attended1, logs1 = attend(place, q1, k1, v1)
-    in_direct = tie(in_direct, attended1)
+    hidden, normed_mlp = mix(tokens, gain_mlp, attended0, w_out, attended1, attn_parts)
+    in_direct = tie(in_direct, hidden)
     in_relayed = links.flip(in_direct, 2)
     in_core = links.flip(in_direct, 1)
-    hidden, normed_mlp = mix(tokens, gain_mlp, attended0, w_out, attended1, attn_parts, after=[in_direct])
-    gate0, lift0, out_low, branch, pulled = mlp_first(place, normed_mlp, cotangent, w_in, w_down, after=[in_core])
-    down_direct = tie(down_direct, hidden)
-    down_relayed = links.flip(down_direct, 2)
-    down_core = links.flip(down_direct, 1)
+    gate0, lift0, out_low, branch, pulled = mlp_first(place, normed_mlp, cotangent, w_in, w_down, after=[in_direct])
     in_relayed = tie(in_relayed, branch)
-    down_relayed = tie(down_relayed, in_relayed)
+    down_direct = tie(down_direct, branch)
     weights = (
-        in_direct, in_relayed, in_core, links.flip(in_relayed, 1),
-        down_direct, down_relayed, down_core, links.flip(down_relayed, 1),
+        in_direct, in_relayed, in_core, links.flip(in_relayed, 1), down_direct, links.flip(down_direct, 1),
     )
     gate1, lift1, output, hidden_grad, hidden_low, gain_mlp_grad, back0, back1 = mlp_last(
         place, normed_mlp, cotangent, weights, hidden, gain_mlp, branch, pulled, w_out, attn_parts
@@ -886,50 +906,55 @@
     inner_a.send_far(trade_outer(0, False, lift1, normed_mlp, [0], after=[back1]))
     inner_b.send_far(trade_outer(1, False, lift1, normed_mlp, [1], after=[inner_a.far]))
     inner.near = trade_outer(2, True, lift0, normed_mlp, [0, 1], after=[inner_b.far])
-    d1, edge1 = attend_back(place, q1, k1, v1, back1, logs1, after=[inner.near])
-    down.send_far(trade_down(3, False, gate1, attended1, out_low, hidden_low, after=[d1, inner_a.crossed]))
-    d0, edge0 = attend_back(place, q0, k0, v0, back0, logs0, after=[down.far])
-    inner.across(d0, parts=[inner_a.crossed, inner_b.crossed])
 
     swap = lambda e: jnp.where(core == 0, e, jnp.concatenate([e[:, size:], e[:, :size]], 1))
-    edge_out = lambda e: jnp.concatenate([swap(e[:, :width]), swap(e[:, width:])], 1)
-    edges = jnp.stack([edge_out(jnp.where(tensor_id == 0, e[1], e[0])) for e in (edge1, edge0)])
-    edges = links.cross(edges)
-    down.near = trade_down(4, True, gate0, attended0, out_low, hidden_low, after=[inner.held])
-    edges = tie(edges, down.near)
+
+    def trade_edge(edge):
+        chosen = jnp.where(tensor_id == 0, edge[1], edge[0])
+        return links.cross(jnp.concatenate([swap(chosen[:, :width]), swap(chosen[:, width:])], 1))
 
     def add_edge(d, edge):
         held = lax.dynamic_slice(d, (start, width), (HALF, 2 * width))
         return lax.dynamic_update_slice(d, held + edge, (start, width))
 
-    d1, d0 = add_edge(d1, edges[1]), add_edge(d0, edges[0])
-    attn.send_far(trade_attn(5, False, normed, d1))
-    attn.near = trade_attn(6, True, normed, d0, after=[attn.far])
-    inner.scatter(attn.near)
+    d0, edge0 = attend_back(place, q0, k0, v0, back0, logs0, after=[inner.near])
+    edge_other = trade_edge(edge0)
+    far = trade_down(3, False, gate1, attended1, out_low, hidden_low, after=[d0, inner_a.crossed])
+    down.send_far(tie(far, edge_other))
+    inner.across(down.far, parts=[inner_a.crossed, inner_b.crossed])
+    d1, edge1 = attend_back(place, q1, k1, v1, back1, logs1, after=[inner.held])
+    edge_own = trade_edge(edge1)
+    d1 = add_edge(d1, edge_other)
+    far = trade_attn(5, False, normed, d1)
+    inner.scatter(far)
+    attn.send_far(tie(far, edge_own))
+    down.near = trade_down(4, True, gate0, attended0, out_low, hidden_low, after=[inner.held])
+    inner.both(down.near)
     down.across(inner.held)
-    input_grad, gain_attn_grad = pull(tokens, hidden_grad, gain_attn, d0, w_qkv, d1, attn_parts, after=[down.held])
-    inner.both(input_grad)
+    d0 = add_edge(tie(d0, down.held), edge_own)
+    attn.near = trade_attn(6, True, normed, d0)
+    down.scatter(attn.near)
+    inner.both_add(down.held)
+    attn.across(inner.held)
+    input_grad, gain_attn_grad = pull(tokens, hidden_grad, gain_attn, d0, w_qkv, d1, attn_parts, after=[attn.held])
     gain_total = jnp.concatenate((gain_attn_grad, gain_mlp_grad))
-    attn.across(inner.held)
-    down.scatter(attn.held)
-    inner.both_add(down.held)
+    inner.gather(input_grad)
+    down.both(inner.held)
+    attn.scatter(down.held)
     gain_total = gain_total + tie(links.cross(gain_total), attn.held)
-    attn.scatter(inner.held)
+    down.both_add(attn.held)
+    attn.both(down.held)
     gain_total = gain_total + tie(links.flip(gain_total, 1), attn.held)
-    down.both(attn.held, gain_total)
-    inner.gather(down.held)
-    attn.both(inner.held)
-    down.both_add(attn.held)
+    down.gather(attn.held)
     attn.both_add(down.held)
-    gain_total = gain_total + tie(links.flip(gain_total, 2), attn.held)
     grads_in = inner.last(attn.held)
-    down.gather(grads_in[0])
-    attn.gather(down.held, gain_total)
-    grad_w_in = assemble(*grads_in, 1, after=[attn.held])
+    grads_down = down.last(grads_in[0])
+    gain_total = gain_total + tie(links.flip(gain_total, 2), grads_down[0])
+    attn.gather(grads_down[0])
+    grad_w_in = assemble(*grads_in, 1, after=[attn.held, gain_total])
     gain_total = gain_total + tie(links.flip(gain_total, 4), grad_w_in)
-    grads_down = down.last(grad_w_in)
-    grads_attn = attn.last(grads_down[0], gain_total)
-    grad_w_down, grad_w_out = assemble_down(*grads_down, units, after=[grads_attn[0]])
+    grads_attn = attn.last(grad_w_in)
+    grad_w_down, grad_w_out = assemble_down(*grads_down, units, after=[grads_attn[0], gain_total])
     gain_total = gain_total + tie(links.flip(gain_total, 8), grad_w_down)
     grad_w_qkv = assemble(*grads_attn, 2, after=[grad_w_down])
     return (

time: 578 us -> 532 us (0.920)
  Pallas kernels: 336 us -> 308 us
  starting transfers between devices: 60.1 us -> 50.9 us
  waiting for transfers between devices: 117 us -> 110 us
    pallas_call x18, Pallas kernels: 319 us -> 291 us  [run(): return call(*lead, *[a for a, _, _ in ins], *extra)]
    ppermute x39 -> x38, starting transfers between devices: 60.1 us -> 50.9 us  [send(): return lax.ppermute(value, AXES, pairs)]
    ppermute x39 -> x38, waiting for transfers between devices: 117 us -> 110 us  [send(): return lax.ppermute(value, AXES, pairs)]
  transfers between devices with their start and end apart: 39 -> 38, of which waited for: 18 -> 16; matrix products, arithmetic and copies ran while one was open for 6% -> 7% of each run, Pallas kernels for 48% -> 47%
where the time goes in v4:
time: 532 us; the launch traced here: 522 us
  Pallas kernels  308 us (58%)
  waiting for transfers between devices  110 us (21%)
  starting transfers between devices  50.9 us (10%)
  other arithmetic  36 us (7%)
  local copies, waits for them, and re-layouts  15.6 us (3%)
    pallas_call x18, Pallas kernels, run(): return call(*lead, *[a for a, _, _ in ins], *extra)  291 us
    ppermute x38, waiting for transfers between devices, send(): return lax.ppermute(value, AXES, pairs)  110 us
    ppermute x38, starting transfers between devices, send(): return lax.ppermute(value, AXES, pairs)  50.9 us
    pallas_call x3, Pallas kernels, assemble_call(): pl.pallas_call(lambda *refs: body(*refs[:3], *refs[3 + len(after):]), gri...  17.3 us
    add x6, other arithmetic, split(): part = lambda k: half(a, k, self.axis) + half(b, k, self.axis)  13.6 us
    select_n x6, other arithmetic, order(): jnp.where(bit == 0, jnp.concatenate([first, second], axis), jnp.concatena...  11.4 us
  transfers between devices with their start and end apart: 38, of which 16 were waited for; matrix products, arithmetic and copies ran while one was open for 7% of the time, Pallas kernels for 47%

profile of v4, /device:TPU:0, one launch (start us, length us, event | category | flops | bytes accessed | tf_op | source)
XLA Modules:
  0.0 522.0 jit_solution(6578277635660519720)
XLA Ops:
  1.7 3.0 collective-permute-start
  4.7 3.5 collective-permute-done.refs_1_.refs_2_
  13.6 5.6 %norm_rows.1.refs_0_ = bf16[1664,1024]{1,0:T(8,128)(2,1)} custom-call(bf16[1536,1024]{1,0:T(8,128)(2,1)} %refs_0_.5, bf16[64,1024]{1,0:T(8,128)(2,1)} %copy-done.23, bf16[64,1024]{1,0:T(8,128)(2,1)} %copy-done.23, f32[1,1024]{1,0:T(1,128)} %bitcast.33), custom_call_target="tpu_custom_call" | custom-call | flops 600 | bytes 1000 | tf_op jit(solution)/shard_map/norm_rows/pallas_call | solution.py:81
  19.9 8.9 %project.1 = (bf16[1664,512]{1,0:T(8,128)(2,1)}, bf16[1664,512]{1,0:T(8,128)(2,1)}, bf16[1664,512]{1,0:T(8,128)(2,1)}) custom-call(bf16[1664,1024]{1,0:T(8,128)(2,1)} %norm_rows.1.refs_0_, bf16[3,1024,512]{2,1,0:T(8,128)(2,1)} %bitcast.25), custom_call_target="tpu_custom_call" | custom-call | flops 900 | bytes 1000 | tf_op jit(solution)/shard_map/project/pallas_call | solution.py:81
  28.8 13.8 %attend.2 = (bf16[1536,512]{1,0:T(8,128)(2,1)}, f32[12,4,256]{2,1,0:T(4,128)}) custom-call(s32[3,12]{1,0:T(4,128)} %pad_add_fusion.refs_0_, bf16[1664,512]{1,0:T(8,128)(2,1)} %get-tuple-element.75.refs_1_, bf16[1664,512]{1,0:T(8,128)(2,1)} %get-tuple-element.76.refs_2_.refs_3_.refs_4_, bf16[1664,512]{1,0:T(8,128)(2,1)} %get-tuple-element.76.refs_2_.refs_3_.refs_4_, ...), custom_call_target="tpu_custom_call" | custom-call | flops 2000 | bytes 1000 | tf_op jit(solution)/shard_map/attend/pallas_call | solution.py:81
  42.6 15.8 %collective-permute-done.1.refs_1_.refs_5_.refs_14_.refs_6_ = bf16[4,1024,256]{2,1,0:T(8,128)(2,1)S(1)} collective-permute-done((bf16[4,1024,256]{2,1,0:T(8,128)(2,1)}, bf16[4,1024,256]{2,1,0:T(8,128)(2,1)S(1)}, u32[]{:S(2)}, u32[]{:S(2)}) %collective-permute-start.1) | collective-permute-done | bytes 2097184 | tf_op jit(solution)/shard_map/ppermute | solution.py:768
  58.4 4.1 constant_dynamic-slice_fusion.2
  65.8 9.0 %project_parts.1 = (bf16[1664,512]{1,0:T(8,128)(2,1)}, bf16[1664,512]{1,0:T(8,128)(2,1)}, bf16[1664,512]{1,0:T(8,128)(2,1)}) custom-call(bf16[1664,1024]{1,0:T(8,128)(2,1)} %norm_rows.1.refs_0_, bf16[4,1024,256]{2,1,0:T(8,128)(2,1)} %copy-done, bf16[4,1024,256]{2,1,0:T(8,128)(2,1)} %collective-permute-done.2.refs_2_.refs_6_.refs_15_.refs_7_, ...), custom_call_target="tpu_custom_call" | custom-call | flops 900 | bytes 1000 | tf_op jit(solution)/shard_map/project_parts/pallas_call | solution.py:81
  74.7 13.8 %attend.3 = (bf16[1536,512]{1,0:T(8,128)(2,1)}, f32[12,4,256]{2,1,0:T(4,128)}) custom-call(s32[3,12]{1,0:T(4,128)} %pad_add_fusion.refs_0_, bf16[1664,512]{1,0:T(8,128)(2,1)} %get-tuple-element.82.refs_1_, bf16[1664,512]{1,0:T(8,128)(2,1)} %get-tuple-element.83.refs_2_.refs_3_.refs_4_, bf16[1664,512]{1,0:T(8,128)(2,1)} %get-tuple-element.83.refs_2_.refs_3_.refs_4_, ...), custom_call_target="tpu_custom_call" | custom-call | flops 2000 | bytes 1000 | tf_op jit(solution)/shard_map/attend/pallas_call | solution.py:81
  88.6 10.9 %mix.1 = (f32[1536,1024]{1,0:T(8,128)}, bf16[1536,1024]{1,0:T(8,128)(2,1)}) custom-call(bf16[1536,1024]{1,0:T(8,128)(2,1)} %refs_0_.5, f32[1,1024]{1,0:T(1,128)} %bitcast.31, bf16[1536,512]{1,0:T(8,128)(2,1)} %get-tuple-element.78.refs_3_.refs_2_.refs_1_, bf16[512,1024]{1,0:T(8,128)(2,1)} %refs_13_.1, bf16[1536,512]{1,0:T(8,128)(2,1)} %get-tuple-element.85.refs_4_.refs_1_, ...), custom_call_target="tpu_custom_call" | custom-call | flops 1100 | bytes 1000 | tf_op jit(solution)/shard_map/mix/pallas_call | solution.py:81
  100.9 38.7 %mlp_first.1 = (bf16[1,1536,1312]{2,1,0:T(8,128)(2,1)}, bf16[2,1536,1312]{2,1,0:T(8,128)(2,1)}, bf16[1536,1024]{1,0:T(8,128)(2,1)}, f32[1536,1024]{1,0:T(8,128)}, f32[1536,1024]{1,0:T(8,128)}) custom-call(s32[3,12]{1,0:T(4,128)} %pad_add_fusion.refs_0_, bf16[1536,1024]{1,0:T(8,128)(2,1)} %get-tuple-element.86.refs_1_, bf16[1536,1024]{1,0:T(8,128)(2,1)} %refs_2_.3, ...), custom_call_target="tpu_custom_call" | custom-call | flops 3900 | bytes 1000 | tf_op jit(solution)/shard_map/mlp_first/pallas_call | solution.py:81
  140.2 2.6 collective-permute-done.8.refs_8_
  145.9 49.3 %mlp_last.1 = (bf16[1,1536,1312]{2,1,0:T(8,128)(2,1)}, bf16[2,1536,1312]{2,1,0:T(8,128)(2,1)}, bf16[1536,1024]{1,0:T(8,128)(2,1)}, f32[1536,1024]{1,0:T(8,128)},...) custom-call(s32[3,12]{1,0:T(4,128)} %pad_add_fusion.refs_0_, ...), custom_call_target="tpu_custom_call" | custom-call | flops 4900 | bytes 1000 | tf_op jit(solution)/shard_map/mlp_last/pallas_call | solution.py:81
  195.2 10.7 %trade_outer.3.refs_2_ = bf16[1,656,1024]{2,1,0:T(8,128)(2,1)} custom-call(bf16[2,1536,1312]{2,1,0:T(8,128)(2,1)} %get-tuple-element.100.refs_0_, bf16[1536,1024]{1,0:T(8,128)(2,1)} %get-tuple-element.86.refs_1_, bf16[1536,512]{1,0:T(8,128)(2,1)} %get-tuple-element.101.refs_2_.refs_8_), custom_call_target="tpu_custom_call" | custom-call | flops 900 | bytes 1000 | tf_op jit(solution)/shard_map/trade_outer/pallas_call | solution.py:81
  207.5 10.6 %trade_outer.4.refs_2_ = bf16[1,656,1024]{2,1,0:T(8,128)(2,1)} custom-call(bf16[2,1536,1312]{2,1,0:T(8,128)(2,1)} %get-tuple-element.100.refs_0_, bf16[1536,1024]{1,0:T(8,128)(2,1)} %get-tuple-element.86.refs_1_, bf16[1,656,1024]{2,1,0:T(8,128)(2,1)} %trade_outer.3.refs_2_), custom_call_target="tpu_custom_call" | custom-call | flops 900 | bytes 1000 | tf_op jit(solution)/shard_map/trade_outer/pallas_call | solution.py:81
  218.7 16.3 %trade_outer.5.refs_10_ = bf16[2,656,1024]{2,1,0:T(8,128)(2,1)} custom-call(bf16[2,1536,1312]{2,1,0:T(8,128)(2,1)} %get-tuple-element.99.refs_0_, bf16[1536,1024]{1,0:T(8,128)(2,1)} %get-tuple-element.86.refs_1_, bf16[1,656,1024]{2,1,0:T(8,128)(2,1)} %trade_outer.4.refs_2_), custom_call_target="tpu_custom_call" | custom-call | flops 900 | bytes 1000 | tf_op jit(solution)/shard_map/trade_outer/pallas_call | solution.py:81
  235.0 16.6 %attend_back.2 = (bf16[1536,1536]{1,0:T(8,128)(2,1)}, bf16[2,64,1024]{2,1,0:T(8,128)(2,1)}) custom-call(s32[3,12]{1,0:T(4,128)} %pad_add_fusion.refs_0_, bf16[1664,512]{1,0:T(8,128)(2,1)} %get-tuple-element.75.refs_1_, bf16[1664,512]{1,0:T(8,128)(2,1)} %get-tuple-element.76.refs_2_.refs_3_.refs_4_, ...), custom_call_target="tpu_custom_call" | custom-call | flops 2500 | bytes 1000 | tf_op jit(solution)/shard_map/attend_back/pallas_call | solution.py:81
  255.3 13.7 %trade_down.2 = bf16[1,912,1024]{2,1,0:T(8,128)(2,1)} custom-call(bf16[1,1536,1312]{2,1,0:T(8,128)(2,1)} %get-tuple-element.106.refs_0_, bf16[1536,512]{1,0:T(8,128)(2,1)} %get-tuple-element.85.refs_4_.refs_1_, bf16[1536,1024]{1,0:T(8,128)(2,1)} %get-tuple-element.104.refs_2_, bf16[1536,1024]{1,0:T(8,128)(2,1)} %get-tuple-element.105.refs_3_, ...), custom_call_target="tpu_custom_call" | custom-call | flops 1200 | bytes 1000 | tf_op jit(solution)/shard_map/trade_down/pallas_call | solution.py:81
  272.7 2.5 dynamic-slice_add_fusion.1
  277.5 16.7 %attend_back.3 = (bf16[1536,1536]{1,0:T(8,128)(2,1)}, bf16[2,64,1024]{2,1,0:T(8,128)(2,1)}) custom-call(s32[3,12]{1,0:T(4,128)} %pad_add_fusion.refs_0_, bf16[1664,512]{1,0:T(8,128)(2,1)} %get-tuple-element.82.refs_1_, bf16[1664,512]{1,0:T(8,128)(2,1)} %get-tuple-element.83.refs_2_.refs_3_.refs_4_, ...), custom_call_target="tpu_custom_call" | custom-call | flops 2500 | bytes 1000 | tf_op jit(solution)/shard_map/attend_back/pallas_call | solution.py:81
  295.7 11.8 %trade_attn.2 = bf16[3,1024,256]{2,1,0:T(8,128)(2,1)} custom-call(bf16[1664,1024]{1,0:T(8,128)(2,1)} %norm_rows.1.refs_0_, bf16[1536,1536]{1,0:T(8,128)(2,1)} %add_dynamic-update-slice_fusion.1.refs_1_.refs_5_), custom_call_target="tpu_custom_call" | custom-call | flops 1000 | bytes 1000 | tf_op jit(solution)/shard_map/trade_attn/pallas_call | solution.py:81
  307.6 2.5 dynamic-slice_add_fusion.6
  312.3 8.6 %collective-permute-done.15 = bf16[64,1024]{1,0:T(8,128)(2,1)S(1)} collective-permute-done((bf16[64,1024]{1,0:T(8,128)(2,1)S(1)}, bf16[64,1024]{1,0:T(8,128)(2,1)S(1)}, u32[]{:S(2)}, u32[]{:S(2)}) %collective-permute-start.15) | collective-permute-done | bytes 131104 | tf_op jit(solution)/shard_map/ppermute | solution.py:768
  321.9 14.1 %trade_down.3 = bf16[1,912,1024]{2,1,0:T(8,128)(2,1)} custom-call(bf16[1,1536,1312]{2,1,0:T(8,128)(2,1)} %get-tuple-element.103.refs_0_, bf16[1536,512]{1,0:T(8,128)(2,1)} %get-tuple-element.78.refs_3_.refs_2_.refs_1_, bf16[1536,1024]{1,0:T(8,128)(2,1)} %get-tuple-element.104.refs_2_, bf16[1536,1024]{1,0:T(8,128)(2,1)} %get-tuple-element.105.refs_3_, ...), custom_call_target="tpu_custom_call" | custom-call | flops 1200 | bytes 1000 | tf_op jit(solution)/shard_map/trade_down/pallas_call | solution.py:81
  337.7 2.3 dynamic-slice_add_fusion.2
  341.6 2.6 collective-permute-start.17
  345.8 11.7 %trade_attn.3 = bf16[3,1024,256]{2,1,0:T(8,128)(2,1)} custom-call(bf16[1664,1024]{1,0:T(8,128)(2,1)} %norm_rows.1.refs_0_, bf16[1536,1536]{1,0:T(8,128)(2,1)} %add_dynamic-update-slice_fusion.refs_1_.refs_3_), custom_call_target="tpu_custom_call" | custom-call | flops 1000 | bytes 1000 | tf_op jit(solution)/shard_map/trade_attn/pallas_call | solution.py:81
  357.5 2.3 dynamic-slice_add_fusion.8
  359.8 14.0 %collective-permute-done.17 = bf16[2,656,256]{2,1,0:T(8,128)(2,1)S(1)} collective-permute-done((bf16[2,656,256]{2,1,0:T(8,128)(2,1)S(1)}, bf16[2,656,256]{2,1,0:T(8,128)(2,1)S(1)}, u32[]{:S(2)}, u32[]{:S(2)}) %collective-permute-start.17) | collective-permute-done | bytes 671776 | tf_op jit(solution)/shard_map/ppermute | solution.py:768
  374.1 2.7 dynamic-slice_add_fusion.4
  380.3 18.4 %pull.1 = (f32[1536,1024]{1,0:T(8,128)}, f32[1,1024]{1,0:T(1,128)}) custom-call(bf16[1536,1024]{1,0:T(8,128)(2,1)} %refs_0_.5, f32[1536,1024]{1,0:T(8,128)} %get-tuple-element.96.refs_1_, f32[1,1024]{1,0:T(1,128)} %bitcast.34, bf16[1536,1536]{1,0:T(8,128)(2,1)} %add_dynamic-update-slice_fusion.refs_1_.refs_3_, bf16[3,1024,512]{2,1,0:T(8,128)(2,1)} %bitcast.26, ...), custom_call_target="tpu_custom_call" | custom-call | flops 1800 | bytes 1000 | tf_op jit(solution)/shard_map/pull/pallas_call | solution.py:81
  401.0 6.2 %collective-permute-done.21 = bf16[1,912,256]{2,1,0:T(8,128)(2,1)} collective-permute-done((bf16[1,912,256]{2,1,0:T(8,128)(2,1)}, bf16[1,912,256]{2,1,0:T(8,128)(2,1)}, u32[]{:S(2)}, u32[]{:S(2)}) %collective-permute-start.21) | collective-permute-done | bytes 466976 | tf_op jit(solution)/shard_map/ppermute | solution.py:768
  410.3 2.5 collective-permute-start.25
  412.9 18.0 %collective-permute-done.24 = bf16[1,912,256]{2,1,0:T(8,128)(2,1)S(1)} collective-permute-done((bf16[1,912,256]{2,1,0:T(8,128)(2,1)S(1)}, bf16[1,912,256]{2,1,0:T(8,128)(2,1)S(1)}, u32[]{:S(2)}, u32[]{:S(2)}) %collective-permute-start.24) | collective-permute-done | bytes 466976 | tf_op jit(solution)/shard_map/ppermute | solution.py:768
  431.2 2.5 collective-permute-start.28
  433.7 9.8 %collective-permute-done.27 = bf16[1,912,256]{2,1,0:T(8,128)(2,1)S(1)} collective-permute-done((bf16[1,912,256]{2,1,0:T(8,128)(2,1)S(1)}, bf16[1,912,256]{2,1,0:T(8,128)(2,1)S(1)}, u32[]{:S(2)}, u32[]{:S(2)}) %collective-permute-start.27) | collective-permute-done | bytes 466976 | tf_op jit(solution)/shard_map/ppermute | solution.py:768
  444.6 5.9 %collective-permute-done.28 = bf16[3,256,256]{2,1,0:T(8,128)(2,1)S(1)} collective-permute-done((bf16[3,256,256]{2,1,0:T(8,128)(2,1)S(1)}, bf16[3,256,256]{2,1,0:T(8,128)(2,1)S(1)}, u32[]{:S(2)}, u32[]{:S(2)}) %collective-permute-start.28) | collective-permute-done | bytes 393248 | tf_op jit(solution)/shard_map/ppermute | solution.py:768
  450.7 3.7 maximum_select_fusion.refs_1_
  454.4 4.7 collective-permute-start.32
  460.6 12.3 %collective-permute-done.30 = bf16[1,912,512]{2,1,0:T(8,128)(2,1)} collective-permute-done((bf16[1,912,512]{2,1,0:T(8,128)(2,1)}, bf16[1,912,512]{2,1,0:T(8,128)(2,1)}, u32[]{:S(2)}, u32[]{:S(2)}) %collective-permute-start.30) | collective-permute-done | bytes 933920 | tf_op jit(solution)/shard_map/ppermute | solution.py:768
  473.0 2.8 maximum_select_fusion.1.refs_1_
  478.3 3.1 collective-permute-done.19
  481.4 5.2 collective-permute-start.35
  486.7 3.2 collective-permute-done.23
  494.3 7.1 %assemble.3 = f32[2,1312,1024]{2,1,0:T(8,128)} custom-call(s32[1]{0:T(128)} %bitcast.1.refs_0_, bf16[2,656,1024]{2,1,0:T(8,128)(2,1)} %copy-done.4, bf16[2,656,1024]{2,1,0:T(8,128)(2,1)} %collective-permute-done.32.refs_2_, bf16[3,512,256]{2,1,0:T(8,128)(2,1)} %copy-done.8, f32[2,1024]{1,0:T(2,128)} %add.236.refs_4_), custom_call_target="tpu_custom_call" | custom-call | tf_op jit(solution)/shard_map/assemble/pallas_call | solution.py:716
  504.7 2.2 collective-permute-done.31
  508.9 5.4 %assemble.4 = (f32[1312,1024]{1,0:T(8,128)}, f32[512,1024]{1,0:T(8,128)}) custom-call(s32[1]{0:T(128)} %bitcast.1.refs_0_, bf16[1,912,1024]{2,1,0:T(8,128)(2,1)} %copy-done.5, bf16[1,912,1024]{2,1,0:T(8,128)(2,1)} %collective-permute-done.35.refs_2_, bf16[3,1024,256]{2,1,0:T(8,128)(2,1)} %copy-done.2, f32[2,1024]{1,0:T(2,128)} %copy-done.30), custom_call_target="tpu_custom_call" | custom-call | tf_op jit(solution)/shard_map/assemble/pallas_call | solution.py:716
  516.7 4.8 assemble.5
  (171 shorter events, 63.8 us)
Async XLA Ops:
  1.7 6.5 %collective-permute-start = (bf16[64,1024]{1,0:T(8,128)(2,1)S(1)}, bf16[64,1024]{1,0:T(8,128)(2,1)S(1)}, u32[]{:S(2)}, u32[]{:S(2)}) collective-permute-start(bf16[64,1024]{1,0:T(8,128)(2,1)S(1)} %constant_dynamic-slice_fusion.4), channel_id=1, source_target_pairs={{0,1},{1,0},{2,3},{3,2},{4,5},{5,4},{6,7},{7,6},{8,9},{9,8},{10,11... | collective-permute-start | bytes 393224 | tf_op jit(solution)/shard_map/ppermute | solution.py:768
  11.4 47.0 %collective-permute-start.1 = (bf16[4,1024,256]{2,1,0:T(8,128)(2,1)}, bf16[4,1024,256]{2,1,0:T(8,128)(2,1)S(1)}, u32[]{:S(2)}, u32[]{:S(2)}) collective-permute-start(bf16[4,1024,256]{2,1,0:T(8,128)(2,1)} %pad_maximum_fusion), channel_id=1, source_target_pairs={{0,1},{1,0},{2,3},{3,2},{4,5},{5,4},{6,7},{7,6},{8,9},{9,8},{10,11... | collective-permute-start | bytes 6291464 | tf_op jit(solution)/shard_map/ppermute | solution.py:768
  58.4 7.3 %collective-permute-start.2 = (bf16[4,1024,256]{2,1,0:T(8,128)(2,1)S(1)}, bf16[4,1024,256]{2,1,0:T(8,128)(2,1)}, u32[]{:S(2)}, u32[]{:S(2)}) collective-permute-start(bf16[4,1024,256]{2,1,0:T(8,128)(2,1)S(1)} %collective-permute-done.1.refs_1_.refs_5_.refs_14_.refs_6_), channel_id=1, source_target_pairs={{0,2},{1,3},{2,0},{3,1},{4,6},{5,7},{6,4},{7,5},{8,10},{9,11},{10,... | collective-permute-start | bytes 6291464 | tf_op jit(solution)/shard_map/ppermute | solution.py:768
  62.5 37.0 %collective-permute-start.3 = (bf16[2,656,512]{2,1,0:T(8,128)(2,1)}, bf16[2,656,512]{2,1,0:T(8,128)(2,1)S(1)}, u32[]{:S(2)}, u32[]{:S(2)}) collective-permute-start(bf16[2,656,512]{2,1,0:T(8,128)(2,1)} %constant_dynamic-slice_fusion.2), channel_id=1, source_target_pairs={{0,1},{1,0},{2,3},{3,2},{4,5},{5,4},{6,7},{7,6},{8,9},{9,8},{10,11... | collective-permute-start | bytes 4030472 | tf_op jit(solution)/shard_map/ppermute | solution.py:768
  65.2 74.4 %collective-permute-start.7 = (bf16[656,1024]{1,0:T(8,128)(2,1)}, bf16[656,1024]{1,0:T(8,128)(2,1)S(1)}, u32[]{:S(2)}, u32[]{:S(2)}) collective-permute-start(bf16[656,1024]{1,0:T(8,128)(2,1)} %constant_dynamic-slice_fusion.1), channel_id=1, source_target_pairs={{0,1},{1,0},{2,3},{3,2},{4,5},{5,4},{6,7},{7,6},{8,9},{9,8},{10,11... | collective-permute-start | bytes 4030472 | tf_op jit(solution)/shard_map/ppermute | solution.py:768
  99.5 40.6 %collective-permute-start.4 = (bf16[2,656,512]{2,1,0:T(8,128)(2,1)S(1)}, bf16[2,656,512]{2,1,0:T(8,128)(2,1)S(1)}, u32[]{:S(2)}, u32[]{:S(2)}) collective-permute-start(bf16[2,656,512]{2,1,0:T(8,128)(2,1)S(1)} %collective-permute-done.3.refs_5_.refs_3_), channel_id=1, source_target_pairs={{0,4},{1,5},{2,6},{3,7},{4,0},{5,1},{6,2},{7,3},{8,12},{9,13},{10,... | collective-permute-start | bytes 4030472 | tf_op jit(solution)/shard_map/ppermute | solution.py:768
  100.9 42.0 %collective-permute-start.5 = (bf16[2,656,512]{2,1,0:T(8,128)(2,1)S(1)}, bf16[2,656,512]{2,1,0:T(8,128)(2,1)S(1)}, u32[]{:S(2)}, u32[]{:S(2)}) collective-permute-start(bf16[2,656,512]{2,1,0:T(8,128)(2,1)S(1)} %collective-permute-done.3.refs_5_.refs_3_), channel_id=1, source_target_pairs={{0,2},{1,3},{2,0},{3,1},{4,6},{5,7},{6,4},{7,5},{8,10},{9,11},{10,... | collective-permute-start | bytes 4030472 | tf_op jit(solution)/shard_map/ppermute | solution.py:768
  139.6 3.3 collective-permute-start.8
  140.1 4.6 collective-permute-start.6
  205.9 48.3 %collective-permute-start.9 = (bf16[1,656,1024]{2,1,0:T(8,128)(2,1)}, bf16[1,656,1024]{2,1,0:T(8,128)(2,1)S(1)}, u32[]{:S(2)}, u32[]{:S(2)}) collective-permute-start(bf16[1,656,1024]{2,1,0:T(8,128)(2,1)} %trade_outer.3.refs_2_), channel_id=1, source_target_pairs={{0,1},{1,0},{2,3},{3,2},{4,5},{5,4},{6,7},{7,6},{8,9},{9,8},{10,11... | collective-permute-start | bytes 4030472 | tf_op jit(solution)/shard_map/ppermute | solution.py:768
  218.1 52.9 %collective-permute-start.11 = (bf16[1,656,1024]{2,1,0:T(8,128)(2,1)}, bf16[1,656,1024]{2,1,0:T(8,128)(2,1)S(1)}, u32[]{:S(2)}, u32[]{:S(2)}) collective-permute-start(bf16[1,656,1024]{2,1,0:T(8,128)(2,1)} %trade_outer.4.refs_2_), channel_id=1, source_target_pairs={{0,1},{1,0},{2,3},{3,2},{4,5},{5,4},{6,7},{7,6},{8,9},{9,8},{10,11... | collective-permute-start | bytes 4030472 | tf_op jit(solution)/shard_map/ppermute | solution.py:768
  252.6 16.9 %collective-permute-start.10 = (bf16[64,1024]{1,0:T(8,128)(2,1)S(1)}, bf16[64,1024]{1,0:T(8,128)(2,1)S(1)}, u32[]{:S(2)}, u32[]{:S(2)}) collective-permute-start(bf16[64,1024]{1,0:T(8,128)(2,1)S(1)} %pad_maximum_fusion.1), channel_id=1, source_target_pairs={{0,1},{1,0},{2,3},{3,2},{4,5},{5,4},{6,7},{7,6},{8,9},{9,8},{10,11... | collective-permute-start | bytes 393224 | tf_op jit(solution)/shard_map/ppermute | solution.py:768
  275.2 32.3 %collective-permute-start.12 = (bf16[2,656,512]{2,1,0:T(8,128)(2,1)S(1)}, bf16[2,656,512]{2,1,0:T(8,128)(2,1)}, u32[]{:S(2)}, u32[]{:S(2)}) collective-permute-start(bf16[2,656,512]{2,1,0:T(8,128)(2,1)S(1)} %get-tuple-element.143), channel_id=1, source_target_pairs={{0,4},{1,5},{2,6},{3,7},{4,0},{5,1},{6,2},{7,3},{8,12},{9,13},{10,... | collective-permute-start | bytes 4030472 | tf_op jit(solution)/shard_map/ppermute | solution.py:768
  276.0 61.5 %collective-permute-start.14 = (bf16[1,912,1024]{2,1,0:T(8,128)(2,1)S(1)}, bf16[1,912,1024]{2,1,0:T(8,128)(2,1)}, u32[]{:S(2)}, u32[]{:S(2)}) collective-permute-start(bf16[1,912,1024]{2,1,0:T(8,128)(2,1)S(1)} %copy-done.16), channel_id=1, source_target_pairs={{0,1},{1,0},{2,3},{3,2},{4,5},{5,4},{6,7},{7,6},{8,9},{9,8},{10,11... | collective-permute-start | bytes 5603336 | tf_op jit(solution)/shard_map/ppermute | solution.py:768
  277.5 16.7 %copy-start.28 = (bf16[64,1024]{1,0:T(8,128)(2,1)S(1)}, bf16[64,1024]{1,0:T(8,128)(2,1)}, u32[]{:S(2)}) copy-start(bf16[64,1024]{1,0:T(8,128)(2,1)} %copy-done.27) | copy-start | bytes 393220
  295.7 11.8 %copy-start.3 = (bf16[2,656,512]{2,1,0:T(8,128)(2,1)S(1)}, bf16[2,656,512]{2,1,0:T(8,128)(2,1)}, u32[]{:S(2)}) copy-start(bf16[2,656,512]{2,1,0:T(8,128)(2,1)} %get-tuple-element.112.refs_10_) | copy-start | bytes 4030468
  310.1 26.0 %collective-permute-start.13 = (bf16[2,656,256]{2,1,0:T(8,128)(2,1)S(1)}, bf16[2,656,256]{2,1,0:T(8,128)(2,1)}, u32[]{:S(2)}, u32[]{:S(2)}) collective-permute-start(bf16[2,656,256]{2,1,0:T(8,128)(2,1)S(1)} %get-tuple-element.148), channel_id=1, source_target_pairs={{0,8},{1,9},{2,10},{3,11},{4,12},{5,13},{6,14},{7,15},{8,0},{9,1},... | collective-permute-start | bytes 2015240 | tf_op jit(solution)/shard_map/ppermute | solution.py:768
  311.7 9.2 %collective-permute-start.15 = (bf16[64,1024]{1,0:T(8,128)(2,1)S(1)}, bf16[64,1024]{1,0:T(8,128)(2,1)S(1)}, u32[]{:S(2)}, u32[]{:S(2)}) collective-permute-start(bf16[64,1024]{1,0:T(8,128)(2,1)S(1)} %pad_maximum_fusion.2), channel_id=1, source_target_pairs={{0,1},{1,0},{2,3},{3,2},{4,5},{5,4},{6,7},{7,6},{8,9},{9,8},{10,11... | collective-permute-start | bytes 393224 | tf_op jit(solution)/shard_map/ppermute | solution.py:768
  320.9 15.1 %copy-start.25 = (bf16[64,1024]{1,0:T(8,128)(2,1)}, bf16[64,1024]{1,0:T(8,128)(2,1)S(1)}, u32[]{:S(2)}) copy-start(bf16[64,1024]{1,0:T(8,128)(2,1)S(1)} %collective-permute-done.15) | copy-start | bytes 393220
  320.9 53.1 %collective-permute-start.18 = (bf16[3,1024,256]{2,1,0:T(8,128)(2,1)}, bf16[3,1024,256]{2,1,0:T(8,128)(2,1)}, u32[]{:S(2)}, u32[]{:S(2)}) collective-permute-start(bf16[3,1024,256]{2,1,0:T(8,128)(2,1)} %trade_attn.2), channel_id=1, source_target_pairs={{0,1},{1,0},{2,3},{3,2},{4,5},{5,4},{6,7},{7,6},{8,9},{9,8},{10,11... | collective-permute-start | bytes 4718600 | tf_op jit(solution)/shard_map/ppermute | solution.py:768
  321.9 14.1 %copy-start.11 = (bf16[2,656,256]{2,1,0:T(8,128)(2,1)S(1)}, bf16[2,656,256]{2,1,0:T(8,128)(2,1)}, u32[]{:S(2)}) copy-start(bf16[2,656,256]{2,1,0:T(8,128)(2,1)} %get-tuple-element.113.refs_4_) | copy-start | bytes 2015236
  340.0 17.5 %collective-permute-start.16 = (bf16[1,912,512]{2,1,0:T(8,128)(2,1)S(1)}, bf16[1,912,512]{2,1,0:T(8,128)(2,1)}, u32[]{:S(2)}, u32[]{:S(2)}) collective-permute-start(bf16[1,912,512]{2,1,0:T(8,128)(2,1)S(1)} %get-tuple-element.144), channel_id=1, source_target_pairs={{0,4},{1,5},{2,10},{3,11},{4,0},{5,1},{6,14},{7,15},{8,12},{9,13},... | collective-permute-start | bytes 2801672 | tf_op jit(solution)/shard_map/ppermute | solution.py:768
  341.6 32.2 %collective-permute-start.17 = (bf16[2,656,256]{2,1,0:T(8,128)(2,1)S(1)}, bf16[2,656,256]{2,1,0:T(8,128)(2,1)S(1)}, u32[]{:S(2)}, u32[]{:S(2)}) collective-permute-start(bf16[2,656,256]{2,1,0:T(8,128)(2,1)S(1)} %add.215), channel_id=1, source_target_pairs={{0,16},{1,17},{2,18},{3,19},{4,20},{5,21},{6,22},{7,23},{8,24},{9,... | collective-permute-start | bytes 2015240 | tf_op jit(solution)/shard_map/ppermute | solution.py:768
  357.5 16.6 %copy-start.10 = (bf16[3,1024,256]{2,1,0:T(8,128)(2,1)S(1)}, bf16[3,1024,256]{2,1,0:T(8,128)(2,1)}, u32[]{:S(2)}) copy-start(bf16[3,1024,256]{2,1,0:T(8,128)(2,1)} %trade_attn.3) | copy-start | bytes 4718596
  374.0 24.8 %collective-permute-start.20 = (bf16[2,656,256]{2,1,0:T(8,128)(2,1)S(1)}, bf16[2,656,256]{2,1,0:T(8,128)(2,1)}, u32[]{:S(2)}, u32[]{:S(2)}) collective-permute-start(bf16[2,656,256]{2,1,0:T(8,128)(2,1)S(1)} %add.223), channel_id=1, source_target_pairs={{0,8},{1,9},{2,10},{3,11},{4,12},{5,13},{6,14},{7,15},{8,0},{9,1},... | collective-permute-start | bytes 2015240 | tf_op jit(solution)/shard_map/ppermute | solution.py:768
  376.8 32.2 %collective-permute-start.22 = (bf16[3,512,256]{2,1,0:T(8,128)(2,1)S(1)}, bf16[3,512,256]{2,1,0:T(8,128)(2,1)}, u32[]{:S(2)}, u32[]{:S(2)}) collective-permute-start(bf16[3,512,256]{2,1,0:T(8,128)(2,1)S(1)} %get-tuple-element.146), channel_id=1, source_target_pairs={{0,4},{1,5},{2,10},{3,11},{4,0},{5,1},{6,14},{7,15},{8,12},{9,13},... | collective-permute-start | bytes 2359304 | tf_op jit(solution)/shard_map/ppermute | solution.py:768
  378.4 28.8 %collective-permute-start.21 = (bf16[1,912,256]{2,1,0:T(8,128)(2,1)}, bf16[1,912,256]{2,1,0:T(8,128)(2,1)}, u32[]{:S(2)}, u32[]{:S(2)}) collective-permute-start(bf16[1,912,256]{2,1,0:T(8,128)(2,1)} %get-tuple-element.150), channel_id=1, source_target_pairs={{0,8},{1,9},{2,18},{3,19},{4,12},{5,13},{6,22},{7,23},{8,0},{9,1},... | collective-permute-start | bytes 1400840 | tf_op jit(solution)/shard_map/ppermute | solution.py:768
  400.4 50.2 %collective-permute-start.29 = (bf16[2,656,512]{2,1,0:T(8,128)(2,1)S(1)}, bf16[2,656,512]{2,1,0:T(8,128)(2,1)}, u32[]{:S(2)}, u32[]{:S(2)}) collective-permute-start(bf16[2,656,512]{2,1,0:T(8,128)(2,1)S(1)} %maximum_select_fusion.3), channel_id=1, source_target_pairs={{0,4},{1,5},{2,6},{3,7},{4,0},{5,1},{6,2},{7,3},{8,12},{9,13},{10,... | collective-permute-start | bytes 4030472 | tf_op jit(solution)/shard_map/ppermute | solution.py:768
  408.3 22.5 %collective-permute-start.24 = (bf16[1,912,256]{2,1,0:T(8,128)(2,1)S(1)}, bf16[1,912,256]{2,1,0:T(8,128)(2,1)S(1)}, u32[]{:S(2)}, u32[]{:S(2)}) collective-permute-start(bf16[1,912,256]{2,1,0:T(8,128)(2,1)S(1)} %add.227), channel_id=1, source_target_pairs={{0,16},{1,17},{2,6},{3,7},{4,20},{5,21},{6,2},{7,3},{8,24},{9,25},... | collective-permute-start | bytes 1400840 | tf_op jit(solution)/shard_map/ppermute | solution.py:768
  410.3 20.7 %collective-permute-start.25 = (bf16[3,256,256]{2,1,0:T(8,128)(2,1)S(1)}, bf16[3,256,256]{2,1,0:T(8,128)(2,1)S(1)}, u32[]{:S(2)}, u32[]{:S(2)}) collective-permute-start(bf16[3,256,256]{2,1,0:T(8,128)(2,1)S(1)} %get-tuple-element.152), channel_id=1, source_target_pairs={{0,8},{1,9},{2,18},{3,19},{4,12},{5,13},{6,22},{7,23},{8,0},{9,1},... | collective-permute-start | bytes 1179656 | tf_op jit(solution)/shard_map/ppermute | solution.py:768
  431.0 12.5 %collective-permute-start.27 = (bf16[1,912,256]{2,1,0:T(8,128)(2,1)S(1)}, bf16[1,912,256]{2,1,0:T(8,128)(2,1)S(1)}, u32[]{:S(2)}, u32[]{:S(2)}) collective-permute-start(bf16[1,912,256]{2,1,0:T(8,128)(2,1)S(1)} %add.231), channel_id=1, source_target_pairs={{0,8},{1,9},{2,18},{3,19},{4,12},{5,13},{6,22},{7,23},{8,0},{9,1},... | collective-permute-start | bytes 1400840 | tf_op jit(solution)/shard_map/ppermute | solution.py:768
  431.2 19.4 %collective-permute-start.28 = (bf16[3,256,256]{2,1,0:T(8,128)(2,1)S(1)}, bf16[3,256,256]{2,1,0:T(8,128)(2,1)S(1)}, u32[]{:S(2)}, u32[]{:S(2)}) collective-permute-start(bf16[3,256,256]{2,1,0:T(8,128)(2,1)S(1)} %add.233), channel_id=1, source_target_pairs={{0,16},{1,17},{2,6},{3,7},{4,20},{5,21},{6,2},{7,3},{8,24},{9,25},... | collective-permute-start | bytes 1179656 | tf_op jit(solution)/shard_map/ppermute | solution.py:768
  454.4 21.4 %copy-start.4 = (bf16[2,656,1024]{2,1,0:T(8,128)(2,1)}, bf16[2,656,1024]{2,1,0:T(8,128)(2,1)S(1)}, u32[]{:S(2)}) copy-start(bf16[2,656,1024]{2,1,0:T(8,128)(2,1)S(1)} %maximum_select_fusion.refs_1_) | copy-start | bytes 8060932
  454.4 39.9 %collective-permute-start.32 = (bf16[2,656,1024]{2,1,0:T(8,128)(2,1)S(1)}, bf16[2,656,1024]{2,1,0:T(8,128)(2,1)}, u32[]{:S(2)}, u32[]{:S(2)}) collective-permute-start(bf16[2,656,1024]{2,1,0:T(8,128)(2,1)S(1)} %maximum_select_fusion.refs_1_), channel_id=1, source_target_pairs={{0,2},{1,3},{2,0},{3,1},{4,6},{5,7},{6,4},{7,5},{8,10},{9,11},{10,... | collective-permute-start | bytes 8060936 | tf_op jit(solution)/shard_map/ppermute | solution.py:768
  459.1 13.9 %collective-permute-start.30 = (bf16[1,912,512]{2,1,0:T(8,128)(2,1)}, bf16[1,912,512]{2,1,0:T(8,128)(2,1)}, u32[]{:S(2)}, u32[]{:S(2)}) collective-permute-start(bf16[1,912,512]{2,1,0:T(8,128)(2,1)} %maximum_select_fusion.4), channel_id=1, source_target_pairs={{0,4},{1,5},{2,10},{3,11},{4,0},{5,1},{6,14},{7,15},{8,12},{9,13},... | collective-permute-start | bytes 2801672 | tf_op jit(solution)/shard_map/ppermute | solution.py:768
  460.6 15.1 %collective-permute-start.33 = (bf16[3,256,256]{2,1,0:T(8,128)(2,1)S(1)}, bf16[3,256,256]{2,1,0:T(8,128)(2,1)S(1)}, u32[]{:S(2)}, u32[]{:S(2)}) collective-permute-start(bf16[3,256,256]{2,1,0:T(8,128)(2,1)S(1)} %add.235), channel_id=1, source_target_pairs={{0,8},{1,9},{2,18},{3,19},{4,12},{5,13},{6,22},{7,23},{8,0},{9,1},... | collective-permute-start | bytes 1179656 | tf_op jit(solution)/shard_map/ppermute | solution.py:768
  460.6 17.1 %copy-start.31 = (f32[1,1024]{1,0:T(1,128)S(1)}, f32[1,1024]{1,0:T(1,128)}, u32[]{:S(2)}) copy-start(f32[1,1024]{1,0:T(1,128)} %get-tuple-element.123) | copy-start | bytes 12292
  460.6 17.1 %copy-start.32 = (f32[1,1024]{1,0:T(1,128)S(1)}, f32[1,1024]{1,0:T(1,128)}, u32[]{:S(2)}) copy-start(f32[1,1024]{1,0:T(1,128)} %get-tuple-element.122) | copy-start | bytes 12292
  475.7 25.6 %copy-start.5 = (bf16[1,912,1024]{2,1,0:T(8,128)(2,1)}, bf16[1,912,1024]{2,1,0:T(8,128)(2,1)S(1)}, u32[]{:S(2)}) copy-start(bf16[1,912,1024]{2,1,0:T(8,128)(2,1)S(1)} %maximum_select_fusion.1.refs_1_) | copy-start | bytes 5603332
  476.1 18.2 %copy-start.8 = (bf16[3,512,256]{2,1,0:T(8,128)(2,1)}, bf16[3,512,256]{2,1,0:T(8,128)(2,1)S(1)}, u32[]{:S(2)}) copy-start(bf16[3,512,256]{2,1,0:T(8,128)(2,1)S(1)} %maximum_select_fusion.5.refs_3_) | copy-start | bytes 2359300
  476.1 25.3 %collective-permute-start.36 = (bf16[3,512,256]{2,1,0:T(8,128)(2,1)S(1)}, bf16[3,512,256]{2,1,0:T(8,128)(2,1)S(1)}, u32[]{:S(2)}, u32[]{:S(2)}) collective-permute-start(bf16[3,512,256]{2,1,0:T(8,128)(2,1)S(1)} %maximum_select_fusion.5.refs_3_), channel_id=1, source_target_pairs={{0,4},{1,5},{2,10},{3,11},{4,0},{5,1},{6,14},{7,15},{8,12},{9,13},... | collective-permute-start | bytes 2359304 | tf_op jit(solution)/shard_map/ppermute | solution.py:768
  477.7 3.7 collective-permute-start.19
  481.4 27.5 %collective-permute-start.35 = (bf16[1,912,1024]{2,1,0:T(8,128)(2,1)S(1)}, bf16[1,912,1024]{2,1,0:T(8,128)(2,1)}, u32[]{:S(2)}, u32[]{:S(2)}) collective-permute-start(bf16[1,912,1024]{2,1,0:T(8,128)(2,1)S(1)} %maximum_select_fusion.1.refs_1_), channel_id=1, source_target_pairs={{0,2},{1,3},{2,0},{3,1},{4,6},{5,7},{6,4},{7,5},{8,10},{9,11},{10,... | collective-permute-start | bytes 5603336 | tf_op jit(solution)/shard_map/ppermute | solution.py:768
  486.6 3.3 collective-permute-start.23
  489.9 3.7 collective-permute-start.26
  503.2 12.4 %collective-permute-start.37 = (bf16[3,1024,256]{2,1,0:T(8,128)(2,1)S(1)}, bf16[3,1024,256]{2,1,0:T(8,128)(2,1)S(1)}, u32[]{:S(2)}, u32[]{:S(2)}) collective-permute-start(bf16[3,1024,256]{2,1,0:T(8,128)(2,1)S(1)} %maximum_select_fusion.2.refs_3_.refs_1_), channel_id=1, source_target_pairs={{0,2},{1,3},{2,0},{3,1},{4,6},{5,7},{6,4},{7,5},{8,10},{9,11},{10,... | collective-permute-start | bytes 4718600 | tf_op jit(solution)/shard_map/ppermute | solution.py:768
  503.2 3.7 collective-permute-start.31
  507.0 7.3 %collective-permute-start.34 = (f32[2,1024]{1,0:T(2,128)S(1)}, f32[2,1024]{1,0:T(2,128)S(1)}, u32[]{:S(2)}, u32[]{:S(2)}) collective-permute-start(f32[2,1024]{1,0:T(2,128)S(1)} %add.237.refs_4_), channel_id=1, source_target_pairs={{0,16},{1,17},{2,18},{3,19},{4,20},{5,21},{6,22},{7,23},{8,24},{9,... | collective-permute-start | bytes 24584 | tf_op jit(solution)/shard_map/ppermute | solution.py:768
  (25 other events, 106.4 us)

commit v5 on v4

--- a/solution.py
+++ b/solution.py
@@ -322,11 +322,6 @@
     )
 
 
-def out_rows(part):
-    size = part.shape[2]
-    return jnp.concatenate([part[3, k * size:(k + 1) * size] for k in range(part.shape[1] // size)], 1)
-
-
 def row_tile(rows):
     return 256 if rows % 256 == 0 else 128
 
@@ -344,8 +339,8 @@
     attended_more, parts, (hidden, normed) = refs[:1], refs[1:-2], refs[-2:]
     total = tokens[...].astype(jnp.float32) + plain_dot(attended[...], weights[...])
     for side, part in enumerate(parts):
-        size = part.shape[2]
-        total = total + plain_dot(attended_more[0][:, side * size:(side + 1) * size], out_rows(part))
+        size = part.shape[0]
+        total = total + plain_dot(attended_more[0][:, side * size:(side + 1) * size], part[...])
     hidden[...] = total
     normed[...] = (norm_parts(total)[0] * gain[...]).astype(LOW)
 
@@ -359,7 +354,7 @@
         mix_kernel, "mix", (rows // tile,),
         [(tokens, (tile, model), row), (gain, (1, model), full), (attended, (tile, width), row), (weights, weights.shape, full)]
         + [(attended if more is None else more, (tile, width), row)]
-        + [(p, p.shape, lambda i: (0, 0, 0)) for p in parts],
+        + [whole(p) for p in parts],
         [(shaped((rows, model), jnp.float32), (tile, model), row), (shaped((rows, model)), (tile, model), row)],
         after,
     )
@@ -447,8 +442,8 @@
     low_ref[...] = low
     attn[...] = cols_dot(low, weights[...]).astype(LOW)
     for side, part in enumerate(parts):
-        size = part.shape[2]
-        refs[7][:, side * size:(side + 1) * size] = cols_dot(low, out_rows(part)).astype(LOW)
+        size = part.shape[0]
+        refs[7][:, side * size:(side + 1) * size] = cols_dot(low, part[...]).astype(LOW)
     add_gain(gain_ref, gain_part)
 
 
@@ -870,22 +865,23 @@
     place = jnp.concatenate([place, jnp.pad(flags, (0, place.shape[1] - flags.shape[0]))[None]], 0)
     width, units = w_out.shape[0], w_down.shape[0]
     size = width // 2
-    out_half = half(tie(w_out, border), core, 0)
-    stacked = jnp.concatenate([out_half[:, k * size:(k + 1) * size] for k in range(model // size)], 0)
-    piece = jnp.concatenate([half(tie(w_qkv, border), core, 2), stacked[None]], 0)
-    attn_direct = links.cross(piece)
+    attn_direct = links.cross(half(tie(w_qkv, border), core, 2))
 
     normed = norm_rows(tokens, border, border, gain_attn)
     quarter = lambda w, a, b: half(half(w, core, a), bits[1], b)
-    in_piece = quarter(tie(w_in, normed), 1, 2)
-    in_direct = links.cross(in_piece)
-    down_direct = links.cross(half(tie(w_down, in_piece), core, 0))
+    out_piece = half(tie(w_out, normed), core, 0)
+    out_direct = links.cross(out_piece)
     q0, k0, v0 = project(normed, w_qkv)
     attended0, logs0 = attend(place, q0, k0, v0)
     attn_parts = (attn_direct, links.flip(tie(attn_direct, attended0), 1))
     q1, k1, v1 = project_parts(normed, attn_parts, after=[attended0])
-    attended1, logs1 = attend(place, q1, k1, v1)
-    hidden, normed_mlp = mix(tokens, gain_mlp, attended0, w_out, attended1, attn_parts)
+    out_direct = tie(out_direct, v1)
+    in_piece = quarter(tie(w_in, out_direct), 1, 2)
+    in_direct = links.cross(in_piece)
+    down_direct = links.cross(half(tie(w_down, in_piece), core, 0))
+    out_parts = (out_direct, links.flip(out_direct, 1))
+    attended1, logs1 = attend(place, q1, k1, v1, after=[out_direct])
+    hidden, normed_mlp = mix(tokens, gain_mlp, attended0, w_out, attended1, out_parts)
     in_direct = tie(in_direct, hidden)
     in_relayed = links.flip(in_direct, 2)
     in_core = links.flip(in_direct, 1)
@@ -896,7 +892,7 @@
         in_direct, in_relayed, in_core, links.flip(in_relayed, 1), down_direct, links.flip(down_direct, 1),
     )
     gate1, lift1, output, hidden_grad, hidden_low, gain_mlp_grad, back0, back1 = mlp_last(
-        place, normed_mlp, cotangent, weights, hidden, gain_mlp, branch, pulled, w_out, attn_parts
+        place, normed_mlp, cotangent, weights, hidden, gain_mlp, branch, pulled, w_out, out_parts
     )
     inner = Summing(links, flags, 2, Summing.ROW_FIRST)
     inner_a, inner_b = (Summing(links, flags, 2, Summing.ROW_FIRST) for _ in range(2))
@@ -942,21 +938,21 @@
     down.both(inner.held)
     attn.scatter(down.held)
     gain_total = gain_total + tie(links.cross(gain_total), attn.held)
-    down.both_add(attn.held)
-    attn.both(down.held)
-    gain_total = gain_total + tie(links.flip(gain_total, 1), attn.held)
+    down.both_add(attn.held, gain_total)
+    gain_total = gain_total + tie(links.flip(gain_total, 1), down.held)
+    attn.both(down.held, gain_total)
     down.gather(attn.held)
     attn.both_add(down.held)
+    gain_total = gain_total + tie(links.flip(gain_total, 2), attn.held)
     grads_in = inner.last(attn.held)
-    grads_down = down.last(grads_in[0])
-    gain_total = gain_total + tie(links.flip(gain_total, 2), grads_down[0])
-    attn.gather(grads_down[0])
-    grad_w_in = assemble(*grads_in, 1, after=[attn.held, gain_total])
-    gain_total = gain_total + tie(links.flip(gain_total, 4), grad_w_in)
-    grads_attn = attn.last(grad_w_in)
-    grad_w_down, grad_w_out = assemble_down(*grads_down, units, after=[grads_attn[0], gain_total])
-    gain_total = gain_total + tie(links.flip(gain_total, 8), grad_w_down)
-    grad_w_qkv = assemble(*grads_attn, 2, after=[grad_w_down])
+    grads_down = down.last(grads_in[0], gain_total)
+    gain_total = gain_total + tie(links.flip(gain_total, 4), grads_down[0])
+    grad_w_in = assemble(*grads_in, 1, after=[grads_down[0]])
+    attn.gather(grad_w_in, gain_total)
+    gain_total = gain_total + tie(links.flip(gain_total, 8), attn.held)
+    grads_attn = attn.last(attn.held)
+    grad_w_down, grad_w_out = assemble_down(*grads_down, units, after=[grads_attn[0]])
+    grad_w_qkv = assemble(*grads_attn, 2, after=[grad_w_down, gain_total])
     return (
         output,
         input_grad,

time: 532 us -> 525 us (0.987)
  waiting for transfers between devices: 110 us -> 104 us
  starting transfers between devices: 50.9 us -> 56.7 us
    ppermute x38 -> x40, waiting for transfers between devices: 110 us -> 104 us  [send(): return lax.ppermute(value, AXES, pairs)]
    ppermute x38 -> x40, starting transfers between devices: 50.9 us -> 56.7 us  [send(): return lax.ppermute(value, AXES, pairs)]
  transfers between devices with their start and end apart: 38 -> 40, of which waited for: 16 -> 18; matrix products, arithmetic and copies ran while one was open for 7% -> 6% of each run, Pallas kernels for 47% -> 47%
where the time goes in v5:
time: 525 us; the launch traced here: 515 us
  Pallas kernels  305 us (58%)
  waiting for transfers between devices  104 us (20%)
  starting transfers between devices  56.7 us (11%)
  other arithmetic  33.1 us (6%)
  local copies, waits for them, and re-layouts  14.7 us (3%)
    pallas_call x18, Pallas kernels, run(): return call(*lead, *[a for a, _, _ in ins], *extra)  288 us
    ppermute x40, waiting for transfers between devices, send(): return lax.ppermute(value, AXES, pairs)  104 us
    ppermute x40, starting transfers between devices, send(): return lax.ppermute(value, AXES, pairs)  56.7 us
    pallas_call x3, Pallas kernels, assemble_call(): pl.pallas_call(lambda *refs: body(*refs[:3], *refs[3 + len(after):]), gri...  17.4 us
    add x6, other arithmetic, split(): part = lambda k: half(a, k, self.axis) + half(b, k, self.axis)  13.6 us
    select_n x6, other arithmetic, order(): jnp.where(bit == 0, jnp.concatenate([first, second], axis), jnp.concatena...  11.2 us
  transfers between devices with their start and end apart: 40, of which 18 were waited for; matrix products, arithmetic and copies ran while one was open for 6% of the time, Pallas kernels for 47%

profile of v5, /device:TPU:0, one launch (start us, length us, event | category | flops | bytes accessed | tf_op | source)
XLA Modules:
  0.0 515.1 jit_solution(4307304225684755475)
XLA Ops:
  1.6 3.0 collective-permute-start
  4.6 3.5 collective-permute-done.refs_1_.refs_2_
  11.9 5.5 %norm_rows.1.refs_0_ = bf16[1664,1024]{1,0:T(8,128)(2,1)} custom-call(bf16[1536,1024]{1,0:T(8,128)(2,1)} %refs_0_.5, bf16[64,1024]{1,0:T(8,128)(2,1)} %copy-done.25, bf16[64,1024]{1,0:T(8,128)(2,1)} %copy-done.25, f32[1,1024]{1,0:T(1,128)} %bitcast.31), custom_call_target="tpu_custom_call" | custom-call | flops 600 | bytes 1000 | tf_op jit(solution)/shard_map/norm_rows/pallas_call | solution.py:81
  18.1 8.9 %project.1 = (bf16[1664,512]{1,0:T(8,128)(2,1)}, bf16[1664,512]{1,0:T(8,128)(2,1)}, bf16[1664,512]{1,0:T(8,128)(2,1)}) custom-call(bf16[1664,1024]{1,0:T(8,128)(2,1)} %norm_rows.1.refs_0_, bf16[3,1024,512]{2,1,0:T(8,128)(2,1)} %bitcast.23), custom_call_target="tpu_custom_call" | custom-call | flops 900 | bytes 1000 | tf_op jit(solution)/shard_map/project/pallas_call | solution.py:81
  27.0 14.0 %attend.2 = (bf16[1536,512]{1,0:T(8,128)(2,1)}, f32[12,4,256]{2,1,0:T(4,128)}) custom-call(s32[3,12]{1,0:T(4,128)} %pad_add_fusion.refs_0_, bf16[1664,512]{1,0:T(8,128)(2,1)} %get-tuple-element.76.refs_1_, bf16[1664,512]{1,0:T(8,128)(2,1)} %get-tuple-element.77.refs_2_.refs_3_.refs_4_, bf16[1664,512]{1,0:T(8,128)(2,1)} %get-tuple-element.77.refs_2_.refs_3_.refs_4_, ...), custom_call_target="tpu_custom_call" | custom-call | flops 2000 | bytes 1000 | tf_op jit(solution)/shard_map/attend/pallas_call | solution.py:81
  41.0 4.3 collective-permute-done.1.refs_1_.refs_6_
  48.8 8.9 %project_parts.1 = (bf16[1664,512]{1,0:T(8,128)(2,1)}, bf16[1664,512]{1,0:T(8,128)(2,1)}, bf16[1664,512]{1,0:T(8,128)(2,1)}) custom-call(bf16[1664,1024]{1,0:T(8,128)(2,1)} %norm_rows.1.refs_0_, bf16[3,1024,256]{2,1,0:T(8,128)(2,1)} %copy-done.9, bf16[3,1024,256]{2,1,0:T(8,128)(2,1)} %collective-permute-done.2.refs_2_.refs_7_, ...), custom_call_target="tpu_custom_call" | custom-call | flops 900 | bytes 1000 | tf_op jit(solution)/shard_map/project_parts/pallas_call | solution.py:81
  59.7 2.4 constant_dynamic-slice_fusion.1
  64.4 13.8 %attend.3 = (bf16[1536,512]{1,0:T(8,128)(2,1)}, f32[12,4,256]{2,1,0:T(4,128)}) custom-call(s32[3,12]{1,0:T(4,128)} %pad_add_fusion.refs_0_, bf16[1664,512]{1,0:T(8,128)(2,1)} %get-tuple-element.82.refs_1_, bf16[1664,512]{1,0:T(8,128)(2,1)} %get-tuple-element.83.refs_2_.refs_3_.refs_4_, bf16[1664,512]{1,0:T(8,128)(2,1)} %get-tuple-element.83.refs_2_.refs_3_.refs_4_, ...), custom_call_target="tpu_custom_call" | custom-call | flops 2000 | bytes 1000 | tf_op jit(solution)/shard_map/attend/pallas_call | solution.py:81
  79.1 9.9 %mix.1 = (f32[1536,1024]{1,0:T(8,128)}, bf16[1536,1024]{1,0:T(8,128)(2,1)}) custom-call(bf16[1536,1024]{1,0:T(8,128)(2,1)} %refs_0_.5, f32[1,1024]{1,0:T(1,128)} %bitcast.29, bf16[1536,512]{1,0:T(8,128)(2,1)} %get-tuple-element.79.refs_3_.refs_2_.refs_1_, bf16[512,1024]{1,0:T(8,128)(2,1)} %refs_13_.1, bf16[1536,512]{1,0:T(8,128)(2,1)} %get-tuple-element.87.refs_4_.refs_1_, ...), custom_call_target="tpu_custom_call" | custom-call | flops 1100 | bytes 1000 | tf_op jit(solution)/shard_map/mix/pallas_call | solution.py:81
  88.9 5.7 %collective-permute-done.5.refs_5_.refs_3_ = bf16[2,656,512]{2,1,0:T(8,128)(2,1)S(1)} collective-permute-done((bf16[2,656,512]{2,1,0:T(8,128)(2,1)S(1)}, bf16[2,656,512]{2,1,0:T(8,128)(2,1)S(1)}, u32[]{:S(2)}, u32[]{:S(2)}) %collective-permute-start.5) | collective-permute-done | bytes 1343520 | tf_op jit(solution)/shard_map/ppermute | solution.py:763
  95.9 38.6 %mlp_first.1 = (bf16[1,1536,1312]{2,1,0:T(8,128)(2,1)}, bf16[2,1536,1312]{2,1,0:T(8,128)(2,1)}, bf16[1536,1024]{1,0:T(8,128)(2,1)}, f32[1536,1024]{1,0:T(8,128)}, f32[1536,1024]{1,0:T(8,128)}) custom-call(s32[3,12]{1,0:T(4,128)} %pad_add_fusion.refs_0_, bf16[1536,1024]{1,0:T(8,128)(2,1)} %get-tuple-element.88.refs_1_, bf16[1536,1024]{1,0:T(8,128)(2,1)} %refs_2_.3, ...), custom_call_target="tpu_custom_call" | custom-call | flops 3900 | bytes 1000 | tf_op jit(solution)/shard_map/mlp_first/pallas_call | solution.py:81
  135.3 2.6 collective-permute-done.10.refs_8_
  140.9 47.9 %mlp_last.1 = (bf16[1,1536,1312]{2,1,0:T(8,128)(2,1)}, bf16[2,1536,1312]{2,1,0:T(8,128)(2,1)}, bf16[1536,1024]{1,0:T(8,128)(2,1)}, f32[1536,1024]{1,0:T(8,128)},...) custom-call(s32[3,12]{1,0:T(4,128)} %pad_add_fusion.refs_0_, ...), custom_call_target="tpu_custom_call" | custom-call | flops 4900 | bytes 1000 | tf_op jit(solution)/shard_map/mlp_last/pallas_call | solution.py:81
  188.8 10.7 %trade_outer.3.refs_2_ = bf16[1,656,1024]{2,1,0:T(8,128)(2,1)} custom-call(bf16[2,1536,1312]{2,1,0:T(8,128)(2,1)} %get-tuple-element.102.refs_0_, bf16[1536,1024]{1,0:T(8,128)(2,1)} %get-tuple-element.88.refs_1_, bf16[1536,512]{1,0:T(8,128)(2,1)} %get-tuple-element.103.refs_2_.refs_8_), custom_call_target="tpu_custom_call" | custom-call | flops 900 | bytes 1000 | tf_op jit(solution)/shard_map/trade_outer/pallas_call | solution.py:81
  201.1 10.6 %trade_outer.4.refs_2_ = bf16[1,656,1024]{2,1,0:T(8,128)(2,1)} custom-call(bf16[2,1536,1312]{2,1,0:T(8,128)(2,1)} %get-tuple-element.102.refs_0_, bf16[1536,1024]{1,0:T(8,128)(2,1)} %get-tuple-element.88.refs_1_, bf16[1,656,1024]{2,1,0:T(8,128)(2,1)} %trade_outer.3.refs_2_), custom_call_target="tpu_custom_call" | custom-call | flops 900 | bytes 1000 | tf_op jit(solution)/shard_map/trade_outer/pallas_call | solution.py:81
  212.3 16.3 %trade_outer.5.refs_10_ = bf16[2,656,1024]{2,1,0:T(8,128)(2,1)} custom-call(bf16[2,1536,1312]{2,1,0:T(8,128)(2,1)} %get-tuple-element.101.refs_0_, bf16[1536,1024]{1,0:T(8,128)(2,1)} %get-tuple-element.88.refs_1_, bf16[1,656,1024]{2,1,0:T(8,128)(2,1)} %trade_outer.4.refs_2_), custom_call_target="tpu_custom_call" | custom-call | flops 900 | bytes 1000 | tf_op jit(solution)/shard_map/trade_outer/pallas_call | solution.py:81
  228.6 16.6 %attend_back.2 = (bf16[1536,1536]{1,0:T(8,128)(2,1)}, bf16[2,64,1024]{2,1,0:T(8,128)(2,1)}) custom-call(s32[3,12]{1,0:T(4,128)} %pad_add_fusion.refs_0_, bf16[1664,512]{1,0:T(8,128)(2,1)} %get-tuple-element.76.refs_1_, bf16[1664,512]{1,0:T(8,128)(2,1)} %get-tuple-element.77.refs_2_.refs_3_.refs_4_, ...), custom_call_target="tpu_custom_call" | custom-call | flops 2500 | bytes 1000 | tf_op jit(solution)/shard_map/attend_back/pallas_call | solution.py:81
  248.9 13.7 %trade_down.2 = bf16[1,912,1024]{2,1,0:T(8,128)(2,1)} custom-call(bf16[1,1536,1312]{2,1,0:T(8,128)(2,1)} %get-tuple-element.108.refs_0_, bf16[1536,512]{1,0:T(8,128)(2,1)} %get-tuple-element.87.refs_4_.refs_1_, bf16[1536,1024]{1,0:T(8,128)(2,1)} %get-tuple-element.106.refs_2_, bf16[1536,1024]{1,0:T(8,128)(2,1)} %get-tuple-element.107.refs_3_, ...), custom_call_target="tpu_custom_call" | custom-call | flops 1200 | bytes 1000 | tf_op jit(solution)/shard_map/trade_down/pallas_call | solution.py:81
  266.4 2.5 dynamic-slice_add_fusion.1
  271.1 16.7 %attend_back.3 = (bf16[1536,1536]{1,0:T(8,128)(2,1)}, bf16[2,64,1024]{2,1,0:T(8,128)(2,1)}) custom-call(s32[3,12]{1,0:T(4,128)} %pad_add_fusion.refs_0_, bf16[1664,512]{1,0:T(8,128)(2,1)} %get-tuple-element.82.refs_1_, bf16[1664,512]{1,0:T(8,128)(2,1)} %get-tuple-element.83.refs_2_.refs_3_.refs_4_, ...), custom_call_target="tpu_custom_call" | custom-call | flops 2500 | bytes 1000 | tf_op jit(solution)/shard_map/attend_back/pallas_call | solution.py:81
  289.4 11.8 %trade_attn.2 = bf16[3,1024,256]{2,1,0:T(8,128)(2,1)} custom-call(bf16[1664,1024]{1,0:T(8,128)(2,1)} %norm_rows.1.refs_0_, bf16[1536,1536]{1,0:T(8,128)(2,1)} %add_dynamic-update-slice_fusion.1.refs_1_.refs_5_), custom_call_target="tpu_custom_call" | custom-call | flops 1000 | bytes 1000 | tf_op jit(solution)/shard_map/trade_attn/pallas_call | solution.py:81
  301.2 2.5 dynamic-slice_add_fusion.6
  306.0 8.6 %collective-permute-done.17 = bf16[64,1024]{1,0:T(8,128)(2,1)S(1)} collective-permute-done((bf16[64,1024]{1,0:T(8,128)(2,1)S(1)}, bf16[64,1024]{1,0:T(8,128)(2,1)S(1)}, u32[]{:S(2)}, u32[]{:S(2)}) %collective-permute-start.17) | collective-permute-done | bytes 131104 | tf_op jit(solution)/shard_map/ppermute | solution.py:763
  315.6 14.1 %trade_down.3 = bf16[1,912,1024]{2,1,0:T(8,128)(2,1)} custom-call(bf16[1,1536,1312]{2,1,0:T(8,128)(2,1)} %get-tuple-element.105.refs_0_, bf16[1536,512]{1,0:T(8,128)(2,1)} %get-tuple-element.79.refs_3_.refs_2_.refs_1_, bf16[1536,1024]{1,0:T(8,128)(2,1)} %get-tuple-element.106.refs_2_, bf16[1536,1024]{1,0:T(8,128)(2,1)} %get-tuple-element.107.refs_3_, ...), custom_call_target="tpu_custom_call" | custom-call | flops 1200 | bytes 1000 | tf_op jit(solution)/shard_map/trade_down/pallas_call | solution.py:81
  335.2 2.6 collective-permute-start.19
  339.4 11.7 %trade_attn.3 = bf16[3,1024,256]{2,1,0:T(8,128)(2,1)} custom-call(bf16[1664,1024]{1,0:T(8,128)(2,1)} %norm_rows.1.refs_0_, bf16[1536,1536]{1,0:T(8,128)(2,1)} %add_dynamic-update-slice_fusion.refs_1_.refs_3_), custom_call_target="tpu_custom_call" | custom-call | flops 1000 | bytes 1000 | tf_op jit(solution)/shard_map/trade_attn/pallas_call | solution.py:81
  351.1 2.3 dynamic-slice_add_fusion.8
  353.4 14.0 %collective-permute-done.19 = bf16[2,656,256]{2,1,0:T(8,128)(2,1)S(1)} collective-permute-done((bf16[2,656,256]{2,1,0:T(8,128)(2,1)S(1)}, bf16[2,656,256]{2,1,0:T(8,128)(2,1)S(1)}, u32[]{:S(2)}, u32[]{:S(2)}) %collective-permute-start.19) | collective-permute-done | bytes 671776 | tf_op jit(solution)/shard_map/ppermute | solution.py:763
  367.7 2.7 dynamic-slice_add_fusion.4
  374.0 18.4 %pull.1 = (f32[1536,1024]{1,0:T(8,128)}, f32[1,1024]{1,0:T(1,128)}) custom-call(bf16[1536,1024]{1,0:T(8,128)(2,1)} %refs_0_.5, f32[1536,1024]{1,0:T(8,128)} %get-tuple-element.98.refs_1_, f32[1,1024]{1,0:T(1,128)} %bitcast.32, bf16[1536,1536]{1,0:T(8,128)(2,1)} %add_dynamic-update-slice_fusion.refs_1_.refs_3_, bf16[3,1024,512]{2,1,0:T(8,128)(2,1)} %bitcast.24, ...), custom_call_target="tpu_custom_call" | custom-call | flops 1800 | bytes 1000 | tf_op jit(solution)/shard_map/pull/pallas_call | solution.py:81
  394.6 6.2 %collective-permute-done.23 = bf16[1,912,256]{2,1,0:T(8,128)(2,1)} collective-permute-done((bf16[1,912,256]{2,1,0:T(8,128)(2,1)}, bf16[1,912,256]{2,1,0:T(8,128)(2,1)}, u32[]{:S(2)}, u32[]{:S(2)}) %collective-permute-start.23) | collective-permute-done | bytes 466976 | tf_op jit(solution)/shard_map/ppermute | solution.py:763
  406.3 2.5 collective-permute-start.28
  409.6 14.9 %collective-permute-done.26 = bf16[1,912,256]{2,1,0:T(8,128)(2,1)S(1)} collective-permute-done((bf16[1,912,256]{2,1,0:T(8,128)(2,1)S(1)}, bf16[1,912,256]{2,1,0:T(8,128)(2,1)S(1)}, u32[]{:S(2)}, u32[]{:S(2)}) %collective-permute-start.26) | collective-permute-done | bytes 466976 | tf_op jit(solution)/shard_map/ppermute | solution.py:763
  424.8 2.5 collective-permute-start.30
  427.4 9.7 %collective-permute-done.29 = bf16[1,912,256]{2,1,0:T(8,128)(2,1)S(1)} collective-permute-done((bf16[1,912,256]{2,1,0:T(8,128)(2,1)S(1)}, bf16[1,912,256]{2,1,0:T(8,128)(2,1)S(1)}, u32[]{:S(2)}, u32[]{:S(2)}) %collective-permute-start.29) | collective-permute-done | bytes 466976 | tf_op jit(solution)/shard_map/ppermute | solution.py:763
  438.3 6.0 %collective-permute-done.30 = bf16[3,256,256]{2,1,0:T(8,128)(2,1)S(1)} collective-permute-done((bf16[3,256,256]{2,1,0:T(8,128)(2,1)S(1)}, bf16[3,256,256]{2,1,0:T(8,128)(2,1)S(1)}, u32[]{:S(2)}, u32[]{:S(2)}) %collective-permute-start.30) | collective-permute-done | bytes 393248 | tf_op jit(solution)/shard_map/ppermute | solution.py:763
  444.3 3.6 maximum_select_fusion.refs_1_
  448.0 4.7 collective-permute-start.35
  454.7 11.9 %collective-permute-done.27 = f32[2,1024]{1,0:T(2,128)S(1)} collective-permute-done((f32[2,1024]{1,0:T(2,128)S(1)}, f32[2,1024]{1,0:T(2,128)S(1)}, u32[]{:S(2)}, u32[]{:S(2)}) %collective-permute-start.27) | collective-permute-done | bytes 8224 | tf_op jit(solution)/shard_map/ppermute | solution.py:763
  466.7 4.0 maximum_select_fusion.1.refs_3_.refs_1_
  470.8 7.2 %assemble.3 = f32[2,1312,1024]{2,1,0:T(8,128)} custom-call(s32[1]{0:T(128)} %bitcast.1.refs_0_, bf16[2,656,1024]{2,1,0:T(8,128)(2,1)} %copy-done.4, bf16[2,656,1024]{2,1,0:T(8,128)(2,1)} %collective-permute-done.35.refs_2_, bf16[1,912,1024]{2,1,0:T(8,128)(2,1)} %maximum_select_fusion.1.refs_3_.refs_1_), custom_call_target="tpu_custom_call" | custom-call | tf_op jit(solution)/shard_map/assemble/pallas_call | solution.py:711
  479.9 5.9 %collective-permute-start.39 = (bf16[1,912,1024]{2,1,0:T(8,128)(2,1)S(1)}, bf16[1,912,1024]{2,1,0:T(8,128)(2,1)S(1)}, u32[]{:S(2)}, u32[]{:S(2)}) collective-permute-start(bf16[1,912,1024]{2,1,0:T(8,128)(2,1)S(1)} %copy-done.1), channel_id=1, source_target_pairs={{0,2},{1,3},{2,0},{3,1},{4,6},{5,7},{6,4},{7,5},{8,10},{9,11},{10,... | collective-permute-start | bytes 5603336 | tf_op jit(solution)/shard_map/ppermute | solution.py:763
  485.8 4.6 collective-permute-done.37
  490.8 6.2 %collective-permute-start.38 = (bf16[3,1024,256]{2,1,0:T(8,128)(2,1)S(1)}, bf16[3,1024,256]{2,1,0:T(8,128)(2,1)S(1)}, u32[]{:S(2)}, u32[]{:S(2)}) collective-permute-start(bf16[3,1024,256]{2,1,0:T(8,128)(2,1)S(1)} %maximum_select_fusion.2.refs_3_.refs_1_), channel_id=1, source_target_pairs={{0,2},{1,3},{2,0},{3,1},{4,6},{5,7},{6,4},{7,5},{8,10},{9,11},{10,... | collective-permute-start | bytes 4718600 | tf_op jit(solution)/shard_map/ppermute | solution.py:763
  497.8 3.8 collective-permute-done.34
  503.4 5.3 %assemble.4 = (f32[1312,1024]{1,0:T(8,128)}, f32[512,1024]{1,0:T(8,128)}) custom-call(s32[1]{0:T(128)} %bitcast.1.refs_0_, bf16[1,912,1024]{2,1,0:T(8,128)(2,1)} %maximum_select_fusion.1.refs_3_.refs_1_, bf16[1,912,1024]{2,1,0:T(8,128)(2,1)} %copy-done.18, bf16[3,1024,256]{2,1,0:T(8,128)(2,1)} %copy-done.2), custom_call_target="tpu_custom_call" | custom-call | tf_op jit(solution)/shard_map/assemble/pallas_call | solution.py:711
  509.9 4.8 assemble.5
  (175 shorter events, 64.7 us)
Async XLA Ops:
  1.6 6.5 %collective-permute-start = (bf16[64,1024]{1,0:T(8,128)(2,1)S(1)}, bf16[64,1024]{1,0:T(8,128)(2,1)S(1)}, u32[]{:S(2)}, u32[]{:S(2)}) collective-permute-start(bf16[64,1024]{1,0:T(8,128)(2,1)S(1)} %constant_dynamic-slice_fusion.4), channel_id=1, source_target_pairs={{0,1},{1,0},{2,3},{3,2},{4,5},{5,4},{6,7},{7,6},{8,9},{9,8},{10,11... | collective-permute-start | bytes 393224 | tf_op jit(solution)/shard_map/ppermute | solution.py:763
  9.6 35.6 %collective-permute-start.1 = (bf16[3,1024,256]{2,1,0:T(8,128)(2,1)S(1)}, bf16[3,1024,256]{2,1,0:T(8,128)(2,1)S(1)}, u32[]{:S(2)}, u32[]{:S(2)}) collective-permute-start(bf16[3,1024,256]{2,1,0:T(8,128)(2,1)S(1)} %constant_dynamic-slice_fusion.3), channel_id=1, source_target_pairs={{0,1},{1,0},{2,3},{3,2},{4,5},{5,4},{6,7},{7,6},{8,9},{9,8},{10,11... | collective-permute-start | bytes 4718600 | tf_op jit(solution)/shard_map/ppermute | solution.py:763
  27.0 18.3 %copy-start.7 = (bf16[512,1024]{1,0:T(8,128)(2,1)S(1)}, bf16[512,1024]{1,0:T(8,128)(2,1)}, u32[]{:S(2)}) copy-start(bf16[512,1024]{1,0:T(8,128)(2,1)} %refs_13_.1) | copy-start | bytes 3145732
  45.3 3.5 collective-permute-start.2
  45.4 14.4 %collective-permute-start.3 = (bf16[256,1024]{1,0:T(8,128)(2,1)S(1)}, bf16[256,1024]{1,0:T(8,128)(2,1)S(1)}, u32[]{:S(2)}, u32[]{:S(2)}) collective-permute-start(bf16[256,1024]{1,0:T(8,128)(2,1)S(1)} %constant_dynamic-slice_fusion.2), channel_id=1, source_target_pairs={{0,1},{1,0},{2,3},{3,2},{4,5},{5,4},{6,7},{7,6},{8,9},{9,8},{10,11... | collective-permute-start | bytes 1572872 | tf_op jit(solution)/shard_map/ppermute | solution.py:763
  62.2 32.5 %collective-permute-start.5 = (bf16[2,656,512]{2,1,0:T(8,128)(2,1)S(1)}, bf16[2,656,512]{2,1,0:T(8,128)(2,1)S(1)}, u32[]{:S(2)}, u32[]{:S(2)}) collective-permute-start(bf16[2,656,512]{2,1,0:T(8,128)(2,1)S(1)} %constant_dynamic-slice_fusion.1), channel_id=1, source_target_pairs={{0,1},{1,0},{2,3},{3,2},{4,5},{5,4},{6,7},{7,6},{8,9},{9,8},{10,11... | collective-permute-start | bytes 4030472 | tf_op jit(solution)/shard_map/ppermute | solution.py:763
  63.6 14.6 %collective-permute-start.4 = (bf16[256,1024]{1,0:T(8,128)(2,1)S(1)}, bf16[256,1024]{1,0:T(8,128)(2,1)S(1)}, u32[]{:S(2)}, u32[]{:S(2)}) collective-permute-start(bf16[256,1024]{1,0:T(8,128)(2,1)S(1)} %collective-permute-done.3.refs_8_.refs_5_.refs_14_), channel_id=1, source_target_pairs={{0,2},{1,3},{2,0},{3,1},{4,6},{5,7},{6,4},{7,5},{8,10},{9,11},{10,... | collective-permute-start | bytes 1572872 | tf_op jit(solution)/shard_map/ppermute | solution.py:763
  63.8 70.8 %collective-permute-start.9 = (bf16[656,1024]{1,0:T(8,128)(2,1)S(1)}, bf16[656,1024]{1,0:T(8,128)(2,1)S(1)}, u32[]{:S(2)}, u32[]{:S(2)}) collective-permute-start(bf16[656,1024]{1,0:T(8,128)(2,1)S(1)} %constant_dynamic-slice_fusion), channel_id=1, source_target_pairs={{0,1},{1,0},{2,3},{3,2},{4,5},{5,4},{6,7},{7,6},{8,9},{9,8},{10,11... | collective-permute-start | bytes 4030472 | tf_op jit(solution)/shard_map/ppermute | solution.py:763
  94.6 40.6 %collective-permute-start.6 = (bf16[2,656,512]{2,1,0:T(8,128)(2,1)S(1)}, bf16[2,656,512]{2,1,0:T(8,128)(2,1)S(1)}, u32[]{:S(2)}, u32[]{:S(2)}) collective-permute-start(bf16[2,656,512]{2,1,0:T(8,128)(2,1)S(1)} %collective-permute-done.5.refs_5_.refs_3_), channel_id=1, source_target_pairs={{0,4},{1,5},{2,6},{3,7},{4,0},{5,1},{6,2},{7,3},{8,12},{9,13},{10,... | collective-permute-start | bytes 4030472 | tf_op jit(solution)/shard_map/ppermute | solution.py:763
  95.9 41.9 %collective-permute-start.7 = (bf16[2,656,512]{2,1,0:T(8,128)(2,1)S(1)}, bf16[2,656,512]{2,1,0:T(8,128)(2,1)S(1)}, u32[]{:S(2)}, u32[]{:S(2)}) collective-permute-start(bf16[2,656,512]{2,1,0:T(8,128)(2,1)S(1)} %collective-permute-done.5.refs_5_.refs_3_), channel_id=1, source_target_pairs={{0,2},{1,3},{2,0},{3,1},{4,6},{5,7},{6,4},{7,5},{8,10},{9,11},{10,... | collective-permute-start | bytes 4030472 | tf_op jit(solution)/shard_map/ppermute | solution.py:763
  134.6 3.3 collective-permute-start.10
  135.2 4.6 collective-permute-start.8
  199.5 48.3 %collective-permute-start.11 = (bf16[1,656,1024]{2,1,0:T(8,128)(2,1)}, bf16[1,656,1024]{2,1,0:T(8,128)(2,1)S(1)}, u32[]{:S(2)}, u32[]{:S(2)}) collective-permute-start(bf16[1,656,1024]{2,1,0:T(8,128)(2,1)} %trade_outer.3.refs_2_), channel_id=1, source_target_pairs={{0,1},{1,0},{2,3},{3,2},{4,5},{5,4},{6,7},{7,6},{8,9},{9,8},{10,11... | collective-permute-start | bytes 4030472 | tf_op jit(solution)/shard_map/ppermute | solution.py:763
  211.7 52.9 %collective-permute-start.13 = (bf16[1,656,1024]{2,1,0:T(8,128)(2,1)}, bf16[1,656,1024]{2,1,0:T(8,128)(2,1)S(1)}, u32[]{:S(2)}, u32[]{:S(2)}) collective-permute-start(bf16[1,656,1024]{2,1,0:T(8,128)(2,1)} %trade_outer.4.refs_2_), channel_id=1, source_target_pairs={{0,1},{1,0},{2,3},{3,2},{4,5},{5,4},{6,7},{7,6},{8,9},{9,8},{10,11... | collective-permute-start | bytes 4030472 | tf_op jit(solution)/shard_map/ppermute | solution.py:763
  246.3 16.9 %collective-permute-start.12 = (bf16[64,1024]{1,0:T(8,128)(2,1)S(1)}, bf16[64,1024]{1,0:T(8,128)(2,1)S(1)}, u32[]{:S(2)}, u32[]{:S(2)}) collective-permute-start(bf16[64,1024]{1,0:T(8,128)(2,1)S(1)} %pad_maximum_fusion), channel_id=1, source_target_pairs={{0,1},{1,0},{2,3},{3,2},{4,5},{5,4},{6,7},{7,6},{8,9},{9,8},{10,11... | collective-permute-start | bytes 393224 | tf_op jit(solution)/shard_map/ppermute | solution.py:763
  268.9 32.3 %collective-permute-start.14 = (bf16[2,656,512]{2,1,0:T(8,128)(2,1)S(1)}, bf16[2,656,512]{2,1,0:T(8,128)(2,1)}, u32[]{:S(2)}, u32[]{:S(2)}) collective-permute-start(bf16[2,656,512]{2,1,0:T(8,128)(2,1)S(1)} %get-tuple-element.145), channel_id=1, source_target_pairs={{0,4},{1,5},{2,6},{3,7},{4,0},{5,1},{6,2},{7,3},{8,12},{9,13},{10,... | collective-permute-start | bytes 4030472 | tf_op jit(solution)/shard_map/ppermute | solution.py:763
  269.6 61.5 %collective-permute-start.16 = (bf16[1,912,1024]{2,1,0:T(8,128)(2,1)S(1)}, bf16[1,912,1024]{2,1,0:T(8,128)(2,1)}, u32[]{:S(2)}, u32[]{:S(2)}) collective-permute-start(bf16[1,912,1024]{2,1,0:T(8,128)(2,1)S(1)} %copy-done.17), channel_id=1, source_target_pairs={{0,1},{1,0},{2,3},{3,2},{4,5},{5,4},{6,7},{7,6},{8,9},{9,8},{10,11... | collective-permute-start | bytes 5603336 | tf_op jit(solution)/shard_map/ppermute | solution.py:763
  271.1 16.7 %copy-start.30 = (bf16[64,1024]{1,0:T(8,128)(2,1)S(1)}, bf16[64,1024]{1,0:T(8,128)(2,1)}, u32[]{:S(2)}) copy-start(bf16[64,1024]{1,0:T(8,128)(2,1)} %copy-done.29) | copy-start | bytes 393220
  289.4 11.8 %copy-start.26 = (bf16[2,64,1024]{2,1,0:T(8,128)(2,1)S(1)}, bf16[2,64,1024]{2,1,0:T(8,128)(2,1)}, u32[]{:S(2)}) copy-start(bf16[2,64,1024]{2,1,0:T(8,128)(2,1)} %get-tuple-element.118) | copy-start | bytes 786436
  289.4 11.8 %copy-start.3 = (bf16[2,656,512]{2,1,0:T(8,128)(2,1)S(1)}, bf16[2,656,512]{2,1,0:T(8,128)(2,1)}, u32[]{:S(2)}) copy-start(bf16[2,656,512]{2,1,0:T(8,128)(2,1)} %get-tuple-element.114.refs_10_) | copy-start | bytes 4030468
  303.7 25.9 %collective-permute-start.15 = (bf16[2,656,256]{2,1,0:T(8,128)(2,1)S(1)}, bf16[2,656,256]{2,1,0:T(8,128)(2,1)}, u32[]{:S(2)}, u32[]{:S(2)}) collective-permute-start(bf16[2,656,256]{2,1,0:T(8,128)(2,1)S(1)} %get-tuple-element.150), channel_id=1, source_target_pairs={{0,8},{1,9},{2,10},{3,11},{4,12},{5,13},{6,14},{7,15},{8,0},{9,1},... | collective-permute-start | bytes 2015240 | tf_op jit(solution)/shard_map/ppermute | solution.py:763
  305.4 9.2 %collective-permute-start.17 = (bf16[64,1024]{1,0:T(8,128)(2,1)S(1)}, bf16[64,1024]{1,0:T(8,128)(2,1)S(1)}, u32[]{:S(2)}, u32[]{:S(2)}) collective-permute-start(bf16[64,1024]{1,0:T(8,128)(2,1)S(1)} %pad_maximum_fusion.1), channel_id=1, source_target_pairs={{0,1},{1,0},{2,3},{3,2},{4,5},{5,4},{6,7},{7,6},{8,9},{9,8},{10,11... | collective-permute-start | bytes 393224 | tf_op jit(solution)/shard_map/ppermute | solution.py:763
  314.6 15.1 %copy-start.27 = (bf16[64,1024]{1,0:T(8,128)(2,1)}, bf16[64,1024]{1,0:T(8,128)(2,1)S(1)}, u32[]{:S(2)}) copy-start(bf16[64,1024]{1,0:T(8,128)(2,1)S(1)} %collective-permute-done.17) | copy-start | bytes 393220
  314.6 53.1 %collective-permute-start.20 = (bf16[3,1024,256]{2,1,0:T(8,128)(2,1)}, bf16[3,1024,256]{2,1,0:T(8,128)(2,1)}, u32[]{:S(2)}, u32[]{:S(2)}) collective-permute-start(bf16[3,1024,256]{2,1,0:T(8,128)(2,1)} %trade_attn.2), channel_id=1, source_target_pairs={{0,1},{1,0},{2,3},{3,2},{4,5},{5,4},{6,7},{7,6},{8,9},{9,8},{10,11... | collective-permute-start | bytes 4718600 | tf_op jit(solution)/shard_map/ppermute | solution.py:763
  315.6 14.1 %copy-start.10 = (bf16[2,656,256]{2,1,0:T(8,128)(2,1)S(1)}, bf16[2,656,256]{2,1,0:T(8,128)(2,1)}, u32[]{:S(2)}) copy-start(bf16[2,656,256]{2,1,0:T(8,128)(2,1)} %get-tuple-element.115.refs_4_) | copy-start | bytes 2015236
  333.6 17.5 %collective-permute-start.18 = (bf16[1,912,512]{2,1,0:T(8,128)(2,1)S(1)}, bf16[1,912,512]{2,1,0:T(8,128)(2,1)}, u32[]{:S(2)}, u32[]{:S(2)}) collective-permute-start(bf16[1,912,512]{2,1,0:T(8,128)(2,1)S(1)} %get-tuple-element.146), channel_id=1, source_target_pairs={{0,4},{1,5},{2,10},{3,11},{4,0},{5,1},{6,14},{7,15},{8,12},{9,13},... | collective-permute-start | bytes 2801672 | tf_op jit(solution)/shard_map/ppermute | solution.py:763
  335.2 32.2 %collective-permute-start.19 = (bf16[2,656,256]{2,1,0:T(8,128)(2,1)S(1)}, bf16[2,656,256]{2,1,0:T(8,128)(2,1)S(1)}, u32[]{:S(2)}, u32[]{:S(2)}) collective-permute-start(bf16[2,656,256]{2,1,0:T(8,128)(2,1)S(1)} %add.215), channel_id=1, source_target_pairs={{0,16},{1,17},{2,18},{3,19},{4,20},{5,21},{6,22},{7,23},{8,24},{9,... | collective-permute-start | bytes 2015240 | tf_op jit(solution)/shard_map/ppermute | solution.py:763
  351.1 16.6 %copy-start.8 = (bf16[3,1024,256]{2,1,0:T(8,128)(2,1)S(1)}, bf16[3,1024,256]{2,1,0:T(8,128)(2,1)}, u32[]{:S(2)}) copy-start(bf16[3,1024,256]{2,1,0:T(8,128)(2,1)} %trade_attn.3) | copy-start | bytes 4718596
  367.6 24.8 %collective-permute-start.22 = (bf16[2,656,256]{2,1,0:T(8,128)(2,1)S(1)}, bf16[2,656,256]{2,1,0:T(8,128)(2,1)}, u32[]{:S(2)}, u32[]{:S(2)}) collective-permute-start(bf16[2,656,256]{2,1,0:T(8,128)(2,1)S(1)} %add.223), channel_id=1, source_target_pairs={{0,8},{1,9},{2,10},{3,11},{4,12},{5,13},{6,14},{7,15},{8,0},{9,1},... | collective-permute-start | bytes 2015240 | tf_op jit(solution)/shard_map/ppermute | solution.py:763
  370.4 33.3 %collective-permute-start.24 = (bf16[3,512,256]{2,1,0:T(8,128)(2,1)S(1)}, bf16[3,512,256]{2,1,0:T(8,128)(2,1)}, u32[]{:S(2)}, u32[]{:S(2)}) collective-permute-start(bf16[3,512,256]{2,1,0:T(8,128)(2,1)S(1)} %get-tuple-element.148), channel_id=1, source_target_pairs={{0,4},{1,5},{2,10},{3,11},{4,0},{5,1},{6,14},{7,15},{8,12},{9,13},... | collective-permute-start | bytes 2359304 | tf_op jit(solution)/shard_map/ppermute | solution.py:763
  372.0 28.8 %collective-permute-start.23 = (bf16[1,912,256]{2,1,0:T(8,128)(2,1)}, bf16[1,912,256]{2,1,0:T(8,128)(2,1)}, u32[]{:S(2)}, u32[]{:S(2)}) collective-permute-start(bf16[1,912,256]{2,1,0:T(8,128)(2,1)} %get-tuple-element.152), channel_id=1, source_target_pairs={{0,8},{1,9},{2,18},{3,19},{4,12},{5,13},{6,22},{7,23},{8,0},{9,1},... | collective-permute-start | bytes 1400840 | tf_op jit(solution)/shard_map/ppermute | solution.py:763
  394.1 50.2 %collective-permute-start.32 = (bf16[2,656,512]{2,1,0:T(8,128)(2,1)S(1)}, bf16[2,656,512]{2,1,0:T(8,128)(2,1)}, u32[]{:S(2)}, u32[]{:S(2)}) collective-permute-start(bf16[2,656,512]{2,1,0:T(8,128)(2,1)S(1)} %maximum_select_fusion.3), channel_id=1, source_target_pairs={{0,4},{1,5},{2,6},{3,7},{4,0},{5,1},{6,2},{7,3},{8,12},{9,13},{10,... | collective-permute-start | bytes 4030472 | tf_op jit(solution)/shard_map/ppermute | solution.py:763
  401.9 22.5 %collective-permute-start.26 = (bf16[1,912,256]{2,1,0:T(8,128)(2,1)S(1)}, bf16[1,912,256]{2,1,0:T(8,128)(2,1)S(1)}, u32[]{:S(2)}, u32[]{:S(2)}) collective-permute-start(bf16[1,912,256]{2,1,0:T(8,128)(2,1)S(1)} %add.227), channel_id=1, source_target_pairs={{0,16},{1,17},{2,6},{3,7},{4,20},{5,21},{6,2},{7,3},{8,24},{9,25},... | collective-permute-start | bytes 1400840 | tf_op jit(solution)/shard_map/ppermute | solution.py:763
  402.6 3.7 collective-permute-start.21
  406.3 18.4 %collective-permute-start.28 = (bf16[3,256,256]{2,1,0:T(8,128)(2,1)S(1)}, bf16[3,256,256]{2,1,0:T(8,128)(2,1)S(1)}, u32[]{:S(2)}, u32[]{:S(2)}) collective-permute-start(bf16[3,256,256]{2,1,0:T(8,128)(2,1)S(1)} %get-tuple-element.154), channel_id=1, source_target_pairs={{0,8},{1,9},{2,18},{3,19},{4,12},{5,13},{6,22},{7,23},{8,0},{9,1},... | collective-permute-start | bytes 1179656 | tf_op jit(solution)/shard_map/ppermute | solution.py:763
  408.8 15.9 %collective-permute-start.25 = (f32[2,1024]{1,0:T(2,128)S(1)}, f32[2,1024]{1,0:T(2,128)S(1)}, u32[]{:S(2)}, u32[]{:S(2)}) collective-permute-start(f32[2,1024]{1,0:T(2,128)S(1)} %fusion.1), channel_id=1, source_target_pairs={{0,2},{1,3},{2,0},{3,1},{4,6},{5,7},{6,4},{7,5},{8,10},{9,11},{10,... | collective-permute-start | bytes 24584 | tf_op jit(solution)/shard_map/ppermute | solution.py:763
  424.6 12.5 %collective-permute-start.29 = (bf16[1,912,256]{2,1,0:T(8,128)(2,1)S(1)}, bf16[1,912,256]{2,1,0:T(8,128)(2,1)S(1)}, u32[]{:S(2)}, u32[]{:S(2)}) collective-permute-start(bf16[1,912,256]{2,1,0:T(8,128)(2,1)S(1)} %add.231), channel_id=1, source_target_pairs={{0,8},{1,9},{2,18},{3,19},{4,12},{5,13},{6,22},{7,23},{8,0},{9,1},... | collective-permute-start | bytes 1400840 | tf_op jit(solution)/shard_map/ppermute | solution.py:763
  424.8 19.4 %collective-permute-start.30 = (bf16[3,256,256]{2,1,0:T(8,128)(2,1)S(1)}, bf16[3,256,256]{2,1,0:T(8,128)(2,1)S(1)}, u32[]{:S(2)}, u32[]{:S(2)}) collective-permute-start(bf16[3,256,256]{2,1,0:T(8,128)(2,1)S(1)} %add.234), channel_id=1, source_target_pairs={{0,16},{1,17},{2,6},{3,7},{4,20},{5,21},{6,2},{7,3},{8,24},{9,25},... | collective-permute-start | bytes 1179656 | tf_op jit(solution)/shard_map/ppermute | solution.py:763
  448.0 22.7 %copy-start.4 = (bf16[2,656,1024]{2,1,0:T(8,128)(2,1)}, bf16[2,656,1024]{2,1,0:T(8,128)(2,1)S(1)}, u32[]{:S(2)}) copy-start(bf16[2,656,1024]{2,1,0:T(8,128)(2,1)S(1)} %maximum_select_fusion.refs_1_) | copy-start | bytes 8060932
  448.0 22.8 %collective-permute-start.35 = (bf16[2,656,1024]{2,1,0:T(8,128)(2,1)S(1)}, bf16[2,656,1024]{2,1,0:T(8,128)(2,1)}, u32[]{:S(2)}, u32[]{:S(2)}) collective-permute-start(bf16[2,656,1024]{2,1,0:T(8,128)(2,1)S(1)} %maximum_select_fusion.refs_1_), channel_id=1, source_target_pairs={{0,2},{1,3},{2,0},{3,1},{4,6},{5,7},{6,4},{7,5},{8,10},{9,11},{10,... | collective-permute-start | bytes 8060936 | tf_op jit(solution)/shard_map/ppermute | solution.py:763
  452.7 14.0 %collective-permute-start.33 = (bf16[1,912,512]{2,1,0:T(8,128)(2,1)}, bf16[1,912,512]{2,1,0:T(8,128)(2,1)}, u32[]{:S(2)}, u32[]{:S(2)}) collective-permute-start(bf16[1,912,512]{2,1,0:T(8,128)(2,1)} %maximum_select_fusion.4), channel_id=1, source_target_pairs={{0,4},{1,5},{2,10},{3,11},{4,0},{5,1},{6,14},{7,15},{8,12},{9,13},... | collective-permute-start | bytes 2801672 | tf_op jit(solution)/shard_map/ppermute | solution.py:763
  454.2 23.8 %collective-permute-start.36 = (bf16[3,256,256]{2,1,0:T(8,128)(2,1)S(1)}, bf16[3,256,256]{2,1,0:T(8,128)(2,1)S(1)}, u32[]{:S(2)}, u32[]{:S(2)}) collective-permute-start(bf16[3,256,256]{2,1,0:T(8,128)(2,1)S(1)} %add.235), channel_id=1, source_target_pairs={{0,8},{1,9},{2,18},{3,19},{4,12},{5,13},{6,22},{7,23},{8,0},{9,1},... | collective-permute-start | bytes 1179656 | tf_op jit(solution)/shard_map/ppermute | solution.py:763
  454.2 12.4 %collective-permute-start.27 = (f32[2,1024]{1,0:T(2,128)S(1)}, f32[2,1024]{1,0:T(2,128)S(1)}, u32[]{:S(2)}, u32[]{:S(2)}) collective-permute-start(f32[2,1024]{1,0:T(2,128)S(1)} %fusion.5), channel_id=1, source_target_pairs={{0,4},{1,5},{2,6},{3,7},{4,0},{5,1},{6,2},{7,3},{8,12},{9,13},{10,... | collective-permute-start | bytes 24584 | tf_op jit(solution)/shard_map/ppermute | solution.py:763
  466.6 4.1 collective-permute-start.31
  478.3 12.1 %collective-permute-start.37 = (bf16[3,512,256]{2,1,0:T(8,128)(2,1)S(1)}, bf16[3,512,256]{2,1,0:T(8,128)(2,1)S(1)}, u32[]{:S(2)}, u32[]{:S(2)}) collective-permute-start(bf16[3,512,256]{2,1,0:T(8,128)(2,1)S(1)} %maximum_select_fusion.5), channel_id=1, source_target_pairs={{0,4},{1,5},{2,10},{3,11},{4,0},{5,1},{6,14},{7,15},{8,12},{9,13},... | collective-permute-start | bytes 2359304 | tf_op jit(solution)/shard_map/ppermute | solution.py:763
  479.9 22.3 %collective-permute-start.39 = (bf16[1,912,1024]{2,1,0:T(8,128)(2,1)S(1)}, bf16[1,912,1024]{2,1,0:T(8,128)(2,1)S(1)}, u32[]{:S(2)}, u32[]{:S(2)}) collective-permute-start(bf16[1,912,1024]{2,1,0:T(8,128)(2,1)S(1)} %copy-done.1), channel_id=1, source_target_pairs={{0,2},{1,3},{2,0},{3,1},{4,6},{5,7},{6,4},{7,5},{8,10},{9,11},{10,... | collective-permute-start | bytes 5603336 | tf_op jit(solution)/shard_map/ppermute | solution.py:763
  490.8 18.0 %collective-permute-start.38 = (bf16[3,1024,256]{2,1,0:T(8,128)(2,1)S(1)}, bf16[3,1024,256]{2,1,0:T(8,128)(2,1)S(1)}, u32[]{:S(2)}, u32[]{:S(2)}) collective-permute-start(bf16[3,1024,256]{2,1,0:T(8,128)(2,1)S(1)} %maximum_select_fusion.2.refs_3_.refs_1_), channel_id=1, source_target_pairs={{0,2},{1,3},{2,0},{3,1},{4,6},{5,7},{6,4},{7,5},{8,10},{9,11},{10,... | collective-permute-start | bytes 4718600 | tf_op jit(solution)/shard_map/ppermute | solution.py:763
  497.0 4.5 collective-permute-start.34
  (28 other events, 146.8 us)

commit v6 on v5

--- a/solution.py
+++ b/solution.py
@@ -930,9 +930,9 @@
     d0 = add_edge(tie(d0, down.held), edge_own)
     attn.near = trade_attn(6, True, normed, d0)
     down.scatter(attn.near)
-    inner.both_add(down.held)
-    attn.across(inner.held)
-    input_grad, gain_attn_grad = pull(tokens, hidden_grad, gain_attn, d0, w_qkv, d1, attn_parts, after=[attn.held])
+    attn.across(down.held)
+    inner.both_add(attn.held)
+    input_grad, gain_attn_grad = pull(tokens, hidden_grad, gain_attn, d0, w_qkv, d1, attn_parts, after=[inner.held])
     gain_total = jnp.concatenate((gain_attn_grad, gain_mlp_grad))
     inner.gather(input_grad)
     down.both(inner.held)

time: 525 us -> 527 us (level)
  transfers between devices with their start and end apart: 40 -> 40, of which waited for: 18 -> 19; matrix products, arithmetic and copies ran while one was open for 6% -> 5% of each run, Pallas kernels for 47% -> 47%
where the time goes in v6:
time: 527 us; the launch traced here: 517 us
  Pallas kernels  305 us (58%)
  waiting for transfers between devices  105 us (20%)
  starting transfers between devices  56.4 us (11%)
  other arithmetic  32.6 us (6%)
  local copies, waits for them, and re-layouts  16.2 us (3%)
    pallas_call x18, Pallas kernels, run(): return call(*lead, *[a for a, _, _ in ins], *extra)  288 us
    ppermute x40, waiting for transfers between devices, send(): return lax.ppermute(value, AXES, pairs)  105 us
    ppermute x40, starting transfers between devices, send(): return lax.ppermute(value, AXES, pairs)  56.4 us
    pallas_call x3, Pallas kernels, assemble_call(): pl.pallas_call(lambda *refs: body(*refs[:3], *refs[3 + len(after):]), gri...  17.4 us
    add x6, other arithmetic, split(): part = lambda k: half(a, k, self.axis) + half(b, k, self.axis)  13.2 us
    select_n x6, other arithmetic, order(): jnp.where(bit == 0, jnp.concatenate([first, second], axis), jnp.concatena...  11.3 us
  transfers between devices with their start and end apart: 40, of which 19 were waited for; matrix products, arithmetic and copies ran while one was open for 5% of the time, Pallas kernels for 47%

profile of v6, /device:TPU:0, one launch (start us, length us, event | category | flops | bytes accessed | tf_op | source)
XLA Modules:
  0.0 516.7 jit_solution(1199504052126088522)
XLA Ops:
  1.6 3.0 collective-permute-start
  4.6 3.5 collective-permute-done.refs_1_.refs_2_
  11.9 5.6 %norm_rows.1.refs_0_ = bf16[1664,1024]{1,0:T(8,128)(2,1)} custom-call(bf16[1536,1024]{1,0:T(8,128)(2,1)} %refs_0_.5, bf16[64,1024]{1,0:T(8,128)(2,1)} %copy-done.25, bf16[64,1024]{1,0:T(8,128)(2,1)} %copy-done.25, f32[1,1024]{1,0:T(1,128)} %bitcast.31), custom_call_target="tpu_custom_call" | custom-call | flops 600 | bytes 1000 | tf_op jit(solution)/shard_map/norm_rows/pallas_call | solution.py:81
  18.1 8.9 %project.1 = (bf16[1664,512]{1,0:T(8,128)(2,1)}, bf16[1664,512]{1,0:T(8,128)(2,1)}, bf16[1664,512]{1,0:T(8,128)(2,1)}) custom-call(bf16[1664,1024]{1,0:T(8,128)(2,1)} %norm_rows.1.refs_0_, bf16[3,1024,512]{2,1,0:T(8,128)(2,1)} %bitcast.23), custom_call_target="tpu_custom_call" | custom-call | flops 900 | bytes 1000 | tf_op jit(solution)/shard_map/project/pallas_call | solution.py:81
  27.0 14.0 %attend.2 = (bf16[1536,512]{1,0:T(8,128)(2,1)}, f32[12,4,256]{2,1,0:T(4,128)}) custom-call(s32[3,12]{1,0:T(4,128)} %pad_add_fusion.refs_0_, bf16[1664,512]{1,0:T(8,128)(2,1)} %get-tuple-element.76.refs_1_, bf16[1664,512]{1,0:T(8,128)(2,1)} %get-tuple-element.77.refs_2_.refs_3_.refs_4_, bf16[1664,512]{1,0:T(8,128)(2,1)} %get-tuple-element.77.refs_2_.refs_3_.refs_4_, ...), custom_call_target="tpu_custom_call" | custom-call | flops 2000 | bytes 1000 | tf_op jit(solution)/shard_map/attend/pallas_call | solution.py:81
  41.0 4.3 collective-permute-done.1.refs_1_.refs_6_
  48.8 8.9 %project_parts.1 = (bf16[1664,512]{1,0:T(8,128)(2,1)}, bf16[1664,512]{1,0:T(8,128)(2,1)}, bf16[1664,512]{1,0:T(8,128)(2,1)}) custom-call(bf16[1664,1024]{1,0:T(8,128)(2,1)} %norm_rows.1.refs_0_, bf16[3,1024,256]{2,1,0:T(8,128)(2,1)} %copy-done.8, bf16[3,1024,256]{2,1,0:T(8,128)(2,1)} %collective-permute-done.2.refs_2_.refs_7_, ...), custom_call_target="tpu_custom_call" | custom-call | flops 900 | bytes 1000 | tf_op jit(solution)/shard_map/project_parts/pallas_call | solution.py:81
  59.7 2.4 constant_dynamic-slice_fusion.1
  64.4 13.8 %attend.3 = (bf16[1536,512]{1,0:T(8,128)(2,1)}, f32[12,4,256]{2,1,0:T(4,128)}) custom-call(s32[3,12]{1,0:T(4,128)} %pad_add_fusion.refs_0_, bf16[1664,512]{1,0:T(8,128)(2,1)} %get-tuple-element.82.refs_1_, bf16[1664,512]{1,0:T(8,128)(2,1)} %get-tuple-element.83.refs_2_.refs_3_.refs_4_, bf16[1664,512]{1,0:T(8,128)(2,1)} %get-tuple-element.83.refs_2_.refs_3_.refs_4_, ...), custom_call_target="tpu_custom_call" | custom-call | flops 2000 | bytes 1000 | tf_op jit(solution)/shard_map/attend/pallas_call | solution.py:81
  79.1 9.9 %mix.1 = (f32[1536,1024]{1,0:T(8,128)}, bf16[1536,1024]{1,0:T(8,128)(2,1)}) custom-call(bf16[1536,1024]{1,0:T(8,128)(2,1)} %refs_0_.5, f32[1,1024]{1,0:T(1,128)} %bitcast.29, bf16[1536,512]{1,0:T(8,128)(2,1)} %get-tuple-element.79.refs_3_.refs_2_.refs_1_, bf16[512,1024]{1,0:T(8,128)(2,1)} %refs_13_.1, bf16[1536,512]{1,0:T(8,128)(2,1)} %get-tuple-element.87.refs_4_.refs_1_, ...), custom_call_target="tpu_custom_call" | custom-call | flops 1100 | bytes 1000 | tf_op jit(solution)/shard_map/mix/pallas_call | solution.py:81
  88.9 5.7 %collective-permute-done.5.refs_5_.refs_3_ = bf16[2,656,512]{2,1,0:T(8,128)(2,1)S(1)} collective-permute-done((bf16[2,656,512]{2,1,0:T(8,128)(2,1)S(1)}, bf16[2,656,512]{2,1,0:T(8,128)(2,1)S(1)}, u32[]{:S(2)}, u32[]{:S(2)}) %collective-permute-start.5) | collective-permute-done | bytes 1343520 | tf_op jit(solution)/shard_map/ppermute | solution.py:763
  95.9 38.6 %mlp_first.1 = (bf16[1,1536,1312]{2,1,0:T(8,128)(2,1)}, bf16[2,1536,1312]{2,1,0:T(8,128)(2,1)}, bf16[1536,1024]{1,0:T(8,128)(2,1)}, f32[1536,1024]{1,0:T(8,128)}, f32[1536,1024]{1,0:T(8,128)}) custom-call(s32[3,12]{1,0:T(4,128)} %pad_add_fusion.refs_0_, bf16[1536,1024]{1,0:T(8,128)(2,1)} %get-tuple-element.88.refs_1_, bf16[1536,1024]{1,0:T(8,128)(2,1)} %refs_2_.3, ...), custom_call_target="tpu_custom_call" | custom-call | flops 3900 | bytes 1000 | tf_op jit(solution)/shard_map/mlp_first/pallas_call | solution.py:81
  135.3 2.6 collective-permute-done.10.refs_8_
  140.9 47.9 %mlp_last.1 = (bf16[1,1536,1312]{2,1,0:T(8,128)(2,1)}, bf16[2,1536,1312]{2,1,0:T(8,128)(2,1)}, bf16[1536,1024]{1,0:T(8,128)(2,1)}, f32[1536,1024]{1,0:T(8,128)},...) custom-call(s32[3,12]{1,0:T(4,128)} %pad_add_fusion.refs_0_, ...), custom_call_target="tpu_custom_call" | custom-call | flops 4900 | bytes 1000 | tf_op jit(solution)/shard_map/mlp_last/pallas_call | solution.py:81
  188.8 10.7 %trade_outer.3.refs_2_ = bf16[1,656,1024]{2,1,0:T(8,128)(2,1)} custom-call(bf16[2,1536,1312]{2,1,0:T(8,128)(2,1)} %get-tuple-element.102.refs_0_, bf16[1536,1024]{1,0:T(8,128)(2,1)} %get-tuple-element.88.refs_1_, bf16[1536,512]{1,0:T(8,128)(2,1)} %get-tuple-element.103.refs_2_.refs_8_), custom_call_target="tpu_custom_call" | custom-call | flops 900 | bytes 1000 | tf_op jit(solution)/shard_map/trade_outer/pallas_call | solution.py:81
  201.1 10.6 %trade_outer.4.refs_2_ = bf16[1,656,1024]{2,1,0:T(8,128)(2,1)} custom-call(bf16[2,1536,1312]{2,1,0:T(8,128)(2,1)} %get-tuple-element.102.refs_0_, bf16[1536,1024]{1,0:T(8,128)(2,1)} %get-tuple-element.88.refs_1_, bf16[1,656,1024]{2,1,0:T(8,128)(2,1)} %trade_outer.3.refs_2_), custom_call_target="tpu_custom_call" | custom-call | flops 900 | bytes 1000 | tf_op jit(solution)/shard_map/trade_outer/pallas_call | solution.py:81
  212.3 16.3 %trade_outer.5.refs_10_ = bf16[2,656,1024]{2,1,0:T(8,128)(2,1)} custom-call(bf16[2,1536,1312]{2,1,0:T(8,128)(2,1)} %get-tuple-element.101.refs_0_, bf16[1536,1024]{1,0:T(8,128)(2,1)} %get-tuple-element.88.refs_1_, bf16[1,656,1024]{2,1,0:T(8,128)(2,1)} %trade_outer.4.refs_2_), custom_call_target="tpu_custom_call" | custom-call | flops 900 | bytes 1000 | tf_op jit(solution)/shard_map/trade_outer/pallas_call | solution.py:81
  228.6 16.6 %attend_back.2 = (bf16[1536,1536]{1,0:T(8,128)(2,1)}, bf16[2,64,1024]{2,1,0:T(8,128)(2,1)}) custom-call(s32[3,12]{1,0:T(4,128)} %pad_add_fusion.refs_0_, bf16[1664,512]{1,0:T(8,128)(2,1)} %get-tuple-element.76.refs_1_, bf16[1664,512]{1,0:T(8,128)(2,1)} %get-tuple-element.77.refs_2_.refs_3_.refs_4_, ...), custom_call_target="tpu_custom_call" | custom-call | flops 2500 | bytes 1000 | tf_op jit(solution)/shard_map/attend_back/pallas_call | solution.py:81
  248.9 13.7 %trade_down.2 = bf16[1,912,1024]{2,1,0:T(8,128)(2,1)} custom-call(bf16[1,1536,1312]{2,1,0:T(8,128)(2,1)} %get-tuple-element.108.refs_0_, bf16[1536,512]{1,0:T(8,128)(2,1)} %get-tuple-element.87.refs_4_.refs_1_, bf16[1536,1024]{1,0:T(8,128)(2,1)} %get-tuple-element.106.refs_2_, bf16[1536,1024]{1,0:T(8,128)(2,1)} %get-tuple-element.107.refs_3_, ...), custom_call_target="tpu_custom_call" | custom-call | flops 1200 | bytes 1000 | tf_op jit(solution)/shard_map/trade_down/pallas_call | solution.py:81
  266.3 2.5 dynamic-slice_add_fusion.1
  271.0 16.6 %attend_back.3 = (bf16[1536,1536]{1,0:T(8,128)(2,1)}, bf16[2,64,1024]{2,1,0:T(8,128)(2,1)}) custom-call(s32[3,12]{1,0:T(4,128)} %pad_add_fusion.refs_0_, bf16[1664,512]{1,0:T(8,128)(2,1)} %get-tuple-element.82.refs_1_, bf16[1664,512]{1,0:T(8,128)(2,1)} %get-tuple-element.83.refs_2_.refs_3_.refs_4_, ...), custom_call_target="tpu_custom_call" | custom-call | flops 2500 | bytes 1000 | tf_op jit(solution)/shard_map/attend_back/pallas_call | solution.py:81
  289.2 11.8 %trade_attn.2 = bf16[3,1024,256]{2,1,0:T(8,128)(2,1)} custom-call(bf16[1664,1024]{1,0:T(8,128)(2,1)} %norm_rows.1.refs_0_, bf16[1536,1536]{1,0:T(8,128)(2,1)} %add_dynamic-update-slice_fusion.1.refs_1_.refs_5_), custom_call_target="tpu_custom_call" | custom-call | flops 1000 | bytes 1000 | tf_op jit(solution)/shard_map/trade_attn/pallas_call | solution.py:81
  301.0 2.5 dynamic-slice_add_fusion.6
  305.8 8.7 %collective-permute-done.17 = bf16[64,1024]{1,0:T(8,128)(2,1)S(1)} collective-permute-done((bf16[64,1024]{1,0:T(8,128)(2,1)S(1)}, bf16[64,1024]{1,0:T(8,128)(2,1)S(1)}, u32[]{:S(2)}, u32[]{:S(2)}) %collective-permute-start.17) | collective-permute-done | bytes 131104 | tf_op jit(solution)/shard_map/ppermute | solution.py:763
  315.5 14.1 %trade_down.3 = bf16[1,912,1024]{2,1,0:T(8,128)(2,1)} custom-call(bf16[1,1536,1312]{2,1,0:T(8,128)(2,1)} %get-tuple-element.105.refs_0_, bf16[1536,512]{1,0:T(8,128)(2,1)} %get-tuple-element.79.refs_3_.refs_2_.refs_1_, bf16[1536,1024]{1,0:T(8,128)(2,1)} %get-tuple-element.106.refs_2_, bf16[1536,1024]{1,0:T(8,128)(2,1)} %get-tuple-element.107.refs_3_, ...), custom_call_target="tpu_custom_call" | custom-call | flops 1200 | bytes 1000 | tf_op jit(solution)/shard_map/trade_down/pallas_call | solution.py:81
  331.1 3.1 dynamic-slice_add_fusion.2
  335.8 2.6 collective-permute-start.20
  339.9 11.6 %trade_attn.3 = bf16[3,1024,256]{2,1,0:T(8,128)(2,1)} custom-call(bf16[1664,1024]{1,0:T(8,128)(2,1)} %norm_rows.1.refs_0_, bf16[1536,1536]{1,0:T(8,128)(2,1)} %add_dynamic-update-slice_fusion.refs_1_.refs_3_), custom_call_target="tpu_custom_call" | custom-call | flops 1000 | bytes 1000 | tf_op jit(solution)/shard_map/trade_attn/pallas_call | solution.py:81
  353.2 2.7 dynamic-slice_add_fusion.4
  355.9 12.2 %collective-permute-done.20 = bf16[2,656,256]{2,1,0:T(8,128)(2,1)} collective-permute-done((bf16[2,656,256]{2,1,0:T(8,128)(2,1)S(1)}, bf16[2,656,256]{2,1,0:T(8,128)(2,1)}, u32[]{:S(2)}, u32[]{:S(2)}) %collective-permute-start.20) | collective-permute-done | bytes 671776 | tf_op jit(solution)/shard_map/ppermute | solution.py:763
  373.0 18.4 %pull.1 = (f32[1536,1024]{1,0:T(8,128)}, f32[1,1024]{1,0:T(1,128)}) custom-call(bf16[1536,1024]{1,0:T(8,128)(2,1)} %refs_0_.5, f32[1536,1024]{1,0:T(8,128)} %get-tuple-element.98.refs_1_, f32[1,1024]{1,0:T(1,128)} %bitcast.32, bf16[1536,1536]{1,0:T(8,128)(2,1)} %add_dynamic-update-slice_fusion.refs_1_.refs_3_, bf16[3,1024,512]{2,1,0:T(8,128)(2,1)} %bitcast.24, ...), custom_call_target="tpu_custom_call" | custom-call | flops 1800 | bytes 1000 | tf_op jit(solution)/shard_map/pull/pallas_call | solution.py:81
  395.6 7.0 %collective-permute-done.23 = bf16[1,912,256]{2,1,0:T(8,128)(2,1)} collective-permute-done((bf16[1,912,256]{2,1,0:T(8,128)(2,1)}, bf16[1,912,256]{2,1,0:T(8,128)(2,1)}, u32[]{:S(2)}, u32[]{:S(2)}) %collective-permute-start.23) | collective-permute-done | bytes 466976 | tf_op jit(solution)/shard_map/ppermute | solution.py:763
  407.7 2.5 collective-permute-start.28
  411.3 14.6 %collective-permute-done.26 = bf16[1,912,256]{2,1,0:T(8,128)(2,1)S(1)} collective-permute-done((bf16[1,912,256]{2,1,0:T(8,128)(2,1)S(1)}, bf16[1,912,256]{2,1,0:T(8,128)(2,1)S(1)}, u32[]{:S(2)}, u32[]{:S(2)}) %collective-permute-start.26) | collective-permute-done | bytes 466976 | tf_op jit(solution)/shard_map/ppermute | solution.py:763
  426.2 2.5 collective-permute-start.30
  428.8 9.7 %collective-permute-done.29 = bf16[1,912,256]{2,1,0:T(8,128)(2,1)S(1)} collective-permute-done((bf16[1,912,256]{2,1,0:T(8,128)(2,1)S(1)}, bf16[1,912,256]{2,1,0:T(8,128)(2,1)S(1)}, u32[]{:S(2)}, u32[]{:S(2)}) %collective-permute-start.29) | collective-permute-done | bytes 466976 | tf_op jit(solution)/shard_map/ppermute | solution.py:763
  439.7 7.5 %collective-permute-done.30 = bf16[3,256,256]{2,1,0:T(8,128)(2,1)S(1)} collective-permute-done((bf16[3,256,256]{2,1,0:T(8,128)(2,1)S(1)}, bf16[3,256,256]{2,1,0:T(8,128)(2,1)S(1)}, u32[]{:S(2)}, u32[]{:S(2)}) %collective-permute-start.30) | collective-permute-done | bytes 393248 | tf_op jit(solution)/shard_map/ppermute | solution.py:763
  447.3 3.7 maximum_select_fusion.refs_1_
  451.0 3.2 collective-permute-start.35
  456.2 11.9 %collective-permute-done.27 = f32[2,1024]{1,0:T(2,128)S(1)} collective-permute-done((f32[2,1024]{1,0:T(2,128)S(1)}, f32[2,1024]{1,0:T(2,128)S(1)}, u32[]{:S(2)}, u32[]{:S(2)}) %collective-permute-start.27) | collective-permute-done | bytes 8224 | tf_op jit(solution)/shard_map/ppermute | solution.py:763
  468.2 4.1 maximum_select_fusion.1.refs_3_.refs_1_
  472.3 7.2 %assemble.3 = f32[2,1312,1024]{2,1,0:T(8,128)} custom-call(s32[1]{0:T(128)} %bitcast.1.refs_0_, bf16[2,656,1024]{2,1,0:T(8,128)(2,1)} %copy-done.4, bf16[2,656,1024]{2,1,0:T(8,128)(2,1)} %collective-permute-done.35.refs_2_, bf16[1,912,1024]{2,1,0:T(8,128)(2,1)} %maximum_select_fusion.1.refs_3_.refs_1_), custom_call_target="tpu_custom_call" | custom-call | tf_op jit(solution)/shard_map/assemble/pallas_call | solution.py:711
  481.8 5.5 %collective-permute-start.39 = (bf16[1,912,1024]{2,1,0:T(8,128)(2,1)S(1)}, bf16[1,912,1024]{2,1,0:T(8,128)(2,1)S(1)}, u32[]{:S(2)}, u32[]{:S(2)}) collective-permute-start(bf16[1,912,1024]{2,1,0:T(8,128)(2,1)S(1)} %copy-done.1), channel_id=1, source_target_pairs={{0,2},{1,3},{2,0},{3,1},{4,6},{5,7},{6,4},{7,5},{8,10},{9,11},{10,... | collective-permute-start | bytes 5603336 | tf_op jit(solution)/shard_map/ppermute | solution.py:763
  487.3 4.6 collective-permute-done.37
  492.3 6.2 %collective-permute-start.38 = (bf16[3,1024,256]{2,1,0:T(8,128)(2,1)S(1)}, bf16[3,1024,256]{2,1,0:T(8,128)(2,1)S(1)}, u32[]{:S(2)}, u32[]{:S(2)}) collective-permute-start(bf16[3,1024,256]{2,1,0:T(8,128)(2,1)S(1)} %maximum_select_fusion.2.refs_3_.refs_1_), channel_id=1, source_target_pairs={{0,2},{1,3},{2,0},{3,1},{4,6},{5,7},{6,4},{7,5},{8,10},{9,11},{10,... | collective-permute-start | bytes 4718600 | tf_op jit(solution)/shard_map/ppermute | solution.py:763
  499.3 3.8 collective-permute-done.34
  505.0 5.3 %assemble.4 = (f32[1312,1024]{1,0:T(8,128)}, f32[512,1024]{1,0:T(8,128)}) custom-call(s32[1]{0:T(128)} %bitcast.1.refs_0_, bf16[1,912,1024]{2,1,0:T(8,128)(2,1)} %maximum_select_fusion.1.refs_3_.refs_1_, bf16[1,912,1024]{2,1,0:T(8,128)(2,1)} %copy-done.18, bf16[3,1024,256]{2,1,0:T(8,128)(2,1)} %copy-done.2), custom_call_target="tpu_custom_call" | custom-call | tf_op jit(solution)/shard_map/assemble/pallas_call | solution.py:711
  511.4 4.8 assemble.5
  (171 shorter events, 67.0 us)
Async XLA Ops:
  1.6 6.5 %collective-permute-start = (bf16[64,1024]{1,0:T(8,128)(2,1)S(1)}, bf16[64,1024]{1,0:T(8,128)(2,1)S(1)}, u32[]{:S(2)}, u32[]{:S(2)}) collective-permute-start(bf16[64,1024]{1,0:T(8,128)(2,1)S(1)} %constant_dynamic-slice_fusion.4), channel_id=1, source_target_pairs={{0,1},{1,0},{2,3},{3,2},{4,5},{5,4},{6,7},{7,6},{8,9},{9,8},{10,11... | collective-permute-start | bytes 393224 | tf_op jit(solution)/shard_map/ppermute | solution.py:763
  9.6 35.6 %collective-permute-start.1 = (bf16[3,1024,256]{2,1,0:T(8,128)(2,1)S(1)}, bf16[3,1024,256]{2,1,0:T(8,128)(2,1)S(1)}, u32[]{:S(2)}, u32[]{:S(2)}) collective-permute-start(bf16[3,1024,256]{2,1,0:T(8,128)(2,1)S(1)} %constant_dynamic-slice_fusion.3), channel_id=1, source_target_pairs={{0,1},{1,0},{2,3},{3,2},{4,5},{5,4},{6,7},{7,6},{8,9},{9,8},{10,11... | collective-permute-start | bytes 4718600 | tf_op jit(solution)/shard_map/ppermute | solution.py:763
  27.0 18.3 %copy-start.6 = (bf16[512,1024]{1,0:T(8,128)(2,1)S(1)}, bf16[512,1024]{1,0:T(8,128)(2,1)}, u32[]{:S(2)}) copy-start(bf16[512,1024]{1,0:T(8,128)(2,1)} %refs_13_.1) | copy-start | bytes 3145732
  45.3 3.5 collective-permute-start.2
  45.4 14.4 %collective-permute-start.3 = (bf16[256,1024]{1,0:T(8,128)(2,1)S(1)}, bf16[256,1024]{1,0:T(8,128)(2,1)S(1)}, u32[]{:S(2)}, u32[]{:S(2)}) collective-permute-start(bf16[256,1024]{1,0:T(8,128)(2,1)S(1)} %constant_dynamic-slice_fusion.2), channel_id=1, source_target_pairs={{0,1},{1,0},{2,3},{3,2},{4,5},{5,4},{6,7},{7,6},{8,9},{9,8},{10,11... | collective-permute-start | bytes 1572872 | tf_op jit(solution)/shard_map/ppermute | solution.py:763
  62.2 32.5 %collective-permute-start.5 = (bf16[2,656,512]{2,1,0:T(8,128)(2,1)S(1)}, bf16[2,656,512]{2,1,0:T(8,128)(2,1)S(1)}, u32[]{:S(2)}, u32[]{:S(2)}) collective-permute-start(bf16[2,656,512]{2,1,0:T(8,128)(2,1)S(1)} %constant_dynamic-slice_fusion.1), channel_id=1, source_target_pairs={{0,1},{1,0},{2,3},{3,2},{4,5},{5,4},{6,7},{7,6},{8,9},{9,8},{10,11... | collective-permute-start | bytes 4030472 | tf_op jit(solution)/shard_map/ppermute | solution.py:763
  63.6 14.6 %collective-permute-start.4 = (bf16[256,1024]{1,0:T(8,128)(2,1)S(1)}, bf16[256,1024]{1,0:T(8,128)(2,1)S(1)}, u32[]{:S(2)}, u32[]{:S(2)}) collective-permute-start(bf16[256,1024]{1,0:T(8,128)(2,1)S(1)} %collective-permute-done.3.refs_8_.refs_5_.refs_14_), channel_id=1, source_target_pairs={{0,2},{1,3},{2,0},{3,1},{4,6},{5,7},{6,4},{7,5},{8,10},{9,11},{10,... | collective-permute-start | bytes 1572872 | tf_op jit(solution)/shard_map/ppermute | solution.py:763
  63.8 70.8 %collective-permute-start.9 = (bf16[656,1024]{1,0:T(8,128)(2,1)S(1)}, bf16[656,1024]{1,0:T(8,128)(2,1)S(1)}, u32[]{:S(2)}, u32[]{:S(2)}) collective-permute-start(bf16[656,1024]{1,0:T(8,128)(2,1)S(1)} %constant_dynamic-slice_fusion), channel_id=1, source_target_pairs={{0,1},{1,0},{2,3},{3,2},{4,5},{5,4},{6,7},{7,6},{8,9},{9,8},{10,11... | collective-permute-start | bytes 4030472 | tf_op jit(solution)/shard_map/ppermute | solution.py:763
  94.6 40.6 %collective-permute-start.6 = (bf16[2,656,512]{2,1,0:T(8,128)(2,1)S(1)}, bf16[2,656,512]{2,1,0:T(8,128)(2,1)S(1)}, u32[]{:S(2)}, u32[]{:S(2)}) collective-permute-start(bf16[2,656,512]{2,1,0:T(8,128)(2,1)S(1)} %collective-permute-done.5.refs_5_.refs_3_), channel_id=1, source_target_pairs={{0,4},{1,5},{2,6},{3,7},{4,0},{5,1},{6,2},{7,3},{8,12},{9,13},{10,... | collective-permute-start | bytes 4030472 | tf_op jit(solution)/shard_map/ppermute | solution.py:763
  95.9 42.0 %collective-permute-start.7 = (bf16[2,656,512]{2,1,0:T(8,128)(2,1)S(1)}, bf16[2,656,512]{2,1,0:T(8,128)(2,1)S(1)}, u32[]{:S(2)}, u32[]{:S(2)}) collective-permute-start(bf16[2,656,512]{2,1,0:T(8,128)(2,1)S(1)} %collective-permute-done.5.refs_5_.refs_3_), channel_id=1, source_target_pairs={{0,2},{1,3},{2,0},{3,1},{4,6},{5,7},{6,4},{7,5},{8,10},{9,11},{10,... | collective-permute-start | bytes 4030472 | tf_op jit(solution)/shard_map/ppermute | solution.py:763
  134.6 3.3 collective-permute-start.10
  135.2 4.6 collective-permute-start.8
  199.5 48.3 %collective-permute-start.11 = (bf16[1,656,1024]{2,1,0:T(8,128)(2,1)}, bf16[1,656,1024]{2,1,0:T(8,128)(2,1)S(1)}, u32[]{:S(2)}, u32[]{:S(2)}) collective-permute-start(bf16[1,656,1024]{2,1,0:T(8,128)(2,1)} %trade_outer.3.refs_2_), channel_id=1, source_target_pairs={{0,1},{1,0},{2,3},{3,2},{4,5},{5,4},{6,7},{7,6},{8,9},{9,8},{10,11... | collective-permute-start | bytes 4030472 | tf_op jit(solution)/shard_map/ppermute | solution.py:763
  211.7 52.9 %collective-permute-start.13 = (bf16[1,656,1024]{2,1,0:T(8,128)(2,1)}, bf16[1,656,1024]{2,1,0:T(8,128)(2,1)S(1)}, u32[]{:S(2)}, u32[]{:S(2)}) collective-permute-start(bf16[1,656,1024]{2,1,0:T(8,128)(2,1)} %trade_outer.4.refs_2_), channel_id=1, source_target_pairs={{0,1},{1,0},{2,3},{3,2},{4,5},{5,4},{6,7},{7,6},{8,9},{9,8},{10,11... | collective-permute-start | bytes 4030472 | tf_op jit(solution)/shard_map/ppermute | solution.py:763
  246.3 16.9 %collective-permute-start.12 = (bf16[64,1024]{1,0:T(8,128)(2,1)S(1)}, bf16[64,1024]{1,0:T(8,128)(2,1)S(1)}, u32[]{:S(2)}, u32[]{:S(2)}) collective-permute-start(bf16[64,1024]{1,0:T(8,128)(2,1)S(1)} %pad_maximum_fusion), channel_id=1, source_target_pairs={{0,1},{1,0},{2,3},{3,2},{4,5},{5,4},{6,7},{7,6},{8,9},{9,8},{10,11... | collective-permute-start | bytes 393224 | tf_op jit(solution)/shard_map/ppermute | solution.py:763
  268.8 32.2 %collective-permute-start.14 = (bf16[2,656,512]{2,1,0:T(8,128)(2,1)S(1)}, bf16[2,656,512]{2,1,0:T(8,128)(2,1)}, u32[]{:S(2)}, u32[]{:S(2)}) collective-permute-start(bf16[2,656,512]{2,1,0:T(8,128)(2,1)S(1)} %get-tuple-element.145), channel_id=1, source_target_pairs={{0,4},{1,5},{2,6},{3,7},{4,0},{5,1},{6,2},{7,3},{8,12},{9,13},{10,... | collective-permute-start | bytes 4030472 | tf_op jit(solution)/shard_map/ppermute | solution.py:763
  269.5 60.2 %collective-permute-start.16 = (bf16[1,912,1024]{2,1,0:T(8,128)(2,1)S(1)}, bf16[1,912,1024]{2,1,0:T(8,128)(2,1)}, u32[]{:S(2)}, u32[]{:S(2)}) collective-permute-start(bf16[1,912,1024]{2,1,0:T(8,128)(2,1)S(1)} %copy-done.17), channel_id=1, source_target_pairs={{0,1},{1,0},{2,3},{3,2},{4,5},{5,4},{6,7},{7,6},{8,9},{9,8},{10,11... | collective-permute-start | bytes 5603336 | tf_op jit(solution)/shard_map/ppermute | solution.py:763
  289.2 11.8 %copy-start.3 = (bf16[2,656,512]{2,1,0:T(8,128)(2,1)S(1)}, bf16[2,656,512]{2,1,0:T(8,128)(2,1)}, u32[]{:S(2)}) copy-start(bf16[2,656,512]{2,1,0:T(8,128)(2,1)} %get-tuple-element.114.refs_10_) | copy-start | bytes 4030468
  303.5 26.1 %collective-permute-start.15 = (bf16[2,656,256]{2,1,0:T(8,128)(2,1)S(1)}, bf16[2,656,256]{2,1,0:T(8,128)(2,1)S(1)}, u32[]{:S(2)}, u32[]{:S(2)}) collective-permute-start(bf16[2,656,256]{2,1,0:T(8,128)(2,1)S(1)} %get-tuple-element.150), channel_id=1, source_target_pairs={{0,8},{1,9},{2,10},{3,11},{4,12},{5,13},{6,14},{7,15},{8,0},{9,1},... | collective-permute-start | bytes 2015240 | tf_op jit(solution)/shard_map/ppermute | solution.py:763
  305.2 9.3 %collective-permute-start.17 = (bf16[64,1024]{1,0:T(8,128)(2,1)S(1)}, bf16[64,1024]{1,0:T(8,128)(2,1)S(1)}, u32[]{:S(2)}, u32[]{:S(2)}) collective-permute-start(bf16[64,1024]{1,0:T(8,128)(2,1)S(1)} %pad_maximum_fusion.1), channel_id=1, source_target_pairs={{0,1},{1,0},{2,3},{3,2},{4,5},{5,4},{6,7},{7,6},{8,9},{9,8},{10,11... | collective-permute-start | bytes 393224 | tf_op jit(solution)/shard_map/ppermute | solution.py:763
  314.5 15.1 %copy-start.27 = (bf16[64,1024]{1,0:T(8,128)(2,1)}, bf16[64,1024]{1,0:T(8,128)(2,1)S(1)}, u32[]{:S(2)}) copy-start(bf16[64,1024]{1,0:T(8,128)(2,1)S(1)} %collective-permute-done.17) | copy-start | bytes 393220
  314.5 38.2 %collective-permute-start.19 = (bf16[3,1024,256]{2,1,0:T(8,128)(2,1)}, bf16[3,1024,256]{2,1,0:T(8,128)(2,1)}, u32[]{:S(2)}, u32[]{:S(2)}) collective-permute-start(bf16[3,1024,256]{2,1,0:T(8,128)(2,1)} %trade_attn.2), channel_id=1, source_target_pairs={{0,1},{1,0},{2,3},{3,2},{4,5},{5,4},{6,7},{7,6},{8,9},{9,8},{10,11... | collective-permute-start | bytes 4718600 | tf_op jit(solution)/shard_map/ppermute | solution.py:763
  315.5 14.1 %copy-start.9 = (bf16[2,656,256]{2,1,0:T(8,128)(2,1)S(1)}, bf16[2,656,256]{2,1,0:T(8,128)(2,1)}, u32[]{:S(2)}) copy-start(bf16[2,656,256]{2,1,0:T(8,128)(2,1)} %get-tuple-element.115.refs_4_) | copy-start | bytes 2015236
  334.2 17.4 %collective-permute-start.18 = (bf16[1,912,512]{2,1,0:T(8,128)(2,1)}, bf16[1,912,512]{2,1,0:T(8,128)(2,1)S(1)}, u32[]{:S(2)}, u32[]{:S(2)}) collective-permute-start(bf16[1,912,512]{2,1,0:T(8,128)(2,1)} %get-tuple-element.146), channel_id=1, source_target_pairs={{0,4},{1,5},{2,10},{3,11},{4,0},{5,1},{6,14},{7,15},{8,12},{9,13},... | collective-permute-start | bytes 2801672 | tf_op jit(solution)/shard_map/ppermute | solution.py:763
  335.8 32.3 %collective-permute-start.20 = (bf16[2,656,256]{2,1,0:T(8,128)(2,1)S(1)}, bf16[2,656,256]{2,1,0:T(8,128)(2,1)}, u32[]{:S(2)}, u32[]{:S(2)}) collective-permute-start(bf16[2,656,256]{2,1,0:T(8,128)(2,1)S(1)} %add.215), channel_id=1, source_target_pairs={{0,16},{1,17},{2,18},{3,19},{4,20},{5,21},{6,22},{7,23},{8,24},{9,... | collective-permute-start | bytes 2015240 | tf_op jit(solution)/shard_map/ppermute | solution.py:763
  369.4 23.1 %collective-permute-start.22 = (bf16[2,656,256]{2,1,0:T(8,128)(2,1)S(1)}, bf16[2,656,256]{2,1,0:T(8,128)(2,1)S(1)}, u32[]{:S(2)}, u32[]{:S(2)}) collective-permute-start(bf16[2,656,256]{2,1,0:T(8,128)(2,1)S(1)} %add.224.refs_8_), channel_id=1, source_target_pairs={{0,8},{1,9},{2,10},{3,11},{4,12},{5,13},{6,14},{7,15},{8,0},{9,1},... | collective-permute-start | bytes 2015240 | tf_op jit(solution)/shard_map/ppermute | solution.py:763
  369.4 36.0 %collective-permute-start.24 = (bf16[3,512,256]{2,1,0:T(8,128)(2,1)}, bf16[3,512,256]{2,1,0:T(8,128)(2,1)}, u32[]{:S(2)}, u32[]{:S(2)}) collective-permute-start(bf16[3,512,256]{2,1,0:T(8,128)(2,1)} %get-tuple-element.148), channel_id=1, source_target_pairs={{0,4},{1,5},{2,10},{3,11},{4,0},{5,1},{6,14},{7,15},{8,12},{9,13},... | collective-permute-start | bytes 2359304 | tf_op jit(solution)/shard_map/ppermute | solution.py:763
  371.0 31.5 %collective-permute-start.23 = (bf16[1,912,256]{2,1,0:T(8,128)(2,1)}, bf16[1,912,256]{2,1,0:T(8,128)(2,1)}, u32[]{:S(2)}, u32[]{:S(2)}) collective-permute-start(bf16[1,912,256]{2,1,0:T(8,128)(2,1)} %get-tuple-element.152), channel_id=1, source_target_pairs={{0,8},{1,9},{2,18},{3,19},{4,12},{5,13},{6,22},{7,23},{8,0},{9,1},... | collective-permute-start | bytes 1400840 | tf_op jit(solution)/shard_map/ppermute | solution.py:763
  391.4 12.6 %copy-start.30 = (f32[1,1024]{1,0:T(1,128)S(1)}, f32[1,1024]{1,0:T(1,128)}, u32[]{:S(2)}) copy-start(f32[1,1024]{1,0:T(1,128)} %get-tuple-element.125) | copy-start | bytes 12292
  391.4 12.6 %copy-start.31 = (f32[1,1024]{1,0:T(1,128)S(1)}, f32[1,1024]{1,0:T(1,128)}, u32[]{:S(2)}) copy-start(f32[1,1024]{1,0:T(1,128)} %get-tuple-element.124) | copy-start | bytes 12292
  394.1 12.7 %copy-start.14 = (bf16[2,656,512]{2,1,0:T(8,128)(2,1)}, bf16[2,656,512]{2,1,0:T(8,128)(2,1)S(1)}, u32[]{:S(2)}) copy-start(bf16[2,656,512]{2,1,0:T(8,128)(2,1)S(1)} %maximum_select_fusion.3) | copy-start | bytes 4030468
  394.1 53.2 %collective-permute-start.32 = (bf16[2,656,512]{2,1,0:T(8,128)(2,1)S(1)}, bf16[2,656,512]{2,1,0:T(8,128)(2,1)}, u32[]{:S(2)}, u32[]{:S(2)}) collective-permute-start(bf16[2,656,512]{2,1,0:T(8,128)(2,1)S(1)} %maximum_select_fusion.3), channel_id=1, source_target_pairs={{0,4},{1,5},{2,6},{3,7},{4,0},{5,1},{6,2},{7,3},{8,12},{9,13},{10,... | collective-permute-start | bytes 4030472 | tf_op jit(solution)/shard_map/ppermute | solution.py:763
  403.7 22.2 %collective-permute-start.26 = (bf16[1,912,256]{2,1,0:T(8,128)(2,1)S(1)}, bf16[1,912,256]{2,1,0:T(8,128)(2,1)S(1)}, u32[]{:S(2)}, u32[]{:S(2)}) collective-permute-start(bf16[1,912,256]{2,1,0:T(8,128)(2,1)S(1)} %add.227), channel_id=1, source_target_pairs={{0,16},{1,17},{2,6},{3,7},{4,20},{5,21},{6,2},{7,3},{8,24},{9,25},... | collective-permute-start | bytes 1400840 | tf_op jit(solution)/shard_map/ppermute | solution.py:763
  404.0 3.7 collective-permute-start.21
  407.7 18.4 %collective-permute-start.28 = (bf16[3,256,256]{2,1,0:T(8,128)(2,1)S(1)}, bf16[3,256,256]{2,1,0:T(8,128)(2,1)S(1)}, u32[]{:S(2)}, u32[]{:S(2)}) collective-permute-start(bf16[3,256,256]{2,1,0:T(8,128)(2,1)S(1)} %get-tuple-element.154), channel_id=1, source_target_pairs={{0,8},{1,9},{2,18},{3,19},{4,12},{5,13},{6,22},{7,23},{8,0},{9,1},... | collective-permute-start | bytes 1179656 | tf_op jit(solution)/shard_map/ppermute | solution.py:763
  410.2 15.9 %collective-permute-start.25 = (f32[2,1024]{1,0:T(2,128)S(1)}, f32[2,1024]{1,0:T(2,128)S(1)}, u32[]{:S(2)}, u32[]{:S(2)}) collective-permute-start(f32[2,1024]{1,0:T(2,128)S(1)} %fusion.1), channel_id=1, source_target_pairs={{0,2},{1,3},{2,0},{3,1},{4,6},{5,7},{6,4},{7,5},{8,10},{9,11},{10,... | collective-permute-start | bytes 24584 | tf_op jit(solution)/shard_map/ppermute | solution.py:763
  426.0 12.5 %collective-permute-start.29 = (bf16[1,912,256]{2,1,0:T(8,128)(2,1)S(1)}, bf16[1,912,256]{2,1,0:T(8,128)(2,1)S(1)}, u32[]{:S(2)}, u32[]{:S(2)}) collective-permute-start(bf16[1,912,256]{2,1,0:T(8,128)(2,1)S(1)} %add.231), channel_id=1, source_target_pairs={{0,8},{1,9},{2,18},{3,19},{4,12},{5,13},{6,22},{7,23},{8,0},{9,1},... | collective-permute-start | bytes 1400840 | tf_op jit(solution)/shard_map/ppermute | solution.py:763
  426.2 20.9 %collective-permute-start.30 = (bf16[3,256,256]{2,1,0:T(8,128)(2,1)S(1)}, bf16[3,256,256]{2,1,0:T(8,128)(2,1)S(1)}, u32[]{:S(2)}, u32[]{:S(2)}) collective-permute-start(bf16[3,256,256]{2,1,0:T(8,128)(2,1)S(1)} %add.234), channel_id=1, source_target_pairs={{0,16},{1,17},{2,6},{3,7},{4,20},{5,21},{6,2},{7,3},{8,24},{9,25},... | collective-permute-start | bytes 1179656 | tf_op jit(solution)/shard_map/ppermute | solution.py:763
  451.0 21.3 %copy-start.4 = (bf16[2,656,1024]{2,1,0:T(8,128)(2,1)}, bf16[2,656,1024]{2,1,0:T(8,128)(2,1)S(1)}, u32[]{:S(2)}) copy-start(bf16[2,656,1024]{2,1,0:T(8,128)(2,1)S(1)} %maximum_select_fusion.refs_1_) | copy-start | bytes 8060932
  451.0 21.3 %collective-permute-start.35 = (bf16[2,656,1024]{2,1,0:T(8,128)(2,1)S(1)}, bf16[2,656,1024]{2,1,0:T(8,128)(2,1)}, u32[]{:S(2)}, u32[]{:S(2)}) collective-permute-start(bf16[2,656,1024]{2,1,0:T(8,128)(2,1)S(1)} %maximum_select_fusion.refs_1_), channel_id=1, source_target_pairs={{0,2},{1,3},{2,0},{3,1},{4,6},{5,7},{6,4},{7,5},{8,10},{9,11},{10,... | collective-permute-start | bytes 8060936 | tf_op jit(solution)/shard_map/ppermute | solution.py:763
  454.2 14.0 %collective-permute-start.33 = (bf16[1,912,512]{2,1,0:T(8,128)(2,1)}, bf16[1,912,512]{2,1,0:T(8,128)(2,1)}, u32[]{:S(2)}, u32[]{:S(2)}) collective-permute-start(bf16[1,912,512]{2,1,0:T(8,128)(2,1)} %maximum_select_fusion.4), channel_id=1, source_target_pairs={{0,4},{1,5},{2,10},{3,11},{4,0},{5,1},{6,14},{7,15},{8,12},{9,13},... | collective-permute-start | bytes 2801672 | tf_op jit(solution)/shard_map/ppermute | solution.py:763
  456.1 23.5 %collective-permute-start.36 = (bf16[3,256,256]{2,1,0:T(8,128)(2,1)S(1)}, bf16[3,256,256]{2,1,0:T(8,128)(2,1)S(1)}, u32[]{:S(2)}, u32[]{:S(2)}) collective-permute-start(bf16[3,256,256]{2,1,0:T(8,128)(2,1)S(1)} %add.235), channel_id=1, source_target_pairs={{0,8},{1,9},{2,18},{3,19},{4,12},{5,13},{6,22},{7,23},{8,0},{9,1},... | collective-permute-start | bytes 1179656 | tf_op jit(solution)/shard_map/ppermute | solution.py:763
  456.1 12.1 %collective-permute-start.27 = (f32[2,1024]{1,0:T(2,128)S(1)}, f32[2,1024]{1,0:T(2,128)S(1)}, u32[]{:S(2)}, u32[]{:S(2)}) collective-permute-start(f32[2,1024]{1,0:T(2,128)S(1)} %fusion.5), channel_id=1, source_target_pairs={{0,4},{1,5},{2,6},{3,7},{4,0},{5,1},{6,2},{7,3},{8,12},{9,13},{10,... | collective-permute-start | bytes 24584 | tf_op jit(solution)/shard_map/ppermute | solution.py:763
  468.2 4.1 collective-permute-start.31
  479.8 12.1 %collective-permute-start.37 = (bf16[3,512,256]{2,1,0:T(8,128)(2,1)S(1)}, bf16[3,512,256]{2,1,0:T(8,128)(2,1)S(1)}, u32[]{:S(2)}, u32[]{:S(2)}) collective-permute-start(bf16[3,512,256]{2,1,0:T(8,128)(2,1)S(1)} %maximum_select_fusion.5), channel_id=1, source_target_pairs={{0,4},{1,5},{2,10},{3,11},{4,0},{5,1},{6,14},{7,15},{8,12},{9,13},... | collective-permute-start | bytes 2359304 | tf_op jit(solution)/shard_map/ppermute | solution.py:763
  481.8 21.9 %collective-permute-start.39 = (bf16[1,912,1024]{2,1,0:T(8,128)(2,1)S(1)}, bf16[1,912,1024]{2,1,0:T(8,128)(2,1)S(1)}, u32[]{:S(2)}, u32[]{:S(2)}) collective-permute-start(bf16[1,912,1024]{2,1,0:T(8,128)(2,1)S(1)} %copy-done.1), channel_id=1, source_target_pairs={{0,2},{1,3},{2,0},{3,1},{4,6},{5,7},{6,4},{7,5},{8,10},{9,11},{10,... | collective-permute-start | bytes 5603336 | tf_op jit(solution)/shard_map/ppermute | solution.py:763
  492.3 18.0 %collective-permute-start.38 = (bf16[3,1024,256]{2,1,0:T(8,128)(2,1)S(1)}, bf16[3,1024,256]{2,1,0:T(8,128)(2,1)S(1)}, u32[]{:S(2)}, u32[]{:S(2)}) collective-permute-start(bf16[3,1024,256]{2,1,0:T(8,128)(2,1)S(1)} %maximum_select_fusion.2.refs_3_.refs_1_), channel_id=1, source_target_pairs={{0,2},{1,3},{2,0},{3,1},{4,6},{5,7},{6,4},{7,5},{8,10},{9,11},{10,... | collective-permute-start | bytes 4718600 | tf_op jit(solution)/shard_map/ppermute | solution.py:763
  498.5 4.5 collective-permute-start.34
  (26 other events, 121.8 us)
